TPU v7x, 32 devices: a whole 2x2x4 slice. The times are simulated.
32 devices in a mesh: row: 4 (over x, core), col: 8 (over z, y).
Axes of the slice: x: 2, y: 2, z: 4, core: 2. Of those that a mesh axis runs over, the one named last changes fastest.
Arguments:
- trail: bfloat16 [8192, 8192], P('row', 'col'), may hold values from -0.0625 to 0.0625
- row_one: bfloat16 [128, 8192], P('row', 'col'), may hold values from -0.5 to 0.5
- row_two: bfloat16 [128, 8192], P('row', 'col'), may hold values from -0.5 to 0.5
- diag_one: float32 [128, 128], replicated, may hold values from -1 to 2, as said below
- diag_two: float32 [128, 128], replicated, may hold values from -1 to 2, as said below
- adj_trail: float32 [8192, 8192], P('row', 'col'), may hold values from -6 to 6
- adj_row_one: float32 [128, 8192], P('row', 'col'), may hold values from -6 to 6
- adj_row_two: float32 [128, 8192], P('row', 'col'), may hold values from -6 to 6
- adj_diag_one: float32 [128, 128], replicated, may hold values from -6 to 6
- adj_diag_two: float32 [128, 128], replicated, may hold values from -6 to 6
Outputs:
- grad_trail: bfloat16 [8192, 8192], P('row', 'col')
- grad_row_one: float32 [128, 8192], P('row', 'col')
- grad_row_two: float32 [128, 8192], P('row', 'col')
- grad_diag_one: float32 [128, 128], replicated
- grad_diag_two: float32 [128, 128], replicated
Inputs may be any that keep to these rules, and one draw needn't show every extreme that they name: `diag_one`: lower triangular with a positive diagonal. `diag_two`: lower triangular with a positive diagonal.
All inputs are finite; a program needn't handle non-finite values.
Results may differ from a plain program's by a relative error of at most 0.014.
Values may be sent and summed in bfloat16 or wider, within the bound.
No kernel may reach another device: no remote copies, remote signals or barrier semaphores. Data moves between devices by JAX's collectives and lax.ppermute only.
A program may use at most 128 MiB of HBM per device.

v0:
```python
import jax
import jax.numpy as jnp
from jax import lax
from jax.sharding import PartitionSpec as P

exact_mode = lax.Precision.HIGHEST


def from_root(value, axis, source):
    kept = jnp.where(lax.axis_index(axis) == source, value, 0).astype(value.dtype)
    return lax.psum(kept, axis)


def halved_lower(matrix):
    order = matrix.shape[0]
    keep = jnp.tril(jnp.ones((order, order), matrix.dtype)) - 0.5 * jnp.eye(
        order, dtype=matrix.dtype
    )
    return matrix * keep


def inverse_lower(block):
    ident = jnp.eye(block.shape[0], dtype=block.dtype)
    return lax.linalg.triangular_solve(block, ident, left_side=True, lower=True)


def block_adjoint(block, inverse, seed_adj):
    inner = halved_lower(jnp.dot(block.T, seed_adj, precision=exact_mode))
    middle = jnp.dot(inverse.T, inner, precision=exact_mode)
    return halved_lower(jnp.dot(middle, inverse, precision=exact_mode))


def per_device(
    trail,
    row_one,
    row_two,
    diag_one,
    diag_two,
    adj_trail,
    adj_row_one,
    adj_row_two,
    adj_diag_one,
    adj_diag_two,
):
    panel = diag_one.shape[0]
    width = trail.shape[1]
    band = row_one.shape[0]
    last = width - panel
    col_count = lax.axis_size("col")
    col_here = lax.axis_index("col")
    row_start = lax.axis_index("row") * band
    here_one = col_here == col_count - 2
    here_two = col_here == col_count - 1
    full_one, full_two = (
        lax.all_gather(row_one, "row", axis=0, tiled=True),
        lax.all_gather(row_two, "row", axis=0, tiled=True),
    )

    def own_rows(matrix):
        return lax.dynamic_slice_in_dim(matrix, row_start, band, 0)

    def solve_panel(rows, inverse, root):
        whole = from_root(rows, "col", root)
        return jnp.dot(whole, inverse, precision=exact_mode).astype(jnp.bfloat16)

    def summed_block(partial_value, root):
        rows_sum = lax.psum(partial_value, "row")
        return from_root(rows_sum, "col", root)

    inverse_two = inverse_lower(diag_two)
    solved_two = solve_panel(adj_trail[:, last:], inverse_two, col_count - 1)
    partial_two = jnp.dot(solved_two.T, trail[:, last:], preferred_element_type=jnp.float32)
    seed_two = jnp.tril(adj_diag_two - summed_block(partial_two, col_count - 1))
    grad_diag_two = block_adjoint(diag_two, inverse_two, seed_two)
    mirror_two = own_rows(grad_diag_two + grad_diag_two.T)
    rest_two = jnp.dot(mirror_two, full_two.astype(jnp.float32), precision=exact_mode)
    inverse_one = inverse_lower(diag_one)
    crossed = lax.psum_scatter(
        jnp.dot(solved_two.T, trail, preferred_element_type=jnp.float32).astype(jnp.bfloat16),
        "row",
        scatter_dimension=0,
        tiled=True,
    ).astype(jnp.float32)
    adj_two = adj_row_two - crossed - rest_two
    adj_next = adj_trail - jnp.dot(solved_two, full_two, preferred_element_type=jnp.float32)
    stacked = jnp.concatenate([adj_two[:, last:], adj_next[:, last:]], 0)
    solved_one = solve_panel(stacked, inverse_one, col_count - 2)
    head_rows = solved_one[:band]
    tail_rows = solved_one[band:]
    partial_one = jnp.dot(
        head_rows.T, row_two[:, last:], preferred_element_type=jnp.float32
    ) + jnp.dot(tail_rows.T, trail[:, last:], preferred_element_type=jnp.float32)
    seed_one = jnp.tril(adj_diag_one - summed_block(partial_one, col_count - 2))
    grad_diag_one = block_adjoint(diag_one, inverse_one, seed_one)
    mirror_one = own_rows(grad_diag_one + grad_diag_one.T)
    rest_one = jnp.dot(mirror_one, full_one.astype(jnp.float32), precision=exact_mode)
    head_update = jnp.dot(head_rows, full_one, preferred_element_type=jnp.float32)
    two_left = adj_two - head_update
    trail_left = adj_next - jnp.dot(tail_rows, full_one, preferred_element_type=jnp.float32)
    crossed_one = lax.psum_scatter(
        (
            jnp.dot(head_rows.T, row_two, preferred_element_type=jnp.float32)
            + jnp.dot(tail_rows.T, trail, preferred_element_type=jnp.float32)
        ).astype(jnp.bfloat16),
        "row",
        scatter_dimension=0,
        tiled=True,
    ).astype(jnp.float32)
    one_left = adj_row_one - crossed_one - rest_one
    trail_block = jnp.where(
        here_one,
        tail_rows.astype(jnp.float32),
        jnp.where(here_two, solved_two.astype(jnp.float32), trail_left[:, last:]),
    )
    grad_trail = jnp.concatenate([trail_left[:, :last], trail_block], 1).astype(jnp.bfloat16)
    zero_block = jnp.zeros((band, panel), jnp.float32)
    one_block = jnp.where(here_one | here_two, zero_block, one_left[:, last:])
    grad_row_one = jnp.concatenate([one_left[:, :last], one_block], 1)
    two_block = jnp.where(
        here_one, head_rows.astype(jnp.float32), jnp.where(here_two, zero_block, two_left[:, last:])
    )
    grad_row_two = jnp.concatenate([two_left[:, :last], two_block], 1)
    return (grad_trail, grad_row_one, grad_row_two, grad_diag_one, grad_diag_two)


def solution(mesh):
    in_specs = (
        P("row", "col"),
        P("row", "col"),
        P("row", "col"),
        P(),
        P(),
        P("row", "col"),
        P("row", "col"),
        P("row", "col"),
        P(),
        P(),
    )
    out_specs = (P("row", "col"), P("row", "col"), P("row", "col"), P(), P())
    return jax.shard_map(
        per_device, mesh=mesh, in_specs=in_specs, out_specs=out_specs, check_vma=False
    )
```

profile of v0, /device:TPU:0, one launch (start us, length us, event | category | flops | bytes accessed | tf_op | source)
XLA Modules:
  0.0 454.9 jit_solution(1923117250528483585)
XLA Ops:
  7.2 2.3 slice_select_fusion.1
  10.4 9.8 %custom-call.4 = f32[1,128,128]{1,2,0:T(8,128)S(1)} custom-call(f32[1,128,128]{2,1,0:T(8,128)S(1)} %select_bitcast_fusion.1), custom_call_target="InvertDiagBlocksLowerTriangular" | custom-call | tf_op jit(solution)/shard_map/triangular_solve/custom-call.1 | solution.py:24
  20.2 7.4 %all_gather.6 = bf16[128,1024]{1,0:T(8,128)(2,1)S(1)} all-gather(bf16[32,1024]{1,0:T(8,128)(2,1)} %param.14), channel_id=1, replica_groups=mesh['row'=4,'col'=8] {'row'}, dimensions={0}, use_global_device_ids=true | all-gather | bytes 327680 | tf_op jit(solution)/shard_map/all_gather | solution.py:56
  28.0 64.9 %all-reduce.7.cloned.1.call-done = f32[2048,128]{1,0:T(8,128)} async-done(((f32[2048,128]{1,0:T(8,128)}), f32[2048,128]{1,0:T(8,128)}) %all-reduce.7.cloned.1.call-update) | async-done | bytes 1048592 | tf_op jit(solution)/shard_map/psum | solution.py:11
  92.8 2.2 convolution_convert_fusion.1
  95.0 2.0 fusion.6
  97.1 7.8 %convolution_subtract_fusion.1 = f32[2048,1024]{1,0:T(8,128)} fusion(f32[2048,1024]{1,0:T(8,128)} %param.17, bf16[2048,128]{1,0:T(8,128)(2,1)S(1)} %convolution_convert_fusion.1, bf16[128,1024]{1,0:T(8,128)(2,1)S(1)} %all_gather.6), kind=kOutput, calls=%fused_computation.2 | convolution fusion | flops 538968064 | bytes 17563648 | tf_op jit(solution)/shard_map/dot_general | solution.py:85
  105.0 22.9 %all-reduce.9.cloned.1.call-done = f32[128,128]{1,0:T(8,128)} async-done(((f32[128,128]{1,0:T(8,128)}), f32[128,128]{1,0:T(8,128)}) %all-reduce.9.cloned.1.call-update) | async-done | bytes 65552 | tf_op jit(solution)/shard_map/psum | solution.py:67
  128.6 3.7 convolution_convert_fusion.2
  132.4 68.0 %all-reduce.11.cloned.1.call-done = f32[128,128]{1,0:T(8,128)} async-done(((f32[128,128]{1,0:T(8,128)}), f32[128,128]{1,0:T(8,128)}) %all-reduce.11.cloned.1.call-update) | async-done | bytes 65552 | tf_op jit(solution)/shard_map/psum | solution.py:11
  202.1 21.1 %reduce-scatter.7.cloned.1.call-done = bf16[32,1024]{1,0:T(8,128)(2,1)} async-done(((bf16[128,1024]{1,0:T(8,128)(2,1)}), bf16[32,1024]{1,0:T(8,128)(2,1)}) %reduce-scatter.7.cloned.1.call-update) | async-done | bytes 65552 | tf_op jit(solution)/shard_map/reduce_scatter | solution.py:78
  225.5 9.8 %custom-call.5 = f32[1,128,128]{1,2,0:T(8,128)S(1)} custom-call(f32[1,128,128]{2,1,0:T(8,128)S(1)} %select_bitcast_fusion), custom_call_target="InvertDiagBlocksLowerTriangular" | custom-call | tf_op jit(solution)/shard_map/triangular_solve/custom-call.1 | solution.py:24
  235.4 6.0 %all_gather.7 = bf16[128,1024]{1,0:T(8,128)(2,1)S(1)} all-gather(bf16[32,1024]{1,0:T(8,128)(2,1)S(1)} %copy-done.8), channel_id=1, replica_groups=mesh['row'=4,'col'=8] {'row'}, dimensions={0}, use_global_device_ids=true | all-gather | bytes 327680 | tf_op jit(solution)/shard_map/all_gather | solution.py:55
  241.6 64.7 %all-reduce.13.cloned.1.call-done = f32[2080,128]{1,0:T(8,128)} async-done(((f32[2080,128]{1,0:T(8,128)}), f32[2080,128]{1,0:T(8,128)}) %all-reduce.13.cloned.1.call-update) | async-done | bytes 1064976 | tf_op jit(solution)/shard_map/psum | solution.py:11
  306.3 2.2 convolution_convert_fusion
  308.5 4.6 %convolution_subtract_fusion = bf16[2048,1024]{1,0:T(8,128)(2,1)S(1)} fusion(f32[2048,1024]{1,0:T(8,128)} %convolution_subtract_fusion.1, bf16[128,1024]{1,0:T(8,128)(2,1)S(1)} %all_gather.7, bf16[2080,128]{1,0:T(8,128)(2,1)S(1)} %convolution_convert_fusion), kind=kOutput, calls=%fused_computation.1 | convolution fusion | flops 541065216 | bytes 13369344 | tf_op jit(solution)/shard_map/dot_general | solution.py:99
  313.4 2.3 slice.97
  316.9 1.5 fusion
  318.4 2.0 convolution_add_fusion.1
  320.5 4.7 %pad_maximum_fusion = bf16[2048,1024]{1,0:T(8,128)(2,1)} fusion(bf16[2048,128]{1,0:T(8,128)(2,1)S(1)} %fusion.4, bf16[2048,896]{1,0:T(8,128)(2,1)} %slice.97), kind=kLoop, calls=%fused_computation.3 | loop fusion | flops 8388608 | bytes 8388608 | tf_op jit(solution)/shard_map/concatenate | solution.py:115
  325.4 25.4 %all-reduce.15.cloned.1.call-done = f32[128,128]{1,0:T(8,128)} async-done(((f32[128,128]{1,0:T(8,128)}), f32[128,128]{1,0:T(8,128)}) %all-reduce.15.cloned.1.call-update) | async-done | bytes 65552 | tf_op jit(solution)/shard_map/psum | solution.py:67
  352.9 70.8 %all-reduce.17.cloned.1.call-done = f32[128,128]{1,0:T(8,128)} async-done(((f32[128,128]{1,0:T(8,128)}), f32[128,128]{1,0:T(8,128)}) %all-reduce.17.cloned.1.call-update) | async-done | bytes 65552 | tf_op jit(solution)/shard_map/psum | solution.py:11
  423.7 1.1 fusion.1
  425.4 20.9 %reduce-scatter.9.cloned.1.call-done = bf16[32,1024]{1,0:T(8,128)(2,1)} async-done(((bf16[128,1024]{1,0:T(8,128)(2,1)}), bf16[32,1024]{1,0:T(8,128)(2,1)}) %reduce-scatter.9.cloned.1.call-update) | async-done | bytes 65552 | tf_op jit(solution)/shard_map/reduce_scatter | solution.py:100
  (68 shorter events, 12.3 us)
Async XLA Ops:
  7.2 85.7 %all-reduce.7.cloned.1.call-start = ((), (), s32[]{:S(2)}) async-start(), calls=%async_computation.2 | async-start | bytes 2097152 | tf_op jit(solution)/shard_map/psum | solution.py:11
  9.5 118.4 %all-reduce.9.cloned.1.call-start = ((), (), s32[]{:S(2)}) async-start(), calls=%async_computation.3 | async-start | bytes 131072 | tf_op jit(solution)/shard_map/psum | solution.py:67
  97.1 103.3 %all-reduce.11.cloned.1.call-start = ((), (), s32[]{:S(2)}) async-start(), calls=%async_computation.4 | async-start | bytes 131072 | tf_op jit(solution)/shard_map/psum | solution.py:11
  105.0 95.4 %copy-start.2 = (f32[128,128]{1,0:T(8,128)S(1)}, f32[128,128]{1,0:T(8,128)}, u32[]{:S(2)}) copy-start(f32[128,128]{1,0:T(8,128)} %param.16) | copy-start | bytes 196612
  105.0 95.4 %copy-start.9 = (f32[128,128]{1,0:T(8,128)S(1)}, f32[128,128]{1,0:T(8,128)}, u32[]{:S(2)}) copy-start(f32[128,128]{1,0:T(8,128)} %param.21) | copy-start | bytes 196612
  105.0 118.3 %copy-start.4 = (f32[32,1024]{1,0:T(8,128)S(1)}, f32[32,1024]{1,0:T(8,128)}, u32[]{:S(2)}) copy-start(f32[32,1024]{1,0:T(8,128)} %param.19) | copy-start | bytes 393220
  128.5 95.8 %slice-start = ((f32[2048,1024]{1,0:T(8,128)}), f32[2048,128]{1,0:T(8,128)S(1)}, s32[]{:S(2)}) async-start(f32[2048,1024]{1,0:T(8,128)} %convolution_subtract_fusion.1), calls=%async_computation.10 | async-start | bytes 2097152 | tf_op jit(solution)/shard_map/slice | solution.py:86
  128.6 94.7 %reduce-scatter.7.cloned.1.call-start = ((), (), s32[]{:S(2)}) async-start(), calls=%async_computation.8 | async-start | bytes 327680 | tf_op jit(solution)/shard_map/reduce_scatter | solution.py:78
  132.3 93.2 %copy-start.3 = (f32[128,128]{1,0:T(8,128)S(1)}, f32[128,128]{1,0:T(8,128)}, u32[]{:S(2)}) copy-start(f32[128,128]{1,0:T(8,128)} %param.15) | copy-start | bytes 196612
  132.3 103.0 %copy-start.8 = (bf16[32,1024]{1,0:T(8,128)(2,1)S(1)}, bf16[32,1024]{1,0:T(8,128)(2,1)}, u32[]{:S(2)}) copy-start(bf16[32,1024]{1,0:T(8,128)(2,1)} %param.13) | copy-start | bytes 196612
  132.4 173.9 %all-reduce.13.cloned.1.call-start = ((), (), s32[]{:S(2)}) async-start(), calls=%async_computation.5 | async-start | bytes 2129920 | tf_op jit(solution)/shard_map/psum | solution.py:11
  202.0 111.1 %copy-start.6 = (f32[128,128]{1,0:T(8,128)}, f32[128,128]{1,0:T(8,128)S(1)}, u32[]{:S(2)}) copy-start(f32[128,128]{1,0:T(8,128)S(1)} %get-tuple-element.16) | copy-start | bytes 196612
  225.5 125.3 %all-reduce.15.cloned.1.call-start = ((), (), s32[]{:S(2)}) async-start(), calls=%async_computation.6 | async-start | bytes 131072 | tf_op jit(solution)/shard_map/psum | solution.py:67
  313.4 2.3 copy-start.1
  313.4 3.5 copy-start
  320.4 103.2 %copy-start.10 = (f32[128,128]{1,0:T(8,128)S(1)}, f32[128,128]{1,0:T(8,128)}, u32[]{:S(2)}) copy-start(f32[128,128]{1,0:T(8,128)} %param.20) | copy-start | bytes 196612
  320.5 125.8 %copy-start.5 = (f32[32,1024]{1,0:T(8,128)S(1)}, f32[32,1024]{1,0:T(8,128)}, u32[]{:S(2)}) copy-start(f32[32,1024]{1,0:T(8,128)} %param.18) | copy-start | bytes 393220
  320.5 103.2 %all-reduce.17.cloned.1.call-start = ((), (), s32[]{:S(2)}) async-start(), calls=%async_computation.7 | async-start | bytes 131072 | tf_op jit(solution)/shard_map/psum | solution.py:11
  351.4 94.8 %reduce-scatter.9.cloned.1.call-start = ((), (), s32[]{:S(2)}) async-start(), calls=%async_computation.9 | async-start | bytes 327680 | tf_op jit(solution)/shard_map/reduce_scatter | solution.py:100
  425.3 22.7 %copy-start.7 = (f32[128,128]{1,0:T(8,128)}, f32[128,128]{1,0:T(8,128)S(1)}, u32[]{:S(2)}) copy-start(f32[128,128]{1,0:T(8,128)S(1)} %get-tuple-element.18) | copy-start | bytes 196612
Sparse Core Ops, SparseCore 0:
  12.1 80.7 all-reduce.6
  97.2 30.6 all-reduce.8
  131.9 68.4 all-reduce.10
  203.3 19.9 reduce-scatter.6
  227.6 78.6 all-reduce.12
  320.6 30.1 all-reduce.14
  355.1 68.4 all-reduce.16
  426.3 19.9 reduce-scatter.8
where the time goes:
time: 456 us; the launch traced here: 455 us
  waiting for transfers between devices  359 us (79%)
  matrix products  32.6 us (7%)
  other arithmetic  31.4 us (7%)
  between operations  14.5 us (3%)
  blocking collectives  13.4 us (3%)
    psum x4, waiting for transfers between devices, from_root(): return lax.psum(kept, axis)  268 us
    psum x2, waiting for transfers between devices, summed_block(): rows_sum = lax.psum(partial_value, 'row')  48.3 us
    reduce_scatter x1, waiting for transfers between devices, per_device(): lax.psum_scatter(jnp.dot(solved_two.T, trail, preferred_element_type=jnp....  21.1 us
    reduce_scatter x1, waiting for transfers between devices, per_device(): lax.psum_scatter((jnp.dot(head_rows.T, row_two, preferred_element_type=jn...  20.9 us
    another operation x2, other arithmetic, inverse_lower(): return lax.linalg.triangular_solve(block, ident, left_side=True, lower=True)  19.6 us
  transfers between devices with their start and end apart: 8, of which 8 were waited for; matrix products, arithmetic and copies ran while one was open for 9% of the time, Pallas kernels for 0%

commit v1 on v0

v1 whole, which is shorter than its diff:
```python
import jax
import jax.numpy as jnp
from jax import lax
from jax.sharding import PartitionSpec as P

EXACT = lax.Precision.HIGHEST
F32 = jnp.float32
BF16 = jnp.bfloat16


def exact_dot(a, b):
    return jnp.dot(a, b, precision=EXACT)


def wide_dot(a, b):
    return jnp.dot(a, b, preferred_element_type=F32)


def halved_lower(matrix):
    order = matrix.shape[0]
    rows = lax.broadcasted_iota(jnp.int32, (order, order), 0)
    cols = lax.broadcasted_iota(jnp.int32, (order, order), 1)
    return jnp.where(rows > cols, matrix, jnp.where(rows == cols, 0.5 * matrix, 0))


def inverse_lower(blocks):
    order = blocks.shape[-1]
    rows = lax.broadcasted_iota(jnp.int32, (order, order), 0)
    cols = lax.broadcasted_iota(jnp.int32, (order, order), 1)
    diag = jnp.sum(jnp.where(rows == cols, blocks, 0), 2)
    recip = 1.0 / diag
    inverse = jnp.where(rows == cols, recip[:, :, None], 0)
    size = 1
    while size < order:
        pair = rows // (2 * size) == cols // (2 * size)
        below = (rows // size) % 2 > (cols // size) % 2
        corner = jnp.where(pair & below, blocks, 0)
        if size == 1:
            change = recip[:, :, None] * corner * recip[:, None, :]
        else:
            change = jnp.matmul(
                jnp.matmul(inverse, corner, precision=EXACT), inverse, precision=EXACT
            )
        inverse = inverse - change
        size *= 2
    return inverse


def block_adjoint(block, inverse, seed_adj):
    inner = halved_lower(exact_dot(block.T, seed_adj))
    middle = exact_dot(inverse.T, inner)
    return halved_lower(exact_dot(middle, inverse))


def per_device(
    trail,
    row_one,
    row_two,
    diag_one,
    diag_two,
    adj_trail,
    adj_row_one,
    adj_row_two,
    adj_diag_one,
    adj_diag_two,
):
    panel = diag_one.shape[0]
    height, width = trail.shape
    band = row_one.shape[0]
    last = width - panel
    row_count = lax.axis_size("row")
    col_count = lax.axis_size("col")
    levels = col_count // 2
    row_here = lax.axis_index("row")
    col_here = lax.axis_index("col")
    row_start = row_here * band
    level = col_here // 2
    is_two = col_here % 2 == 1
    here_one = col_here == col_count - 2
    here_two = col_here == col_count - 1

    def own_rows(matrix):
        return lax.dynamic_slice_in_dim(matrix, row_start, band, 0)

    def row_swap(value, step):
        return lax.ppermute(value, "row", [(i, i ^ step) for i in range(row_count)])

    def pair_swap(value, which):
        pairs = [(2 * k + s, 2 * k + 1 - s) for k in which for s in range(2)]
        return lax.ppermute(value, "col", pairs)

    def spread(value):
        step = levels // 2
        holders = [0]
        while step >= 1:
            hops = [(d, d + step) for d in holders]
            pairs = []
            arrived = jnp.zeros((), jnp.bool_)
            for source, target in hops:
                for s in range(2):
                    pairs.append(
                        (
                            2 * (levels - 1 - source) + s,
                            2 * (levels - 1 - target) + s,
                        )
                    )
                arrived = arrived | (level == levels - 1 - target)
            value = jnp.where(arrived, lax.ppermute(value, "col", pairs), value)
            holders += [target for _, target in hops]
            step //= 2
        return value

    rows_all = jnp.stack([row_two, row_one])[:, None]
    step = 1
    while step < row_count:
        other = row_swap(rows_all, step)
        low = (row_here // step) % 2 == 0
        rows_all = jnp.concatenate(
            [jnp.where(low, rows_all, other), jnp.where(low, other, rows_all)], 1
        )
        step *= 2
    full_two = rows_all[0].reshape(panel, width)
    full_one = rows_all[1].reshape(panel, width)

    inverses = inverse_lower(jnp.stack([diag_one, diag_two]))
    inverse_one, inverse_two = inverses[0], inverses[1]
    solved = exact_dot(
        adj_trail[:, last:], jnp.where(is_two, inverse_two, inverse_one)
    ).astype(BF16)
    packet = jnp.concatenate([solved, full_two[:, last:]], 0)

    def tail_of(own, other):
        solved_two = jnp.where(is_two, own[:height], other[:height])
        base_one = jnp.where(is_two, other[:height], own[:height])
        cross = jnp.where(is_two, other[height:], own[height:])
        carried = exact_dot(cross.astype(F32), inverse_one)
        high = carried.astype(BF16)
        low = (carried - high.astype(F32)).astype(BF16)
        tail = base_one.astype(F32) - wide_dot(
            jnp.concatenate([solved_two, solved_two], 1), jnp.concatenate([high, low], 0)
        )
        return solved_two, tail.astype(BF16), cross

    top_other = pair_swap(packet, [levels - 1])
    top_two, top_tail, _ = tail_of(packet, top_other)
    terms = wide_dot(jnp.concatenate([top_two, top_tail], 1).T, trail[:, last:])
    placed = lax.dynamic_update_slice_in_dim(
        jnp.zeros((2 * panel, panel), F32),
        jnp.where(is_two, 0, adj_row_two[:, last:]),
        row_start,
        0,
    )
    terms = terms - placed
    step = 1
    while step < row_count:
        terms = terms + row_swap(terms, step)
        step *= 2
    terms = spread(terms.astype(BF16))
    terms_other = pair_swap(terms, range(levels))
    terms, terms_other = terms.astype(F32), terms_other.astype(F32)
    diag_term_two = jnp.where(is_two, terms[:panel], terms_other[:panel])
    crossing = jnp.where(is_two, terms_other[:panel], terms[:panel])
    diag_term_one = jnp.where(is_two, terms_other[panel:], terms[panel:])

    packet = spread(packet)
    packet_other = pair_swap(packet, range(levels - 1))
    packet_other = jnp.where(level == levels - 1, top_other, packet_other)
    solved_two, tail, cross = tail_of(packet, packet_other)
    both = jnp.concatenate([solved_two, tail], 1)
    sums = wide_dot(both.T, trail).reshape(2, panel, width)

    grad_diag_two = block_adjoint(
        diag_two, inverse_two, jnp.tril(adj_diag_two - diag_term_two)
    )
    mirror_two = grad_diag_two + grad_diag_two.T
    adj_two = -crossing - exact_dot(mirror_two, cross.astype(F32))
    head = exact_dot(adj_two, inverse_one).astype(BF16)
    seed_one = jnp.tril(adj_diag_one - wide_dot(head.T, cross) - diag_term_one)
    grad_diag_one = block_adjoint(diag_one, inverse_one, seed_one)
    mirror_one = grad_diag_one + grad_diag_one.T

    parts = sums.reshape(2, row_count, band, width)
    step = 1
    while step < row_count:
        low = (row_here // step) % 2 == 0
        parts = parts.reshape(2, -1, 2, band, width)
        keep = jnp.where(low, parts[:, :, 0], parts[:, :, 1])
        give = jnp.where(low, parts[:, :, 1], parts[:, :, 0])
        parts = keep + row_swap(give.astype(BF16), step).astype(F32)
        step *= 2
    parts = parts.reshape(2, band, width)

    head_wide = head.astype(F32)
    mix_two = jnp.concatenate([own_rows(mirror_two), own_rows(head_wide)], 1)
    mix_one = jnp.concatenate([own_rows(head_wide.T), own_rows(mirror_one)], 1)
    full_both = jnp.concatenate([full_two, full_one], 0)
    mixed = exact_dot(jnp.concatenate([mix_two, mix_one], 0), full_both.astype(F32))
    two_left = adj_row_two - mixed[:band] - parts[0]
    one_left = adj_row_one - mixed[band:] - parts[1]

    trail_left = adj_trail - wide_dot(both, full_both)
    column = lax.broadcasted_iota(jnp.int32, (1, width), 1)
    in_block = column >= last

    def put(matrix, block_one, block_two):
        block = jnp.where(here_one, block_one, block_two).astype(F32)
        block = jnp.pad(block, ((0, 0), (last, 0)))
        return jnp.where(in_block & (here_one | here_two), block, matrix)

    grad_trail = put(trail_left, tail, solved_two).astype(BF16)
    nothing = jnp.zeros((band, panel), F32)
    grad_row_one = put(one_left, nothing, nothing)
    grad_row_two = put(two_left, own_rows(head_wide), nothing)
    return (grad_trail, grad_row_one, grad_row_two, grad_diag_one, grad_diag_two)


def solution(mesh):
    split = P("row", "col")
    in_specs = (split, split, split, P(), P(), split, split, split, P(), P())
    out_specs = (split, split, split, P(), P())
    return jax.shard_map(
        per_device, mesh=mesh, in_specs=in_specs, out_specs=out_specs, check_vma=False
    )
```

time: 456 us -> 108 us (0.24)
  waiting for transfers between devices: 359 us -> 65.2 us
  other arithmetic: 31.4 us -> 4.87 us
  matrix products: 32.6 us -> 17.6 us
  starting transfers between devices: 0.33 us -> 15.3 us
  blocking collectives: 13.4 us -> 0 us
  between operations: 14.5 us -> 1.43 us
    psum x6 -> x0, waiting for transfers between devices: 317 us -> none  [the longest x4 268 us: from_root(): return lax.psum(kept, axis)]
    ppermute x0 -> x13, waiting for transfers between devices: none -> 65.2 us  [the longest x4 38 us: spread(): value = jnp.where(arrived, lax.ppermute(value, 'col', pairs), value)]
    reduce_scatter x2 -> x0, waiting for transfers between devices: 42 us -> none  [the longest x1 21.1 us: per_device(): lax.psum_scatter(jnp.dot(solved_two.T, trail, preferred_element_type=jnp....]
    another operation x3 -> x0, other arithmetic: 19.9 us -> none  [the longest x2 19.6 us: inverse_lower(): return lax.linalg.triangular_solve(block, ident, left_side=True, lower=True)]
    ppermute x0 -> x13, starting transfers between devices: none -> 15.3 us  [the longest x3 5.71 us: pair_swap(): return lax.ppermute(value, 'col', pairs)]
    dot_general x19 -> x30, matrix products: 32 us -> 17.6 us  [the longest x6 6.65 us: wide_dot(): return jnp.dot(a, b, preferred_element_type=F32)]
    all_gather x2 -> x0, blocking collectives: 13.4 us -> none  [the longest x1 7.41 us: per_device(): lax.all_gather(row_two, 'row', axis=0, tiled=True)]
    concatenate x3, other arithmetic: 6.02 us -> 0.11 us  [the longest x2 0.08 us: per_device(): jnp.concatenate([jnp.where(low, rows_all, other), jnp.where(low, other, r...]
  transfers between devices with their start and end apart: 8 -> 13, of which waited for: 8 -> 8; matrix products, arithmetic and copies ran while one was open for 9% -> 14% of each run, Pallas kernels for 0% -> 0%
where the time goes in v1:
time: 108 us; the launch traced here: 107 us
  waiting for transfers between devices  65.2 us (60%)
  matrix products  17.6 us (16%)
  starting transfers between devices  15.3 us (14%)
  other arithmetic  4.87 us (5%)
  local copies, waits for them, and re-layouts  3.05 us (3%)
  between operations  1.43 us (1%)
    ppermute x4, waiting for transfers between devices, spread(): value = jnp.where(arrived, lax.ppermute(value, 'col', pairs), value)  38 us
    ppermute x3, waiting for transfers between devices, pair_swap(): return lax.ppermute(value, 'col', pairs)  14.1 us
    ppermute x6, waiting for transfers between devices, row_swap(): return lax.ppermute(value, 'row', [(i, i ^ step) for i in range(row_count)])  13.1 us
    dot_general x6, matrix products, wide_dot(): return jnp.dot(a, b, preferred_element_type=F32)  6.65 us
    ppermute x3, starting transfers between devices, pair_swap(): return lax.ppermute(value, 'col', pairs)  5.71 us
    ppermute x6, starting transfers between devices, row_swap(): return lax.ppermute(value, 'row', [(i, i ^ step) for i in range(row_count)])  5.67 us
    dot_general x12, matrix products, exact_dot(): return jnp.dot(a, b, precision=EXACT)  4.89 us
    ppermute x4, starting transfers between devices, spread(): value = jnp.where(arrived, lax.ppermute(value, 'col', pairs), value)  3.93 us
  transfers between devices with their start and end apart: 13, of which 8 were waited for; matrix products, arithmetic and copies ran while one was open for 14% of the time, Pallas kernels for 0%

profile of v1, /device:TPU:0, one launch (start us, length us, event | category | flops | bytes accessed | tf_op | source)
XLA Modules:
  0.0 107.4 jit_solution(2165195787036630896)
XLA Ops:
  2.3 1.0 select_reduce_fusion
  3.4 1.3 %fusion.31 = f32[2,128,128]{2,1,0:T(8,128)S(1)} fusion(f32[2,128]{1,0:T(2,128)S(1)} %broadcast_divide_fusion, pred[128,128]{1,0:T(8,128)(4,1)S(1)} %get-tuple-element.31, pred[128,128]{1,0:T(8,128)(4,1)S(1)} %get-tuple-element.30, pred[128,128]{1,0:T(8,128)(4,1)S(1)} %iota_compare_fusion.7, f32[1,128,128]{2,1,0:T(8,128)} %bitcast.112, ...), kind=kOutput, calls=%fused_computation.117 | convolution fusion | flops 50593792 | bytes 312320 | tf_op jit(solution)/shard_map/dot_general | solution.py:42
  4.7 1.2 %convolution_subtract_fusion.5 = f32[2,128,128]{2,1,0:T(8,128)S(1)} fusion(f32[2,128,128]{2,1,0:T(8,128)S(1)} %fusion.31, f32[2,128]{1,0:T(2,128)S(1)} %broadcast_divide_fusion, pred[128,128]{1,0:T(8,128)(4,1)S(1)} %get-tuple-element.30, pred[128,128]{1,0:T(8,128)(4,1)S(1)} %iota_compare_fusion.7, f32[1,128,128]{2,1,0:T(8,128)} %bitcast.113, ...), kind=kOutput, calls=%fused_computation.12 | convolution fusion | flops 50561024 | bytes 427008 | tf_op jit(solution)/shard_map/dot_general | solution.py:41
  6.4 1.1 %fusion.29 = f32[2,128,128]{2,1,0:T(8,128)S(1)} fusion(f32[2,128,128]{2,1,0:T(8,128)S(1)} %convolution_subtract_fusion.5, pred[128,128]{1,0:T(8,128)(4,1)S(1)} %get-tuple-element.29, f32[1,128,128]{2,1,0:T(8,128)} %bitcast.114, f32[1,128,128]{2,1,0:T(8,128)} %bitcast.122), kind=kOutput, calls=%fused_computation.115 | convolution fusion | flops 50397184 | bytes 409600 | tf_op jit(solution)/shard_map/dot_general | solution.py:42
  10.1 2.6 %collective-permute-start.1 = (bf16[2,2,32,1024]{3,2,0,1:T(8,128)(2,1)S(1)}, bf16[2,2,32,1024]{3,2,0,1:T(8,128)(2,1)S(1)}, u32[]{:S(2)}, u32[]{:S(2)}) collective-permute-start(bf16[2,2,32,1024]{3,2,0,1:T(8,128)(2,1)S(1)} %pad_maximum_fusion.16), channel_id=1, source_target_pairs={{0,16},{8,24},{16,0},{24,8},{1,17},{9,25},{17,1},{25,9},{2,18},{10... | collective-permute-start | bytes 786440 | tf_op jit(solution)/shard_map/ppermute | solution.py:86
  12.7 2.2 %fusion = bf16[2048,128]{1,0:T(8,128)(2,1)S(1)} fusion(f32[2048,1024]{1,0:T(8,128)} %param.15, f32[2,128,128]{2,1,0:T(8,128)S(1)} %convolution_subtract_fusion, pred[]{:T(512)S(6)} %eq.100), kind=kOutput, calls=%fused_computation.2 | convolution fusion | flops 402931712 | bytes 1703937 | tf_op jit(solution)/shard_map/dot_general | solution.py:12
  14.9 4.7 %collective-permute-done.1 = bf16[2,2,32,1024]{3,2,0,1:T(8,128)(2,1)S(1)} collective-permute-done((bf16[2,2,32,1024]{3,2,0,1:T(8,128)(2,1)S(1)}, bf16[2,2,32,1024]{3,2,0,1:T(8,128)(2,1)S(1)}, u32[]{:S(2)}, u32[]{:S(2)}) %collective-permute-start.1) | collective-permute-done | bytes 262176 | tf_op jit(solution)/shard_map/ppermute | solution.py:86
  21.3 1.5 %convolution_subtract_fusion.6 = f32[256,128]{1,0:T(8,128)S(1)} fusion(f32[256,128]{1,0:T(8,128)S(1)} %select_dynamic-update-slice_fusion, bf16[2048,128]{1,0:T(8,128)(2,1)S(1)} %broadcast_select_fusion.3, bf16[2048,128]{1,0:T(8,128)(2,1)S(1)} %subtract_convert_fusion, bf16[2048,1024]{1,0:T(8,128)(2,1)} %param.10), kind=kOutput, calls=%fused_computation.13 | convolution fusion | flops 136347648 | bytes 1835008 | tf_op jit(solution)/shard_map/dot_general | solution.py:16
  22.9 1.3 %collective-permute-done.6 = f32[256,128]{1,0:T(8,128)S(1)} collective-permute-done((f32[256,128]{1,0:T(8,128)S(1)}, f32[256,128]{1,0:T(8,128)S(1)}, u32[]{:S(2)}, u32[]{:S(2)}) %collective-permute-start.6) | collective-permute-done | bytes 131104 | tf_op jit(solution)/shard_map/ppermute | solution.py:86
  24.2 1.8 %collective-permute-start.7 = (f32[256,128]{1,0:T(8,128)S(1)}, f32[256,128]{1,0:T(8,128)S(1)}, u32[]{:S(2)}, u32[]{:S(2)}) collective-permute-start(f32[256,128]{1,0:T(8,128)S(1)} %add.157), channel_id=1, source_target_pairs={{0,16},{8,24},{16,0},{24,8},{1,17},{9,25},{17,1},{25,9},{2,18},{10... | collective-permute-start | bytes 393224 | tf_op jit(solution)/shard_map/ppermute | solution.py:86
  26.7 3.1 %collective-permute-done.7 = f32[256,128]{1,0:T(8,128)S(1)} collective-permute-done((f32[256,128]{1,0:T(8,128)S(1)}, f32[256,128]{1,0:T(8,128)S(1)}, u32[]{:S(2)}, u32[]{:S(2)}) %collective-permute-start.7) | collective-permute-done | bytes 131104 | tf_op jit(solution)/shard_map/ppermute | solution.py:86
  30.6 1.3 %collective-permute-start.9 = (bf16[256,128]{1,0:T(8,128)(2,1)S(1)}, bf16[256,128]{1,0:T(8,128)(2,1)S(1)}, u32[]{:S(2)}, u32[]{:S(2)}) collective-permute-start(bf16[256,128]{1,0:T(8,128)(2,1)S(1)} %broadcast_select_fusion.10), channel_id=1, source_target_pairs={{6,4},{7,5},{2,0},{3,1},{14,12},{15,13},{10,8},{11,9},{22,20},{23,... | collective-permute-start | bytes 196616 | tf_op jit(solution)/shard_map/ppermute | solution.py:108
  32.1 1.3 %collective-permute-start.4 = (bf16[2176,128]{1,0:T(8,128)(2,1)S(1)}, bf16[2176,128]{1,0:T(8,128)(2,1)S(1)}, u32[]{:S(2)}, u32[]{:S(2)}) collective-permute-start(bf16[2176,128]{1,0:T(8,128)(2,1)S(1)} %broadcast_select_fusion), channel_id=1, source_target_pairs={{6,4},{7,5},{2,0},{3,1},{14,12},{15,13},{10,8},{11,9},{22,20},{23,... | collective-permute-start | bytes 1671176 | tf_op jit(solution)/shard_map/ppermute | solution.py:108
  33.4 31.6 %collective-permute-done.9 = bf16[256,128]{1,0:T(8,128)(2,1)S(1)} collective-permute-done((bf16[256,128]{1,0:T(8,128)(2,1)S(1)}, bf16[256,128]{1,0:T(8,128)(2,1)S(1)}, u32[]{:S(2)}, u32[]{:S(2)}) %collective-permute-start.9) | collective-permute-done | bytes 65568 | tf_op jit(solution)/shard_map/ppermute | solution.py:108
  65.0 1.6 %collective-permute-start.10 = (bf16[256,128]{1,0:T(8,128)(2,1)S(1)}, bf16[256,128]{1,0:T(8,128)(2,1)S(1)}, u32[]{:S(2)}, u32[]{:S(2)}) collective-permute-start(bf16[256,128]{1,0:T(8,128)(2,1)S(1)} %get-tuple-element.10), channel_id=1, source_target_pairs={{0,1},{1,0},{2,3},{3,2},{4,5},{5,4},{6,7},{7,6},{8,9},{9,8},{10,11... | collective-permute-start | bytes 196616 | tf_op jit(solution)/shard_map/ppermute | solution.py:90
  66.6 2.7 %collective-permute-done.10 = bf16[256,128]{1,0:T(8,128)(2,1)S(1)} collective-permute-done((bf16[256,128]{1,0:T(8,128)(2,1)S(1)}, bf16[256,128]{1,0:T(8,128)(2,1)S(1)}, u32[]{:S(2)}, u32[]{:S(2)}) %collective-permute-start.10) | collective-permute-done | bytes 65568 | tf_op jit(solution)/shard_map/ppermute | solution.py:90
  70.0 6.4 %collective-permute-done.4 = bf16[2176,128]{1,0:T(8,128)(2,1)S(1)} collective-permute-done((bf16[2176,128]{1,0:T(8,128)(2,1)S(1)}, bf16[2176,128]{1,0:T(8,128)(2,1)S(1)}, u32[]{:S(2)}, u32[]{:S(2)}) %collective-permute-start.4) | collective-permute-done | bytes 557088 | tf_op jit(solution)/shard_map/ppermute | solution.py:108
  76.4 3.4 %collective-permute-start.5 = (bf16[2176,128]{1,0:T(8,128)(2,1)S(1)}, bf16[2176,128]{1,0:T(8,128)(2,1)S(1)}, u32[]{:S(2)}, u32[]{:S(2)}) collective-permute-start(bf16[2176,128]{1,0:T(8,128)(2,1)S(1)} %broadcast_select_fusion.1), channel_id=1, source_target_pairs={{0,1},{1,0},{2,3},{3,2},{4,5},{5,4},{8,9},{9,8},{10,11},{11,10},{1... | collective-permute-start | bytes 1671176 | tf_op jit(solution)/shard_map/ppermute | solution.py:90
  80.8 11.3 %collective-permute-done.5 = bf16[2176,128]{1,0:T(8,128)(2,1)S(1)} collective-permute-done((bf16[2176,128]{1,0:T(8,128)(2,1)S(1)}, bf16[2176,128]{1,0:T(8,128)(2,1)S(1)}, u32[]{:S(2)}, u32[]{:S(2)}) %collective-permute-start.5) | collective-permute-done | bytes 557088 | tf_op jit(solution)/shard_map/ppermute | solution.py:90
  94.1 1.4 %copy-done.9 = bf16[2048,1024]{1,0:T(8,128)(2,1)S(1)} copy-done((bf16[2048,1024]{1,0:T(8,128)(2,1)S(1)}, bf16[2048,1024]{1,0:T(8,128)(2,1)}, u32[]{:S(2)}) %copy-start.9) | copy-done | bytes 4194328
  95.5 1.3 %fusion.9 = f32[256,1024]{1,0:T(8,128)S(1)} fusion(bf16[2048,1024]{1,0:T(8,128)(2,1)S(1)} %copy-done.9, bf16[2048,128]{1,0:T(8,128)(2,1)S(1)} %broadcast_select_fusion.4, bf16[2048,128]{1,0:T(8,128)(2,1)S(1)} %get-tuple-element.33), kind=kOutput, calls=%fused_computation.28 | convolution fusion | flops 1075838976 | bytes 6291456 | tf_op jit(solution)/shard_map/dot_general | solution.py:16
  97.1 1.1 %slice-done.1 = s8[4194304]{0:T(1024)(128)(4,1)S(1)} async-done(((s8[8388608]{0:T(1024)(128)(4,1)}), s8[4194304]{0:T(1024)(128)(4,1)S(1)}, s32[]{:S(2)}) %slice-start.1) | async-done | bytes 4194328
  98.2 2.8 %select_convert_fusion = bf16[2048,1024]{1,0:T(8,128)(2,1)} fusion(f32[2048,1024]{1,0:T(8,128)S(1)} %bitcast.110, bf16[2048,128]{1,0:T(8,128)(2,1)S(1)} %get-tuple-element.32, pred[1024]{0:T(1024)(128)(4,1)S(1)} %fusion.137, bf16[2048,128]{1,0:T(8,128)(2,1)S(1)} %broadcast_select_fusion.4, bf16[2048,128]{1,0:T(8,128)(2,1)S(1)} %get-tuple-element.33, ...), kind=kOutput, calls=%fused_computation | convolution fusion | flops 1085276160 | bytes 14681088 | tf_op jit(solution)/shard_map/dot_general | solution.py:16
  102.6 4.0 %collective-permute-done.12 = bf16[2,1,32,1024]{3,2,1,0:T(8,128)(2,1)S(1)} collective-permute-done((bf16[2,1,32,1024]{3,2,1,0:T(8,128)(2,1)S(1)}, bf16[2,1,32,1024]{3,2,1,0:T(8,128)(2,1)S(1)}, u32[]{:S(2)}, u32[]{:S(2)}) %collective-permute-start.12) | collective-permute-done | bytes 131104 | tf_op jit(solution)/shard_map/ppermute | solution.py:86
  (111 shorter events, 13.9 us)
Async XLA Ops:
  0.6 7.2 %copy-start = (f32[128,128]{1,0:T(8,128)S(1)}, f32[128,128]{1,0:T(8,128)}, u32[]{:S(2)}) copy-start(f32[128,128]{1,0:T(8,128)} %param.14) | copy-start | bytes 196612
  0.6 7.2 %copy-start.1 = (f32[128,128]{1,0:T(8,128)S(1)}, f32[128,128]{1,0:T(8,128)}, u32[]{:S(2)}) copy-start(f32[128,128]{1,0:T(8,128)} %param.13) | copy-start | bytes 196612
  1.6 8.4 %collective-permute-start = (bf16[2,1,32,1024]{3,2,0,1:T(8,128)(2,1)S(1)}, bf16[2,1,32,1024]{3,2,0,1:T(8,128)(2,1)S(1)}, u32[]{:S(2)}, u32[]{:S(2)}) collective-permute-start(bf16[2,1,32,1024]{3,2,0,1:T(8,128)(2,1)S(1)} %maximum_bitcast_fusion), channel_id=1, source_target_pairs={{0,8},{8,0},{16,24},{24,16},{1,9},{9,1},{17,25},{25,17},{2,10},{10... | collective-permute-start | bytes 393224 | tf_op jit(solution)/shard_map/ppermute | solution.py:86
  5.9 4.1 %copy-start.2 = (bf16[32,1024]{1,0:T(8,128)(2,1)S(1)}, bf16[32,1024]{1,0:T(8,128)(2,1)}, u32[]{:S(2)}) copy-start(bf16[32,1024]{1,0:T(8,128)(2,1)} %param.11) | copy-start | bytes 196612
  6.0 4.1 %copy-start.3 = (bf16[32,1024]{1,0:T(8,128)(2,1)S(1)}, bf16[32,1024]{1,0:T(8,128)(2,1)}, u32[]{:S(2)}) copy-start(bf16[32,1024]{1,0:T(8,128)(2,1)} %param.12) | copy-start | bytes 196612
  10.1 9.5 %collective-permute-start.1 = (bf16[2,2,32,1024]{3,2,0,1:T(8,128)(2,1)S(1)}, bf16[2,2,32,1024]{3,2,0,1:T(8,128)(2,1)S(1)}, u32[]{:S(2)}, u32[]{:S(2)}) collective-permute-start(bf16[2,2,32,1024]{3,2,0,1:T(8,128)(2,1)S(1)} %pad_maximum_fusion.16), channel_id=1, source_target_pairs={{0,16},{8,24},{16,0},{24,8},{1,17},{9,25},{17,1},{25,9},{2,18},{10... | collective-permute-start | bytes 786440 | tf_op jit(solution)/shard_map/ppermute | solution.py:86
  14.9 5.6 %copy-start.4 = (f32[32,1024]{1,0:T(8,128)S(1)}, f32[32,1024]{1,0:T(8,128)}, u32[]{:S(2)}) copy-start(f32[32,1024]{1,0:T(8,128)} %param.17) | copy-start | bytes 393220
  19.8 0.8 collective-permute-start.2
  22.8 46.6 %copy-start.7 = (f32[128,128]{1,0:T(8,128)S(1)}, f32[128,128]{1,0:T(8,128)}, u32[]{:S(2)}) copy-start(f32[128,128]{1,0:T(8,128)} %param.19) | copy-start | bytes 196612
  22.8 1.4 %collective-permute-start.6 = (f32[256,128]{1,0:T(8,128)S(1)}, f32[256,128]{1,0:T(8,128)S(1)}, u32[]{:S(2)}, u32[]{:S(2)}) collective-permute-start(f32[256,128]{1,0:T(8,128)S(1)} %convolution_subtract_fusion.6), channel_id=1, source_target_pairs={{0,8},{8,0},{16,24},{24,16},{1,9},{9,1},{17,25},{25,17},{2,10},{10... | collective-permute-start | bytes 393224 | tf_op jit(solution)/shard_map/ppermute | solution.py:86
  24.2 5.6 %collective-permute-start.7 = (f32[256,128]{1,0:T(8,128)S(1)}, f32[256,128]{1,0:T(8,128)S(1)}, u32[]{:S(2)}, u32[]{:S(2)}) collective-permute-start(f32[256,128]{1,0:T(8,128)S(1)} %add.157), channel_id=1, source_target_pairs={{0,16},{8,24},{16,0},{24,8},{1,17},{9,25},{17,1},{25,9},{2,18},{10... | collective-permute-start | bytes 393224 | tf_op jit(solution)/shard_map/ppermute | solution.py:86
  26.0 5.9 %collective-permute-start.3 = (bf16[2176,128]{1,0:T(8,128)(2,1)S(1)}, bf16[2176,128]{1,0:T(8,128)(2,1)S(1)}, u32[]{:S(2)}, u32[]{:S(2)}) collective-permute-start(bf16[2176,128]{1,0:T(8,128)(2,1)S(1)} %pad_maximum_fusion.11), channel_id=1, source_target_pairs={{6,2},{7,3},{14,10},{15,11},{22,18},{23,19},{30,26},{31,27}} | collective-permute-start | bytes 1671176 | tf_op jit(solution)/shard_map/ppermute | solution.py:108
  29.9 0.7 collective-permute-start.8
  30.6 34.4 %collective-permute-start.9 = (bf16[256,128]{1,0:T(8,128)(2,1)S(1)}, bf16[256,128]{1,0:T(8,128)(2,1)S(1)}, u32[]{:S(2)}, u32[]{:S(2)}) collective-permute-start(bf16[256,128]{1,0:T(8,128)(2,1)S(1)} %broadcast_select_fusion.10), channel_id=1, source_target_pairs={{6,4},{7,5},{2,0},{3,1},{14,12},{15,13},{10,8},{11,9},{22,20},{23,... | collective-permute-start | bytes 196616 | tf_op jit(solution)/shard_map/ppermute | solution.py:108
  32.1 44.3 %collective-permute-start.4 = (bf16[2176,128]{1,0:T(8,128)(2,1)S(1)}, bf16[2176,128]{1,0:T(8,128)(2,1)S(1)}, u32[]{:S(2)}, u32[]{:S(2)}) collective-permute-start(bf16[2176,128]{1,0:T(8,128)(2,1)S(1)} %broadcast_select_fusion), channel_id=1, source_target_pairs={{6,4},{7,5},{2,0},{3,1},{14,12},{15,13},{10,8},{11,9},{22,20},{23,... | collective-permute-start | bytes 1671176 | tf_op jit(solution)/shard_map/ppermute | solution.py:108
  65.0 4.3 %collective-permute-start.10 = (bf16[256,128]{1,0:T(8,128)(2,1)S(1)}, bf16[256,128]{1,0:T(8,128)(2,1)S(1)}, u32[]{:S(2)}, u32[]{:S(2)}) collective-permute-start(bf16[256,128]{1,0:T(8,128)(2,1)S(1)} %get-tuple-element.10), channel_id=1, source_target_pairs={{0,1},{1,0},{2,3},{3,2},{4,5},{5,4},{6,7},{7,6},{8,9},{9,8},{10,11... | collective-permute-start | bytes 196616 | tf_op jit(solution)/shard_map/ppermute | solution.py:90
  76.4 15.7 %collective-permute-start.5 = (bf16[2176,128]{1,0:T(8,128)(2,1)S(1)}, bf16[2176,128]{1,0:T(8,128)(2,1)S(1)}, u32[]{:S(2)}, u32[]{:S(2)}) collective-permute-start(bf16[2176,128]{1,0:T(8,128)(2,1)S(1)} %broadcast_select_fusion.1), channel_id=1, source_target_pairs={{0,1},{1,0},{2,3},{3,2},{4,5},{5,4},{8,9},{9,8},{10,11},{11,10},{1... | collective-permute-start | bytes 1671176 | tf_op jit(solution)/shard_map/ppermute | solution.py:90
  80.8 12.1 %copy-start.8 = (f32[128,128]{1,0:T(8,128)S(1)}, f32[128,128]{1,0:T(8,128)}, u32[]{:S(2)}) copy-start(f32[128,128]{1,0:T(8,128)} %param.18) | copy-start | bytes 196612
  93.7 3.4 %slice-start = ((s8[8388608]{0:T(1024)(128)(4,1)}), s8[4194304]{0:T(1024)(128)(4,1)S(1)}, s32[]{:S(2)}) async-start(s8[8388608]{0:T(1024)(128)(4,1)} %bitcast.109), calls=%async_computation | async-start | bytes 8388608
  95.5 2.7 %slice-start.1 = ((s8[8388608]{0:T(1024)(128)(4,1)}), s8[4194304]{0:T(1024)(128)(4,1)S(1)}, s32[]{:S(2)}) async-start(s8[8388608]{0:T(1024)(128)(4,1)} %bitcast.109), calls=%async_computation.1 | async-start | bytes 8388608
  97.0 4.4 %collective-permute-start.11 = (bf16[2,2,32,1024]{3,2,0,1:T(8,128)(2,1)S(1)}, bf16[2,2,32,1024]{3,2,0,1:T(8,128)(2,1)S(1)}, u32[]{:S(2)}, u32[]{:S(2)}) collective-permute-start(bf16[2,2,32,1024]{3,2,0,1:T(8,128)(2,1)S(1)} %fusion.14), channel_id=1, source_target_pairs={{0,8},{8,0},{16,24},{24,16},{1,9},{9,1},{17,25},{25,17},{2,10},{10... | collective-permute-start | bytes 786440 | tf_op jit(solution)/shard_map/ppermute | solution.py:86
  101.2 5.4 %copy-start.6 = (f32[128,128]{1,0:T(8,128)}, f32[128,128]{1,0:T(8,128)S(1)}, u32[]{:S(2)}) copy-start(f32[128,128]{1,0:T(8,128)S(1)} %get-tuple-element.34) | copy-start | bytes 196612
  101.4 5.2 %copy-start.5 = (f32[32,1024]{1,0:T(8,128)S(1)}, f32[32,1024]{1,0:T(8,128)}, u32[]{:S(2)}) copy-start(f32[32,1024]{1,0:T(8,128)} %param.16) | copy-start | bytes 393220
  101.6 5.0 %collective-permute-start.12 = (bf16[2,1,32,1024]{3,2,1,0:T(8,128)(2,1)S(1)}, bf16[2,1,32,1024]{3,2,1,0:T(8,128)(2,1)S(1)}, u32[]{:S(2)}, u32[]{:S(2)}) collective-permute-start(bf16[2,1,32,1024]{3,2,1,0:T(8,128)(2,1)S(1)} %fusion.16), channel_id=1, source_target_pairs={{0,16},{8,24},{16,0},{24,8},{1,17},{9,25},{17,1},{25,9},{2,18},{10... | collective-permute-start | bytes 393224 | tf_op jit(solution)/shard_map/ppermute | solution.py:86
  (1 other events, 2.2 us)

commit v2 on v1

v2 whole, which is shorter than its diff:
```python
import functools

import jax
import jax.numpy as jnp
from jax import lax
from jax.experimental import pallas as pl
from jax.experimental.pallas import tpu as pltpu
from jax.sharding import PartitionSpec as P

EXACT = lax.Precision.HIGHEST
F32 = jnp.float32
BF16 = jnp.bfloat16
PIECES = 3


def exact_dot(a, b):
    return jnp.dot(a, b, precision=EXACT, preferred_element_type=F32)


def wide_dot(a, b):
    return jnp.dot(a, b, preferred_element_type=F32)


def halves(value):
    high = value.astype(BF16)
    return high, (value - high.astype(F32)).astype(BF16)


def halved_lower(matrix):
    order = matrix.shape[0]
    rows = lax.broadcasted_iota(jnp.int32, (order, order), 0)
    cols = lax.broadcasted_iota(jnp.int32, (order, order), 1)
    return jnp.where(rows > cols, matrix, jnp.where(rows == cols, 0.5 * matrix, 0))


def inverse_lower(blocks):
    order = blocks[0].shape[-1]
    rows = lax.broadcasted_iota(jnp.int32, (order, order), 0)
    cols = lax.broadcasted_iota(jnp.int32, (order, order), 1)
    equal = rows == cols
    inverses = []
    for block in blocks:
        recip_col = 1.0 / jnp.sum(jnp.where(equal, block, 0), 1, keepdims=True)
        recip_row = 1.0 / jnp.sum(jnp.where(equal, block, 0), 0, keepdims=True)
        pair = ((rows ^ cols) == 1) & (rows > cols)
        corner = jnp.where(pair, block, 0)
        inverses.append(jnp.where(equal, recip_col, 0) - recip_col * corner * recip_row)
    size = 2
    while size < order:
        below = ((rows ^ cols) & -size == size) & (rows > cols)
        below = below & ((rows ^ cols) < 2 * size)
        inner = [
            exact_dot(jnp.where(below, block, 0), inverse)
            for block, inverse in zip(blocks, inverses)
        ]
        inverses = [
            inverse - exact_dot(inverse, part) for inverse, part in zip(inverses, inner)
        ]
        size *= 2
    return inverses


def prepare_kernel(cuts, side_ref, one_ref, two_ref, rows_ref, inv_one_ref, inv_two_ref, *out_refs):
    inverse_one, inverse_two = inverse_lower([one_ref[...], two_ref[...]])
    inv_one_ref[...] = inverse_one
    inv_two_ref[...] = inverse_two
    chosen = jnp.where(side_ref[0] == 1, inverse_two, inverse_one)
    high, low = halves(chosen)
    for (start, size), out_ref in zip(cuts, out_refs):
        own_high, own_low = halves(rows_ref[start : start + size, :])
        product = wide_dot(own_high, high) + (
            wide_dot(own_high, low) + wide_dot(own_low, high)
        )
        out_ref[...] = product.astype(BF16)


def prepare(side, diag_one, diag_two, adj_trail, cuts):
    height, width = adj_trail.shape
    panel = diag_one.shape[0]
    square = pl.BlockSpec((panel, panel), lambda i: (0, 0))
    return pl.pallas_call(
        functools.partial(prepare_kernel, cuts),
        grid=(1,),
        in_specs=[
            pl.BlockSpec(memory_space=pltpu.SMEM),
            square,
            square,
            pl.BlockSpec((height, panel), lambda i: (0, width // panel - 1)),
        ],
        out_specs=[square, square]
        + [pl.BlockSpec((size, panel), lambda i: (0, 0)) for _, size in cuts],
        out_shape=[jax.ShapeDtypeStruct((panel, panel), F32)] * 2
        + [jax.ShapeDtypeStruct((size, panel), BF16) for _, size in cuts],
        compiler_params=pltpu.CompilerParams(vmem_limit_bytes=32 * 2**20),
        cost_estimate=pl.CostEstimate(
            flops=8 * height * panel * panel, bytes_accessed=6 * height * panel, transcendentals=0
        ),
        name="prepare",
    )(side, diag_one, diag_two, adj_trail)


def block_adjoint(block, inverse, seed_adj):
    inner = halved_lower(exact_dot(block.T, seed_adj))
    middle = exact_dot(inverse.T, inner)
    return halved_lower(exact_dot(middle, inverse))


def per_device(
    trail,
    row_one,
    row_two,
    diag_one,
    diag_two,
    adj_trail,
    adj_row_one,
    adj_row_two,
    adj_diag_one,
    adj_diag_two,
):
    panel = diag_one.shape[0]
    height, width = trail.shape
    band = row_one.shape[0]
    last = width - panel
    row_count = lax.axis_size("row")
    col_count = lax.axis_size("col")
    levels = col_count // 2
    top = levels - 1
    row_here = lax.axis_index("row")
    col_here = lax.axis_index("col")
    row_start = row_here * band
    level = col_here // 2
    is_two = col_here % 2 == 1
    here_one = col_here == col_count - 2
    here_two = col_here == col_count - 1
    step_rows = -(-height // (16 * PIECES)) * 16
    cuts = [(at, min(step_rows, height - at)) for at in range(0, height, step_rows)]

    def own_rows(matrix):
        return lax.dynamic_slice_in_dim(matrix, row_start, band, 0)

    def row_swap(value, step):
        return lax.ppermute(value, "row", [(i, i ^ step) for i in range(row_count)])

    def pair_swap(value, which):
        pairs = [(2 * k + s, 2 * k + 1 - s) for k in which for s in range(2)]
        return lax.ppermute(value, "col", pairs)

    def gather_rows(value):
        value = value[None]
        step = 1
        while step < row_count:
            other = row_swap(value, step)
            low = (row_here // step) % 2 == 0
            value = jnp.concatenate(
                [jnp.where(low, value, other), jnp.where(low, other, value)], 0
            )
            step *= 2
        return value.reshape(panel, width)

    def spread(value):
        held = {top: value}

        def pick(which):
            groups = []
            for k in which:
                for group in groups:
                    if group[0] is held[k]:
                        group[1].append(k)
                        break
                else:
                    groups.append((held[k], [k]))
            chosen = groups[0][0]
            for array, members in groups[1:]:
                at = functools.reduce(jnp.logical_or, [level == k for k in members])
                chosen = jnp.where(at, array, chosen)
            return chosen

        def send(hops):
            operand = pick([source for source, _ in hops])
            pairs = [(2 * a + s, 2 * b + s) for a, b in hops for s in range(2)]
            arrived = lax.ppermute(operand, "col", pairs)
            return {target: arrived for _, target in hops}

        if levels > 1:
            span = levels // 2
            held.update(send([(top, span - 1)]))
            fresh = [span - 1]
            span //= 2
            while span >= 1:
                up = send([(k, k + span) for k in fresh])
                down = send([(k, k - span) for k in fresh])
                held.update(up)
                held.update(down)
                fresh = [k + d * span for k in fresh for d in (1, -1)]
                span //= 2
        return pick(list(range(levels - 1))) if levels > 1 else value

    full_two = gather_rows(row_two)
    side = is_two.astype(jnp.int32)[None]
    inverse_one, inverse_two, *solved = prepare(side, diag_one, diag_two, adj_trail, cuts)
    cross_piece = min(1, len(cuts) - 1)
    packets = [
        jnp.concatenate([piece, full_two[:, last:]], 0) if k == cross_piece else piece
        for k, piece in enumerate(solved)
    ]

    def cross_factor(own, other):
        size = cuts[cross_piece][1]
        cross = jnp.where(is_two, other[size:], own[size:])
        return cross, jnp.concatenate(halves(exact_dot(cross.astype(F32), inverse_one)), 0)

    def panels_of(own, other, factor, size):
        solved_two = jnp.where(is_two, own[:size], other[:size])
        base_one = jnp.where(is_two, other[:size], own[:size])
        tail = base_one.astype(F32) - wide_dot(
            jnp.concatenate([solved_two, solved_two], 1), factor
        )
        return jnp.concatenate([solved_two, tail.astype(BF16)], 1)

    arrived = [spread(packet) for packet in packets]
    top_other = [pair_swap(packet, [top]) for packet in packets]
    low_other = [pair_swap(packet, range(levels - 1)) for packet in arrived]

    _, top_factor = cross_factor(packets[cross_piece], top_other[cross_piece])
    terms = 0
    for k, (start, size) in enumerate(cuts):
        top_both = panels_of(packets[k], top_other[k], top_factor, size)
        terms = terms + wide_dot(top_both.T, trail[start : start + size, last:])
    placed = lax.dynamic_update_slice_in_dim(
        jnp.zeros((2 * panel, panel), F32),
        jnp.where(is_two, 0, adj_row_two[:, last:]),
        row_start,
        0,
    )
    terms = terms - placed
    step = 1
    while step < row_count:
        terms = terms + row_swap(terms, step)
        step *= 2
    terms = terms.astype(BF16)
    terms = jnp.where(level == top, terms, spread(terms))
    terms_other = pair_swap(terms, range(levels))
    terms, terms_other = terms.astype(F32), terms_other.astype(F32)
    diag_term_two = jnp.where(is_two, terms[:panel], terms_other[:panel])
    crossing = jnp.where(is_two, terms_other[:panel], terms[:panel])
    diag_term_one = jnp.where(is_two, terms_other[panel:], terms[panel:])

    at_top = level == top
    own = [jnp.where(at_top, a, b) for a, b in zip(packets, arrived)]
    other = [jnp.where(at_top, a, b) for a, b in zip(top_other, low_other)]
    cross, factor = cross_factor(own[cross_piece], other[cross_piece])
    both = [
        panels_of(own[k], other[k], factor, size) for k, (_, size) in enumerate(cuts)
    ]
    sums = 0
    for (start, size), piece in zip(cuts, both):
        sums = sums + wide_dot(piece.T, trail[start : start + size])
    both = jnp.concatenate(both, 0)
    solved_two, tail = both[:, :panel], both[:, panel:]
    full_one = gather_rows(row_one)

    grad_diag_two = block_adjoint(
        diag_two, inverse_two, jnp.tril(adj_diag_two - diag_term_two)
    )
    mirror_two = grad_diag_two + grad_diag_two.T
    adj_two = -crossing - exact_dot(mirror_two, cross.astype(F32))
    head = exact_dot(adj_two, inverse_one).astype(BF16)
    seed_one = jnp.tril(adj_diag_one - wide_dot(head.T, cross) - diag_term_one)
    grad_diag_one = block_adjoint(diag_one, inverse_one, seed_one)
    mirror_one = grad_diag_one + grad_diag_one.T

    parts = sums.reshape(2, row_count, band, width)
    step = 1
    while step < row_count:
        low = (row_here // step) % 2 == 0
        parts = parts.reshape(2, -1, 2, band, width)
        keep = jnp.where(low, parts[:, :, 0], parts[:, :, 1])
        give = jnp.where(low, parts[:, :, 1], parts[:, :, 0])
        parts = keep + row_swap(give.astype(BF16), step).astype(F32)
        step *= 2
    parts = parts.reshape(2, band, width)

    head_wide = head.astype(F32)
    mix_two = jnp.concatenate([own_rows(mirror_two), own_rows(head_wide)], 1)
    mix_one = jnp.concatenate([own_rows(head_wide.T), own_rows(mirror_one)], 1)
    full_both = jnp.concatenate([full_two, full_one], 0)
    mix = jnp.concatenate([mix_two, mix_one], 0)
    mixed = wide_dot(
        jnp.concatenate(halves(mix), 1), jnp.concatenate([full_both, full_both], 0)
    )
    two_left = adj_row_two - mixed[:band] - parts[0]
    one_left = adj_row_one - mixed[band:] - parts[1]

    trail_left = adj_trail - wide_dot(both, full_both)
    column = lax.broadcasted_iota(jnp.int32, (1, width), 1)
    in_block = column >= last

    def put(matrix, block_one, block_two):
        block = jnp.where(here_one, block_one, block_two).astype(F32)
        block = jnp.pad(block, ((0, 0), (last, 0)))
        return jnp.where(in_block & (here_one | here_two), block, matrix)

    grad_trail = put(trail_left, tail, solved_two).astype(BF16)
    nothing = jnp.zeros((band, panel), F32)
    grad_row_one = put(one_left, nothing, nothing)
    grad_row_two = put(two_left, own_rows(head_wide), nothing)
    return (grad_trail, grad_row_one, grad_row_two, grad_diag_one, grad_diag_two)


def solution(mesh):
    split = P("row", "col")
    in_specs = (split, split, split, P(), P(), split, split, split, P(), P())
    out_specs = (split, split, split, P(), P())
    return jax.shard_map(
        per_device, mesh=mesh, in_specs=in_specs, out_specs=out_specs, check_vma=False
    )
```

time: 108 us -> 87.6 us (0.81)
  waiting for transfers between devices: 65.2 us -> 30.6 us
  starting transfers between devices: 15.3 us -> 31 us
  matrix products: 17.6 us -> 12 us
  Pallas kernels: 0 us -> 3.92 us
  local copies, waits for them, and re-layouts: 3.05 us -> 5.53 us
  other arithmetic: 4.87 us -> 2.58 us
    ppermute x4 -> x12, waiting for transfers between devices: 38 us -> 15.3 us  [send(): arrived = lax.ppermute(operand, 'col', pairs)]
    dot_general x24 -> x10, matrix products: 10.9 us -> 2.3 us  [exact_dot(): return jnp.dot(a, b, precision=EXACT, preferred_element_type=F32)]
    ppermute x3 -> x7, waiting for transfers between devices: 14.1 us -> 5.47 us  [pair_swap(): return lax.ppermute(value, 'col', pairs)]
    ppermute x4 -> x12, starting transfers between devices: 3.93 us -> 10.9 us  [send(): arrived = lax.ppermute(operand, 'col', pairs)]
    ppermute x3 -> x7, starting transfers between devices: 5.71 us -> 12.2 us  [pair_swap(): return lax.ppermute(value, 'col', pairs)]
    pallas_call x0 -> x1, Pallas kernels: none -> 3.92 us  [prepare(): pl.pallas_call(functools.partial(prepare_kernel, cuts), grid=(1,), in_spe...]
    ppermute x6 -> x8, waiting for transfers between devices: 13.1 us -> 9.87 us  [row_swap(): return lax.ppermute(value, 'row', [(i, i ^ step) for i in range(row_count)])]
    dot_general x6 -> x15, matrix products: 6.65 us -> 9.68 us  [wide_dot(): return jnp.dot(a, b, preferred_element_type=F32)]
  transfers between devices with their start and end apart: 13 -> 27, of which waited for: 8 -> 13; matrix products, arithmetic and copies ran while one was open for 14% -> 16% of each run, Pallas kernels for 0% -> 0%
where the time goes in v2:
time: 87.6 us; the launch traced here: 87.1 us
  starting transfers between devices  31 us (35%)
  waiting for transfers between devices  30.6 us (35%)
  matrix products  12 us (14%)
  local copies, waits for them, and re-layouts  5.53 us (6%)
  Pallas kernels  3.92 us (4%)
  other arithmetic  2.58 us (3%)
  between operations  1.49 us (2%)
    ppermute x12, waiting for transfers between devices, send(): arrived = lax.ppermute(operand, 'col', pairs)  15.3 us
    ppermute x7, starting transfers between devices, pair_swap(): return lax.ppermute(value, 'col', pairs)  12.2 us
    ppermute x12, starting transfers between devices, send(): arrived = lax.ppermute(operand, 'col', pairs)  10.9 us
    ppermute x8, waiting for transfers between devices, row_swap(): return lax.ppermute(value, 'row', [(i, i ^ step) for i in range(row_count)])  9.87 us
    dot_general x15, matrix products, wide_dot(): return jnp.dot(a, b, preferred_element_type=F32)  9.68 us
    ppermute x8, starting transfers between devices, row_swap(): return lax.ppermute(value, 'row', [(i, i ^ step) for i in range(row_count)])  7.84 us
    ppermute x7, waiting for transfers between devices, pair_swap(): return lax.ppermute(value, 'col', pairs)  5.47 us
    unnamed x30, local copies, waits for them, and re-layouts  5.12 us
  transfers between devices with their start and end apart: 27, of which 13 were waited for; matrix products, arithmetic and copies ran while one was open for 16% of the time, Pallas kernels for 0%

profile of v2, /device:TPU:0, one launch (start us, length us, event | category | flops | bytes accessed | tf_op | source)
XLA Modules:
  0.0 87.1 jit_solution(17034206651555714086)
XLA Ops:
  0.7 3.4 %copy-done = f32[2048,1024]{1,0:T(8,128)S(1)} copy-done((f32[2048,1024]{1,0:T(8,128)S(1)}, f32[2048,1024]{1,0:T(8,128)}, u32[]{:S(2)}) %copy-start) | copy-done | bytes 8388632
  5.7 3.9 %prepare.1 = (f32[128,128]{1,0:T(8,128)S(1)}, f32[128,128]{1,0:T(8,128)S(1)}, bf16[688,128]{1,0:T(8,128)(2,1)S(1)}, bf16[688,128]{1,0:T(8,128)(2,1)S(1)}, bf16[672,128]{1,0:T(8,128)(2,1)S(1)}) custom-call(s32[1]{0:T(128)} %bitcast.side_ref, f32[128,128]{1,0:T(8,128)S(1)} %copy-done.3, f32[128,128]{1,0:T(8,128)S(1)} %copy-done.1, f32[2048,1024]{1,0:T(8,128)S(1)} %copy-done), custom_call_target="tpu_custom_call" | custom-call | flops 268435456 | bytes 1572864 | tf_op jit(solution)/shard_map/prepare/pallas_call | solution.py:81
  14.2 0.9 collective-permute-done.17
  15.0 2.8 %collective-permute-start.6 = (bf16[2,32,1024]{2,1,0:T(8,128)(2,1)S(1)}, bf16[2,32,1024]{2,1,0:T(8,128)(2,1)S(1)}, u32[]{:S(2)}, u32[]{:S(2)}) collective-permute-start(bf16[2,32,1024]{2,1,0:T(8,128)(2,1)S(1)} %pad_maximum_fusion.27), channel_id=1, source_target_pairs={{0,16},{8,24},{16,0},{24,8},{1,17},{9,25},{17,1},{25,9},{2,18},{10... | collective-permute-start | bytes 393224 | tf_op jit(solution)/shard_map/ppermute | solution.py:142
  17.9 1.3 %collective-permute-start.14 = (bf16[672,128]{1,0:T(8,128)(2,1)S(1)}, bf16[672,128]{1,0:T(8,128)(2,1)S(1)}, u32[]{:S(2)}, u32[]{:S(2)}) collective-permute-start(bf16[672,128]{1,0:T(8,128)(2,1)S(1)} %collective-permute-done.12), channel_id=1, source_target_pairs={{2,0},{3,1},{10,8},{11,9},{18,16},{19,17},{26,24},{27,25}} | collective-permute-start | bytes 516104 | tf_op jit(solution)/shard_map/ppermute | solution.py:181
  19.2 2.5 %collective-permute-done.6 = bf16[2,32,1024]{2,1,0:T(8,128)(2,1)S(1)} collective-permute-done((bf16[2,32,1024]{2,1,0:T(8,128)(2,1)S(1)}, bf16[2,32,1024]{2,1,0:T(8,128)(2,1)S(1)}, u32[]{:S(2)}, u32[]{:S(2)}) %collective-permute-start.6) | collective-permute-done | bytes 131104 | tf_op jit(solution)/shard_map/ppermute | solution.py:142
  22.5 1.8 %collective-permute-start.18 = (bf16[2,32,1024]{2,1,0:T(8,128)(2,1)S(1)}, bf16[2,32,1024]{2,1,0:T(8,128)(2,1)S(1)}, u32[]{:S(2)}, u32[]{:S(2)}) collective-permute-start(bf16[2,32,1024]{2,1,0:T(8,128)(2,1)S(1)} %pad_maximum_fusion.28), channel_id=1, source_target_pairs={{0,16},{8,24},{16,0},{24,8},{1,17},{9,25},{17,1},{25,9},{2,18},{10... | collective-permute-start | bytes 393224 | tf_op jit(solution)/shard_map/ppermute | solution.py:142
  24.3 4.6 %collective-permute-done.14 = bf16[672,128]{1,0:T(8,128)(2,1)S(1)} collective-permute-done((bf16[672,128]{1,0:T(8,128)(2,1)S(1)}, bf16[672,128]{1,0:T(8,128)(2,1)S(1)}, u32[]{:S(2)}, u32[]{:S(2)}) %collective-permute-start.14) | collective-permute-done | bytes 172064 | tf_op jit(solution)/shard_map/ppermute | solution.py:181
  28.9 1.3 %collective-permute-start.2 = (bf16[688,128]{1,0:T(8,128)(2,1)S(1)}, bf16[688,128]{1,0:T(8,128)(2,1)S(1)}, u32[]{:S(2)}, u32[]{:S(2)}) collective-permute-start(bf16[688,128]{1,0:T(8,128)(2,1)S(1)} %collective-permute-done), channel_id=1, source_target_pairs={{2,0},{3,1},{10,8},{11,9},{18,16},{19,17},{26,24},{27,25}} | collective-permute-start | bytes 528392 | tf_op jit(solution)/shard_map/ppermute | solution.py:181
  30.9 5.3 %collective-permute-done.2 = bf16[688,128]{1,0:T(8,128)(2,1)S(1)} collective-permute-done((bf16[688,128]{1,0:T(8,128)(2,1)S(1)}, bf16[688,128]{1,0:T(8,128)(2,1)S(1)}, u32[]{:S(2)}, u32[]{:S(2)}) %collective-permute-start.2) | collective-permute-done | bytes 176160 | tf_op jit(solution)/shard_map/ppermute | solution.py:181
  37.6 2.4 %collective-permute-start.16 = (bf16[672,128]{1,0:T(8,128)(2,1)S(1)}, bf16[672,128]{1,0:T(8,128)(2,1)S(1)}, u32[]{:S(2)}, u32[]{:S(2)}) collective-permute-start(bf16[672,128]{1,0:T(8,128)(2,1)S(1)} %select_select_fusion.2), channel_id=1, source_target_pairs={{0,1},{1,0},{2,3},{3,2},{4,5},{5,4},{8,9},{9,8},{10,11},{11,10},{1... | collective-permute-start | bytes 516104 | tf_op jit(solution)/shard_map/ppermute | solution.py:146
  40.8 3.5 %collective-permute-start.4 = (bf16[688,128]{1,0:T(8,128)(2,1)S(1)}, bf16[688,128]{1,0:T(8,128)(2,1)S(1)}, u32[]{:S(2)}, u32[]{:S(2)}) collective-permute-start(bf16[688,128]{1,0:T(8,128)(2,1)S(1)} %select_select_fusion.1), channel_id=1, source_target_pairs={{0,1},{1,0},{2,3},{3,2},{4,5},{5,4},{8,9},{9,8},{10,11},{11,10},{1... | collective-permute-start | bytes 528392 | tf_op jit(solution)/shard_map/ppermute | solution.py:146
  44.3 1.3 %collective-permute-start.10 = (bf16[816,128]{1,0:T(8,128)(2,1)S(1)}, bf16[816,128]{1,0:T(8,128)(2,1)S(1)}, u32[]{:S(2)}, u32[]{:S(2)}) collective-permute-start(bf16[816,128]{1,0:T(8,128)(2,1)S(1)} %collective-permute-done.8), channel_id=1, source_target_pairs={{2,0},{3,1},{10,8},{11,9},{18,16},{19,17},{26,24},{27,25}} | collective-permute-start | bytes 626696 | tf_op jit(solution)/shard_map/ppermute | solution.py:181
  47.2 0.9 %collective-permute-done.4 = bf16[688,128]{1,0:T(8,128)(2,1)S(1)} collective-permute-done((bf16[688,128]{1,0:T(8,128)(2,1)S(1)}, bf16[688,128]{1,0:T(8,128)(2,1)S(1)}, u32[]{:S(2)}, u32[]{:S(2)}) %collective-permute-start.4) | collective-permute-done | bytes 176160 | tf_op jit(solution)/shard_map/ppermute | solution.py:146
  48.9 1.3 %collective-permute-done.19 = f32[256,128]{1,0:T(8,128)S(1)} collective-permute-done((f32[256,128]{1,0:T(8,128)S(1)}, f32[256,128]{1,0:T(8,128)S(1)}, u32[]{:S(2)}, u32[]{:S(2)}) %collective-permute-start.19) | collective-permute-done | bytes 131104 | tf_op jit(solution)/shard_map/ppermute | solution.py:142
  50.2 1.6 %collective-permute-start.20 = (f32[256,128]{1,0:T(8,128)S(1)}, f32[256,128]{1,0:T(8,128)S(1)}, u32[]{:S(2)}, u32[]{:S(2)}) collective-permute-start(f32[256,128]{1,0:T(8,128)S(1)} %add.69), channel_id=1, source_target_pairs={{0,16},{8,24},{16,0},{24,8},{1,17},{9,25},{17,1},{25,9},{2,18},{10... | collective-permute-start | bytes 393224 | tf_op jit(solution)/shard_map/ppermute | solution.py:142
  52.1 3.2 %collective-permute-start.11 = (bf16[816,128]{1,0:T(8,128)(2,1)S(1)}, bf16[816,128]{1,0:T(8,128)(2,1)S(1)}, u32[]{:S(2)}, u32[]{:S(2)}) collective-permute-start(bf16[816,128]{1,0:T(8,128)(2,1)S(1)} %get-tuple-element.22), channel_id=1, source_target_pairs={{0,1},{1,0},{2,3},{3,2},{4,5},{5,4},{8,9},{9,8},{10,11},{11,10},{1... | collective-permute-start | bytes 626696 | tf_op jit(solution)/shard_map/ppermute | solution.py:146
  56.5 4.2 %collective-permute-done.11 = bf16[816,128]{1,0:T(8,128)(2,1)S(1)} collective-permute-done((bf16[816,128]{1,0:T(8,128)(2,1)S(1)}, bf16[816,128]{1,0:T(8,128)(2,1)S(1)}, u32[]{:S(2)}, u32[]{:S(2)}) %collective-permute-start.11) | collective-permute-done | bytes 208928 | tf_op jit(solution)/shard_map/ppermute | solution.py:146
  63.9 1.6 %collective-permute-start.23 = (bf16[256,128]{1,0:T(8,128)(2,1)S(1)}, bf16[256,128]{1,0:T(8,128)(2,1)S(1)}, u32[]{:S(2)}, u32[]{:S(2)}) collective-permute-start(bf16[256,128]{1,0:T(8,128)(2,1)S(1)} %collective-permute-done.21), channel_id=1, source_target_pairs={{2,0},{3,1},{10,8},{11,9},{18,16},{19,17},{26,24},{27,25}} | collective-permute-start | bytes 196616 | tf_op jit(solution)/shard_map/ppermute | solution.py:181
  65.4 0.8 collective-permute-start.22
  66.4 5.2 %collective-permute-done.23 = bf16[256,128]{1,0:T(8,128)(2,1)S(1)} collective-permute-done((bf16[256,128]{1,0:T(8,128)(2,1)S(1)}, bf16[256,128]{1,0:T(8,128)(2,1)S(1)}, u32[]{:S(2)}, u32[]{:S(2)}) %collective-permute-start.23) | collective-permute-done | bytes 65568 | tf_op jit(solution)/shard_map/ppermute | solution.py:181
  71.6 1.1 %collective-permute-start.24 = (bf16[256,128]{1,0:T(8,128)(2,1)S(1)}, bf16[256,128]{1,0:T(8,128)(2,1)S(1)}, u32[]{:S(2)}, u32[]{:S(2)}) collective-permute-start(bf16[256,128]{1,0:T(8,128)(2,1)S(1)} %get-tuple-element.20), channel_id=1, source_target_pairs={{0,1},{1,0},{2,3},{3,2},{4,5},{5,4},{6,7},{7,6},{8,9},{9,8},{10,11... | collective-permute-start | bytes 196616 | tf_op jit(solution)/shard_map/ppermute | solution.py:146
  72.8 5.0 %select_convert_fusion = bf16[2048,1024]{1,0:T(8,128)(2,1)} fusion(f32[2048,1024]{1,0:T(8,128)S(1)} %bitcast.70, bf16[2048,128]{1,0:T(8,128)(2,1)S(1)} %slice_select_fusion, pred[1024]{0:T(1024)(128)(4,1)S(1)} %fusion.90, bf16[128,1024]{1,0:T(8,128)(2,1)S(1)} %bitcast.76, bf16[128,1024]{1,0:T(8,128)(2,1)S(1)} %bitcast.74, ...), kind=kOutput, calls=%fused_computation | convolution fusion | flops 1089470464 | bytes 14681088 | tf_op jit(solution)/shard_map/dot_general | solution.py:21
  82.2 4.1 %collective-permute-done.26 = bf16[2,1,32,1024]{3,2,1,0:T(8,128)(2,1)S(1)} collective-permute-done((bf16[2,1,32,1024]{3,2,1,0:T(8,128)(2,1)S(1)}, bf16[2,1,32,1024]{3,2,1,0:T(8,128)(2,1)S(1)}, u32[]{:S(2)}, u32[]{:S(2)}) %collective-permute-start.26) | collective-permute-done | bytes 131104 | tf_op jit(solution)/shard_map/ppermute | solution.py:142
  (134 shorter events, 21.8 us)
Async XLA Ops:
  9.6 31.1 %collective-permute-start.15 = (bf16[672,128]{1,0:T(8,128)(2,1)S(1)}, bf16[672,128]{1,0:T(8,128)(2,1)S(1)}, u32[]{:S(2)}, u32[]{:S(2)}) collective-permute-start(bf16[672,128]{1,0:T(8,128)(2,1)S(1)} %get-tuple-element.13), channel_id=1, source_target_pairs={{6,7},{7,6},{14,15},{15,14},{22,23},{23,22},{30,31},{31,30}} | collective-permute-start | bytes 516104 | tf_op jit(solution)/shard_map/ppermute | solution.py:146
  10.3 7.6 %collective-permute-start.12 = (bf16[672,128]{1,0:T(8,128)(2,1)S(1)}, bf16[672,128]{1,0:T(8,128)(2,1)S(1)}, u32[]{:S(2)}, u32[]{:S(2)}) collective-permute-start(bf16[672,128]{1,0:T(8,128)(2,1)S(1)} %get-tuple-element.13), channel_id=1, source_target_pairs={{6,2},{7,3},{14,10},{15,11},{22,18},{23,19},{30,26},{31,27}} | collective-permute-start | bytes 516104 | tf_op jit(solution)/shard_map/ppermute | solution.py:181
  11.0 36.2 %collective-permute-start.3 = (bf16[688,128]{1,0:T(8,128)(2,1)S(1)}, bf16[688,128]{1,0:T(8,128)(2,1)S(1)}, u32[]{:S(2)}, u32[]{:S(2)}) collective-permute-start(bf16[688,128]{1,0:T(8,128)(2,1)S(1)} %get-tuple-element.10), channel_id=1, source_target_pairs={{6,7},{7,6},{14,15},{15,14},{22,23},{23,22},{30,31},{31,30}} | collective-permute-start | bytes 528392 | tf_op jit(solution)/shard_map/ppermute | solution.py:146
  11.7 10.8 %collective-permute-start = (bf16[688,128]{1,0:T(8,128)(2,1)S(1)}, bf16[688,128]{1,0:T(8,128)(2,1)S(1)}, u32[]{:S(2)}, u32[]{:S(2)}) collective-permute-start(bf16[688,128]{1,0:T(8,128)(2,1)S(1)} %get-tuple-element.10), channel_id=1, source_target_pairs={{6,2},{7,3},{14,10},{15,11},{22,18},{23,19},{30,26},{31,27}} | collective-permute-start | bytes 528392 | tf_op jit(solution)/shard_map/ppermute | solution.py:181
  12.4 1.4 %collective-permute-start.5 = (bf16[1,32,1024]{2,1,0:T(8,128)(2,1)S(1)}, bf16[1,32,1024]{2,1,0:T(8,128)(2,1)S(1)}, u32[]{:S(2)}, u32[]{:S(2)}) collective-permute-start(bf16[1,32,1024]{2,1,0:T(8,128)(2,1)S(1)} %bitcast.79), channel_id=1, source_target_pairs={{0,8},{8,0},{16,24},{24,16},{1,9},{9,1},{17,25},{25,17},{2,10},{10... | collective-permute-start | bytes 196616 | tf_op jit(solution)/shard_map/ppermute | solution.py:142
  15.0 6.7 %collective-permute-start.6 = (bf16[2,32,1024]{2,1,0:T(8,128)(2,1)S(1)}, bf16[2,32,1024]{2,1,0:T(8,128)(2,1)S(1)}, u32[]{:S(2)}, u32[]{:S(2)}) collective-permute-start(bf16[2,32,1024]{2,1,0:T(8,128)(2,1)S(1)} %pad_maximum_fusion.27), channel_id=1, source_target_pairs={{0,16},{8,24},{16,0},{24,8},{1,17},{9,25},{17,1},{25,9},{2,18},{10... | collective-permute-start | bytes 393224 | tf_op jit(solution)/shard_map/ppermute | solution.py:142
  17.9 10.9 %collective-permute-start.14 = (bf16[672,128]{1,0:T(8,128)(2,1)S(1)}, bf16[672,128]{1,0:T(8,128)(2,1)S(1)}, u32[]{:S(2)}, u32[]{:S(2)}) collective-permute-start(bf16[672,128]{1,0:T(8,128)(2,1)S(1)} %collective-permute-done.12), channel_id=1, source_target_pairs={{2,0},{3,1},{10,8},{11,9},{18,16},{19,17},{26,24},{27,25}} | collective-permute-start | bytes 516104 | tf_op jit(solution)/shard_map/ppermute | solution.py:181
  21.7 8.5 %collective-permute-start.13 = (bf16[672,128]{1,0:T(8,128)(2,1)S(1)}, bf16[672,128]{1,0:T(8,128)(2,1)S(1)}, u32[]{:S(2)}, u32[]{:S(2)}) collective-permute-start(bf16[672,128]{1,0:T(8,128)(2,1)S(1)} %collective-permute-done.12), channel_id=1, source_target_pairs={{2,4},{3,5},{10,12},{11,13},{18,20},{19,21},{26,28},{27,29}} | collective-permute-start | bytes 516104 | tf_op jit(solution)/shard_map/ppermute | solution.py:181
  22.5 26.3 %collective-permute-start.18 = (bf16[2,32,1024]{2,1,0:T(8,128)(2,1)S(1)}, bf16[2,32,1024]{2,1,0:T(8,128)(2,1)S(1)}, u32[]{:S(2)}, u32[]{:S(2)}) collective-permute-start(bf16[2,32,1024]{2,1,0:T(8,128)(2,1)S(1)} %pad_maximum_fusion.28), channel_id=1, source_target_pairs={{0,16},{8,24},{16,0},{24,8},{1,17},{9,25},{17,1},{25,9},{2,18},{10... | collective-permute-start | bytes 393224 | tf_op jit(solution)/shard_map/ppermute | solution.py:142
  28.9 7.3 %collective-permute-start.2 = (bf16[688,128]{1,0:T(8,128)(2,1)S(1)}, bf16[688,128]{1,0:T(8,128)(2,1)S(1)}, u32[]{:S(2)}, u32[]{:S(2)}) collective-permute-start(bf16[688,128]{1,0:T(8,128)(2,1)S(1)} %collective-permute-done), channel_id=1, source_target_pairs={{2,0},{3,1},{10,8},{11,9},{18,16},{19,17},{26,24},{27,25}} | collective-permute-start | bytes 528392 | tf_op jit(solution)/shard_map/ppermute | solution.py:181
  30.2 6.7 %collective-permute-start.1 = (bf16[688,128]{1,0:T(8,128)(2,1)S(1)}, bf16[688,128]{1,0:T(8,128)(2,1)S(1)}, u32[]{:S(2)}, u32[]{:S(2)}) collective-permute-start(bf16[688,128]{1,0:T(8,128)(2,1)S(1)} %collective-permute-done), channel_id=1, source_target_pairs={{2,4},{3,5},{10,12},{11,13},{18,20},{19,21},{26,28},{27,29}} | collective-permute-start | bytes 528392 | tf_op jit(solution)/shard_map/ppermute | solution.py:181
  36.2 8.1 %collective-permute-start.8 = (bf16[816,128]{1,0:T(8,128)(2,1)S(1)}, bf16[816,128]{1,0:T(8,128)(2,1)S(1)}, u32[]{:S(2)}, u32[]{:S(2)}) collective-permute-start(bf16[816,128]{1,0:T(8,128)(2,1)S(1)} %pad_maximum_fusion.26), channel_id=1, source_target_pairs={{6,2},{7,3},{14,10},{15,11},{22,18},{23,19},{30,26},{31,27}} | collective-permute-start | bytes 626696 | tf_op jit(solution)/shard_map/ppermute | solution.py:181
  37.6 8.3 %collective-permute-start.16 = (bf16[672,128]{1,0:T(8,128)(2,1)S(1)}, bf16[672,128]{1,0:T(8,128)(2,1)S(1)}, u32[]{:S(2)}, u32[]{:S(2)}) collective-permute-start(bf16[672,128]{1,0:T(8,128)(2,1)S(1)} %select_select_fusion.2), channel_id=1, source_target_pairs={{0,1},{1,0},{2,3},{3,2},{4,5},{5,4},{8,9},{9,8},{10,11},{11,10},{1... | collective-permute-start | bytes 516104 | tf_op jit(solution)/shard_map/ppermute | solution.py:146
  40.8 7.3 %collective-permute-start.4 = (bf16[688,128]{1,0:T(8,128)(2,1)S(1)}, bf16[688,128]{1,0:T(8,128)(2,1)S(1)}, u32[]{:S(2)}, u32[]{:S(2)}) collective-permute-start(bf16[688,128]{1,0:T(8,128)(2,1)S(1)} %select_select_fusion.1), channel_id=1, source_target_pairs={{0,1},{1,0},{2,3},{3,2},{4,5},{5,4},{8,9},{9,8},{10,11},{11,10},{1... | collective-permute-start | bytes 528392 | tf_op jit(solution)/shard_map/ppermute | solution.py:146
  44.3 7.7 %collective-permute-start.10 = (bf16[816,128]{1,0:T(8,128)(2,1)S(1)}, bf16[816,128]{1,0:T(8,128)(2,1)S(1)}, u32[]{:S(2)}, u32[]{:S(2)}) collective-permute-start(bf16[816,128]{1,0:T(8,128)(2,1)S(1)} %collective-permute-done.8), channel_id=1, source_target_pairs={{2,0},{3,1},{10,8},{11,9},{18,16},{19,17},{26,24},{27,25}} | collective-permute-start | bytes 626696 | tf_op jit(solution)/shard_map/ppermute | solution.py:181
  45.9 6.1 %collective-permute-start.9 = (bf16[816,128]{1,0:T(8,128)(2,1)S(1)}, bf16[816,128]{1,0:T(8,128)(2,1)S(1)}, u32[]{:S(2)}, u32[]{:S(2)}) collective-permute-start(bf16[816,128]{1,0:T(8,128)(2,1)S(1)} %collective-permute-done.8), channel_id=1, source_target_pairs={{2,4},{3,5},{10,12},{11,13},{18,20},{19,21},{26,28},{27,29}} | collective-permute-start | bytes 626696 | tf_op jit(solution)/shard_map/ppermute | solution.py:181
  50.2 5.6 %collective-permute-start.20 = (f32[256,128]{1,0:T(8,128)S(1)}, f32[256,128]{1,0:T(8,128)S(1)}, u32[]{:S(2)}, u32[]{:S(2)}) collective-permute-start(f32[256,128]{1,0:T(8,128)S(1)} %add.69), channel_id=1, source_target_pairs={{0,16},{8,24},{16,0},{24,8},{1,17},{9,25},{17,1},{25,9},{2,18},{10... | collective-permute-start | bytes 393224 | tf_op jit(solution)/shard_map/ppermute | solution.py:142
  52.1 8.6 %collective-permute-start.11 = (bf16[816,128]{1,0:T(8,128)(2,1)S(1)}, bf16[816,128]{1,0:T(8,128)(2,1)S(1)}, u32[]{:S(2)}, u32[]{:S(2)}) collective-permute-start(bf16[816,128]{1,0:T(8,128)(2,1)S(1)} %get-tuple-element.22), channel_id=1, source_target_pairs={{0,1},{1,0},{2,3},{3,2},{4,5},{5,4},{8,9},{9,8},{10,11},{11,10},{1... | collective-permute-start | bytes 626696 | tf_op jit(solution)/shard_map/ppermute | solution.py:146
  55.8 8.0 %collective-permute-start.21 = (bf16[256,128]{1,0:T(8,128)(2,1)S(1)}, bf16[256,128]{1,0:T(8,128)(2,1)S(1)}, u32[]{:S(2)}, u32[]{:S(2)}) collective-permute-start(bf16[256,128]{1,0:T(8,128)(2,1)S(1)} %add_convert_fusion), channel_id=1, source_target_pairs={{6,2},{7,3},{14,10},{15,11},{22,18},{23,19},{30,26},{31,27}} | collective-permute-start | bytes 196616 | tf_op jit(solution)/shard_map/ppermute | solution.py:181
  63.9 7.7 %collective-permute-start.23 = (bf16[256,128]{1,0:T(8,128)(2,1)S(1)}, bf16[256,128]{1,0:T(8,128)(2,1)S(1)}, u32[]{:S(2)}, u32[]{:S(2)}) collective-permute-start(bf16[256,128]{1,0:T(8,128)(2,1)S(1)} %collective-permute-done.21), channel_id=1, source_target_pairs={{2,0},{3,1},{10,8},{11,9},{18,16},{19,17},{26,24},{27,25}} | collective-permute-start | bytes 196616 | tf_op jit(solution)/shard_map/ppermute | solution.py:181
  65.4 6.2 %collective-permute-start.22 = (bf16[256,128]{1,0:T(8,128)(2,1)S(1)}, bf16[256,128]{1,0:T(8,128)(2,1)S(1)}, u32[]{:S(2)}, u32[]{:S(2)}) collective-permute-start(bf16[256,128]{1,0:T(8,128)(2,1)S(1)} %collective-permute-done.21), channel_id=1, source_target_pairs={{2,4},{3,5},{10,12},{11,13},{18,20},{19,21},{26,28},{27,29}} | collective-permute-start | bytes 196616 | tf_op jit(solution)/shard_map/ppermute | solution.py:181
  66.3 14.8 %collective-permute-start.25 = (bf16[2,2,32,1024]{3,2,0,1:T(8,128)(2,1)S(1)}, bf16[2,2,32,1024]{3,2,0,1:T(8,128)(2,1)S(1)}, u32[]{:S(2)}, u32[]{:S(2)}) collective-permute-start(bf16[2,2,32,1024]{3,2,0,1:T(8,128)(2,1)S(1)} %fusion.48), channel_id=1, source_target_pairs={{0,8},{8,0},{16,24},{24,16},{1,9},{9,1},{17,25},{25,17},{2,10},{10... | collective-permute-start | bytes 786440 | tf_op jit(solution)/shard_map/ppermute | solution.py:142
  71.6 6.2 %collective-permute-start.24 = (bf16[256,128]{1,0:T(8,128)(2,1)S(1)}, bf16[256,128]{1,0:T(8,128)(2,1)S(1)}, u32[]{:S(2)}, u32[]{:S(2)}) collective-permute-start(bf16[256,128]{1,0:T(8,128)(2,1)S(1)} %get-tuple-element.20), channel_id=1, source_target_pairs={{0,1},{1,0},{2,3},{3,2},{4,5},{5,4},{6,7},{7,6},{8,9},{9,8},{10,11... | collective-permute-start | bytes 196616 | tf_op jit(solution)/shard_map/ppermute | solution.py:146
  81.3 5.0 %collective-permute-start.26 = (bf16[2,1,32,1024]{3,2,1,0:T(8,128)(2,1)S(1)}, bf16[2,1,32,1024]{3,2,1,0:T(8,128)(2,1)S(1)}, u32[]{:S(2)}, u32[]{:S(2)}) collective-permute-start(bf16[2,1,32,1024]{3,2,1,0:T(8,128)(2,1)S(1)} %fusion.52), channel_id=1, source_target_pairs={{0,16},{8,24},{16,0},{24,8},{1,17},{9,25},{17,1},{25,9},{2,18},{10... | collective-permute-start | bytes 393224 | tf_op jit(solution)/shard_map/ppermute | solution.py:142
  (18 other events, 93.7 us)

commit v3 on v2

--- a/solution.py
+++ b/solution.py
@@ -60,43 +60,74 @@
     return inverses
 
 
-def prepare_kernel(cuts, side_ref, one_ref, two_ref, rows_ref, inv_one_ref, inv_two_ref, *out_refs):
+def invert_kernel(one_ref, two_ref, inv_one_ref, inv_two_ref):
     inverse_one, inverse_two = inverse_lower([one_ref[...], two_ref[...]])
     inv_one_ref[...] = inverse_one
     inv_two_ref[...] = inverse_two
-    chosen = jnp.where(side_ref[0] == 1, inverse_two, inverse_one)
+
+
+def invert(diag_one, diag_two):
+    square = jax.ShapeDtypeStruct(diag_one.shape, F32)
+    return pl.pallas_call(
+        invert_kernel,
+        out_shape=[square, square],
+        cost_estimate=pl.CostEstimate(
+            flops=12 * 12 * diag_one.shape[0] ** 3, bytes_accessed=2**18, transcendentals=0
+        ),
+        name="invert",
+    )(diag_one, diag_two)
+
+
+def solve_kernel(side_ref, one_ref, two_ref, rows_ref, cross_ref, out_ref):
+    panel = one_ref.shape[0]
+    chosen = jnp.where(side_ref[0] == 1, two_ref[...], one_ref[...])
     high, low = halves(chosen)
-    for (start, size), out_ref in zip(cuts, out_refs):
-        own_high, own_low = halves(rows_ref[start : start + size, :])
-        product = wide_dot(own_high, high) + (
-            wide_dot(own_high, low) + wide_dot(own_low, high)
-        )
-        out_ref[...] = product.astype(BF16)
-
-
-def prepare(side, diag_one, diag_two, adj_trail, cuts):
-    height, width = adj_trail.shape
-    panel = diag_one.shape[0]
-    square = pl.BlockSpec((panel, panel), lambda i: (0, 0))
+    own_high, own_low = halves(rows_ref[...])
+    product = wide_dot(own_high, high) + (
+        wide_dot(own_high, low) + wide_dot(own_low, high)
+    )
+    out_ref[:panel, :] = cross_ref[...]
+    out_ref[panel:, :] = product.astype(BF16)
+
+
+def solve(side, inverse_one, inverse_two, rows, cross):
+    height, panel = rows.shape
+    vmem = pl.BlockSpec(memory_space=pltpu.VMEM)
     return pl.pallas_call(
-        functools.partial(prepare_kernel, cuts),
-        grid=(1,),
-        in_specs=[
-            pl.BlockSpec(memory_space=pltpu.SMEM),
-            square,
-            square,
-            pl.BlockSpec((height, panel), lambda i: (0, width // panel - 1)),
-        ],
-        out_specs=[square, square]
-        + [pl.BlockSpec((size, panel), lambda i: (0, 0)) for _, size in cuts],
-        out_shape=[jax.ShapeDtypeStruct((panel, panel), F32)] * 2
-        + [jax.ShapeDtypeStruct((size, panel), BF16) for _, size in cuts],
+        solve_kernel,
+        in_specs=[pl.BlockSpec(memory_space=pltpu.SMEM)] + [vmem] * 4,
+        out_specs=vmem,
+        out_shape=jax.ShapeDtypeStruct((panel + height, panel), BF16),
         compiler_params=pltpu.CompilerParams(vmem_limit_bytes=32 * 2**20),
         cost_estimate=pl.CostEstimate(
-            flops=8 * height * panel * panel, bytes_accessed=6 * height * panel, transcendentals=0
+            flops=6 * height * panel * panel, bytes_accessed=6 * height * panel, transcendentals=0
         ),
-        name="prepare",
-    )(side, diag_one, diag_two, adj_trail)
+        name="solve",
+    )(side, inverse_one, inverse_two, rows, cross)
+
+
+def cut_kernel(cuts, whole_ref, *out_refs):
+    for (start, stop), out_ref in zip(cuts, out_refs):
+        out_ref[...] = whole_ref[start:stop, :]
+
+
+def cut(whole, cuts):
+    panel = whole.shape[1]
+    vmem = pl.BlockSpec(memory_space=pltpu.VMEM)
+    return pl.pallas_call(
+        functools.partial(cut_kernel, cuts),
+        in_specs=[vmem],
+        out_specs=[vmem] * len(cuts),
+        out_shape=[jax.ShapeDtypeStruct((stop - start, panel), BF16) for start, stop in cuts],
+        cost_estimate=pl.CostEstimate(
+            flops=0, bytes_accessed=2 * whole.size, transcendentals=0
+        ),
+        name="cut",
+    )(whole)
+
+
+def after(value, *others):
+    return lax.optimization_barrier((value, *others))[0]
 
 
 def block_adjoint(block, inverse, seed_adj):
@@ -132,8 +163,10 @@
     is_two = col_here % 2 == 1
     here_one = col_here == col_count - 2
     here_two = col_here == col_count - 1
-    step_rows = -(-height // (16 * PIECES)) * 16
-    cuts = [(at, min(step_rows, height - at)) for at in range(0, height, step_rows)]
+    step_rows = -(-(height + panel) // (16 * PIECES)) * 16
+    bounds = list(range(step_rows, height + panel, step_rows)) + [height + panel]
+    bounds = [panel] + bounds
+    cuts = list(zip(bounds, bounds[1:]))
 
     def own_rows(matrix):
         return lax.dynamic_slice_in_dim(matrix, row_start, band, 0)
@@ -157,75 +190,78 @@
             step *= 2
         return value.reshape(panel, width)
 
-    def spread(value):
-        held = {top: value}
-
-        def pick(which):
-            groups = []
-            for k in which:
-                for group in groups:
-                    if group[0] is held[k]:
-                        group[1].append(k)
-                        break
-                else:
-                    groups.append((held[k], [k]))
-            chosen = groups[0][0]
-            for array, members in groups[1:]:
-                at = functools.reduce(jnp.logical_or, [level == k for k in members])
-                chosen = jnp.where(at, array, chosen)
-            return chosen
-
-        def send(hops):
-            operand = pick([source for source, _ in hops])
-            pairs = [(2 * a + s, 2 * b + s) for a, b in hops for s in range(2)]
-            arrived = lax.ppermute(operand, "col", pairs)
-            return {target: arrived for _, target in hops}
-
-        if levels > 1:
-            span = levels // 2
-            held.update(send([(top, span - 1)]))
-            fresh = [span - 1]
+    def choose(options):
+        merged = []
+        for members, array in options:
+            for entry in merged:
+                if entry[1] is array:
+                    entry[0].extend(members)
+                    break
+            else:
+                merged.append((list(members), array))
+        chosen = merged[0][1]
+        for members, array in merged[1:]:
+            at = functools.reduce(jnp.logical_or, [level == k for k in members])
+            chosen = jnp.where(at, array, chosen)
+        return chosen
+
+    def hop(value, hops):
+        pairs = [(2 * a + s, 2 * b + s) for a, b in hops for s in range(2)]
+        return lax.ppermute(value, "col", pairs)
+
+    def spread_first(value):
+        return hop(value, [(top, levels // 2 - 1)]) if levels > 1 else value
+
+    def spread_rest(first):
+        held = {max(levels // 2 - 1, 0): first}
+        span = levels // 4
+        while span >= 1:
+            fresh = list(held)
+            operand = choose([([k], held[k]) for k in fresh])
+            up = hop(operand, [(k, k + span) for k in fresh])
+            down = hop(operand, [(k, k - span) for k in fresh if k >= span])
+            for k in fresh:
+                held[k + span] = up
+                if k >= span:
+                    held[k - span] = down
             span //= 2
-            while span >= 1:
-                up = send([(k, k + span) for k in fresh])
-                down = send([(k, k - span) for k in fresh])
-                held.update(up)
-                held.update(down)
-                fresh = [k + d * span for k in fresh for d in (1, -1)]
-                span //= 2
-        return pick(list(range(levels - 1))) if levels > 1 else value
+        return choose([([k], held[k]) for k in sorted(held)])
 
     full_two = gather_rows(row_two)
+    inverse_one, inverse_two = invert(diag_one, diag_two)
     side = is_two.astype(jnp.int32)[None]
-    inverse_one, inverse_two, *solved = prepare(side, diag_one, diag_two, adj_trail, cuts)
-    cross_piece = min(1, len(cuts) - 1)
-    packets = [
-        jnp.concatenate([piece, full_two[:, last:]], 0) if k == cross_piece else piece
-        for k, piece in enumerate(solved)
-    ]
+    whole = solve(
+        side, inverse_one, inverse_two, adj_trail[:, last:], full_two[:, last:]
+    )
+    packets = cut(whole, [(0, cuts[0][1])] + cuts[1:])
 
     def cross_factor(own, other):
-        size = cuts[cross_piece][1]
-        cross = jnp.where(is_two, other[size:], own[size:])
+        cross = jnp.where(is_two, other[:panel], own[:panel])
         return cross, jnp.concatenate(halves(exact_dot(cross.astype(F32), inverse_one)), 0)
 
     def panels_of(own, other, factor, size):
-        solved_two = jnp.where(is_two, own[:size], other[:size])
-        base_one = jnp.where(is_two, other[:size], own[:size])
+        solved_two = jnp.where(is_two, own[-size:], other[-size:])
+        base_one = jnp.where(is_two, other[-size:], own[-size:])
         tail = base_one.astype(F32) - wide_dot(
             jnp.concatenate([solved_two, solved_two], 1), factor
         )
         return jnp.concatenate([solved_two, tail.astype(BF16)], 1)
 
-    arrived = [spread(packet) for packet in packets]
-    top_other = [pair_swap(packet, [top]) for packet in packets]
-    low_other = [pair_swap(packet, range(levels - 1)) for packet in arrived]
-
-    _, top_factor = cross_factor(packets[cross_piece], top_other[cross_piece])
-    terms = 0
-    for k, (start, size) in enumerate(cuts):
-        top_both = panels_of(packets[k], top_other[k], top_factor, size)
-        terms = terms + wide_dot(top_both.T, trail[start : start + size, last:])
+    whole_other = pair_swap(whole, [top])
+    first = [spread_first(packet) for packet in packets]
+    final = len(first) - 1
+    full_one = gather_rows(after(row_one, full_two, first[min(1, final)]))
+    arrived, low_other = [], []
+    for k, value in enumerate(first):
+        arrived.append(spread_rest(value))
+        low_other.append(
+            pair_swap(after(arrived[k], first[min(k + 1, final)]), range(levels - 1))
+        )
+
+    whole_other = after(whole_other, first[final])
+    _, top_factor = cross_factor(whole, whole_other)
+    top_both = panels_of(whole, whole_other, top_factor, height)
+    terms = wide_dot(top_both.T, trail[:, last:])
     placed = lax.dynamic_update_slice_in_dim(
         jnp.zeros((2 * panel, panel), F32),
         jnp.where(is_two, 0, adj_row_two[:, last:]),
@@ -235,10 +271,17 @@
     terms = terms - placed
     step = 1
     while step < row_count:
-        terms = terms + row_swap(terms, step)
+        pairs = [
+            (i * col_count + c, (i ^ step) * col_count + c)
+            for i in range(row_count)
+            for c in (col_count - 2, col_count - 1)
+        ]
+        terms = terms + lax.ppermute(terms, ("row", "col"), pairs)
         step *= 2
-    terms = terms.astype(BF16)
-    terms = jnp.where(level == top, terms, spread(terms))
+    terms = row_terms = terms.astype(BF16)
+    terms = choose(
+        [([top], terms)] + [([k], hop(terms, [(top, k)])) for k in range(levels - 1)]
+    )
     terms_other = pair_swap(terms, range(levels))
     terms, terms_other = terms.astype(F32), terms_other.astype(F32)
     diag_term_two = jnp.where(is_two, terms[:panel], terms_other[:panel])
@@ -247,17 +290,20 @@
 
     at_top = level == top
     own = [jnp.where(at_top, a, b) for a, b in zip(packets, arrived)]
-    other = [jnp.where(at_top, a, b) for a, b in zip(top_other, low_other)]
-    cross, factor = cross_factor(own[cross_piece], other[cross_piece])
+    other = []
+    for k, (start, stop) in enumerate(cuts):
+        piece = whole_other[(0 if k == 0 else start) : stop]
+        other.append(jnp.where(at_top, piece, after(low_other[k], row_terms)))
+    cross, factor = cross_factor(own[0], other[0])
     both = [
-        panels_of(own[k], other[k], factor, size) for k, (_, size) in enumerate(cuts)
+        panels_of(own[k], other[k], factor, stop - start)
+        for k, (start, stop) in enumerate(cuts)
     ]
     sums = 0
-    for (start, size), piece in zip(cuts, both):
-        sums = sums + wide_dot(piece.T, trail[start : start + size])
+    for (start, stop), piece in zip(cuts, both):
+        sums = sums + wide_dot(piece.T, trail[start - panel : stop - panel])
     both = jnp.concatenate(both, 0)
     solved_two, tail = both[:, :panel], both[:, panel:]
-    full_one = gather_rows(row_one)
 
     grad_diag_two = block_adjoint(
         diag_two, inverse_two, jnp.tril(adj_diag_two - diag_term_two)

time: 87.6 us -> 85.7 us (0.978)
  Pallas kernels: 3.92 us -> 7.09 us
  waiting for transfers between devices: 30.6 us -> 27.8 us
  starting transfers between devices: 31 us -> 28.8 us
    ppermute x7 -> x5, waiting for transfers between devices: 5.47 us -> 1.25 us  [pair_swap(): return lax.ppermute(value, 'col', pairs)]
    pallas_call x1 -> x3, Pallas kernels: 3.92 us -> 7.09 us  [the longest x1 4.65 us: invert(): pl.pallas_call(invert_kernel, out_shape=[square, square], cost_estimate=p...]
    ppermute x12 -> x14, waiting for transfers between devices: 15.3 us -> 17.9 us  [the longest x12 17.9 us: hop(): return lax.ppermute(value, 'col', pairs)]
    ppermute x8 -> x6, starting transfers between devices: 7.84 us -> 5.42 us  [row_swap(): return lax.ppermute(value, 'row', [(i, i ^ step) for i in range(row_count)])]
    slice x0 -> x1, local copies, waits for them, and re-layouts: none -> 1.29 us  [per_device(): adj_trail[:, last:]]
    ppermute x8 -> x6, waiting for transfers between devices: 9.87 us -> 8.6 us  [row_swap(): return lax.ppermute(value, 'row', [(i, i ^ step) for i in range(row_count)])]
    ppermute x12 -> x14, starting transfers between devices: 10.9 us -> 12.1 us  [the longest x12 10.8 us: hop(): return lax.ppermute(value, 'col', pairs)]
    ppermute x7 -> x5, starting transfers between devices: 12.2 us -> 11.2 us  [pair_swap(): return lax.ppermute(value, 'col', pairs)]
  transfers between devices with their start and end apart: 27 -> 25, of which waited for: 13 -> 6; matrix products, arithmetic and copies ran while one was open for 16% -> 17% of each run, Pallas kernels for 0% -> 5%
where the time goes in v3:
time: 85.7 us; the launch traced here: 85.1 us
  starting transfers between devices  28.8 us (34%)
  waiting for transfers between devices  27.8 us (32%)
  matrix products  11.2 us (13%)
  Pallas kernels  7.09 us (8%)
  local copies, waits for them, and re-layouts  6.33 us (7%)
  other arithmetic  2.5 us (3%)
  between operations  1.48 us (2%)
    ppermute x12, waiting for transfers between devices, hop(): return lax.ppermute(value, 'col', pairs)  17.9 us
    ppermute x5, starting transfers between devices, pair_swap(): return lax.ppermute(value, 'col', pairs)  11.2 us
    ppermute x12, starting transfers between devices, hop(): return lax.ppermute(value, 'col', pairs)  10.8 us
    dot_general x11, matrix products, wide_dot(): return jnp.dot(a, b, preferred_element_type=F32)  8.84 us
    ppermute x6, waiting for transfers between devices, row_swap(): return lax.ppermute(value, 'row', [(i, i ^ step) for i in range(row_count)])  8.6 us
    ppermute x6, starting transfers between devices, row_swap(): return lax.ppermute(value, 'row', [(i, i ^ step) for i in range(row_count)])  5.42 us
    pallas_call x1, Pallas kernels, invert(): pl.pallas_call(invert_kernel, out_shape=[square, square], cost_estimate=p...  4.65 us
    unnamed x40, local copies, waits for them, and re-layouts  4.61 us
  transfers between devices with their start and end apart: 25, of which 6 were waited for; matrix products, arithmetic and copies ran while one was open for 17% of the time, Pallas kernels for 5%

profile of v3, /device:TPU:0, one launch (start us, length us, event | category | flops | bytes accessed | tf_op | source)
XLA Modules:
  0.0 85.1 jit_solution(7947994992778395521)
XLA Ops:
  1.2 1.3 %slice.108.rows_ref = f32[2048,128]{1,0:T(8,128)S(1)} slice(f32[2048,1024]{1,0:T(8,128)} %param.15), slice={[0:2048], [896:1024]} | slice | bytes 2097152 | tf_op jit(solution)/shard_map/slice | solution.py:234
  2.5 4.6 %invert.1 = (f32[128,128]{1,0:T(8,128)}, f32[128,128]{1,0:T(8,128)}) custom-call(f32[128,128]{1,0:T(8,128)} %one_ref.1, f32[128,128]{1,0:T(8,128)} %two_ref.1), custom_call_target="tpu_custom_call" | custom-call | flops 301989888 | bytes 262144 | tf_op jit(solution)/shard_map/invert/pallas_call | solution.py:71
  7.2 2.7 %collective-permute-start.1 = (bf16[2,32,1024]{2,1,0:T(8,128)(2,1)S(1)}, bf16[2,32,1024]{2,1,0:T(8,128)(2,1)S(1)}, u32[]{:S(2)}, u32[]{:S(2)}) collective-permute-start(bf16[2,32,1024]{2,1,0:T(8,128)(2,1)S(1)} %pad_maximum_fusion.18), channel_id=1, source_target_pairs={{0,16},{8,24},{16,0},{24,8},{1,17},{9,25},{17,1},{25,9},{2,18},{10... | collective-permute-start | bytes 393224 | tf_op jit(solution)/shard_map/ppermute | solution.py:175
  9.9 4.0 %collective-permute-done.1 = bf16[2,32,1024]{2,1,0:T(8,128)(2,1)S(1)} collective-permute-done((bf16[2,32,1024]{2,1,0:T(8,128)(2,1)S(1)}, bf16[2,32,1024]{2,1,0:T(8,128)(2,1)S(1)}, u32[]{:S(2)}, u32[]{:S(2)}) %collective-permute-start.1) | collective-permute-done | bytes 131104 | tf_op jit(solution)/shard_map/ppermute | solution.py:175
  14.0 0.8 copy-done.2
  14.8 0.8 copy-done.4
  16.2 0.8 copy-done
  17.0 1.9 %cut.1 = (bf16[736,128]{1,0:T(8,128)(2,1)}, bf16[736,128]{1,0:T(8,128)(2,1)}, bf16[704,128]{1,0:T(8,128)(2,1)}) custom-call(bf16[2176,128]{1,0:T(8,128)(2,1)} %copy-done), custom_call_target="tpu_custom_call" | custom-call | bytes 557056 | tf_op jit(solution)/shard_map/cut/pallas_call | solution.py:117
  21.9 1.3 %collective-permute-start.15 = (bf16[704,128]{1,0:T(8,128)(2,1)S(1)}, bf16[704,128]{1,0:T(8,128)(2,1)S(1)}, u32[]{:S(2)}, u32[]{:S(2)}) collective-permute-start(bf16[704,128]{1,0:T(8,128)(2,1)S(1)} %collective-permute-done.6), channel_id=1, source_target_pairs={{2,0},{3,1},{10,8},{11,9},{18,16},{19,17},{26,24},{27,25}} | collective-permute-start | bytes 540680 | tf_op jit(solution)/shard_map/ppermute | solution.py:210
  23.9 1.3 %collective-permute-start.4 = (bf16[736,128]{1,0:T(8,128)(2,1)S(1)}, bf16[736,128]{1,0:T(8,128)(2,1)S(1)}, u32[]{:S(2)}, u32[]{:S(2)}) collective-permute-start(bf16[736,128]{1,0:T(8,128)(2,1)S(1)} %collective-permute-done.2), channel_id=1, source_target_pairs={{2,0},{3,1},{10,8},{11,9},{18,16},{19,17},{26,24},{27,25}} | collective-permute-start | bytes 565256 | tf_op jit(solution)/shard_map/ppermute | solution.py:210
  26.0 15.4 %collective-permute-done.15 = bf16[704,128]{1,0:T(8,128)(2,1)S(1)} collective-permute-done((bf16[704,128]{1,0:T(8,128)(2,1)S(1)}, bf16[704,128]{1,0:T(8,128)(2,1)S(1)}, u32[]{:S(2)}, u32[]{:S(2)}) %collective-permute-start.15) | collective-permute-done | bytes 180256 | tf_op jit(solution)/shard_map/ppermute | solution.py:210
  41.3 1.3 %collective-permute-start.12 = (bf16[736,128]{1,0:T(8,128)(2,1)S(1)}, bf16[736,128]{1,0:T(8,128)(2,1)S(1)}, u32[]{:S(2)}, u32[]{:S(2)}) collective-permute-start(bf16[736,128]{1,0:T(8,128)(2,1)S(1)} %collective-permute-done.7), channel_id=1, source_target_pairs={{2,0},{3,1},{10,8},{11,9},{18,16},{19,17},{26,24},{27,25}} | collective-permute-start | bytes 565256 | tf_op jit(solution)/shard_map/ppermute | solution.py:210
  43.4 2.0 %collective-permute-done.4 = bf16[736,128]{1,0:T(8,128)(2,1)S(1)} collective-permute-done((bf16[736,128]{1,0:T(8,128)(2,1)S(1)}, bf16[736,128]{1,0:T(8,128)(2,1)S(1)}, u32[]{:S(2)}, u32[]{:S(2)}) %collective-permute-start.4) | collective-permute-done | bytes 188448 | tf_op jit(solution)/shard_map/ppermute | solution.py:210
  45.4 1.7 %collective-permute-start.18 = (bf16[2,32,1024]{2,1,0:T(8,128)(2,1)S(1)}, bf16[2,32,1024]{2,1,0:T(8,128)(2,1)S(1)}, u32[]{:S(2)}, u32[]{:S(2)}) collective-permute-start(bf16[2,32,1024]{2,1,0:T(8,128)(2,1)S(1)} %pad_maximum_fusion.19), channel_id=1, source_target_pairs={{0,16},{8,24},{16,0},{24,8},{1,17},{9,25},{17,1},{25,9},{2,18},{10... | collective-permute-start | bytes 393224 | tf_op jit(solution)/shard_map/ppermute | solution.py:175
  47.1 3.4 %collective-permute-start.16 = (bf16[704,128]{1,0:T(8,128)(2,1)S(1)}, bf16[704,128]{1,0:T(8,128)(2,1)S(1)}, u32[]{:S(2)}, u32[]{:S(2)}) collective-permute-start(bf16[704,128]{1,0:T(8,128)(2,1)S(1)} %select_select_fusion.2), channel_id=1, source_target_pairs={{0,1},{1,0},{2,3},{3,2},{4,5},{5,4},{8,9},{9,8},{10,11},{11,10},{1... | collective-permute-start | bytes 540680 | tf_op jit(solution)/shard_map/ppermute | solution.py:179
  50.6 2.4 %collective-permute-start.8 = (bf16[736,128]{1,0:T(8,128)(2,1)S(1)}, bf16[736,128]{1,0:T(8,128)(2,1)S(1)}, u32[]{:S(2)}, u32[]{:S(2)}) collective-permute-start(bf16[736,128]{1,0:T(8,128)(2,1)S(1)} %get-tuple-element.24), channel_id=1, source_target_pairs={{0,1},{1,0},{2,3},{3,2},{4,5},{5,4},{8,9},{9,8},{10,11},{11,10},{1... | collective-permute-start | bytes 565256 | tf_op jit(solution)/shard_map/ppermute | solution.py:179
  53.7 1.7 %copy-done.6 = bf16[2048,1024]{1,0:T(8,128)(2,1)S(1)} copy-done((bf16[2048,1024]{1,0:T(8,128)(2,1)S(1)}, bf16[2048,1024]{1,0:T(8,128)(2,1)}, u32[]{:S(2)}) %copy-start.6) | copy-done | bytes 4194328
  56.7 3.6 %collective-permute-start.13 = (bf16[736,128]{1,0:T(8,128)(2,1)S(1)}, bf16[736,128]{1,0:T(8,128)(2,1)S(1)}, u32[]{:S(2)}, u32[]{:S(2)}) collective-permute-start(bf16[736,128]{1,0:T(8,128)(2,1)S(1)} %select_select_fusion), channel_id=1, source_target_pairs={{0,1},{1,0},{2,3},{3,2},{4,5},{5,4},{8,9},{9,8},{10,11},{11,10},{1... | collective-permute-start | bytes 565256 | tf_op jit(solution)/shard_map/ppermute | solution.py:179
  61.1 1.3 %collective-permute-start.21 = (bf16[256,128]{1,0:T(8,128)(2,1)S(1)}, bf16[256,128]{1,0:T(8,128)(2,1)S(1)}, u32[]{:S(2)}, u32[]{:S(2)}) collective-permute-start(bf16[256,128]{1,0:T(8,128)(2,1)S(1)} %add_convert_fusion), channel_id=1, source_target_pairs={{6,0},{7,1},{14,8},{15,9},{22,16},{23,17},{30,24},{31,25}} | collective-permute-start | bytes 196616 | tf_op jit(solution)/shard_map/ppermute | solution.py:210
  63.0 1.2 %collective-permute-done.13 = bf16[736,128]{1,0:T(8,128)(2,1)S(1)} collective-permute-done((bf16[736,128]{1,0:T(8,128)(2,1)S(1)}, bf16[736,128]{1,0:T(8,128)(2,1)S(1)}, u32[]{:S(2)}, u32[]{:S(2)}) %collective-permute-start.13) | collective-permute-done | bytes 188448 | tf_op jit(solution)/shard_map/ppermute | solution.py:179
  64.3 0.8 collective-permute-start.19
  69.0 1.1 %collective-permute-start.22 = (bf16[256,128]{1,0:T(8,128)(2,1)S(1)}, bf16[256,128]{1,0:T(8,128)(2,1)S(1)}, u32[]{:S(2)}, u32[]{:S(2)}) collective-permute-start(bf16[256,128]{1,0:T(8,128)(2,1)S(1)} %get-tuple-element.36), channel_id=1, source_target_pairs={{0,1},{1,0},{2,3},{3,2},{4,5},{5,4},{6,7},{7,6},{8,9},{9,8},{10,11... | collective-permute-start | bytes 196616 | tf_op jit(solution)/shard_map/ppermute | solution.py:179
  70.6 4.9 %select_convert_fusion = bf16[2048,1024]{1,0:T(8,128)(2,1)} fusion(f32[2048,1024]{1,0:T(8,128)S(1)} %bitcast.74, bf16[2048,128]{1,0:T(8,128)(2,1)S(1)} %slice_select_fusion, pred[1024]{0:T(1024)(128)(4,1)S(1)} %fusion.72, bf16[128,1024]{1,0:T(8,128)(2,1)S(1)} %bitcast.71, bf16[128,1024]{1,0:T(8,128)(2,1)S(1)} %bitcast.69, ...), kind=kOutput, calls=%fused_computation | convolution fusion | flops 1089470464 | bytes 14681088 | tf_op jit(solution)/shard_map/dot_general | solution.py:21
  79.7 4.6 %collective-permute-done.24 = bf16[2,1,32,1024]{3,2,1,0:T(8,128)(2,1)S(1)} collective-permute-done((bf16[2,1,32,1024]{3,2,1,0:T(8,128)(2,1)S(1)}, bf16[2,1,32,1024]{3,2,1,0:T(8,128)(2,1)S(1)}, u32[]{:S(2)}, u32[]{:S(2)}) %collective-permute-start.24) | collective-permute-done | bytes 131104 | tf_op jit(solution)/shard_map/ppermute | solution.py:175
  (136 shorter events, 18.6 us)
Async XLA Ops:
  0.7 6.5 %collective-permute-start = (bf16[1,32,1024]{2,1,0:T(8,128)(2,1)}, bf16[1,32,1024]{2,1,0:T(8,128)(2,1)S(1)}, u32[]{:S(2)}, u32[]{:S(2)}) collective-permute-start(bf16[1,32,1024]{2,1,0:T(8,128)(2,1)} %bitcast.76), channel_id=1, source_target_pairs={{0,8},{8,0},{16,24},{24,16},{1,9},{9,1},{17,25},{25,17},{2,10},{10... | collective-permute-start | bytes 196616 | tf_op jit(solution)/shard_map/ppermute | solution.py:175
  7.2 6.7 %collective-permute-start.1 = (bf16[2,32,1024]{2,1,0:T(8,128)(2,1)S(1)}, bf16[2,32,1024]{2,1,0:T(8,128)(2,1)S(1)}, u32[]{:S(2)}, u32[]{:S(2)}) collective-permute-start(bf16[2,32,1024]{2,1,0:T(8,128)(2,1)S(1)} %pad_maximum_fusion.18), channel_id=1, source_target_pairs={{0,16},{8,24},{16,0},{24,8},{1,17},{9,25},{17,1},{25,9},{2,18},{10... | collective-permute-start | bytes 393224 | tf_op jit(solution)/shard_map/ppermute | solution.py:175
  18.9 2.2 %collective-permute-start.7 = (bf16[736,128]{1,0:T(8,128)(2,1)}, bf16[736,128]{1,0:T(8,128)(2,1)S(1)}, u32[]{:S(2)}, u32[]{:S(2)}) collective-permute-start(bf16[736,128]{1,0:T(8,128)(2,1)} %get-tuple-element.23), channel_id=1, source_target_pairs={{6,2},{7,3},{14,10},{15,11},{22,18},{23,19},{30,26},{31,27}} | collective-permute-start | bytes 565256 | tf_op jit(solution)/shard_map/ppermute | solution.py:210
  19.7 2.2 %collective-permute-start.6 = (bf16[704,128]{1,0:T(8,128)(2,1)}, bf16[704,128]{1,0:T(8,128)(2,1)S(1)}, u32[]{:S(2)}, u32[]{:S(2)}) collective-permute-start(bf16[704,128]{1,0:T(8,128)(2,1)} %get-tuple-element.21), channel_id=1, source_target_pairs={{6,2},{7,3},{14,10},{15,11},{22,18},{23,19},{30,26},{31,27}} | collective-permute-start | bytes 540680 | tf_op jit(solution)/shard_map/ppermute | solution.py:210
  20.4 3.5 %collective-permute-start.2 = (bf16[736,128]{1,0:T(8,128)(2,1)}, bf16[736,128]{1,0:T(8,128)(2,1)S(1)}, u32[]{:S(2)}, u32[]{:S(2)}) collective-permute-start(bf16[736,128]{1,0:T(8,128)(2,1)} %get-tuple-element.20), channel_id=1, source_target_pairs={{6,2},{7,3},{14,10},{15,11},{22,18},{23,19},{30,26},{31,27}} | collective-permute-start | bytes 565256 | tf_op jit(solution)/shard_map/ppermute | solution.py:210
  21.1 4.1 %collective-permute-start.17 = (bf16[1,32,1024]{2,1,0:T(8,128)(2,1)S(1)}, bf16[1,32,1024]{2,1,0:T(8,128)(2,1)S(1)}, u32[]{:S(2)}, u32[]{:S(2)}) collective-permute-start(bf16[1,32,1024]{2,1,0:T(8,128)(2,1)S(1)} %bitcast.77), channel_id=1, source_target_pairs={{0,8},{8,0},{16,24},{24,16},{1,9},{9,1},{17,25},{25,17},{2,10},{10... | collective-permute-start | bytes 196616 | tf_op jit(solution)/shard_map/ppermute | solution.py:175
  21.2 29.4 %collective-permute-start.5 = (bf16[2176,128]{1,0:T(8,128)(2,1)}, bf16[2176,128]{1,0:T(8,128)(2,1)S(1)}, u32[]{:S(2)}, u32[]{:S(2)}) collective-permute-start(bf16[2176,128]{1,0:T(8,128)(2,1)} %copy-done), channel_id=1, source_target_pairs={{6,7},{7,6},{14,15},{15,14},{22,23},{23,22},{30,31},{31,30}} | collective-permute-start | bytes 1671176 | tf_op jit(solution)/shard_map/ppermute | solution.py:179
  21.9 19.4 %collective-permute-start.15 = (bf16[704,128]{1,0:T(8,128)(2,1)S(1)}, bf16[704,128]{1,0:T(8,128)(2,1)S(1)}, u32[]{:S(2)}, u32[]{:S(2)}) collective-permute-start(bf16[704,128]{1,0:T(8,128)(2,1)S(1)} %collective-permute-done.6), channel_id=1, source_target_pairs={{2,0},{3,1},{10,8},{11,9},{18,16},{19,17},{26,24},{27,25}} | collective-permute-start | bytes 540680 | tf_op jit(solution)/shard_map/ppermute | solution.py:210
  23.2 19.4 %collective-permute-start.14 = (bf16[704,128]{1,0:T(8,128)(2,1)S(1)}, bf16[704,128]{1,0:T(8,128)(2,1)S(1)}, u32[]{:S(2)}, u32[]{:S(2)}) collective-permute-start(bf16[704,128]{1,0:T(8,128)(2,1)S(1)} %collective-permute-done.6), channel_id=1, source_target_pairs={{2,4},{3,5},{10,12},{11,13},{18,20},{19,21},{26,28},{27,29}} | collective-permute-start | bytes 540680 | tf_op jit(solution)/shard_map/ppermute | solution.py:210
  23.9 21.4 %collective-permute-start.4 = (bf16[736,128]{1,0:T(8,128)(2,1)S(1)}, bf16[736,128]{1,0:T(8,128)(2,1)S(1)}, u32[]{:S(2)}, u32[]{:S(2)}) collective-permute-start(bf16[736,128]{1,0:T(8,128)(2,1)S(1)} %collective-permute-done.2), channel_id=1, source_target_pairs={{2,0},{3,1},{10,8},{11,9},{18,16},{19,17},{26,24},{27,25}} | collective-permute-start | bytes 565256 | tf_op jit(solution)/shard_map/ppermute | solution.py:210
  25.2 21.8 %collective-permute-start.3 = (bf16[736,128]{1,0:T(8,128)(2,1)S(1)}, bf16[736,128]{1,0:T(8,128)(2,1)S(1)}, u32[]{:S(2)}, u32[]{:S(2)}) collective-permute-start(bf16[736,128]{1,0:T(8,128)(2,1)S(1)} %collective-permute-done.2), channel_id=1, source_target_pairs={{2,4},{3,5},{10,12},{11,13},{18,20},{19,21},{26,28},{27,29}} | collective-permute-start | bytes 565256 | tf_op jit(solution)/shard_map/ppermute | solution.py:210
  41.3 14.6 %collective-permute-start.12 = (bf16[736,128]{1,0:T(8,128)(2,1)S(1)}, bf16[736,128]{1,0:T(8,128)(2,1)S(1)}, u32[]{:S(2)}, u32[]{:S(2)}) collective-permute-start(bf16[736,128]{1,0:T(8,128)(2,1)S(1)} %collective-permute-done.7), channel_id=1, source_target_pairs={{2,0},{3,1},{10,8},{11,9},{18,16},{19,17},{26,24},{27,25}} | collective-permute-start | bytes 565256 | tf_op jit(solution)/shard_map/ppermute | solution.py:210
  42.6 14.0 %collective-permute-start.11 = (bf16[736,128]{1,0:T(8,128)(2,1)S(1)}, bf16[736,128]{1,0:T(8,128)(2,1)S(1)}, u32[]{:S(2)}, u32[]{:S(2)}) collective-permute-start(bf16[736,128]{1,0:T(8,128)(2,1)S(1)} %collective-permute-done.7), channel_id=1, source_target_pairs={{2,4},{3,5},{10,12},{11,13},{18,20},{19,21},{26,28},{27,29}} | collective-permute-start | bytes 565256 | tf_op jit(solution)/shard_map/ppermute | solution.py:210
  45.4 15.6 %collective-permute-start.18 = (bf16[2,32,1024]{2,1,0:T(8,128)(2,1)S(1)}, bf16[2,32,1024]{2,1,0:T(8,128)(2,1)S(1)}, u32[]{:S(2)}, u32[]{:S(2)}) collective-permute-start(bf16[2,32,1024]{2,1,0:T(8,128)(2,1)S(1)} %pad_maximum_fusion.19), channel_id=1, source_target_pairs={{0,16},{8,24},{16,0},{24,8},{1,17},{9,25},{17,1},{25,9},{2,18},{10... | collective-permute-start | bytes 393224 | tf_op jit(solution)/shard_map/ppermute | solution.py:175
  47.1 18.4 %collective-permute-start.16 = (bf16[704,128]{1,0:T(8,128)(2,1)S(1)}, bf16[704,128]{1,0:T(8,128)(2,1)S(1)}, u32[]{:S(2)}, u32[]{:S(2)}) collective-permute-start(bf16[704,128]{1,0:T(8,128)(2,1)S(1)} %select_select_fusion.2), channel_id=1, source_target_pairs={{0,1},{1,0},{2,3},{3,2},{4,5},{5,4},{8,9},{9,8},{10,11},{11,10},{1... | collective-permute-start | bytes 540680 | tf_op jit(solution)/shard_map/ppermute | solution.py:179
  50.6 14.5 %collective-permute-start.8 = (bf16[736,128]{1,0:T(8,128)(2,1)S(1)}, bf16[736,128]{1,0:T(8,128)(2,1)S(1)}, u32[]{:S(2)}, u32[]{:S(2)}) collective-permute-start(bf16[736,128]{1,0:T(8,128)(2,1)S(1)} %get-tuple-element.24), channel_id=1, source_target_pairs={{0,1},{1,0},{2,3},{3,2},{4,5},{5,4},{8,9},{9,8},{10,11},{11,10},{1... | collective-permute-start | bytes 565256 | tf_op jit(solution)/shard_map/ppermute | solution.py:179
  55.9 4.3 %collective-permute-start.9 = (f32[256,128]{1,0:T(8,128)S(1)}, f32[256,128]{1,0:T(8,128)S(1)}, u32[]{:S(2)}, u32[]{:S(2)}) collective-permute-start(f32[256,128]{1,0:T(8,128)S(1)} %convolution_subtract_fusion.1), channel_id=1, source_target_pairs={{6,14},{7,15},{14,6},{15,7},{22,30},{23,31},{30,22},{31,23}} | collective-permute-start | bytes 393224 | tf_op jit(solution)/shard_map/ppermute | solution.py:279
  56.7 7.6 %collective-permute-start.13 = (bf16[736,128]{1,0:T(8,128)(2,1)S(1)}, bf16[736,128]{1,0:T(8,128)(2,1)S(1)}, u32[]{:S(2)}, u32[]{:S(2)}) collective-permute-start(bf16[736,128]{1,0:T(8,128)(2,1)S(1)} %select_select_fusion), channel_id=1, source_target_pairs={{0,1},{1,0},{2,3},{3,2},{4,5},{5,4},{8,9},{9,8},{10,11},{11,10},{1... | collective-permute-start | bytes 565256 | tf_op jit(solution)/shard_map/ppermute | solution.py:179
  61.1 8.0 %collective-permute-start.21 = (bf16[256,128]{1,0:T(8,128)(2,1)S(1)}, bf16[256,128]{1,0:T(8,128)(2,1)S(1)}, u32[]{:S(2)}, u32[]{:S(2)}) collective-permute-start(bf16[256,128]{1,0:T(8,128)(2,1)S(1)} %add_convert_fusion), channel_id=1, source_target_pairs={{6,0},{7,1},{14,8},{15,9},{22,16},{23,17},{30,24},{31,25}} | collective-permute-start | bytes 196616 | tf_op jit(solution)/shard_map/ppermute | solution.py:210
  62.4 6.7 %collective-permute-start.20 = (bf16[256,128]{1,0:T(8,128)(2,1)S(1)}, bf16[256,128]{1,0:T(8,128)(2,1)S(1)}, u32[]{:S(2)}, u32[]{:S(2)}) collective-permute-start(bf16[256,128]{1,0:T(8,128)(2,1)S(1)} %add_convert_fusion), channel_id=1, source_target_pairs={{6,2},{7,3},{14,10},{15,11},{22,18},{23,19},{30,26},{31,27}} | collective-permute-start | bytes 196616 | tf_op jit(solution)/shard_map/ppermute | solution.py:210
  64.3 4.7 %collective-permute-start.19 = (bf16[256,128]{1,0:T(8,128)(2,1)S(1)}, bf16[256,128]{1,0:T(8,128)(2,1)S(1)}, u32[]{:S(2)}, u32[]{:S(2)}) collective-permute-start(bf16[256,128]{1,0:T(8,128)(2,1)S(1)} %add_convert_fusion), channel_id=1, source_target_pairs={{6,4},{7,5},{14,12},{15,13},{22,20},{23,21},{30,28},{31,29}} | collective-permute-start | bytes 196616 | tf_op jit(solution)/shard_map/ppermute | solution.py:210
  68.4 10.4 %collective-permute-start.23 = (bf16[2,2,32,1024]{3,2,0,1:T(8,128)(2,1)S(1)}, bf16[2,2,32,1024]{3,2,0,1:T(8,128)(2,1)S(1)}, u32[]{:S(2)}, u32[]{:S(2)}) collective-permute-start(bf16[2,2,32,1024]{3,2,0,1:T(8,128)(2,1)S(1)} %fusion.35), channel_id=1, source_target_pairs={{0,8},{8,0},{16,24},{24,16},{1,9},{9,1},{17,25},{25,17},{2,10},{10... | collective-permute-start | bytes 786440 | tf_op jit(solution)/shard_map/ppermute | solution.py:175
  69.0 6.4 %collective-permute-start.22 = (bf16[256,128]{1,0:T(8,128)(2,1)S(1)}, bf16[256,128]{1,0:T(8,128)(2,1)S(1)}, u32[]{:S(2)}, u32[]{:S(2)}) collective-permute-start(bf16[256,128]{1,0:T(8,128)(2,1)S(1)} %get-tuple-element.36), channel_id=1, source_target_pairs={{0,1},{1,0},{2,3},{3,2},{4,5},{5,4},{6,7},{7,6},{8,9},{9,8},{10,11... | collective-permute-start | bytes 196616 | tf_op jit(solution)/shard_map/ppermute | solution.py:179
  79.0 5.3 %collective-permute-start.24 = (bf16[2,1,32,1024]{3,2,1,0:T(8,128)(2,1)S(1)}, bf16[2,1,32,1024]{3,2,1,0:T(8,128)(2,1)S(1)}, u32[]{:S(2)}, u32[]{:S(2)}) collective-permute-start(bf16[2,1,32,1024]{3,2,1,0:T(8,128)(2,1)S(1)} %fusion.36), channel_id=1, source_target_pairs={{0,16},{8,24},{16,0},{24,8},{1,17},{9,25},{17,1},{25,9},{2,18},{10... | collective-permute-start | bytes 393224 | tf_op jit(solution)/shard_map/ppermute | solution.py:175
  (21 other events, 161.8 us)

commit v4 on v3

--- a/solution.py
+++ b/solution.py
@@ -60,70 +60,98 @@
     return inverses
 
 
-def invert_kernel(one_ref, two_ref, inv_one_ref, inv_two_ref):
+def prepare_kernel(
+    cuts, side_ref, one_ref, two_ref, adj_ref, inv_one_ref, inv_two_ref, whole_ref, *rest
+):
+    *piece_refs, rows_ref, sem = rest
+    height, panel = rows_ref.shape
+    fetch = pltpu.make_async_copy(
+        adj_ref.at[:, pl.ds(adj_ref.shape[1] - panel, panel)], rows_ref, sem
+    )
+    fetch.start()
     inverse_one, inverse_two = inverse_lower([one_ref[...], two_ref[...]])
     inv_one_ref[...] = inverse_one
     inv_two_ref[...] = inverse_two
-
-
-def invert(diag_one, diag_two):
-    square = jax.ShapeDtypeStruct(diag_one.shape, F32)
+    chosen = jnp.where(side_ref[0] == 1, inverse_two, inverse_one)
+    high, low = halves(chosen)
+    whole_ref[:panel, :] = jnp.zeros((panel, panel), BF16)
+    piece_refs[0][:panel, :] = jnp.zeros((panel, panel), BF16)
+    fetch.wait()
+    for k, ((start, stop), piece_ref) in enumerate(zip(cuts, piece_refs)):
+        own_high, own_low = halves(rows_ref[start:stop, :])
+        product = wide_dot(own_high, high) + (
+            wide_dot(own_high, low) + wide_dot(own_low, high)
+        )
+        product = product.astype(BF16)
+        whole_ref[panel + start : panel + stop, :] = product
+        piece_ref[(panel if k == 0 else 0) :, :] = product
+
+
+def prepare(side, diag_one, diag_two, adj_trail, cuts):
+    height = adj_trail.shape[0]
+    panel = diag_one.shape[0]
+    vmem = pl.BlockSpec(memory_space=pltpu.VMEM)
+    sizes = [stop - start for start, stop in cuts]
+    sizes[0] += panel
     return pl.pallas_call(
-        invert_kernel,
-        out_shape=[square, square],
+        functools.partial(prepare_kernel, cuts),
+        in_specs=[
+            pl.BlockSpec(memory_space=pltpu.SMEM),
+            vmem,
+            vmem,
+            pl.BlockSpec(memory_space=pl.ANY),
+        ],
+        out_specs=[vmem] * (3 + len(cuts)),
+        out_shape=[jax.ShapeDtypeStruct((panel, panel), F32)] * 2
+        + [jax.ShapeDtypeStruct((size, panel), BF16) for size in [panel + height] + sizes],
+        scratch_shapes=[pltpu.VMEM((height, panel), F32), pltpu.SemaphoreType.DMA],
+        compiler_params=pltpu.CompilerParams(vmem_limit_bytes=60 * 2**20),
         cost_estimate=pl.CostEstimate(
-            flops=12 * 12 * diag_one.shape[0] ** 3, bytes_accessed=2**18, transcendentals=0
+            flops=8 * height * panel * panel, bytes_accessed=6 * height * panel, transcendentals=0
         ),
-        name="invert",
-    )(diag_one, diag_two)
-
-
-def solve_kernel(side_ref, one_ref, two_ref, rows_ref, cross_ref, out_ref):
-    panel = one_ref.shape[0]
-    chosen = jnp.where(side_ref[0] == 1, two_ref[...], one_ref[...])
-    high, low = halves(chosen)
-    own_high, own_low = halves(rows_ref[...])
-    product = wide_dot(own_high, high) + (
-        wide_dot(own_high, low) + wide_dot(own_low, high)
-    )
-    out_ref[:panel, :] = cross_ref[...]
-    out_ref[panel:, :] = product.astype(BF16)
-
-
-def solve(side, inverse_one, inverse_two, rows, cross):
-    height, panel = rows.shape
-    vmem = pl.BlockSpec(memory_space=pltpu.VMEM)
+        name="prepare",
+    )(side, diag_one, diag_two, adj_trail)
+
+
+def update_kernel(flags_ref, both_ref, rows_ref, adj_ref, *rest):
+    out_ref = rest[-1]
+    panel = both_ref.shape[1] // 2
+    last = out_ref.shape[1] - panel
+    both = both_ref[...]
+    left = adj_ref[...] - wide_dot(both, rows_ref[...])
+    out_ref[:, :last] = left[:, :last].astype(BF16)
+    block = jnp.where(flags_ref[0] == 1, both[:, panel:], left[:, last:].astype(BF16))
+    out_ref[:, last:] = jnp.where(flags_ref[1] == 1, both[:, :panel], block)
+
+
+def update(flags, both, full_both, adj_trail, start, previous):
+    height, width = adj_trail.shape
+    rows, depth = both.shape
+    tile = depth // 2
+    first = start // tile
+    operands = [flags, both, full_both, adj_trail]
+    in_specs = [
+        pl.BlockSpec(memory_space=pltpu.SMEM),
+        pl.BlockSpec((tile, depth), lambda i: (i, 0)),
+        pl.BlockSpec((depth, width), lambda i: (0, 0)),
+        pl.BlockSpec((tile, width), lambda i: (first + i, 0)),
+    ]
+    if previous is not None:
+        operands.append(previous)
+        in_specs.append(pl.BlockSpec(memory_space=pl.ANY))
     return pl.pallas_call(
-        solve_kernel,
-        in_specs=[pl.BlockSpec(memory_space=pltpu.SMEM)] + [vmem] * 4,
-        out_specs=vmem,
-        out_shape=jax.ShapeDtypeStruct((panel + height, panel), BF16),
-        compiler_params=pltpu.CompilerParams(vmem_limit_bytes=32 * 2**20),
+        update_kernel,
+        grid=(rows // tile,),
+        in_specs=in_specs,
+        out_specs=pl.BlockSpec((tile, width), lambda i: (first + i, 0)),
+        out_shape=jax.ShapeDtypeStruct((height, width), BF16),
+        input_output_aliases={} if previous is None else {4: 0},
+        compiler_params=pltpu.CompilerParams(vmem_limit_bytes=16 * 2**20),
         cost_estimate=pl.CostEstimate(
-            flops=6 * height * panel * panel, bytes_accessed=6 * height * panel, transcendentals=0
+            flops=2 * rows * depth * width, bytes_accessed=6 * rows * width, transcendentals=0
         ),
-        name="solve",
-    )(side, inverse_one, inverse_two, rows, cross)
-
-
-def cut_kernel(cuts, whole_ref, *out_refs):
-    for (start, stop), out_ref in zip(cuts, out_refs):
-        out_ref[...] = whole_ref[start:stop, :]
-
-
-def cut(whole, cuts):
-    panel = whole.shape[1]
-    vmem = pl.BlockSpec(memory_space=pltpu.VMEM)
-    return pl.pallas_call(
-        functools.partial(cut_kernel, cuts),
-        in_specs=[vmem],
-        out_specs=[vmem] * len(cuts),
-        out_shape=[jax.ShapeDtypeStruct((stop - start, panel), BF16) for start, stop in cuts],
-        cost_estimate=pl.CostEstimate(
-            flops=0, bytes_accessed=2 * whole.size, transcendentals=0
-        ),
-        name="cut",
-    )(whole)
+        name="update",
+    )(*operands)
 
 
 def after(value, *others):
@@ -163,10 +191,11 @@
     is_two = col_here % 2 == 1
     here_one = col_here == col_count - 2
     here_two = col_here == col_count - 1
-    step_rows = -(-(height + panel) // (16 * PIECES)) * 16
-    bounds = list(range(step_rows, height + panel, step_rows)) + [height + panel]
-    bounds = [panel] + bounds
-    cuts = list(zip(bounds, bounds[1:]))
+    tiles = height // panel
+    marks = [(k * (tiles + 1) + PIECES - 1) // PIECES - 1 for k in range(1, PIECES)]
+    marks = [0] + marks + [tiles]
+    cuts = [(a * panel, b * panel) for a, b in zip(marks, marks[1:])]
+    final = len(cuts) - 1
 
     def own_rows(matrix):
         return lax.dynamic_slice_in_dim(matrix, row_start, band, 0)
@@ -178,15 +207,17 @@
         pairs = [(2 * k + s, 2 * k + 1 - s) for k in which for s in range(2)]
         return lax.ppermute(value, "col", pairs)
 
-    def gather_rows(value):
-        value = value[None]
-        step = 1
+    def gather_step(value, step):
+        other = row_swap(value, step)
+        low = (row_here // step) % 2 == 0
+        return jnp.concatenate(
+            [jnp.where(low, value, other), jnp.where(low, other, value)], 1
+        )
+
+    def gather_rest(value):
+        step = 2
         while step < row_count:
-            other = row_swap(value, step)
-            low = (row_here // step) % 2 == 0
-            value = jnp.concatenate(
-                [jnp.where(low, value, other), jnp.where(low, other, value)], 0
-            )
+            value = gather_step(value, step)
             step *= 2
         return value.reshape(panel, width)
 
@@ -227,13 +258,15 @@
             span //= 2
         return choose([([k], held[k]) for k in sorted(held)])
 
-    full_two = gather_rows(row_two)
-    inverse_one, inverse_two = invert(diag_one, diag_two)
+    near = gather_step(jnp.stack([row_two, row_one])[:, None], 1)
+    near_two, near_one = near[:1], near[1:]
+    full_two = gather_rest(near_two)
     side = is_two.astype(jnp.int32)[None]
-    whole = solve(
-        side, inverse_one, inverse_two, adj_trail[:, last:], full_two[:, last:]
-    )
-    packets = cut(whole, [(0, cuts[0][1])] + cuts[1:])
+    inverse_one, inverse_two, whole, *packets = prepare(
+        side, after(diag_one, near_two), diag_two, adj_trail, cuts
+    )
+    whole = lax.dynamic_update_slice(whole, full_two[:, last:], (0, 0))
+    packets[0] = lax.dynamic_update_slice(packets[0], full_two[:, last:], (0, 0))
 
     def cross_factor(own, other):
         cross = jnp.where(is_two, other[:panel], own[:panel])
@@ -249,16 +282,17 @@
 
     whole_other = pair_swap(whole, [top])
     first = [spread_first(packet) for packet in packets]
-    final = len(first) - 1
-    full_one = gather_rows(after(row_one, full_two, first[min(1, final)]))
+    full_one = gather_rest(after(near_one, whole))
+    full_both = jnp.concatenate([full_two, full_one], 0)
     arrived, low_other = [], []
     for k, value in enumerate(first):
+        value = after(value, *first[max(k - 1, 0) : k], *arrived[: max(k - 1, 0)])
         arrived.append(spread_rest(value))
-        low_other.append(
-            pair_swap(after(arrived[k], first[min(k + 1, final)]), range(levels - 1))
-        )
-
-    whole_other = after(whole_other, first[final])
+    for k, value in enumerate(arrived):
+        value = after(value, first[min(k + 1, final)], *arrived[:k])
+        low_other.append(pair_swap(value, range(levels - 1)))
+
+    whole_other = after(whole_other, arrived[min(1, final)])
     _, top_factor = cross_factor(whole, whole_other)
     top_both = panels_of(whole, whole_other, top_factor, height)
     terms = wide_dot(top_both.T, trail[:, last:])
@@ -269,6 +303,7 @@
         0,
     )
     terms = terms - placed
+    own_terms = terms
     step = 1
     while step < row_count:
         pairs = [
@@ -289,31 +324,22 @@
     diag_term_one = jnp.where(is_two, terms_other[panel:], terms[panel:])
 
     at_top = level == top
-    own = [jnp.where(at_top, a, b) for a, b in zip(packets, arrived)]
-    other = []
+    flags = jnp.stack([here_one, here_two]).astype(jnp.int32)
+    sums = 0
+    grad_trail = cross = None
     for k, (start, stop) in enumerate(cuts):
-        piece = whole_other[(0 if k == 0 else start) : stop]
-        other.append(jnp.where(at_top, piece, after(low_other[k], row_terms)))
-    cross, factor = cross_factor(own[0], other[0])
-    both = [
-        panels_of(own[k], other[k], factor, stop - start)
-        for k, (start, stop) in enumerate(cuts)
-    ]
-    sums = 0
-    for (start, stop), piece in zip(cuts, both):
-        sums = sums + wide_dot(piece.T, trail[start - panel : stop - panel])
-    both = jnp.concatenate(both, 0)
-    solved_two, tail = both[:, :panel], both[:, panel:]
-
-    grad_diag_two = block_adjoint(
-        diag_two, inverse_two, jnp.tril(adj_diag_two - diag_term_two)
-    )
-    mirror_two = grad_diag_two + grad_diag_two.T
-    adj_two = -crossing - exact_dot(mirror_two, cross.astype(F32))
-    head = exact_dot(adj_two, inverse_one).astype(BF16)
-    seed_one = jnp.tril(adj_diag_one - wide_dot(head.T, cross) - diag_term_one)
-    grad_diag_one = block_adjoint(diag_one, inverse_one, seed_one)
-    mirror_one = grad_diag_one + grad_diag_one.T
+        top_piece = whole_other[(0 if k == 0 else panel + start) : panel + stop]
+        low = after(low_other[k], own_terms)
+        if k == final:
+            low = after(low, row_terms, grad_trail)
+        own = jnp.where(at_top, packets[k], arrived[k])
+        other = jnp.where(at_top, top_piece, low)
+        if k == 0:
+            cross, factor = cross_factor(own, other)
+        both = panels_of(own, other, factor, stop - start)
+        sums = sums + wide_dot(both.T, trail[start:stop])
+        if k < final:
+            grad_trail = update(flags, both, full_both, adj_trail, start, grad_trail)
 
     parts = sums.reshape(2, row_count, band, width)
     step = 1
@@ -322,14 +348,28 @@
         parts = parts.reshape(2, -1, 2, band, width)
         keep = jnp.where(low, parts[:, :, 0], parts[:, :, 1])
         give = jnp.where(low, parts[:, :, 1], parts[:, :, 0])
-        parts = keep + row_swap(give.astype(BF16), step).astype(F32)
+        give = give.astype(BF16)
+        if 2 * step >= row_count:
+            start = cuts[final][0]
+            grad_trail = update(flags, both, full_both, adj_trail, start, grad_trail)
+            give = sent = after(give, grad_trail)
+        parts = keep + row_swap(give, step).astype(F32)
         step *= 2
     parts = parts.reshape(2, band, width)
+
+    grad_diag_two = block_adjoint(
+        diag_two, inverse_two, jnp.tril(adj_diag_two - after(diag_term_two, sent))
+    )
+    mirror_two = grad_diag_two + grad_diag_two.T
+    adj_two = -crossing - exact_dot(mirror_two, cross.astype(F32))
+    head = exact_dot(adj_two, inverse_one).astype(BF16)
+    seed_one = jnp.tril(adj_diag_one - wide_dot(head.T, cross) - diag_term_one)
+    grad_diag_one = block_adjoint(diag_one, inverse_one, seed_one)
+    mirror_one = grad_diag_one + grad_diag_one.T
 
     head_wide = head.astype(F32)
     mix_two = jnp.concatenate([own_rows(mirror_two), own_rows(head_wide)], 1)
     mix_one = jnp.concatenate([own_rows(head_wide.T), own_rows(mirror_one)], 1)
-    full_both = jnp.concatenate([full_two, full_one], 0)
     mix = jnp.concatenate([mix_two, mix_one], 0)
     mixed = wide_dot(
         jnp.concatenate(halves(mix), 1), jnp.concatenate([full_both, full_both], 0)
@@ -337,7 +377,6 @@
     two_left = adj_row_two - mixed[:band] - parts[0]
     one_left = adj_row_one - mixed[band:] - parts[1]
 
-    trail_left = adj_trail - wide_dot(both, full_both)
     column = lax.broadcasted_iota(jnp.int32, (1, width), 1)
     in_block = column >= last
 
@@ -346,7 +385,6 @@
         block = jnp.pad(block, ((0, 0), (last, 0)))
         return jnp.where(in_block & (here_one | here_two), block, matrix)
 
-    grad_trail = put(trail_left, tail, solved_two).astype(BF16)
     nothing = jnp.zeros((band, panel), F32)
     grad_row_one = put(one_left, nothing, nothing)
     grad_row_two = put(two_left, own_rows(head_wide), nothing)

time: 85.7 us -> 87.2 us (1.018)
  Pallas kernels: 7.09 us -> 15.7 us
  matrix products: 11.2 us -> 6.22 us
  local copies, waits for them, and re-layouts: 6.33 us -> 3.27 us
  other arithmetic: 2.5 us -> 5 us
  waiting for transfers between devices: 27.8 us -> 26.9 us
    pallas_call x3 -> x4, Pallas kernels: 7.09 us -> 15.7 us  [the longest x3 10.5 us: update(): pl.pallas_call(update_kernel, grid=(rows // tile,), in_specs=in_specs, ou...]
    ppermute x12, waiting for transfers between devices: 17.9 us -> 24.3 us  [hop(): return lax.ppermute(value, 'col', pairs)]
    ppermute x6 -> x5, waiting for transfers between devices: 8.6 us -> 2.33 us  [row_swap(): return lax.ppermute(value, 'row', [(i, i ^ step) for i in range(row_count)])]
    dot_general x11 -> x10, matrix products: 8.84 us -> 3.92 us  [wide_dot(): return jnp.dot(a, b, preferred_element_type=F32)]
    unnamed x40 -> x32, local copies, waits for them, and re-layouts: 4.61 us -> 2.2 us
    slice x2 -> x0, local copies, waits for them, and re-layouts: 1.3 us -> none  [the longest x1 1.29 us: per_device(): adj_trail[:, last:]]
    select_n x5 -> x7, other arithmetic: 0.15 us -> 1.1 us  [the longest x1 0.89 us: gather_step(): jnp.where(low, other, value)]
    ppermute x5, waiting for transfers between devices: 1.25 us -> 0.31 us  [pair_swap(): return lax.ppermute(value, 'col', pairs)]
  transfers between devices with their start and end apart: 25 -> 24, of which waited for: 6 -> 5; matrix products, arithmetic and copies ran while one was open for 17% -> 10% of each run, Pallas kernels for 5% -> 18%
where the time goes in v4:
time: 87.2 us; the launch traced here: 86.5 us
  starting transfers between devices  28.1 us (32%)
  waiting for transfers between devices  26.9 us (31%)
  Pallas kernels  15.7 us (18%)
  matrix products  6.22 us (7%)
  other arithmetic  5 us (6%)
  local copies, waits for them, and re-layouts  3.27 us (4%)
  between operations  1.42 us (2%)
    ppermute x12, waiting for transfers between devices, hop(): return lax.ppermute(value, 'col', pairs)  24.3 us
    ppermute x12, starting transfers between devices, hop(): return lax.ppermute(value, 'col', pairs)  10.7 us
    ppermute x5, starting transfers between devices, pair_swap(): return lax.ppermute(value, 'col', pairs)  10.5 us
    pallas_call x3, Pallas kernels, update(): pl.pallas_call(update_kernel, grid=(rows // tile,), in_specs=in_specs, ou...  10.5 us
    ppermute x5, starting transfers between devices, row_swap(): return lax.ppermute(value, 'row', [(i, i ^ step) for i in range(row_count)])  5.38 us
    pallas_call x1, Pallas kernels, prepare(): pl.pallas_call(functools.partial(prepare_kernel, cuts), in_specs=[pl.Bloc...  5.19 us
    dot_general x10, matrix products, wide_dot(): return jnp.dot(a, b, preferred_element_type=F32)  3.92 us
    ppermute x5, waiting for transfers between devices, row_swap(): return lax.ppermute(value, 'row', [(i, i ^ step) for i in range(row_count)])  2.33 us
  transfers between devices with their start and end apart: 24, of which 5 were waited for; matrix products, arithmetic and copies ran while one was open for 10% of the time, Pallas kernels for 18%

profile of v4, /device:TPU:0, one launch (start us, length us, event | category | flops | bytes accessed | tf_op | source)
XLA Modules:
  0.0 86.5 jit_solution(8368904774615563758)
XLA Ops:
  0.6 0.9 %maximum_bitcast_fusion = bf16[2,1,32,1024]{3,2,0,1:T(8,128)(2,1)S(1)} fusion(bf16[1,32,1024]{2,1,0:T(8,128)(2,1)} %bitcast.82, bf16[1,32,1024]{2,1,0:T(8,128)(2,1)} %bitcast.84), kind=kLoop, calls=%fused_computation.80 | loop fusion | flops 65536 | bytes 262144 | tf_op jit(solution)/shard_map/broadcast_in_dim | solution.py:261
  2.1 0.7 select_dynamic-update-slice_fusion
  3.0 0.9 %broadcast_select_fusion.11 = (bf16[2,1,32,1024]{3,2,0,1:T(8,128)(2,1)S(1)}, bf16[2,1,32,1024]{3,2,0,1:T(8,128)(2,1)S(1)}) fusion(bf16[2,1,32,1024]{3,2,0,1:T(8,128)(2,1)S(1)} %collective-permute-done, pred[]{:T(512)S(6)} %eq.65, bf16[1,32,1024]{2,1,0:T(8,128)(2,1)} %bitcast.83, bf16[1,32,1024]{2,1,0:T(8,128)(2,1)} %bitcast.85), kind=kLoop, calls=%fused_computation.86 | loop fusion | flops 196608 | bytes 524289 | tf_op jit(solution)/shard_map/jit(_where)/select_n | solution.py:214
  4.0 2.9 %collective-permute-start.3 = (bf16[1,2,32,1024]{3,2,0,1:T(8,128)(2,1)S(1)}, bf16[1,2,32,1024]{3,2,0,1:T(8,128)(2,1)S(1)}, u32[]{:S(2)}, u32[]{:S(2)}) collective-permute-start(bf16[1,2,32,1024]{3,2,0,1:T(8,128)(2,1)S(1)} %get-tuple-element.64), channel_id=1, source_target_pairs={{0,16},{8,24},{16,0},{24,8},{1,17},{9,25},{17,1},{25,9},{2,18},{10... | collective-permute-start | bytes 393224 | tf_op jit(solution)/shard_map/ppermute | solution.py:204
  6.9 5.2 %prepare.1 = (f32[128,128]{1,0:T(8,128)}, f32[128,128]{1,0:T(8,128)}, bf16[2176,128]{1,0:T(8,128)(2,1)}, bf16[768,128]{1,0:T(8,128)(2,1)}, bf16[768,128]{1,0:T(8,128)(2,1)}, /*index=5*/bf16[640,128]{1,0:T(8,128)(2,1)}) custom-call(s32[1]{0:T(128)} %bitcast.2.side_ref, f32[128,128]{1,0:T(8,128)} %one_ref, f32[128,128]{1,0:T(8,128)} %two_ref.1, ...), custom_call_target="tpu_custom_call" | custom-call | flops 268435456 | bytes 1572864 | tf_op jit(solution)/shard_map/prepare/pallas_call | solution.py:96
  14.6 0.7 collective-permute-start.9
  16.0 2.1 %collective-permute-done.17 = bf16[1,2,32,1024]{3,2,0,1:T(8,128)(2,1)S(1)} collective-permute-done((bf16[1,2,32,1024]{3,2,0,1:T(8,128)(2,1)S(1)}, bf16[1,2,32,1024]{3,2,0,1:T(8,128)(2,1)S(1)}, u32[]{:S(2)}, u32[]{:S(2)}) %collective-permute-start.17) | collective-permute-done | bytes 131104 | tf_op jit(solution)/shard_map/ppermute | solution.py:204
  18.8 1.3 %collective-permute-start.6 = (bf16[768,128]{1,0:T(8,128)(2,1)S(1)}, bf16[768,128]{1,0:T(8,128)(2,1)S(1)}, u32[]{:S(2)}, u32[]{:S(2)}) collective-permute-start(bf16[768,128]{1,0:T(8,128)(2,1)S(1)} %collective-permute-done.4), channel_id=1, source_target_pairs={{2,0},{3,1},{10,8},{11,9},{18,16},{19,17},{26,24},{27,25}} | collective-permute-start | bytes 589832 | tf_op jit(solution)/shard_map/ppermute | solution.py:241
  20.2 0.8 collective-permute-start.10
  21.0 1.3 %collective-permute-start.11 = (bf16[768,128]{1,0:T(8,128)(2,1)S(1)}, bf16[768,128]{1,0:T(8,128)(2,1)S(1)}, u32[]{:S(2)}, u32[]{:S(2)}) collective-permute-start(bf16[768,128]{1,0:T(8,128)(2,1)S(1)} %collective-permute-done.2), channel_id=1, source_target_pairs={{2,0},{3,1},{10,8},{11,9},{18,16},{19,17},{26,24},{27,25}} | collective-permute-start | bytes 589832 | tf_op jit(solution)/shard_map/ppermute | solution.py:241
  22.3 17.5 %collective-permute-done.6 = bf16[768,128]{1,0:T(8,128)(2,1)S(1)} collective-permute-done((bf16[768,128]{1,0:T(8,128)(2,1)S(1)}, bf16[768,128]{1,0:T(8,128)(2,1)S(1)}, u32[]{:S(2)}, u32[]{:S(2)}) %collective-permute-start.6) | collective-permute-done | bytes 196640 | tf_op jit(solution)/shard_map/ppermute | solution.py:241
  40.5 1.3 %collective-permute-start.8 = (bf16[640,128]{1,0:T(8,128)(2,1)S(1)}, bf16[640,128]{1,0:T(8,128)(2,1)S(1)}, u32[]{:S(2)}, u32[]{:S(2)}) collective-permute-start(bf16[640,128]{1,0:T(8,128)(2,1)S(1)} %collective-permute-done.1), channel_id=1, source_target_pairs={{2,0},{3,1},{10,8},{11,9},{18,16},{19,17},{26,24},{27,25}} | collective-permute-start | bytes 491528 | tf_op jit(solution)/shard_map/ppermute | solution.py:241
  41.9 3.4 %collective-permute-start.16 = (bf16[768,128]{1,0:T(8,128)(2,1)S(1)}, bf16[768,128]{1,0:T(8,128)(2,1)S(1)}, u32[]{:S(2)}, u32[]{:S(2)}) collective-permute-start(bf16[768,128]{1,0:T(8,128)(2,1)S(1)} %get-tuple-element.38), channel_id=1, source_target_pairs={{0,1},{1,0},{2,3},{3,2},{4,5},{5,4},{8,9},{9,8},{10,11},{11,10},{1... | collective-permute-start | bytes 589832 | tf_op jit(solution)/shard_map/ppermute | solution.py:208
  45.3 2.4 %collective-permute-start.15 = (bf16[768,128]{1,0:T(8,128)(2,1)S(1)}, bf16[768,128]{1,0:T(8,128)(2,1)S(1)}, u32[]{:S(2)}, u32[]{:S(2)}) collective-permute-start(bf16[768,128]{1,0:T(8,128)(2,1)S(1)} %select_select_fusion), channel_id=1, source_target_pairs={{0,1},{1,0},{2,3},{3,2},{4,5},{5,4},{8,9},{9,8},{10,11},{11,10},{1... | collective-permute-start | bytes 589832 | tf_op jit(solution)/shard_map/ppermute | solution.py:208
  47.8 3.4 %collective-permute-start.12 = (bf16[640,128]{1,0:T(8,128)(2,1)S(1)}, bf16[640,128]{1,0:T(8,128)(2,1)S(1)}, u32[]{:S(2)}, u32[]{:S(2)}) collective-permute-start(bf16[640,128]{1,0:T(8,128)(2,1)S(1)} %select_select_fusion.2), channel_id=1, source_target_pairs={{0,1},{1,0},{2,3},{3,2},{4,5},{5,4},{8,9},{9,8},{10,11},{11,10},{1... | collective-permute-start | bytes 491528 | tf_op jit(solution)/shard_map/ppermute | solution.py:208
  52.0 1.5 %copy-done.1 = bf16[2048,1024]{1,0:T(8,128)(2,1)S(1)} copy-done((bf16[2048,1024]{1,0:T(8,128)(2,1)S(1)}, bf16[2048,1024]{1,0:T(8,128)(2,1)}, u32[]{:S(2)}) %copy-start.1) | copy-done | bytes 4194328
  54.0 0.8 collective-permute-start.13
  56.4 3.4 %update.3.rest_0_ = bf16[2048,1024]{1,0:T(8,128)(2,1)} custom-call(s32[2]{0:T(128)S(1)} %add_convert_fusion.1.flags_ref, bf16[640,256]{1,0:T(8,128)(2,1)S(1)} %pad_maximum_fusion.9.both_ref, bf16[256,1024]{1,0:T(8,128)(2,1)S(1)} %pad_maximum_fusion.4.rows_ref, f32[2048,1024]{1,0:T(8,128)S(1)} %bitcast.74), custom_call_target="tpu_custom_call" | custom-call | flops 335544320 | bytes 3932160 | tf_op jit(solution)/shard_map/update/pallas_call | solution.py:142
  60.5 3.7 %update.4.rest_0_ = bf16[2048,1024]{1,0:T(8,128)(2,1)} custom-call(s32[2]{0:T(128)S(1)} %add_convert_fusion.1.flags_ref, bf16[768,256]{1,0:T(8,128)(2,1)S(1)} %pad_maximum_fusion.6.both_ref, bf16[256,1024]{1,0:T(8,128)(2,1)S(1)} %pad_maximum_fusion.4.rows_ref, f32[2048,1024]{1,0:T(8,128)S(1)} %bitcast.74, ...), custom_call_target="tpu_custom_call", output_to_operand_aliasing={{}: (4, {})} | custom-call | flops 402653184 | bytes 4718592 | tf_op jit(solution)/shard_map/update/pallas_call | solution.py:142
  65.6 1.3 %collective-permute-start.20 = (bf16[256,128]{1,0:T(8,128)(2,1)S(1)}, bf16[256,128]{1,0:T(8,128)(2,1)S(1)}, u32[]{:S(2)}, u32[]{:S(2)}) collective-permute-start(bf16[256,128]{1,0:T(8,128)(2,1)S(1)} %add_convert_fusion), channel_id=1, source_target_pairs={{6,0},{7,1},{14,8},{15,9},{22,16},{23,17},{30,24},{31,25}} | collective-permute-start | bytes 196616 | tf_op jit(solution)/shard_map/ppermute | solution.py:241
  68.6 6.7 %collective-permute-done.20 = bf16[256,128]{1,0:T(8,128)(2,1)S(1)} collective-permute-done((bf16[256,128]{1,0:T(8,128)(2,1)S(1)}, bf16[256,128]{1,0:T(8,128)(2,1)S(1)}, u32[]{:S(2)}, u32[]{:S(2)}) %collective-permute-start.20) | collective-permute-done | bytes 65568 | tf_op jit(solution)/shard_map/ppermute | solution.py:241
  76.0 3.4 %update.5 = bf16[2048,1024]{1,0:T(8,128)(2,1)} custom-call(s32[2]{0:T(128)S(1)} %add_convert_fusion.1.flags_ref, bf16[640,256]{1,0:T(8,128)(2,1)S(1)} %pad_maximum_fusion.11.both_ref, bf16[256,1024]{1,0:T(8,128)(2,1)S(1)} %pad_maximum_fusion.4.rows_ref, f32[2048,1024]{1,0:T(8,128)S(1)} %bitcast.74, ...), custom_call_target="tpu_custom_call", output_to_operand_aliasing={{}: (4, {})} | custom-call | flops 335544320 | bytes 3932160 | tf_op jit(solution)/shard_map/update/pallas_call | solution.py:142
  79.9 1.6 %collective-permute-start.23 = (bf16[2,1,32,1024]{3,2,1,0:T(8,128)(2,1)S(1)}, bf16[2,1,32,1024]{3,2,1,0:T(8,128)(2,1)S(1)}, u32[]{:S(2)}, u32[]{:S(2)}) collective-permute-start(bf16[2,1,32,1024]{3,2,1,0:T(8,128)(2,1)S(1)} %fusion.34), channel_id=1, source_target_pairs={{0,16},{8,24},{16,0},{24,8},{1,17},{9,25},{17,1},{25,9},{2,18},{10... | collective-permute-start | bytes 393224 | tf_op jit(solution)/shard_map/ppermute | solution.py:204
  85.8 0.8 fusion.37
  (129 shorter events, 17.2 us)
Async XLA Ops:
  1.5 1.5 %collective-permute-start = (bf16[2,1,32,1024]{3,2,0,1:T(8,128)(2,1)S(1)}, bf16[2,1,32,1024]{3,2,0,1:T(8,128)(2,1)S(1)}, u32[]{:S(2)}, u32[]{:S(2)}) collective-permute-start(bf16[2,1,32,1024]{3,2,0,1:T(8,128)(2,1)S(1)} %maximum_bitcast_fusion), channel_id=1, source_target_pairs={{0,8},{8,0},{16,24},{24,16},{1,9},{9,1},{17,25},{25,17},{2,10},{10... | collective-permute-start | bytes 393224 | tf_op jit(solution)/shard_map/ppermute | solution.py:204
  4.0 8.1 %collective-permute-start.3 = (bf16[1,2,32,1024]{3,2,0,1:T(8,128)(2,1)S(1)}, bf16[1,2,32,1024]{3,2,0,1:T(8,128)(2,1)S(1)}, u32[]{:S(2)}, u32[]{:S(2)}) collective-permute-start(bf16[1,2,32,1024]{3,2,0,1:T(8,128)(2,1)S(1)} %get-tuple-element.64), channel_id=1, source_target_pairs={{0,16},{8,24},{16,0},{24,8},{1,17},{9,25},{17,1},{25,9},{2,18},{10... | collective-permute-start | bytes 393224 | tf_op jit(solution)/shard_map/ppermute | solution.py:204
  12.8 5.3 %collective-permute-start.17 = (bf16[1,2,32,1024]{3,2,0,1:T(8,128)(2,1)S(1)}, bf16[1,2,32,1024]{3,2,0,1:T(8,128)(2,1)S(1)}, u32[]{:S(2)}, u32[]{:S(2)}) collective-permute-start(bf16[1,2,32,1024]{3,2,0,1:T(8,128)(2,1)S(1)} %get-tuple-element.40), channel_id=1, source_target_pairs={{0,16},{8,24},{16,0},{24,8},{1,17},{9,25},{17,1},{25,9},{2,18},{10... | collective-permute-start | bytes 393224 | tf_op jit(solution)/shard_map/ppermute | solution.py:204
  13.2 26.6 %collective-permute-start.1 = (bf16[640,128]{1,0:T(8,128)(2,1)}, bf16[640,128]{1,0:T(8,128)(2,1)S(1)}, u32[]{:S(2)}, u32[]{:S(2)}) collective-permute-start(bf16[640,128]{1,0:T(8,128)(2,1)} %get-tuple-element.26), channel_id=1, source_target_pairs={{6,2},{7,3},{14,10},{15,11},{22,18},{23,19},{30,26},{31,27}} | collective-permute-start | bytes 491528 | tf_op jit(solution)/shard_map/ppermute | solution.py:241
  13.9 6.3 %collective-permute-start.2 = (bf16[768,128]{1,0:T(8,128)(2,1)}, bf16[768,128]{1,0:T(8,128)(2,1)S(1)}, u32[]{:S(2)}, u32[]{:S(2)}) collective-permute-start(bf16[768,128]{1,0:T(8,128)(2,1)} %get-tuple-element.27), channel_id=1, source_target_pairs={{6,2},{7,3},{14,10},{15,11},{22,18},{23,19},{30,26},{31,27}} | collective-permute-start | bytes 589832 | tf_op jit(solution)/shard_map/ppermute | solution.py:241
  14.6 36.7 %collective-permute-start.9 = (bf16[2176,128]{1,0:T(8,128)(2,1)}, bf16[2176,128]{1,0:T(8,128)(2,1)S(1)}, u32[]{:S(2)}, u32[]{:S(2)}) collective-permute-start(bf16[2176,128]{1,0:T(8,128)(2,1)} %get-tuple-element.65), channel_id=1, source_target_pairs={{6,7},{7,6},{14,15},{15,14},{22,23},{23,22},{30,31},{31,30}} | collective-permute-start | bytes 1671176 | tf_op jit(solution)/shard_map/ppermute | solution.py:208
  15.3 2.8 %collective-permute-start.4 = (bf16[768,128]{1,0:T(8,128)(2,1)}, bf16[768,128]{1,0:T(8,128)(2,1)S(1)}, u32[]{:S(2)}, u32[]{:S(2)}) collective-permute-start(bf16[768,128]{1,0:T(8,128)(2,1)} %get-tuple-element.66), channel_id=1, source_target_pairs={{6,2},{7,3},{14,10},{15,11},{22,18},{23,19},{30,26},{31,27}} | collective-permute-start | bytes 589832 | tf_op jit(solution)/shard_map/ppermute | solution.py:241
  18.1 2.9 %collective-permute-start.5 = (bf16[768,128]{1,0:T(8,128)(2,1)S(1)}, bf16[768,128]{1,0:T(8,128)(2,1)S(1)}, u32[]{:S(2)}, u32[]{:S(2)}) collective-permute-start(bf16[768,128]{1,0:T(8,128)(2,1)S(1)} %collective-permute-done.4), channel_id=1, source_target_pairs={{2,4},{3,5},{10,12},{11,13},{18,20},{19,21},{26,28},{27,29}} | collective-permute-start | bytes 589832 | tf_op jit(solution)/shard_map/ppermute | solution.py:241
  18.8 21.0 %collective-permute-start.6 = (bf16[768,128]{1,0:T(8,128)(2,1)S(1)}, bf16[768,128]{1,0:T(8,128)(2,1)S(1)}, u32[]{:S(2)}, u32[]{:S(2)}) collective-permute-start(bf16[768,128]{1,0:T(8,128)(2,1)S(1)} %collective-permute-done.4), channel_id=1, source_target_pairs={{2,0},{3,1},{10,8},{11,9},{18,16},{19,17},{26,24},{27,25}} | collective-permute-start | bytes 589832 | tf_op jit(solution)/shard_map/ppermute | solution.py:241
  20.2 21.7 %collective-permute-start.10 = (bf16[768,128]{1,0:T(8,128)(2,1)S(1)}, bf16[768,128]{1,0:T(8,128)(2,1)S(1)}, u32[]{:S(2)}, u32[]{:S(2)}) collective-permute-start(bf16[768,128]{1,0:T(8,128)(2,1)S(1)} %collective-permute-done.2), channel_id=1, source_target_pairs={{2,4},{3,5},{10,12},{11,13},{18,20},{19,21},{26,28},{27,29}} | collective-permute-start | bytes 589832 | tf_op jit(solution)/shard_map/ppermute | solution.py:241
  21.0 24.3 %collective-permute-start.11 = (bf16[768,128]{1,0:T(8,128)(2,1)S(1)}, bf16[768,128]{1,0:T(8,128)(2,1)S(1)}, u32[]{:S(2)}, u32[]{:S(2)}) collective-permute-start(bf16[768,128]{1,0:T(8,128)(2,1)S(1)} %collective-permute-done.2), channel_id=1, source_target_pairs={{2,0},{3,1},{10,8},{11,9},{18,16},{19,17},{26,24},{27,25}} | collective-permute-start | bytes 589832 | tf_op jit(solution)/shard_map/ppermute | solution.py:241
  39.9 7.9 %collective-permute-start.7 = (bf16[640,128]{1,0:T(8,128)(2,1)S(1)}, bf16[640,128]{1,0:T(8,128)(2,1)S(1)}, u32[]{:S(2)}, u32[]{:S(2)}) collective-permute-start(bf16[640,128]{1,0:T(8,128)(2,1)S(1)} %collective-permute-done.1), channel_id=1, source_target_pairs={{2,4},{3,5},{10,12},{11,13},{18,20},{19,21},{26,28},{27,29}} | collective-permute-start | bytes 491528 | tf_op jit(solution)/shard_map/ppermute | solution.py:241
  40.5 7.2 %collective-permute-start.8 = (bf16[640,128]{1,0:T(8,128)(2,1)S(1)}, bf16[640,128]{1,0:T(8,128)(2,1)S(1)}, u32[]{:S(2)}, u32[]{:S(2)}) collective-permute-start(bf16[640,128]{1,0:T(8,128)(2,1)S(1)} %collective-permute-done.1), channel_id=1, source_target_pairs={{2,0},{3,1},{10,8},{11,9},{18,16},{19,17},{26,24},{27,25}} | collective-permute-start | bytes 491528 | tf_op jit(solution)/shard_map/ppermute | solution.py:241
  41.9 12.9 %collective-permute-start.16 = (bf16[768,128]{1,0:T(8,128)(2,1)S(1)}, bf16[768,128]{1,0:T(8,128)(2,1)S(1)}, u32[]{:S(2)}, u32[]{:S(2)}) collective-permute-start(bf16[768,128]{1,0:T(8,128)(2,1)S(1)} %get-tuple-element.38), channel_id=1, source_target_pairs={{0,1},{1,0},{2,3},{3,2},{4,5},{5,4},{8,9},{9,8},{10,11},{11,10},{1... | collective-permute-start | bytes 589832 | tf_op jit(solution)/shard_map/ppermute | solution.py:208
  45.3 9.4 %collective-permute-start.15 = (bf16[768,128]{1,0:T(8,128)(2,1)S(1)}, bf16[768,128]{1,0:T(8,128)(2,1)S(1)}, u32[]{:S(2)}, u32[]{:S(2)}) collective-permute-start(bf16[768,128]{1,0:T(8,128)(2,1)S(1)} %select_select_fusion), channel_id=1, source_target_pairs={{0,1},{1,0},{2,3},{3,2},{4,5},{5,4},{8,9},{9,8},{10,11},{11,10},{1... | collective-permute-start | bytes 589832 | tf_op jit(solution)/shard_map/ppermute | solution.py:208
  47.8 16.4 %collective-permute-start.12 = (bf16[640,128]{1,0:T(8,128)(2,1)S(1)}, bf16[640,128]{1,0:T(8,128)(2,1)S(1)}, u32[]{:S(2)}, u32[]{:S(2)}) collective-permute-start(bf16[640,128]{1,0:T(8,128)(2,1)S(1)} %select_select_fusion.2), channel_id=1, source_target_pairs={{0,1},{1,0},{2,3},{3,2},{4,5},{5,4},{8,9},{9,8},{10,11},{11,10},{1... | collective-permute-start | bytes 491528 | tf_op jit(solution)/shard_map/ppermute | solution.py:208
  54.0 5.8 %collective-permute-start.13 = (f32[256,128]{1,0:T(8,128)S(1)}, f32[256,128]{1,0:T(8,128)S(1)}, u32[]{:S(2)}, u32[]{:S(2)}) collective-permute-start(f32[256,128]{1,0:T(8,128)S(1)} %convolution_subtract_fusion.1), channel_id=1, source_target_pairs={{6,14},{7,15},{14,6},{15,7},{22,30},{23,31},{30,22},{31,23}} | collective-permute-start | bytes 393224 | tf_op jit(solution)/shard_map/ppermute | solution.py:314
  59.8 4.4 %collective-permute-start.14 = (f32[256,128]{1,0:T(8,128)S(1)}, f32[256,128]{1,0:T(8,128)S(1)}, u32[]{:S(2)}, u32[]{:S(2)}) collective-permute-start(f32[256,128]{1,0:T(8,128)S(1)} %add.58), channel_id=1, source_target_pairs={{6,22},{7,23},{14,30},{15,31},{22,6},{23,7},{30,14},{31,15}} | collective-permute-start | bytes 393224 | tf_op jit(solution)/shard_map/ppermute | solution.py:314
  64.2 4.4 %collective-permute-start.18 = (bf16[256,128]{1,0:T(8,128)(2,1)S(1)}, bf16[256,128]{1,0:T(8,128)(2,1)S(1)}, u32[]{:S(2)}, u32[]{:S(2)}) collective-permute-start(bf16[256,128]{1,0:T(8,128)(2,1)S(1)} %add_convert_fusion), channel_id=1, source_target_pairs={{6,4},{7,5},{14,12},{15,13},{22,20},{23,21},{30,28},{31,29}} | collective-permute-start | bytes 196616 | tf_op jit(solution)/shard_map/ppermute | solution.py:241
  64.9 3.7 %collective-permute-start.19 = (bf16[256,128]{1,0:T(8,128)(2,1)S(1)}, bf16[256,128]{1,0:T(8,128)(2,1)S(1)}, u32[]{:S(2)}, u32[]{:S(2)}) collective-permute-start(bf16[256,128]{1,0:T(8,128)(2,1)S(1)} %add_convert_fusion), channel_id=1, source_target_pairs={{6,2},{7,3},{14,10},{15,11},{22,18},{23,19},{30,26},{31,27}} | collective-permute-start | bytes 196616 | tf_op jit(solution)/shard_map/ppermute | solution.py:241
  65.6 9.8 %collective-permute-start.20 = (bf16[256,128]{1,0:T(8,128)(2,1)S(1)}, bf16[256,128]{1,0:T(8,128)(2,1)S(1)}, u32[]{:S(2)}, u32[]{:S(2)}) collective-permute-start(bf16[256,128]{1,0:T(8,128)(2,1)S(1)} %add_convert_fusion), channel_id=1, source_target_pairs={{6,0},{7,1},{14,8},{15,9},{22,16},{23,17},{30,24},{31,25}} | collective-permute-start | bytes 196616 | tf_op jit(solution)/shard_map/ppermute | solution.py:241
  68.5 11.2 %collective-permute-start.22 = (bf16[2,2,32,1024]{3,2,0,1:T(8,128)(2,1)S(1)}, bf16[2,2,32,1024]{3,2,0,1:T(8,128)(2,1)S(1)}, u32[]{:S(2)}, u32[]{:S(2)}) collective-permute-start(bf16[2,2,32,1024]{3,2,0,1:T(8,128)(2,1)S(1)} %fusion.33), channel_id=1, source_target_pairs={{0,8},{8,0},{16,24},{24,16},{1,9},{9,1},{17,25},{25,17},{2,10},{10... | collective-permute-start | bytes 786440 | tf_op jit(solution)/shard_map/ppermute | solution.py:204
  75.4 4.3 %collective-permute-start.21 = (bf16[256,128]{1,0:T(8,128)(2,1)S(1)}, bf16[256,128]{1,0:T(8,128)(2,1)S(1)}, u32[]{:S(2)}, u32[]{:S(2)}) collective-permute-start(bf16[256,128]{1,0:T(8,128)(2,1)S(1)} %get-tuple-element.50), channel_id=1, source_target_pairs={{0,1},{1,0},{2,3},{3,2},{4,5},{5,4},{6,7},{7,6},{8,9},{9,8},{10,11... | collective-permute-start | bytes 196616 | tf_op jit(solution)/shard_map/ppermute | solution.py:208
  79.9 5.3 %collective-permute-start.23 = (bf16[2,1,32,1024]{3,2,1,0:T(8,128)(2,1)S(1)}, bf16[2,1,32,1024]{3,2,1,0:T(8,128)(2,1)S(1)}, u32[]{:S(2)}, u32[]{:S(2)}) collective-permute-start(bf16[2,1,32,1024]{3,2,1,0:T(8,128)(2,1)S(1)} %fusion.34), channel_id=1, source_target_pairs={{0,16},{8,24},{16,0},{24,8},{1,17},{9,25},{17,1},{25,9},{2,18},{10... | collective-permute-start | bytes 393224 | tf_op jit(solution)/shard_map/ppermute | solution.py:204
  (16 other events, 125.3 us)

commit v5 on v4

--- a/solution.py
+++ b/solution.py
@@ -10,7 +10,7 @@
 EXACT = lax.Precision.HIGHEST
 F32 = jnp.float32
 BF16 = jnp.bfloat16
-PIECES = 3
+PIECES = 2
 
 
 def exact_dot(a, b):
@@ -31,6 +31,14 @@
     rows = lax.broadcasted_iota(jnp.int32, (order, order), 0)
     cols = lax.broadcasted_iota(jnp.int32, (order, order), 1)
     return jnp.where(rows > cols, matrix, jnp.where(rows == cols, 0.5 * matrix, 0))
+
+
+def split_dot(left, right):
+    (left_high, left_low), (right_high, right_low) = left, right
+    return wide_dot(
+        jnp.concatenate([left_high, left_high, left_low], 1),
+        jnp.concatenate([right_high, right_low, right_high], 0),
+    )
 
 
 def inverse_lower(blocks):
@@ -49,63 +57,61 @@
     while size < order:
         below = ((rows ^ cols) & -size == size) & (rows > cols)
         below = below & ((rows ^ cols) < 2 * size)
+        known = [halves(inverse) for inverse in inverses]
         inner = [
-            exact_dot(jnp.where(below, block, 0), inverse)
-            for block, inverse in zip(blocks, inverses)
+            split_dot(halves(jnp.where(below, block, 0)), pair)
+            for block, pair in zip(blocks, known)
         ]
         inverses = [
-            inverse - exact_dot(inverse, part) for inverse, part in zip(inverses, inner)
+            inverse - split_dot(pair, halves(part))
+            for inverse, pair, part in zip(inverses, known, inner)
         ]
         size *= 2
     return inverses
 
 
 def prepare_kernel(
-    cuts, side_ref, one_ref, two_ref, adj_ref, inv_one_ref, inv_two_ref, whole_ref, *rest
+    cuts,
+    side_ref,
+    one_ref,
+    two_ref,
+    adj_ref,
+    inv_one_ref,
+    inv_two_ref,
+    whole_ref,
+    *rest,
 ):
     *piece_refs, rows_ref, sem = rest
-    height, panel = rows_ref.shape
-    fetch = pltpu.make_async_copy(
-        adj_ref.at[:, pl.ds(adj_ref.shape[1] - panel, panel)], rows_ref, sem
-    )
+    panel = one_ref.shape[0]
+    block = pl.ds(adj_ref.shape[1] - panel, panel)
+    fetch = pltpu.make_async_copy(adj_ref.at[:, block], rows_ref, sem)
     fetch.start()
     inverse_one, inverse_two = inverse_lower([one_ref[...], two_ref[...]])
     inv_one_ref[...] = inverse_one
     inv_two_ref[...] = inverse_two
-    chosen = jnp.where(side_ref[0] == 1, inverse_two, inverse_one)
-    high, low = halves(chosen)
-    whole_ref[:panel, :] = jnp.zeros((panel, panel), BF16)
-    piece_refs[0][:panel, :] = jnp.zeros((panel, panel), BF16)
+    chosen = halves(jnp.where(side_ref[0] == 1, inverse_two, inverse_one))
     fetch.wait()
-    for k, ((start, stop), piece_ref) in enumerate(zip(cuts, piece_refs)):
-        own_high, own_low = halves(rows_ref[start:stop, :])
-        product = wide_dot(own_high, high) + (
-            wide_dot(own_high, low) + wide_dot(own_low, high)
-        )
-        product = product.astype(BF16)
-        whole_ref[panel + start : panel + stop, :] = product
-        piece_ref[(panel if k == 0 else 0) :, :] = product
+    for (start, stop), piece_ref in zip(cuts, piece_refs):
+        product = split_dot(halves(rows_ref[start:stop, :]), chosen).astype(BF16)
+        whole_ref[start:stop, :] = product
+        piece_ref[:panel, :] = jnp.zeros((panel, panel), BF16)
+        piece_ref[panel:, :] = product
 
 
 def prepare(side, diag_one, diag_two, adj_trail, cuts):
     height = adj_trail.shape[0]
     panel = diag_one.shape[0]
     vmem = pl.BlockSpec(memory_space=pltpu.VMEM)
-    sizes = [stop - start for start, stop in cuts]
-    sizes[0] += panel
+    hbm = pl.BlockSpec(memory_space=pl.ANY)
+    sizes = [panel + stop - start for start, stop in cuts]
     return pl.pallas_call(
         functools.partial(prepare_kernel, cuts),
-        in_specs=[
-            pl.BlockSpec(memory_space=pltpu.SMEM),
-            vmem,
-            vmem,
-            pl.BlockSpec(memory_space=pl.ANY),
-        ],
+        in_specs=[pl.BlockSpec(memory_space=pltpu.SMEM), vmem, vmem, hbm],
         out_specs=[vmem] * (3 + len(cuts)),
         out_shape=[jax.ShapeDtypeStruct((panel, panel), F32)] * 2
-        + [jax.ShapeDtypeStruct((size, panel), BF16) for size in [panel + height] + sizes],
+        + [jax.ShapeDtypeStruct((size, panel), BF16) for size in [height] + sizes],
         scratch_shapes=[pltpu.VMEM((height, panel), F32), pltpu.SemaphoreType.DMA],
-        compiler_params=pltpu.CompilerParams(vmem_limit_bytes=60 * 2**20),
+        compiler_params=pltpu.CompilerParams(vmem_limit_bytes=56 * 2**20),
         cost_estimate=pl.CostEstimate(
             flops=8 * height * panel * panel, bytes_accessed=6 * height * panel, transcendentals=0
         ),
@@ -127,7 +133,7 @@
 def update(flags, both, full_both, adj_trail, start, previous):
     height, width = adj_trail.shape
     rows, depth = both.shape
-    tile = depth // 2
+    tile = depth
     first = start // tile
     operands = [flags, both, full_both, adj_trail]
     in_specs = [
@@ -191,10 +197,9 @@
     is_two = col_here % 2 == 1
     here_one = col_here == col_count - 2
     here_two = col_here == col_count - 1
-    tiles = height // panel
-    marks = [(k * (tiles + 1) + PIECES - 1) // PIECES - 1 for k in range(1, PIECES)]
-    marks = [0] + marks + [tiles]
-    cuts = [(a * panel, b * panel) for a, b in zip(marks, marks[1:])]
+    tile = 2 * panel
+    marks = [k * (height // tile) // PIECES * tile for k in range(PIECES + 1)]
+    cuts = list(zip(marks, marks[1:]))
     final = len(cuts) - 1
 
     def own_rows(matrix):
@@ -240,37 +245,59 @@
         pairs = [(2 * a + s, 2 * b + s) for a, b in hops for s in range(2)]
         return lax.ppermute(value, "col", pairs)
 
-    def spread_first(value):
-        return hop(value, [(top, levels // 2 - 1)]) if levels > 1 else value
-
-    def spread_rest(first):
-        held = {max(levels // 2 - 1, 0): first}
-        span = levels // 4
+    def spread(pieces, gate):
+        middle, span = levels // 2 - 1, levels // 4
+        first, down = [], []
+        for k in range(len(pieces) + 1):
+            if k == 0:
+                operand, hops = pieces[0], [(top, middle)]
+            elif k < len(pieces):
+                operand = jnp.where(level == top, pieces[k], first[-1])
+                hops = [(top, middle), (middle, middle - span)]
+            else:
+                operand, hops = first[-1], [(middle, middle - span)]
+            moved = hop(operand, hops)
+            if k > 0:
+                down.append(moved)
+            if k < len(pieces):
+                first.append(after(moved, gate) if k == 0 else moved)
+        held = [
+            {middle: here, middle - span: low, middle + span: hop(here, [(middle, middle + span)])}
+            for here, low in zip(first, down)
+        ]
+        span //= 2
         while span >= 1:
-            fresh = list(held)
-            operand = choose([([k], held[k]) for k in fresh])
-            up = hop(operand, [(k, k + span) for k in fresh])
-            down = hop(operand, [(k, k - span) for k in fresh if k >= span])
-            for k in fresh:
-                held[k + span] = up
-                if k >= span:
-                    held[k - span] = down
+            for piece in held:
+                fresh = list(piece)
+                operand = choose([([k], piece[k]) for k in fresh])
+                up = hop(operand, [(k, k + span) for k in fresh])
+                low = hop(operand, [(k, k - span) for k in fresh if k >= span])
+                for k in fresh:
+                    piece[k + span] = up
+                    if k >= span:
+                        piece[k - span] = low
             span //= 2
-        return choose([([k], held[k]) for k in sorted(held)])
-
-    near = gather_step(jnp.stack([row_two, row_one])[:, None], 1)
-    near_two, near_one = near[:1], near[1:]
+        arrived = []
+        for piece in held:
+            options = [([k], after(piece[k], *arrived)) for k in sorted(piece)]
+            arrived.append(choose(options))
+        return first, arrived
+
+    near_two = gather_step(row_two[None, None], 1)
+    near_one = gather_step(row_one[None, None], 1)
     full_two = gather_rest(near_two)
     side = is_two.astype(jnp.int32)[None]
     inverse_one, inverse_two, whole, *packets = prepare(
-        side, after(diag_one, near_two), diag_two, adj_trail, cuts
-    )
-    whole = lax.dynamic_update_slice(whole, full_two[:, last:], (0, 0))
-    packets[0] = lax.dynamic_update_slice(packets[0], full_two[:, last:], (0, 0))
-
-    def cross_factor(own, other):
-        cross = jnp.where(is_two, other[:panel], own[:panel])
-        return cross, jnp.concatenate(halves(exact_dot(cross.astype(F32), inverse_one)), 0)
+        side, after(diag_one, near_two, near_one), diag_two, adj_trail, cuts
+    )
+    own_cross = full_two[:, last:]
+    packets[0] = lax.dynamic_update_slice(packets[0], own_cross, (0, 0))
+    full_one = gather_rest(after(near_one, packets[0]))
+    full_both = jnp.concatenate([full_two, full_one], 0)
+    edge = after(trail[:, last:], packets[0])
+
+    def factor_of(cross):
+        return jnp.concatenate(halves(exact_dot(cross.astype(F32), inverse_one)), 0)
 
     def panels_of(own, other, factor, size):
         solved_two = jnp.where(is_two, own[-size:], other[-size:])
@@ -281,21 +308,17 @@
         return jnp.concatenate([solved_two, tail.astype(BF16)], 1)
 
     whole_other = pair_swap(whole, [top])
-    first = [spread_first(packet) for packet in packets]
-    full_one = gather_rest(after(near_one, whole))
-    full_both = jnp.concatenate([full_two, full_one], 0)
-    arrived, low_other = [], []
-    for k, value in enumerate(first):
-        value = after(value, *first[max(k - 1, 0) : k], *arrived[: max(k - 1, 0)])
-        arrived.append(spread_rest(value))
+    first, arrived = spread(packets, full_one)
+    at_top = level == top
+    other = []
+    own = [jnp.where(at_top, a, b) for a, b in zip(packets, arrived)]
     for k, value in enumerate(arrived):
-        value = after(value, first[min(k + 1, final)], *arrived[:k])
-        low_other.append(pair_swap(value, range(levels - 1)))
-
-    whole_other = after(whole_other, arrived[min(1, final)])
-    _, top_factor = cross_factor(whole, whole_other)
-    top_both = panels_of(whole, whole_other, top_factor, height)
-    terms = wide_dot(top_both.T, trail[:, last:])
+        value = own[0] if k == 0 else value
+        other.append(pair_swap(value, range(levels if k == 0 else levels - 1)))
+
+    whole_other = after(whole_other, first[final])
+    top_both = panels_of(whole, whole_other, factor_of(own_cross), height)
+    terms = wide_dot(top_both.T, edge)
     placed = lax.dynamic_update_slice_in_dim(
         jnp.zeros((2 * panel, panel), F32),
         jnp.where(is_two, 0, adj_row_two[:, last:]),
@@ -312,6 +335,8 @@
             for c in (col_count - 2, col_count - 1)
         ]
         terms = terms + lax.ppermute(terms, ("row", "col"), pairs)
+        if step == 1:
+            terms = after(terms, other[0])
         step *= 2
     terms = row_terms = terms.astype(BF16)
     terms = choose(
@@ -323,20 +348,18 @@
     crossing = jnp.where(is_two, terms_other[:panel], terms[:panel])
     diag_term_one = jnp.where(is_two, terms_other[panel:], terms[panel:])
 
-    at_top = level == top
     flags = jnp.stack([here_one, here_two]).astype(jnp.int32)
+    cross = jnp.where(is_two, other[0][:panel], own[0][:panel])
+    factor = factor_of(cross)
     sums = 0
-    grad_trail = cross = None
+    grad_trail = None
     for k, (start, stop) in enumerate(cuts):
-        top_piece = whole_other[(0 if k == 0 else panel + start) : panel + stop]
-        low = after(low_other[k], own_terms)
+        theirs = after(other[k], own_terms)
         if k == final:
-            low = after(low, row_terms, grad_trail)
-        own = jnp.where(at_top, packets[k], arrived[k])
-        other = jnp.where(at_top, top_piece, low)
-        if k == 0:
-            cross, factor = cross_factor(own, other)
-        both = panels_of(own, other, factor, stop - start)
+            theirs = after(theirs, row_terms, grad_trail)
+        if k > 0:
+            theirs = jnp.where(at_top, whole_other[start:stop], theirs[panel:])
+        both = panels_of(own[k], theirs, factor, stop - start)
         sums = sums + wide_dot(both.T, trail[start:stop])
         if k < final:
             grad_trail = update(flags, both, full_both, adj_trail, start, grad_trail)

time: 87.2 us -> 87.2 us (level)
  waiting for transfers between devices: 26.9 us -> 36.3 us
  starting transfers between devices: 28.1 us -> 20.7 us
  local copies, waits for them, and re-layouts: 3.27 us -> 8.34 us
  Pallas kernels: 15.7 us -> 10.8 us
  other arithmetic: 5 us -> 3.4 us
    ppermute x5 -> x4, starting transfers between devices: 10.5 us -> 5.4 us  [pair_swap(): return lax.ppermute(value, 'col', pairs)]
    unnamed x32 -> x36, local copies, waits for them, and re-layouts: 2.2 us -> 7.29 us
    pallas_call x3 -> x2, Pallas kernels: 10.5 us -> 6.16 us  [update(): pl.pallas_call(update_kernel, grid=(rows // tile,), in_specs=in_specs, ou...]
    ppermute x12 -> x8, waiting for transfers between devices: 24.3 us -> 28.4 us  [hop(): return lax.ppermute(value, 'col', pairs)]
    ppermute x12 -> x8, starting transfers between devices: 10.7 us -> 7.23 us  [hop(): return lax.ppermute(value, 'col', pairs)]
    ppermute x5 -> x6, waiting for transfers between devices: 2.33 us -> 5.45 us  [row_swap(): return lax.ppermute(value, 'row', [(i, i ^ step) for i in range(row_count)])]
    ppermute x5 -> x4, waiting for transfers between devices: 0.31 us -> 2.46 us  [pair_swap(): return lax.ppermute(value, 'col', pairs)]
    ppermute x5 -> x6, starting transfers between devices: 5.38 us -> 6.76 us  [row_swap(): return lax.ppermute(value, 'row', [(i, i ^ step) for i in range(row_count)])]
  transfers between devices with their start and end apart: 24 -> 20, of which waited for: 5 -> 8; matrix products, arithmetic and copies ran while one was open for 10% -> 4% of each run, Pallas kernels for 18% -> 12%
where the time goes in v5:
time: 87.2 us; the launch traced here: 86.7 us
  waiting for transfers between devices  36.3 us (42%)
  starting transfers between devices  20.7 us (24%)
  Pallas kernels  10.8 us (12%)
  local copies, waits for them, and re-layouts  8.34 us (10%)
  matrix products  5.74 us (7%)
  other arithmetic  3.4 us (4%)
  between operations  1.45 us (2%)
    ppermute x8, waiting for transfers between devices, hop(): return lax.ppermute(value, 'col', pairs)  28.4 us
    unnamed x36, local copies, waits for them, and re-layouts  7.29 us
    ppermute x8, starting transfers between devices, hop(): return lax.ppermute(value, 'col', pairs)  7.23 us
    ppermute x6, starting transfers between devices, row_swap(): return lax.ppermute(value, 'row', [(i, i ^ step) for i in range(row_count)])  6.76 us
    pallas_call x2, Pallas kernels, update(): pl.pallas_call(update_kernel, grid=(rows // tile,), in_specs=in_specs, ou...  6.16 us
    ppermute x6, waiting for transfers between devices, row_swap(): return lax.ppermute(value, 'row', [(i, i ^ step) for i in range(row_count)])  5.45 us
    ppermute x4, starting transfers between devices, pair_swap(): return lax.ppermute(value, 'col', pairs)  5.4 us
    pallas_call x1, Pallas kernels, prepare(): pl.pallas_call(functools.partial(prepare_kernel, cuts), in_specs=[pl.Bloc...  4.6 us
  transfers between devices with their start and end apart: 20, of which 8 were waited for; matrix products, arithmetic and copies ran while one was open for 4% of the time, Pallas kernels for 12%

profile of v5, /device:TPU:0, one launch (start us, length us, event | category | flops | bytes accessed | tf_op | source)
XLA Modules:
  0.0 86.7 jit_solution(13527215782232699957)
XLA Ops:
  1.2 1.0 %collective-permute-done = bf16[1,1,32,1024]{3,2,1,0:T(8,128)(2,1)S(1)} collective-permute-done((bf16[1,1,32,1024]{3,2,1,0:T(8,128)(2,1)}, bf16[1,1,32,1024]{3,2,1,0:T(8,128)(2,1)S(1)}, u32[]{:S(2)}, u32[]{:S(2)}) %collective-permute-start) | collective-permute-done | bytes 65568 | tf_op jit(solution)/shard_map/ppermute | solution.py:209
  2.6 0.9 %broadcast_select_fusion.10 = (bf16[1,1,32,1024]{3,2,1,0:T(8,128)(2,1)S(1)}, bf16[1,1,32,1024]{3,2,1,0:T(8,128)(2,1)S(1)}, bf16[1,1,32,1024]{3,2,1,0:T(8,128)(2,1)S(1)}, bf16[1,1,32,1024]{3,2,1,0:T(8,128)(2,1)S(1)}) fusion(bf16[1,1,32,1024]{3,2,1,0:T(8,128)(2,1)S(1)} %collective-permute-done.1, pred[]{:T(512)S(6)} %eq.66, bf16[32,1024]{1,0:T(8,128)(2,1)} %param.11, ...), kind=kLoop, calls=%fused_computation.109 | loop fusion | flops 131072 | bytes 524289 | tf_op jit(solution)/shard_map/jit(_where)/select_n | solution.py:219
  3.5 2.7 %collective-permute-start.2 = (bf16[1,2,32,1024]{3,2,1,0:T(8,128)(2,1)S(1)}, bf16[1,2,32,1024]{3,2,1,0:T(8,128)(2,1)S(1)}, u32[]{:S(2)}, u32[]{:S(2)}) collective-permute-start(bf16[1,2,32,1024]{3,2,1,0:T(8,128)(2,1)S(1)} %pad_maximum_fusion.13), channel_id=1, source_target_pairs={{0,16},{8,24},{16,0},{24,8},{1,17},{9,25},{17,1},{25,9},{2,18},{10... | collective-permute-start | bytes 393224 | tf_op jit(solution)/shard_map/ppermute | solution.py:209
  6.3 4.6 %prepare.1 = (f32[128,128]{1,0:T(8,128)}, f32[128,128]{1,0:T(8,128)}, bf16[2048,128]{1,0:T(8,128)(2,1)}, bf16[1152,128]{1,0:T(8,128)(2,1)}, bf16[1152,128]{1,0:T(8,128)(2,1)}) custom-call(s32[1]{0:T(128)} %bitcast.2.side_ref, f32[128,128]{1,0:T(8,128)} %one_ref, f32[128,128]{1,0:T(8,128)} %two_ref.1, f32[2048,1024]{1,0:T(8,128)} %adj_ref.5), custom_call_target="tpu_custom_call" | custom-call | flops 268435456 | bytes 1572864 | tf_op jit(solution)/shard_map/prepare/pallas_call | solution.py:107
  11.6 1.1 %collective-permute-start.4 = (bf16[1,2,32,1024]{3,2,1,0:T(8,128)(2,1)S(1)}, bf16[1,2,32,1024]{3,2,1,0:T(8,128)(2,1)S(1)}, u32[]{:S(2)}, u32[]{:S(2)}) collective-permute-start(bf16[1,2,32,1024]{3,2,1,0:T(8,128)(2,1)S(1)} %pad_maximum_fusion.14), channel_id=1, source_target_pairs={{0,16},{8,24},{16,0},{24,8},{1,17},{9,25},{17,1},{25,9},{2,18},{10... | collective-permute-start | bytes 393224 | tf_op jit(solution)/shard_map/ppermute | solution.py:209
  12.8 0.8 collective-permute-start.9
  14.3 2.7 %collective-permute-done.4 = bf16[1,2,32,1024]{3,2,1,0:T(8,128)(2,1)S(1)} collective-permute-done((bf16[1,2,32,1024]{3,2,1,0:T(8,128)(2,1)S(1)}, bf16[1,2,32,1024]{3,2,1,0:T(8,128)(2,1)S(1)}, u32[]{:S(2)}, u32[]{:S(2)}) %collective-permute-start.4) | collective-permute-done | bytes 131104 | tf_op jit(solution)/shard_map/ppermute | solution.py:209
  17.2 1.3 %collective-permute-start.5 = (bf16[1152,128]{1,0:T(8,128)(2,1)S(1)}, bf16[1152,128]{1,0:T(8,128)(2,1)S(1)}, u32[]{:S(2)}, u32[]{:S(2)}) collective-permute-start(bf16[1152,128]{1,0:T(8,128)(2,1)S(1)} %broadcast_select_fusion.2), channel_id=1, source_target_pairs={{6,2},{7,3},{2,0},{3,1},{14,10},{15,11},{10,8},{11,9},{22,18},{23,... | collective-permute-start | bytes 884744 | tf_op jit(solution)/shard_map/ppermute | solution.py:246
  19.4 16.2 %collective-permute-done.5 = bf16[1152,128]{1,0:T(8,128)(2,1)S(1)} collective-permute-done((bf16[1152,128]{1,0:T(8,128)(2,1)S(1)}, bf16[1152,128]{1,0:T(8,128)(2,1)S(1)}, u32[]{:S(2)}, u32[]{:S(2)}) %collective-permute-start.5) | collective-permute-done | bytes 294944 | tf_op jit(solution)/shard_map/ppermute | solution.py:246
  36.9 1.3 %collective-permute-start.8 = (bf16[1152,128]{1,0:T(8,128)(2,1)S(1)}, bf16[1152,128]{1,0:T(8,128)(2,1)S(1)}, u32[]{:S(2)}, u32[]{:S(2)}) collective-permute-start(bf16[1152,128]{1,0:T(8,128)(2,1)S(1)} %collective-permute-done.5), channel_id=1, source_target_pairs={{2,0},{3,1},{10,8},{11,9},{18,16},{19,17},{26,24},{27,25}} | collective-permute-start | bytes 884744 | tf_op jit(solution)/shard_map/ppermute | solution.py:246
  40.2 2.5 %collective-permute-done.12 = bf16[1152,128]{1,0:T(8,128)(2,1)S(1)} collective-permute-done((bf16[1152,128]{1,0:T(8,128)(2,1)S(1)}, bf16[1152,128]{1,0:T(8,128)(2,1)S(1)}, u32[]{:S(2)}, u32[]{:S(2)}) %collective-permute-start.12) | collective-permute-done | bytes 294944 | tf_op jit(solution)/shard_map/ppermute | solution.py:213
  43.3 2.2 %collective-permute-done.8 = bf16[1152,128]{1,0:T(8,128)(2,1)S(1)} collective-permute-done((bf16[1152,128]{1,0:T(8,128)(2,1)S(1)}, bf16[1152,128]{1,0:T(8,128)(2,1)S(1)}, u32[]{:S(2)}, u32[]{:S(2)}) %collective-permute-start.8) | collective-permute-done | bytes 294944 | tf_op jit(solution)/shard_map/ppermute | solution.py:246
  45.6 3.4 %collective-permute-start.10 = (bf16[1152,128]{1,0:T(8,128)(2,1)S(1)}, bf16[1152,128]{1,0:T(8,128)(2,1)S(1)}, u32[]{:S(2)}, u32[]{:S(2)}) collective-permute-start(bf16[1152,128]{1,0:T(8,128)(2,1)S(1)} %select_select_fusion), channel_id=1, source_target_pairs={{0,1},{1,0},{2,3},{3,2},{4,5},{5,4},{8,9},{9,8},{10,11},{11,10},{1... | collective-permute-start | bytes 884744 | tf_op jit(solution)/shard_map/ppermute | solution.py:213
  50.6 1.3 %collective-permute-start.16 = (bf16[256,128]{1,0:T(8,128)(2,1)S(1)}, bf16[256,128]{1,0:T(8,128)(2,1)S(1)}, u32[]{:S(2)}, u32[]{:S(2)}) collective-permute-start(bf16[256,128]{1,0:T(8,128)(2,1)S(1)} %add_convert_fusion), channel_id=1, source_target_pairs={{6,0},{7,1},{14,8},{15,9},{22,16},{23,17},{30,24},{31,25}} | collective-permute-start | bytes 196616 | tf_op jit(solution)/shard_map/ppermute | solution.py:246
  52.2 10.0 %collective-permute-done.16 = bf16[256,128]{1,0:T(8,128)(2,1)S(1)} collective-permute-done((bf16[256,128]{1,0:T(8,128)(2,1)S(1)}, bf16[256,128]{1,0:T(8,128)(2,1)S(1)}, u32[]{:S(2)}, u32[]{:S(2)}) %collective-permute-start.16) | collective-permute-done | bytes 65568 | tf_op jit(solution)/shard_map/ppermute | solution.py:246
  62.9 3.4 %copy-done = f32[2048,1024]{1,0:T(8,128)S(1)} copy-done((f32[2048,1024]{1,0:T(8,128)S(1)}, f32[2048,1024]{1,0:T(8,128)}, u32[]{:S(2)}) %copy-start) | copy-done | bytes 8388632
  66.3 3.1 %update.2.rest_0_ = bf16[2048,1024]{1,0:T(8,128)(2,1)} custom-call(s32[2]{0:T(128)S(1)} %add_convert_fusion.1.flags_ref, bf16[1024,256]{1,0:T(8,128)(2,1)S(1)} %pad_maximum_fusion.5.both_ref, bf16[256,1024]{1,0:T(8,128)(2,1)S(1)} %pad_maximum_fusion.10.rows_ref, f32[2048,1024]{1,0:T(8,128)S(1)} %copy-done), custom_call_target="tpu_custom_call" | custom-call | flops 536870912 | bytes 6291456 | tf_op jit(solution)/shard_map/update/pallas_call | solution.py:148
  69.8 1.8 %copy-done.1 = bf16[2048,1024]{1,0:T(8,128)(2,1)S(1)} copy-done((bf16[2048,1024]{1,0:T(8,128)(2,1)S(1)}, bf16[2048,1024]{1,0:T(8,128)(2,1)}, u32[]{:S(2)}) %copy-start.1) | copy-done | bytes 4194328
  72.3 0.7 fusion.4
  73.4 1.3 %slice-done.1 = s8[4194304]{0:T(1024)(128)(4,1)S(1)} async-done(((s8[8388608]{0:T(1024)(128)(4,1)}), s8[4194304]{0:T(1024)(128)(4,1)S(1)}, s32[]{:S(2)}) %slice-start.1) | async-done | bytes 4194328
  74.6 3.1 %update.3 = bf16[2048,1024]{1,0:T(8,128)(2,1)} custom-call(s32[2]{0:T(128)S(1)} %add_convert_fusion.1.flags_ref, bf16[1024,256]{1,0:T(8,128)(2,1)S(1)} %pad_maximum_fusion.7.both_ref, bf16[256,1024]{1,0:T(8,128)(2,1)S(1)} %pad_maximum_fusion.10.rows_ref, f32[2048,1024]{1,0:T(8,128)S(1)} %bitcast.73, ...), custom_call_target="tpu_custom_call", output_to_operand_aliasing={{}: (4, {})} | custom-call | flops 536870912 | bytes 6291456 | tf_op jit(solution)/shard_map/update/pallas_call | solution.py:148
  80.7 2.3 %collective-permute-start.19 = (bf16[2,1,32,1024]{3,2,1,0:T(8,128)(2,1)S(1)}, bf16[2,1,32,1024]{3,2,1,0:T(8,128)(2,1)S(1)}, u32[]{:S(2)}, u32[]{:S(2)}) collective-permute-start(bf16[2,1,32,1024]{3,2,1,0:T(8,128)(2,1)S(1)} %fusion.26), channel_id=1, source_target_pairs={{0,16},{8,24},{16,0},{24,8},{1,17},{9,25},{17,1},{25,9},{2,18},{10... | collective-permute-start | bytes 393224 | tf_op jit(solution)/shard_map/ppermute | solution.py:209
  84.6 1.3 %collective-permute-done.19 = bf16[2,1,32,1024]{3,2,1,0:T(8,128)(2,1)S(1)} collective-permute-done((bf16[2,1,32,1024]{3,2,1,0:T(8,128)(2,1)S(1)}, bf16[2,1,32,1024]{3,2,1,0:T(8,128)(2,1)S(1)}, u32[]{:S(2)}, u32[]{:S(2)}) %collective-permute-start.19) | collective-permute-done | bytes 131104 | tf_op jit(solution)/shard_map/ppermute | solution.py:209
  86.0 0.7 fusion.28
  (122 shorter events, 15.5 us)
Async XLA Ops:
  0.6 1.6 %collective-permute-start = (bf16[1,1,32,1024]{3,2,1,0:T(8,128)(2,1)}, bf16[1,1,32,1024]{3,2,1,0:T(8,128)(2,1)S(1)}, u32[]{:S(2)}, u32[]{:S(2)}) collective-permute-start(bf16[1,1,32,1024]{3,2,1,0:T(8,128)(2,1)} %bitcast.83), channel_id=1, source_target_pairs={{0,8},{8,0},{16,24},{24,16},{1,9},{9,1},{17,25},{25,17},{2,10},{10... | collective-permute-start | bytes 196616 | tf_op jit(solution)/shard_map/ppermute | solution.py:209
  1.1 1.5 %collective-permute-start.1 = (bf16[1,1,32,1024]{3,2,1,0:T(8,128)(2,1)}, bf16[1,1,32,1024]{3,2,1,0:T(8,128)(2,1)S(1)}, u32[]{:S(2)}, u32[]{:S(2)}) collective-permute-start(bf16[1,1,32,1024]{3,2,1,0:T(8,128)(2,1)} %bitcast.82), channel_id=1, source_target_pairs={{0,8},{8,0},{16,24},{24,16},{1,9},{9,1},{17,25},{25,17},{2,10},{10... | collective-permute-start | bytes 196616 | tf_op jit(solution)/shard_map/ppermute | solution.py:209
  3.5 7.4 %collective-permute-start.2 = (bf16[1,2,32,1024]{3,2,1,0:T(8,128)(2,1)S(1)}, bf16[1,2,32,1024]{3,2,1,0:T(8,128)(2,1)S(1)}, u32[]{:S(2)}, u32[]{:S(2)}) collective-permute-start(bf16[1,2,32,1024]{3,2,1,0:T(8,128)(2,1)S(1)} %pad_maximum_fusion.13), channel_id=1, source_target_pairs={{0,16},{8,24},{16,0},{24,8},{1,17},{9,25},{17,1},{25,9},{2,18},{10... | collective-permute-start | bytes 393224 | tf_op jit(solution)/shard_map/ppermute | solution.py:209
  6.3 6.4 %copy-start.9 = (f32[32,1024]{1,0:T(8,128)S(1)}, f32[32,1024]{1,0:T(8,128)}, u32[]{:S(2)}) copy-start(f32[32,1024]{1,0:T(8,128)} %param.17) | copy-start | bytes 393220
  10.9 6.3 %copy-start.3 = (bf16[1152,128]{1,0:T(8,128)(2,1)S(1)}, bf16[1152,128]{1,0:T(8,128)(2,1)}, u32[]{:S(2)}) copy-start(bf16[1152,128]{1,0:T(8,128)(2,1)} %get-tuple-element.25) | copy-start | bytes 884740
  10.9 7.6 %copy-start.2 = (f32[128,128]{1,0:T(8,128)S(1)}, f32[128,128]{1,0:T(8,128)}, u32[]{:S(2)}) copy-start(f32[128,128]{1,0:T(8,128)} %get-tuple-element.34) | copy-start | bytes 196612
  11.6 5.5 %collective-permute-start.4 = (bf16[1,2,32,1024]{3,2,1,0:T(8,128)(2,1)S(1)}, bf16[1,2,32,1024]{3,2,1,0:T(8,128)(2,1)S(1)}, u32[]{:S(2)}, u32[]{:S(2)}) collective-permute-start(bf16[1,2,32,1024]{3,2,1,0:T(8,128)(2,1)S(1)} %pad_maximum_fusion.14), channel_id=1, source_target_pairs={{0,16},{8,24},{16,0},{24,8},{1,17},{9,25},{17,1},{25,9},{2,18},{10... | collective-permute-start | bytes 393224 | tf_op jit(solution)/shard_map/ppermute | solution.py:209
  12.8 23.0 %copy-start.5 = (bf16[1152,128]{1,0:T(8,128)(2,1)S(1)}, bf16[1152,128]{1,0:T(8,128)(2,1)}, u32[]{:S(2)}) copy-start(bf16[1152,128]{1,0:T(8,128)(2,1)} %slice_dynamic-update-slice_fusion) | copy-start | bytes 884740
  12.8 6.6 %collective-permute-start.9 = (bf16[2048,128]{1,0:T(8,128)(2,1)S(1)}, bf16[2048,128]{1,0:T(8,128)(2,1)S(1)}, u32[]{:S(2)}, u32[]{:S(2)}) collective-permute-start(bf16[2048,128]{1,0:T(8,128)(2,1)S(1)} %copy-done.4), channel_id=1, source_target_pairs={{6,7},{7,6},{14,15},{15,14},{22,23},{23,22},{30,31},{31,30}} | collective-permute-start | bytes 1572872 | tf_op jit(solution)/shard_map/ppermute | solution.py:213
  13.6 3.5 %collective-permute-start.3 = (bf16[1152,128]{1,0:T(8,128)(2,1)}, bf16[1152,128]{1,0:T(8,128)(2,1)S(1)}, u32[]{:S(2)}, u32[]{:S(2)}) collective-permute-start(bf16[1152,128]{1,0:T(8,128)(2,1)} %slice_dynamic-update-slice_fusion), channel_id=1, source_target_pairs={{6,2},{7,3},{14,10},{15,11},{22,18},{23,19},{30,26},{31,27}} | collective-permute-start | bytes 884744 | tf_op jit(solution)/shard_map/ppermute | solution.py:246
  17.2 18.4 %collective-permute-start.5 = (bf16[1152,128]{1,0:T(8,128)(2,1)S(1)}, bf16[1152,128]{1,0:T(8,128)(2,1)S(1)}, u32[]{:S(2)}, u32[]{:S(2)}) collective-permute-start(bf16[1152,128]{1,0:T(8,128)(2,1)S(1)} %broadcast_select_fusion.2), channel_id=1, source_target_pairs={{6,2},{7,3},{2,0},{3,1},{14,10},{15,11},{10,8},{11,9},{22,18},{23,... | collective-permute-start | bytes 884744 | tf_op jit(solution)/shard_map/ppermute | solution.py:246
  18.7 17.0 %collective-permute-start.7 = (bf16[1152,128]{1,0:T(8,128)(2,1)S(1)}, bf16[1152,128]{1,0:T(8,128)(2,1)S(1)}, u32[]{:S(2)}, u32[]{:S(2)}) collective-permute-start(bf16[1152,128]{1,0:T(8,128)(2,1)S(1)} %collective-permute-done.3), channel_id=1, source_target_pairs={{2,4},{3,5},{10,12},{11,13},{18,20},{19,21},{26,28},{27,29}} | collective-permute-start | bytes 884744 | tf_op jit(solution)/shard_map/ppermute | solution.py:246
  35.9 6.8 %collective-permute-start.12 = (bf16[1152,128]{1,0:T(8,128)(2,1)S(1)}, bf16[1152,128]{1,0:T(8,128)(2,1)S(1)}, u32[]{:S(2)}, u32[]{:S(2)}) collective-permute-start(bf16[1152,128]{1,0:T(8,128)(2,1)S(1)} %broadcast_select_fusion.1), channel_id=1, source_target_pairs={{0,1},{1,0},{2,3},{3,2},{4,5},{5,4},{6,7},{7,6},{8,9},{9,8},{10,11... | collective-permute-start | bytes 884744 | tf_op jit(solution)/shard_map/ppermute | solution.py:213
  36.9 8.6 %collective-permute-start.8 = (bf16[1152,128]{1,0:T(8,128)(2,1)S(1)}, bf16[1152,128]{1,0:T(8,128)(2,1)S(1)}, u32[]{:S(2)}, u32[]{:S(2)}) collective-permute-start(bf16[1152,128]{1,0:T(8,128)(2,1)S(1)} %collective-permute-done.5), channel_id=1, source_target_pairs={{2,0},{3,1},{10,8},{11,9},{18,16},{19,17},{26,24},{27,25}} | collective-permute-start | bytes 884744 | tf_op jit(solution)/shard_map/ppermute | solution.py:246
  38.7 1.5 %collective-permute-start.11 = (f32[256,128]{1,0:T(8,128)S(1)}, f32[256,128]{1,0:T(8,128)S(1)}, u32[]{:S(2)}, u32[]{:S(2)}) collective-permute-start(f32[256,128]{1,0:T(8,128)S(1)} %convolution_subtract_fusion.2), channel_id=1, source_target_pairs={{6,14},{7,15},{14,6},{15,7},{22,30},{23,31},{30,22},{31,23}} | collective-permute-start | bytes 393224 | tf_op jit(solution)/shard_map/ppermute | solution.py:337
  39.4 6.1 %collective-permute-start.6 = (bf16[1152,128]{1,0:T(8,128)(2,1)S(1)}, bf16[1152,128]{1,0:T(8,128)(2,1)S(1)}, u32[]{:S(2)}, u32[]{:S(2)}) collective-permute-start(bf16[1152,128]{1,0:T(8,128)(2,1)S(1)} %collective-permute-done.5), channel_id=1, source_target_pairs={{2,4},{3,5},{10,12},{11,13},{18,20},{19,21},{26,28},{27,29}} | collective-permute-start | bytes 884744 | tf_op jit(solution)/shard_map/ppermute | solution.py:246
  42.6 6.6 %collective-permute-start.13 = (f32[256,128]{1,0:T(8,128)S(1)}, f32[256,128]{1,0:T(8,128)S(1)}, u32[]{:S(2)}, u32[]{:S(2)}) collective-permute-start(f32[256,128]{1,0:T(8,128)S(1)} %add.56), channel_id=1, source_target_pairs={{6,22},{7,23},{14,30},{15,31},{22,6},{23,7},{30,14},{31,15}} | collective-permute-start | bytes 393224 | tf_op jit(solution)/shard_map/ppermute | solution.py:337
  45.6 23.8 %collective-permute-start.10 = (bf16[1152,128]{1,0:T(8,128)(2,1)S(1)}, bf16[1152,128]{1,0:T(8,128)(2,1)S(1)}, u32[]{:S(2)}, u32[]{:S(2)}) collective-permute-start(bf16[1152,128]{1,0:T(8,128)(2,1)S(1)} %select_select_fusion), channel_id=1, source_target_pairs={{0,1},{1,0},{2,3},{3,2},{4,5},{5,4},{8,9},{9,8},{10,11},{11,10},{1... | collective-permute-start | bytes 884744 | tf_op jit(solution)/shard_map/ppermute | solution.py:213
  49.2 3.0 %collective-permute-start.14 = (bf16[256,128]{1,0:T(8,128)(2,1)S(1)}, bf16[256,128]{1,0:T(8,128)(2,1)S(1)}, u32[]{:S(2)}, u32[]{:S(2)}) collective-permute-start(bf16[256,128]{1,0:T(8,128)(2,1)S(1)} %add_convert_fusion), channel_id=1, source_target_pairs={{6,4},{7,5},{14,12},{15,13},{22,20},{23,21},{30,28},{31,29}} | collective-permute-start | bytes 196616 | tf_op jit(solution)/shard_map/ppermute | solution.py:246
  49.9 2.3 %collective-permute-start.15 = (bf16[256,128]{1,0:T(8,128)(2,1)S(1)}, bf16[256,128]{1,0:T(8,128)(2,1)S(1)}, u32[]{:S(2)}, u32[]{:S(2)}) collective-permute-start(bf16[256,128]{1,0:T(8,128)(2,1)S(1)} %add_convert_fusion), channel_id=1, source_target_pairs={{6,2},{7,3},{14,10},{15,11},{22,18},{23,19},{30,26},{31,27}} | collective-permute-start | bytes 196616 | tf_op jit(solution)/shard_map/ppermute | solution.py:246
  50.6 11.6 %collective-permute-start.16 = (bf16[256,128]{1,0:T(8,128)(2,1)S(1)}, bf16[256,128]{1,0:T(8,128)(2,1)S(1)}, u32[]{:S(2)}, u32[]{:S(2)}) collective-permute-start(bf16[256,128]{1,0:T(8,128)(2,1)S(1)} %add_convert_fusion), channel_id=1, source_target_pairs={{6,0},{7,1},{14,8},{15,9},{22,16},{23,17},{30,24},{31,25}} | collective-permute-start | bytes 196616 | tf_op jit(solution)/shard_map/ppermute | solution.py:246
  62.2 7.1 %collective-permute-start.17 = (bf16[256,128]{1,0:T(8,128)(2,1)S(1)}, bf16[256,128]{1,0:T(8,128)(2,1)S(1)}, u32[]{:S(2)}, u32[]{:S(2)}) collective-permute-start(bf16[256,128]{1,0:T(8,128)(2,1)S(1)} %get-tuple-element.48), channel_id=1, source_target_pairs={{0,1},{1,0},{2,3},{3,2},{4,5},{5,4},{6,7},{7,6},{8,9},{9,8},{10,11... | collective-permute-start | bytes 196616 | tf_op jit(solution)/shard_map/ppermute | solution.py:213
  73.2 4.5 %collective-permute-start.18 = (bf16[2,2,32,1024]{3,2,0,1:T(8,128)(2,1)S(1)}, bf16[2,2,32,1024]{3,2,0,1:T(8,128)(2,1)S(1)}, u32[]{:S(2)}, u32[]{:S(2)}) collective-permute-start(bf16[2,2,32,1024]{3,2,0,1:T(8,128)(2,1)S(1)} %fusion.25), channel_id=1, source_target_pairs={{0,8},{8,0},{16,24},{24,16},{1,9},{9,1},{17,25},{25,17},{2,10},{10... | collective-permute-start | bytes 786440 | tf_op jit(solution)/shard_map/ppermute | solution.py:209
  80.7 5.3 %collective-permute-start.19 = (bf16[2,1,32,1024]{3,2,1,0:T(8,128)(2,1)S(1)}, bf16[2,1,32,1024]{3,2,1,0:T(8,128)(2,1)S(1)}, u32[]{:S(2)}, u32[]{:S(2)}) collective-permute-start(bf16[2,1,32,1024]{3,2,1,0:T(8,128)(2,1)S(1)} %fusion.26), channel_id=1, source_target_pairs={{0,16},{8,24},{16,0},{24,8},{1,17},{9,25},{17,1},{25,9},{2,18},{10... | collective-permute-start | bytes 393224 | tf_op jit(solution)/shard_map/ppermute | solution.py:209
  (15 other events, 36.2 us)

commit v6 on v5

--- a/solution.py
+++ b/solution.py
@@ -76,16 +76,20 @@
     one_ref,
     two_ref,
     adj_ref,
+    trail_ref,
     inv_one_ref,
     inv_two_ref,
+    edge_ref,
     whole_ref,
     *rest,
 ):
-    *piece_refs, rows_ref, sem = rest
+    *piece_refs, rows_ref, sem, edge_sem = rest
     panel = one_ref.shape[0]
     block = pl.ds(adj_ref.shape[1] - panel, panel)
     fetch = pltpu.make_async_copy(adj_ref.at[:, block], rows_ref, sem)
     fetch.start()
+    fetch_edge = pltpu.make_async_copy(trail_ref.at[:, block], edge_ref, edge_sem)
+    fetch_edge.start()
     inverse_one, inverse_two = inverse_lower([one_ref[...], two_ref[...]])
     inv_one_ref[...] = inverse_one
     inv_two_ref[...] = inverse_two
@@ -96,63 +100,132 @@
         whole_ref[start:stop, :] = product
         piece_ref[:panel, :] = jnp.zeros((panel, panel), BF16)
         piece_ref[panel:, :] = product
-
-
-def prepare(side, diag_one, diag_two, adj_trail, cuts):
+    fetch_edge.wait()
+
+
+def prepare(side, diag_one, diag_two, adj_trail, trail, cuts):
     height = adj_trail.shape[0]
     panel = diag_one.shape[0]
     vmem = pl.BlockSpec(memory_space=pltpu.VMEM)
-    hbm = pl.BlockSpec(memory_space=pl.ANY)
+    hbm = pl.BlockSpec(memory_space=pltpu.HBM)
     sizes = [panel + stop - start for start, stop in cuts]
     return pl.pallas_call(
         functools.partial(prepare_kernel, cuts),
-        in_specs=[pl.BlockSpec(memory_space=pltpu.SMEM), vmem, vmem, hbm],
-        out_specs=[vmem] * (3 + len(cuts)),
+        in_specs=[pl.BlockSpec(memory_space=pltpu.SMEM), vmem, vmem, hbm, hbm],
+        out_specs=[vmem] * (4 + len(cuts)),
         out_shape=[jax.ShapeDtypeStruct((panel, panel), F32)] * 2
-        + [jax.ShapeDtypeStruct((size, panel), BF16) for size in [height] + sizes],
-        scratch_shapes=[pltpu.VMEM((height, panel), F32), pltpu.SemaphoreType.DMA],
-        compiler_params=pltpu.CompilerParams(vmem_limit_bytes=56 * 2**20),
+        + [jax.ShapeDtypeStruct((size, panel), BF16) for size in [height, height] + sizes],
+        scratch_shapes=[
+            pltpu.VMEM((height, panel), F32),
+            pltpu.SemaphoreType.DMA,
+            pltpu.SemaphoreType.DMA,
+        ],
+        compiler_params=pltpu.CompilerParams(vmem_limit_bytes=60 * 2**20),
         cost_estimate=pl.CostEstimate(
-            flops=8 * height * panel * panel, bytes_accessed=6 * height * panel, transcendentals=0
+            flops=8 * height * panel * panel, bytes_accessed=8 * height * panel, transcendentals=0
         ),
         name="prepare",
-    )(side, diag_one, diag_two, adj_trail)
-
-
-def update_kernel(flags_ref, both_ref, rows_ref, adj_ref, *rest):
-    out_ref = rest[-1]
-    panel = both_ref.shape[1] // 2
+    )(side, diag_one, diag_two, adj_trail, trail)
+
+
+def gather_sums_kernel(start, both_ref, trail_ref, past_ref, out_ref, rows_ref, sems):
+    rows, depth = both_ref.shape
+    steps = [pl.ds(at, depth) for at in range(0, rows, depth)]
+    fetches = [
+        pltpu.make_async_copy(
+            trail_ref.at[pl.ds(start + k * depth, depth), :], rows_ref.at[step, :], sems.at[k]
+        )
+        for k, step in enumerate(steps)
+    ]
+    for fetch in fetches:
+        fetch.start()
+    total = past_ref[...]
+    for fetch, step in zip(fetches, steps):
+        fetch.wait()
+        total += lax.dot_general(
+            both_ref[step, :],
+            rows_ref[step, :],
+            (((0,), (0,)), ((), ())),
+            preferred_element_type=F32,
+        )
+    out_ref[...] = total
+
+
+def gather_sums(both, trail, start, past):
+    width = trail.shape[1]
+    rows, depth = both.shape
+    vmem = pl.BlockSpec(memory_space=pltpu.VMEM)
+    return pl.pallas_call(
+        functools.partial(gather_sums_kernel, start),
+        in_specs=[vmem, pl.BlockSpec(memory_space=pltpu.HBM), vmem],
+        out_specs=vmem,
+        out_shape=jax.ShapeDtypeStruct((depth, width), F32),
+        scratch_shapes=[
+            pltpu.VMEM((rows, width), BF16),
+            pltpu.SemaphoreType.DMA((rows // depth,)),
+        ],
+        compiler_params=pltpu.CompilerParams(vmem_limit_bytes=60 * 2**20),
+        cost_estimate=pl.CostEstimate(
+            flops=2 * rows * depth * width, bytes_accessed=2 * rows * width, transcendentals=0
+        ),
+        name="gather_sums",
+    )(both, trail, past)
+
+
+def update_kernel(start, flags_ref, both_ref, rows_ref, adj_ref, *rest):
+    out_ref, adj_rows, out_rows, in_sems, out_sems = rest[-5:]
+    rows, depth = both_ref.shape
+    panel = depth // 2
     last = out_ref.shape[1] - panel
-    both = both_ref[...]
-    left = adj_ref[...] - wide_dot(both, rows_ref[...])
-    out_ref[:, :last] = left[:, :last].astype(BF16)
-    block = jnp.where(flags_ref[0] == 1, both[:, panel:], left[:, last:].astype(BF16))
-    out_ref[:, last:] = jnp.where(flags_ref[1] == 1, both[:, :panel], block)
+    fetches, stores, steps = [], [], []
+    for k in range(rows // depth):
+        step = pl.ds(k * depth, depth)
+        place = pl.ds(start + k * depth, depth)
+        steps.append(step)
+        fetches.append(
+            pltpu.make_async_copy(adj_ref.at[place, :], adj_rows.at[step, :], in_sems.at[k])
+        )
+        stores.append(
+            pltpu.make_async_copy(out_rows.at[step, :], out_ref.at[place, :], out_sems.at[k])
+        )
+    for fetch in fetches:
+        fetch.start()
+    for fetch, store, step in zip(fetches, stores, steps):
+        both = both_ref[step, :]
+        product = wide_dot(both, rows_ref[...])
+        fetch.wait()
+        left = (adj_rows[step, :] - product).astype(BF16)
+        out_rows[step, :last] = left[:, :last]
+        block = jnp.where(flags_ref[0] == 1, both[:, panel:], left[:, last:])
+        out_rows[step, last:] = jnp.where(flags_ref[1] == 1, both[:, :panel], block)
+        store.start()
+    for store in stores:
+        store.wait()
 
 
 def update(flags, both, full_both, adj_trail, start, previous):
     height, width = adj_trail.shape
     rows, depth = both.shape
-    tile = depth
-    first = start // tile
     operands = [flags, both, full_both, adj_trail]
-    in_specs = [
-        pl.BlockSpec(memory_space=pltpu.SMEM),
-        pl.BlockSpec((tile, depth), lambda i: (i, 0)),
-        pl.BlockSpec((depth, width), lambda i: (0, 0)),
-        pl.BlockSpec((tile, width), lambda i: (first + i, 0)),
-    ]
+    vmem = pl.BlockSpec(memory_space=pltpu.VMEM)
+    hbm = pl.BlockSpec(memory_space=pltpu.HBM)
+    in_specs = [pl.BlockSpec(memory_space=pltpu.SMEM), vmem, vmem, hbm]
     if previous is not None:
         operands.append(previous)
-        in_specs.append(pl.BlockSpec(memory_space=pl.ANY))
+        in_specs.append(hbm)
     return pl.pallas_call(
-        update_kernel,
-        grid=(rows // tile,),
+        functools.partial(update_kernel, start),
         in_specs=in_specs,
-        out_specs=pl.BlockSpec((tile, width), lambda i: (first + i, 0)),
+        out_specs=hbm,
         out_shape=jax.ShapeDtypeStruct((height, width), BF16),
         input_output_aliases={} if previous is None else {4: 0},
-        compiler_params=pltpu.CompilerParams(vmem_limit_bytes=16 * 2**20),
+        scratch_shapes=[
+            pltpu.VMEM((rows, width), F32),
+            pltpu.VMEM((rows, width), BF16),
+            pltpu.SemaphoreType.DMA((rows // depth,)),
+            pltpu.SemaphoreType.DMA((rows // depth,)),
+        ],
+        compiler_params=pltpu.CompilerParams(vmem_limit_bytes=60 * 2**20),
         cost_estimate=pl.CostEstimate(
             flops=2 * rows * depth * width, bytes_accessed=6 * rows * width, transcendentals=0
         ),
@@ -287,14 +360,13 @@
     near_one = gather_step(row_one[None, None], 1)
     full_two = gather_rest(near_two)
     side = is_two.astype(jnp.int32)[None]
-    inverse_one, inverse_two, whole, *packets = prepare(
-        side, after(diag_one, near_two, near_one), diag_two, adj_trail, cuts
+    inverse_one, inverse_two, edge, whole, *packets = prepare(
+        side, after(diag_one, near_two, near_one), diag_two, adj_trail, trail, cuts
     )
     own_cross = full_two[:, last:]
     packets[0] = lax.dynamic_update_slice(packets[0], own_cross, (0, 0))
     full_one = gather_rest(after(near_one, packets[0]))
     full_both = jnp.concatenate([full_two, full_one], 0)
-    edge = after(trail[:, last:], packets[0])
 
     def factor_of(cross):
         return jnp.concatenate(halves(exact_dot(cross.astype(F32), inverse_one)), 0)
@@ -307,14 +379,13 @@
         )
         return jnp.concatenate([solved_two, tail.astype(BF16)], 1)
 
-    whole_other = pair_swap(whole, [top])
+    whole_other = lax.ppermute(whole, "col", [(col_count - 1, col_count - 2)])
     first, arrived = spread(packets, full_one)
     at_top = level == top
     other = []
     own = [jnp.where(at_top, a, b) for a, b in zip(packets, arrived)]
-    for k, value in enumerate(arrived):
-        value = own[0] if k == 0 else value
-        other.append(pair_swap(value, range(levels if k == 0 else levels - 1)))
+    for value in own:
+        other.append(pair_swap(value, range(levels)))
 
     whole_other = after(whole_other, first[final])
     top_both = panels_of(whole, whole_other, factor_of(own_cross), height)
@@ -334,35 +405,37 @@
             for i in range(row_count)
             for c in (col_count - 2, col_count - 1)
         ]
-        terms = terms + lax.ppermute(terms, ("row", "col"), pairs)
+        if step > 1:
+            terms = terms.astype(BF16)
+        moved = lax.ppermute(terms, ("row", "col"), pairs)
+        terms = terms.astype(F32) + moved.astype(F32)
         if step == 1:
             terms = after(terms, other[0])
         step *= 2
-    terms = row_terms = terms.astype(BF16)
+    terms = terms.astype(BF16)
+
+    flags = jnp.stack([here_one, here_two]).astype(jnp.int32)
+    cross = jnp.where(is_two, other[0][:panel], own[0][:panel])
+    factor = factor_of(cross)
+    sums = jnp.zeros((2 * panel, width), F32)
+    grad_trail = None
+    for (start, stop), mine, theirs in zip(cuts[:-1], own, other):
+        both = panels_of(mine, after(theirs, own_terms), factor, stop - start)
+        sums = gather_sums(both, trail, start, sums)
+        grad_trail = update(flags, both, full_both, adj_trail, start, grad_trail)
     terms = choose(
         [([top], terms)] + [([k], hop(terms, [(top, k)])) for k in range(levels - 1)]
     )
-    terms_other = pair_swap(terms, range(levels))
+    terms_other = pair_swap(after(terms, grad_trail), range(levels))
     terms, terms_other = terms.astype(F32), terms_other.astype(F32)
     diag_term_two = jnp.where(is_two, terms[:panel], terms_other[:panel])
     crossing = jnp.where(is_two, terms_other[:panel], terms[:panel])
     diag_term_one = jnp.where(is_two, terms_other[panel:], terms[panel:])
 
-    flags = jnp.stack([here_one, here_two]).astype(jnp.int32)
-    cross = jnp.where(is_two, other[0][:panel], own[0][:panel])
-    factor = factor_of(cross)
-    sums = 0
-    grad_trail = None
-    for k, (start, stop) in enumerate(cuts):
-        theirs = after(other[k], own_terms)
-        if k == final:
-            theirs = after(theirs, row_terms, grad_trail)
-        if k > 0:
-            theirs = jnp.where(at_top, whole_other[start:stop], theirs[panel:])
-        both = panels_of(own[k], theirs, factor, stop - start)
-        sums = sums + wide_dot(both.T, trail[start:stop])
-        if k < final:
-            grad_trail = update(flags, both, full_both, adj_trail, start, grad_trail)
+    start, stop = cuts[-1]
+    theirs = after(other[-1], terms, sums, grad_trail)
+    both = panels_of(own[-1], theirs, factor, stop - start)
+    sums = gather_sums(both, trail, start, sums)
 
     parts = sums.reshape(2, row_count, band, width)
     step = 1
@@ -373,7 +446,6 @@
         give = jnp.where(low, parts[:, :, 1], parts[:, :, 0])
         give = give.astype(BF16)
         if 2 * step >= row_count:
-            start = cuts[final][0]
             grad_trail = update(flags, both, full_both, adj_trail, start, grad_trail)
             give = sent = after(give, grad_trail)
         parts = keep + row_swap(give, step).astype(F32)

time: 87.2 us -> 94 us (1.078)
  Pallas kernels: 10.8 us -> 22.9 us
  waiting for transfers between devices: 36.3 us -> 30.9 us
  other arithmetic: 3.4 us -> 7.07 us
  local copies, waits for them, and re-layouts: 8.34 us -> 4.77 us
  matrix products: 5.74 us -> 4.28 us
  starting transfers between devices: 20.7 us -> 22 us
    pallas_call x2 -> x4, Pallas kernels: 6.16 us -> 18 us  [the longest x2 9.21 us: update(): pl.pallas_call(functools.partial(update_kernel, start), in_specs=in_specs...]
    unnamed x36 -> x26, local copies, waits for them, and re-layouts: 7.29 us -> 1.4 us
    ppermute x8, waiting for transfers between devices: 28.4 us -> 25.1 us  [hop(): return lax.ppermute(value, 'col', pairs)]
    ppermute x4 -> x3, waiting for transfers between devices: 2.46 us -> 0.01 us  [pair_swap(): return lax.ppermute(value, 'col', pairs)]
    concatenate x2, other arithmetic: 0.12 us -> 1.77 us  [panels_of(): return jnp.concatenate([solved_two, tail.astype(BF16)], 1)]
    dot_general x8 -> x6, matrix products: 3.45 us -> 1.99 us  [wide_dot(): return jnp.dot(a, b, preferred_element_type=F32)]
    ppermute x4 -> x3, starting transfers between devices: 5.4 us -> 6.8 us  [pair_swap(): return lax.ppermute(value, 'col', pairs)]
    slice x1, local copies, waits for them, and re-layouts: 0.08 us -> 1.31 us  [per_device(): keep = jnp.where(low, parts[:, :, 0], parts[:, :, 1])]
  transfers between devices with their start and end apart: 20 -> 20, of which waited for: 8 -> 7; matrix products, arithmetic and copies ran while one was open for 4% -> 8% of each run, Pallas kernels for 12% -> 20%
where the time goes in v6:
time: 94 us; the launch traced here: 93.3 us
  waiting for transfers between devices  30.9 us (33%)
  Pallas kernels  22.9 us (24%)
  starting transfers between devices  22 us (23%)
  other arithmetic  7.07 us (8%)
  local copies, waits for them, and re-layouts  4.77 us (5%)
  matrix products  4.28 us (5%)
  between operations  1.34 us (1%)
    ppermute x8, waiting for transfers between devices, hop(): return lax.ppermute(value, 'col', pairs)  25.1 us
    pallas_call x2, Pallas kernels, update(): pl.pallas_call(functools.partial(update_kernel, start), in_specs=in_specs...  9.21 us
    pallas_call x2, Pallas kernels, gather_sums(): pl.pallas_call(functools.partial(gather_sums_kernel, start), in_specs=[vm...  8.8 us
    ppermute x8, starting transfers between devices, hop(): return lax.ppermute(value, 'col', pairs)  7.23 us
    ppermute x3, starting transfers between devices, pair_swap(): return lax.ppermute(value, 'col', pairs)  6.8 us
    ppermute x6, starting transfers between devices, row_swap(): return lax.ppermute(value, 'row', [(i, i ^ step) for i in range(row_count)])  5.93 us
    ppermute x6, waiting for transfers between devices, row_swap(): return lax.ppermute(value, 'row', [(i, i ^ step) for i in range(row_count)])  5.82 us
    pallas_call x1, Pallas kernels, prepare(): pl.pallas_call(functools.partial(prepare_kernel, cuts), in_specs=[pl.Bloc...  4.93 us
  transfers between devices with their start and end apart: 20, of which 7 were waited for; matrix products, arithmetic and copies ran while one was open for 8% of the time, Pallas kernels for 20%

profile of v6, /device:TPU:0, one launch (start us, length us, event | category | flops | bytes accessed | tf_op | source)
XLA Modules:
  0.0 93.3 jit_solution(4457789574089261438)
XLA Ops:
  2.6 0.9 broadcast_select_fusion.10
  3.5 2.7 %collective-permute-start.2 = (bf16[1,2,32,1024]{3,2,1,0:T(8,128)(2,1)S(1)}, bf16[1,2,32,1024]{3,2,1,0:T(8,128)(2,1)S(1)}, u32[]{:S(2)}, u32[]{:S(2)}) collective-permute-start(bf16[1,2,32,1024]{3,2,1,0:T(8,128)(2,1)S(1)} %pad_maximum_fusion.13), channel_id=1, source_target_pairs={{0,16},{8,24},{16,0},{24,8},{1,17},{9,25},{17,1},{25,9},{2,18},{10... | collective-permute-start | bytes 393224 | tf_op jit(solution)/shard_map/ppermute | solution.py:282
  6.3 4.9 %prepare.1 = (f32[128,128]{1,0:T(8,128)}, f32[128,128]{1,0:T(8,128)}, bf16[2048,128]{1,0:T(8,128)(2,1)}, bf16[2048,128]{1,0:T(8,128)(2,1)}, bf16[1152,128]{1,0:T(8,128)(2,1)}, /*index=5*/bf16[1152,128]{1,0:T(8,128)(2,1)}) custom-call(s32[1]{0:T(128)} %bitcast.2.side_ref, f32[128,128]{1,0:T(8,128)} %one_ref, f32[128,128]{1,0:T(8,128)} %two_ref.1, ...), custom_call_target="tpu_custom_call" | custom-call | flops 268435456 | bytes 2097152 | tf_op jit(solution)/shard_map/prepare/pallas_call | solution.py:112
  14.7 2.6 %collective-permute-done.4 = bf16[1,2,32,1024]{3,2,1,0:T(8,128)(2,1)S(1)} collective-permute-done((bf16[1,2,32,1024]{3,2,1,0:T(8,128)(2,1)S(1)}, bf16[1,2,32,1024]{3,2,1,0:T(8,128)(2,1)S(1)}, u32[]{:S(2)}, u32[]{:S(2)}) %collective-permute-start.4) | collective-permute-done | bytes 131104 | tf_op jit(solution)/shard_map/ppermute | solution.py:282
  17.5 1.3 %collective-permute-start.5 = (bf16[1152,128]{1,0:T(8,128)(2,1)S(1)}, bf16[1152,128]{1,0:T(8,128)(2,1)S(1)}, u32[]{:S(2)}, u32[]{:S(2)}) collective-permute-start(bf16[1152,128]{1,0:T(8,128)(2,1)S(1)} %broadcast_select_fusion.2), channel_id=1, source_target_pairs={{6,2},{7,3},{2,0},{3,1},{14,10},{15,11},{10,8},{11,9},{22,18},{23,... | collective-permute-start | bytes 884744 | tf_op jit(solution)/shard_map/ppermute | solution.py:319
  19.0 0.8 pad_maximum_fusion.10.rows_ref
  20.5 14.3 %collective-permute-done.5 = bf16[1152,128]{1,0:T(8,128)(2,1)S(1)} collective-permute-done((bf16[1152,128]{1,0:T(8,128)(2,1)S(1)}, bf16[1152,128]{1,0:T(8,128)(2,1)S(1)}, u32[]{:S(2)}, u32[]{:S(2)}) %collective-permute-start.5) | collective-permute-done | bytes 294944 | tf_op jit(solution)/shard_map/ppermute | solution.py:319
  37.8 1.3 %collective-permute-start.8 = (bf16[1152,128]{1,0:T(8,128)(2,1)S(1)}, bf16[1152,128]{1,0:T(8,128)(2,1)S(1)}, u32[]{:S(2)}, u32[]{:S(2)}) collective-permute-start(bf16[1152,128]{1,0:T(8,128)(2,1)S(1)} %collective-permute-done.5), channel_id=1, source_target_pairs={{2,0},{3,1},{10,8},{11,9},{18,16},{19,17},{26,24},{27,25}} | collective-permute-start | bytes 884744 | tf_op jit(solution)/shard_map/ppermute | solution.py:319
  39.2 2.4 %collective-permute-start.12 = (bf16[1152,128]{1,0:T(8,128)(2,1)S(1)}, bf16[1152,128]{1,0:T(8,128)(2,1)S(1)}, u32[]{:S(2)}, u32[]{:S(2)}) collective-permute-start(bf16[1152,128]{1,0:T(8,128)(2,1)S(1)} %broadcast_select_fusion.1), channel_id=1, source_target_pairs={{0,1},{1,0},{2,3},{3,2},{4,5},{5,4},{6,7},{7,6},{8,9},{9,8},{10,11... | collective-permute-start | bytes 884744 | tf_op jit(solution)/shard_map/ppermute | solution.py:286
  41.7 5.6 %collective-permute-done.8 = bf16[1152,128]{1,0:T(8,128)(2,1)S(1)} collective-permute-done((bf16[1152,128]{1,0:T(8,128)(2,1)S(1)}, bf16[1152,128]{1,0:T(8,128)(2,1)S(1)}, u32[]{:S(2)}, u32[]{:S(2)}) %collective-permute-start.8) | collective-permute-done | bytes 294944 | tf_op jit(solution)/shard_map/ppermute | solution.py:319
  47.3 2.4 %collective-permute-start.9 = (bf16[1152,128]{1,0:T(8,128)(2,1)S(1)}, bf16[1152,128]{1,0:T(8,128)(2,1)S(1)}, u32[]{:S(2)}, u32[]{:S(2)}) collective-permute-start(bf16[1152,128]{1,0:T(8,128)(2,1)S(1)} %select_select_fusion), channel_id=1, source_target_pairs={{0,1},{1,0},{2,3},{3,2},{4,5},{5,4},{6,7},{7,6},{8,9},{9,8},{10,11... | collective-permute-start | bytes 884744 | tf_op jit(solution)/shard_map/ppermute | solution.py:286
  52.3 1.3 %collective-permute-start.16 = (bf16[256,128]{1,0:T(8,128)(2,1)S(1)}, bf16[256,128]{1,0:T(8,128)(2,1)S(1)}, u32[]{:S(2)}, u32[]{:S(2)}) collective-permute-start(bf16[256,128]{1,0:T(8,128)(2,1)S(1)} %add_convert_fusion), channel_id=1, source_target_pairs={{6,0},{7,1},{14,8},{15,9},{22,16},{23,17},{30,24},{31,25}} | collective-permute-start | bytes 196616 | tf_op jit(solution)/shard_map/ppermute | solution.py:319
  53.6 0.9 pad_maximum_fusion.5.both_ref
  54.5 4.6 %update.2.rest_0_ = bf16[2048,1024]{1,0:T(8,128)(2,1)} custom-call(s32[2]{0:T(128)} %add_convert_fusion.1.flags_ref, bf16[1024,256]{1,0:T(8,128)(2,1)} %pad_maximum_fusion.5.both_ref, bf16[256,1024]{1,0:T(8,128)(2,1)} %pad_maximum_fusion.10.rows_ref, f32[2048,1024]{1,0:T(8,128)} %adj_ref.5), custom_call_target="tpu_custom_call" | custom-call | flops 536870912 | bytes 6291456 | tf_op jit(solution)/shard_map/update/pallas_call | solution.py:216
  59.2 5.1 %collective-permute-done.16 = bf16[256,128]{1,0:T(8,128)(2,1)S(1)} collective-permute-done((bf16[256,128]{1,0:T(8,128)(2,1)S(1)}, bf16[256,128]{1,0:T(8,128)(2,1)S(1)}, u32[]{:S(2)}, u32[]{:S(2)}) %collective-permute-start.16) | collective-permute-done | bytes 65568 | tf_op jit(solution)/shard_map/ppermute | solution.py:319
  64.3 2.0 %collective-permute-start.17 = (bf16[256,128]{1,0:T(8,128)(2,1)S(1)}, bf16[256,128]{1,0:T(8,128)(2,1)S(1)}, u32[]{:S(2)}, u32[]{:S(2)}) collective-permute-start(bf16[256,128]{1,0:T(8,128)(2,1)S(1)} %get-tuple-element.40), channel_id=1, source_target_pairs={{0,1},{1,0},{2,3},{3,2},{4,5},{5,4},{6,7},{7,6},{8,9},{9,8},{10,11... | collective-permute-start | bytes 196616 | tf_op jit(solution)/shard_map/ppermute | solution.py:286
  66.3 1.1 %broadcast_in_dim.49.past_ref = f32[256,1024]{1,0:T(8,128)} broadcast(f32[]{:T(128)} %constant.91.clone.1), dimensions={} | broadcast | bytes 1048580 | tf_op jit(solution)/shard_map/broadcast_in_dim | solution.py:420
  67.4 4.4 %gather_sums.2.past_ref = f32[256,1024]{1,0:T(8,128)} custom-call(bf16[1024,256]{1,0:T(8,128)(2,1)} %pad_maximum_fusion.5.both_ref, bf16[2048,1024]{1,0:T(8,128)(2,1)} %trail_ref.5, f32[256,1024]{1,0:T(8,128)} %broadcast_in_dim.49.past_ref), custom_call_target="tpu_custom_call" | custom-call | flops 536870912 | bytes 2097152 | tf_op jit(solution)/shard_map/gather_sums/pallas_call | solution.py:158
  72.2 0.9 pad_maximum_fusion.7.both_ref
  73.1 4.4 %gather_sums.3 = f32[256,1024]{1,0:T(8,128)} custom-call(bf16[1024,256]{1,0:T(8,128)(2,1)} %pad_maximum_fusion.7.both_ref, bf16[2048,1024]{1,0:T(8,128)(2,1)} %trail_ref.5, f32[256,1024]{1,0:T(8,128)} %gather_sums.2.past_ref), custom_call_target="tpu_custom_call" | custom-call | flops 536870912 | bytes 2097152 | tf_op jit(solution)/shard_map/gather_sums/pallas_call | solution.py:158
  77.5 1.3 %fusion.70 = (f32[2,2,1,32,1024]{4,3,2,1,0:T(8,128)S(1)}, f32[2,2,1,32,1024]{4,3,2,1,0:T(8,128)S(1)}) fusion(f32[2,2,2,32,1024]{4,3,2,1,0:T(8,128)} %bitcast.72), kind=kLoop, calls=%fused_computation.138 | loop fusion | bytes 2097152 | tf_op jit(solution)/shard_map/slice | solution.py:445
  79.0 4.6 %update.3 = bf16[2048,1024]{1,0:T(8,128)(2,1)} custom-call(s32[2]{0:T(128)} %add_convert_fusion.1.flags_ref, bf16[1024,256]{1,0:T(8,128)(2,1)} %pad_maximum_fusion.7.both_ref, bf16[256,1024]{1,0:T(8,128)(2,1)} %pad_maximum_fusion.10.rows_ref, f32[2048,1024]{1,0:T(8,128)} %adj_ref.5, bf16[2048,1024]{1,0:T(8,128)(2,1)} %update.2.rest_0_), custom_call_target="tpu_custom_call", output_to_operand_aliasing={{}: (4, {})} | custom-call | flops 536870912 | bytes 6291456 | tf_op jit(solution)/shard_map/update/pallas_call | solution.py:216
  86.6 1.8 %collective-permute-start.19 = (bf16[2,1,32,1024]{3,2,1,0:T(8,128)(2,1)S(1)}, bf16[2,1,32,1024]{3,2,1,0:T(8,128)(2,1)S(1)}, u32[]{:S(2)}, u32[]{:S(2)}) collective-permute-start(bf16[2,1,32,1024]{3,2,1,0:T(8,128)(2,1)S(1)} %fusion.19), channel_id=1, source_target_pairs={{0,16},{8,24},{16,0},{24,8},{1,17},{9,25},{17,1},{25,9},{2,18},{10... | collective-permute-start | bytes 393224 | tf_op jit(solution)/shard_map/ppermute | solution.py:282
  90.0 2.5 %collective-permute-done.19 = bf16[2,1,32,1024]{3,2,1,0:T(8,128)(2,1)S(1)} collective-permute-done((bf16[2,1,32,1024]{3,2,1,0:T(8,128)(2,1)S(1)}, bf16[2,1,32,1024]{3,2,1,0:T(8,128)(2,1)S(1)}, u32[]{:S(2)}, u32[]{:S(2)}) %collective-permute-start.19) | collective-permute-done | bytes 131104 | tf_op jit(solution)/shard_map/ppermute | solution.py:282
  (110 shorter events, 17.7 us)
Async XLA Ops:
  0.6 1.6 %collective-permute-start = (bf16[1,1,32,1024]{3,2,1,0:T(8,128)(2,1)}, bf16[1,1,32,1024]{3,2,1,0:T(8,128)(2,1)S(1)}, u32[]{:S(2)}, u32[]{:S(2)}) collective-permute-start(bf16[1,1,32,1024]{3,2,1,0:T(8,128)(2,1)} %bitcast.81), channel_id=1, source_target_pairs={{0,8},{8,0},{16,24},{24,16},{1,9},{9,1},{17,25},{25,17},{2,10},{10... | collective-permute-start | bytes 196616 | tf_op jit(solution)/shard_map/ppermute | solution.py:282
  1.1 1.5 %collective-permute-start.1 = (bf16[1,1,32,1024]{3,2,1,0:T(8,128)(2,1)}, bf16[1,1,32,1024]{3,2,1,0:T(8,128)(2,1)S(1)}, u32[]{:S(2)}, u32[]{:S(2)}) collective-permute-start(bf16[1,1,32,1024]{3,2,1,0:T(8,128)(2,1)} %bitcast.80), channel_id=1, source_target_pairs={{0,8},{8,0},{16,24},{24,16},{1,9},{9,1},{17,25},{25,17},{2,10},{10... | collective-permute-start | bytes 196616 | tf_op jit(solution)/shard_map/ppermute | solution.py:282
  3.5 7.7 %collective-permute-start.2 = (bf16[1,2,32,1024]{3,2,1,0:T(8,128)(2,1)S(1)}, bf16[1,2,32,1024]{3,2,1,0:T(8,128)(2,1)S(1)}, u32[]{:S(2)}, u32[]{:S(2)}) collective-permute-start(bf16[1,2,32,1024]{3,2,1,0:T(8,128)(2,1)S(1)} %pad_maximum_fusion.13), channel_id=1, source_target_pairs={{0,16},{8,24},{16,0},{24,8},{1,17},{9,25},{17,1},{25,9},{2,18},{10... | collective-permute-start | bytes 393224 | tf_op jit(solution)/shard_map/ppermute | solution.py:282
  11.2 6.3 %copy-start.1 = (bf16[1152,128]{1,0:T(8,128)(2,1)S(1)}, bf16[1152,128]{1,0:T(8,128)(2,1)}, u32[]{:S(2)}) copy-start(bf16[1152,128]{1,0:T(8,128)(2,1)} %get-tuple-element.25) | copy-start | bytes 884740
  11.2 7.6 %copy-start = (f32[128,128]{1,0:T(8,128)S(1)}, f32[128,128]{1,0:T(8,128)}, u32[]{:S(2)}) copy-start(f32[128,128]{1,0:T(8,128)} %get-tuple-element.34) | copy-start | bytes 196612
  11.2 23.7 %copy-start.2 = (bf16[2048,128]{1,0:T(8,128)(2,1)S(1)}, bf16[2048,128]{1,0:T(8,128)(2,1)}, u32[]{:S(2)}) copy-start(bf16[2048,128]{1,0:T(8,128)(2,1)} %get-tuple-element.32) | copy-start | bytes 1572868
  11.9 5.5 %collective-permute-start.4 = (bf16[1,2,32,1024]{3,2,1,0:T(8,128)(2,1)S(1)}, bf16[1,2,32,1024]{3,2,1,0:T(8,128)(2,1)S(1)}, u32[]{:S(2)}, u32[]{:S(2)}) collective-permute-start(bf16[1,2,32,1024]{3,2,1,0:T(8,128)(2,1)S(1)} %pad_maximum_fusion.14), channel_id=1, source_target_pairs={{0,16},{8,24},{16,0},{24,8},{1,17},{9,25},{17,1},{25,9},{2,18},{10... | collective-permute-start | bytes 393224 | tf_op jit(solution)/shard_map/ppermute | solution.py:282
  13.4 7.2 %collective-permute-start.10 = (bf16[2048,128]{1,0:T(8,128)(2,1)}, bf16[2048,128]{1,0:T(8,128)(2,1)S(1)}, u32[]{:S(2)}, u32[]{:S(2)}) collective-permute-start(bf16[2048,128]{1,0:T(8,128)(2,1)} %get-tuple-element.32), channel_id=1, source_target_pairs={{7,6},{15,14},{23,22},{31,30}} | collective-permute-start | bytes 1572872 | tf_op jit(solution)/shard_map/ppermute | solution.py:382
  14.1 3.4 %collective-permute-start.3 = (bf16[1152,128]{1,0:T(8,128)(2,1)}, bf16[1152,128]{1,0:T(8,128)(2,1)S(1)}, u32[]{:S(2)}, u32[]{:S(2)}) collective-permute-start(bf16[1152,128]{1,0:T(8,128)(2,1)} %slice_dynamic-update-slice_fusion), channel_id=1, source_target_pairs={{6,2},{7,3},{14,10},{15,11},{22,18},{23,19},{30,26},{31,27}} | collective-permute-start | bytes 884744 | tf_op jit(solution)/shard_map/ppermute | solution.py:319
  17.5 17.4 %collective-permute-start.5 = (bf16[1152,128]{1,0:T(8,128)(2,1)S(1)}, bf16[1152,128]{1,0:T(8,128)(2,1)S(1)}, u32[]{:S(2)}, u32[]{:S(2)}) collective-permute-start(bf16[1152,128]{1,0:T(8,128)(2,1)S(1)} %broadcast_select_fusion.2), channel_id=1, source_target_pairs={{6,2},{7,3},{2,0},{3,1},{14,10},{15,11},{10,8},{11,9},{22,18},{23,... | collective-permute-start | bytes 884744 | tf_op jit(solution)/shard_map/ppermute | solution.py:319
  19.9 19.3 %collective-permute-start.7 = (bf16[1152,128]{1,0:T(8,128)(2,1)S(1)}, bf16[1152,128]{1,0:T(8,128)(2,1)S(1)}, u32[]{:S(2)}, u32[]{:S(2)}) collective-permute-start(bf16[1152,128]{1,0:T(8,128)(2,1)S(1)} %collective-permute-done.3), channel_id=1, source_target_pairs={{2,4},{3,5},{10,12},{11,13},{18,20},{19,21},{26,28},{27,29}} | collective-permute-start | bytes 884744 | tf_op jit(solution)/shard_map/ppermute | solution.py:319
  36.5 5.1 %collective-permute-start.11 = (f32[256,128]{1,0:T(8,128)S(1)}, f32[256,128]{1,0:T(8,128)S(1)}, u32[]{:S(2)}, u32[]{:S(2)}) collective-permute-start(f32[256,128]{1,0:T(8,128)S(1)} %convolution_subtract_fusion.2), channel_id=1, source_target_pairs={{6,14},{7,15},{14,6},{15,7},{22,30},{23,31},{30,22},{31,23}} | collective-permute-start | bytes 393224 | tf_op jit(solution)/shard_map/ppermute | solution.py:410
  37.2 4.5 %collective-permute-start.6 = (bf16[1152,128]{1,0:T(8,128)(2,1)S(1)}, bf16[1152,128]{1,0:T(8,128)(2,1)S(1)}, u32[]{:S(2)}, u32[]{:S(2)}) collective-permute-start(bf16[1152,128]{1,0:T(8,128)(2,1)S(1)} %collective-permute-done.5), channel_id=1, source_target_pairs={{2,4},{3,5},{10,12},{11,13},{18,20},{19,21},{26,28},{27,29}} | collective-permute-start | bytes 884744 | tf_op jit(solution)/shard_map/ppermute | solution.py:319
  37.8 9.4 %collective-permute-start.8 = (bf16[1152,128]{1,0:T(8,128)(2,1)S(1)}, bf16[1152,128]{1,0:T(8,128)(2,1)S(1)}, u32[]{:S(2)}, u32[]{:S(2)}) collective-permute-start(bf16[1152,128]{1,0:T(8,128)(2,1)S(1)} %collective-permute-done.5), channel_id=1, source_target_pairs={{2,0},{3,1},{10,8},{11,9},{18,16},{19,17},{26,24},{27,25}} | collective-permute-start | bytes 884744 | tf_op jit(solution)/shard_map/ppermute | solution.py:319
  39.2 10.5 %collective-permute-start.12 = (bf16[1152,128]{1,0:T(8,128)(2,1)S(1)}, bf16[1152,128]{1,0:T(8,128)(2,1)S(1)}, u32[]{:S(2)}, u32[]{:S(2)}) collective-permute-start(bf16[1152,128]{1,0:T(8,128)(2,1)S(1)} %broadcast_select_fusion.1), channel_id=1, source_target_pairs={{0,1},{1,0},{2,3},{3,2},{4,5},{5,4},{6,7},{7,6},{8,9},{9,8},{10,11... | collective-permute-start | bytes 884744 | tf_op jit(solution)/shard_map/ppermute | solution.py:286
  47.3 24.5 %collective-permute-start.9 = (bf16[1152,128]{1,0:T(8,128)(2,1)S(1)}, bf16[1152,128]{1,0:T(8,128)(2,1)S(1)}, u32[]{:S(2)}, u32[]{:S(2)}) collective-permute-start(bf16[1152,128]{1,0:T(8,128)(2,1)S(1)} %select_select_fusion), channel_id=1, source_target_pairs={{0,1},{1,0},{2,3},{3,2},{4,5},{5,4},{6,7},{7,6},{8,9},{9,8},{10,11... | collective-permute-start | bytes 884744 | tf_op jit(solution)/shard_map/ppermute | solution.py:286
  50.0 1.0 %collective-permute-start.13 = (bf16[256,128]{1,0:T(8,128)(2,1)S(1)}, bf16[256,128]{1,0:T(8,128)(2,1)S(1)}, u32[]{:S(2)}, u32[]{:S(2)}) collective-permute-start(bf16[256,128]{1,0:T(8,128)(2,1)S(1)} %add.53), channel_id=1, source_target_pairs={{6,22},{7,23},{14,30},{15,31},{22,6},{23,7},{30,14},{31,15}} | collective-permute-start | bytes 196616 | tf_op jit(solution)/shard_map/ppermute | solution.py:410
  51.0 8.1 %collective-permute-start.14 = (bf16[256,128]{1,0:T(8,128)(2,1)S(1)}, bf16[256,128]{1,0:T(8,128)(2,1)S(1)}, u32[]{:S(2)}, u32[]{:S(2)}) collective-permute-start(bf16[256,128]{1,0:T(8,128)(2,1)S(1)} %add_convert_fusion), channel_id=1, source_target_pairs={{6,4},{7,5},{14,12},{15,13},{22,20},{23,21},{30,28},{31,29}} | collective-permute-start | bytes 196616 | tf_op jit(solution)/shard_map/ppermute | solution.py:319
  51.7 7.5 %collective-permute-start.15 = (bf16[256,128]{1,0:T(8,128)(2,1)S(1)}, bf16[256,128]{1,0:T(8,128)(2,1)S(1)}, u32[]{:S(2)}, u32[]{:S(2)}) collective-permute-start(bf16[256,128]{1,0:T(8,128)(2,1)S(1)} %add_convert_fusion), channel_id=1, source_target_pairs={{6,2},{7,3},{14,10},{15,11},{22,18},{23,19},{30,26},{31,27}} | collective-permute-start | bytes 196616 | tf_op jit(solution)/shard_map/ppermute | solution.py:319
  52.3 11.9 %collective-permute-start.16 = (bf16[256,128]{1,0:T(8,128)(2,1)S(1)}, bf16[256,128]{1,0:T(8,128)(2,1)S(1)}, u32[]{:S(2)}, u32[]{:S(2)}) collective-permute-start(bf16[256,128]{1,0:T(8,128)(2,1)S(1)} %add_convert_fusion), channel_id=1, source_target_pairs={{6,0},{7,1},{14,8},{15,9},{22,16},{23,17},{30,24},{31,25}} | collective-permute-start | bytes 196616 | tf_op jit(solution)/shard_map/ppermute | solution.py:319
  64.3 7.6 %collective-permute-start.17 = (bf16[256,128]{1,0:T(8,128)(2,1)S(1)}, bf16[256,128]{1,0:T(8,128)(2,1)S(1)}, u32[]{:S(2)}, u32[]{:S(2)}) collective-permute-start(bf16[256,128]{1,0:T(8,128)(2,1)S(1)} %get-tuple-element.40), channel_id=1, source_target_pairs={{0,1},{1,0},{2,3},{3,2},{4,5},{5,4},{6,7},{7,6},{8,9},{9,8},{10,11... | collective-permute-start | bytes 196616 | tf_op jit(solution)/shard_map/ppermute | solution.py:286
  78.9 4.8 %collective-permute-start.18 = (bf16[2,2,32,1024]{3,2,0,1:T(8,128)(2,1)S(1)}, bf16[2,2,32,1024]{3,2,0,1:T(8,128)(2,1)S(1)}, u32[]{:S(2)}, u32[]{:S(2)}) collective-permute-start(bf16[2,2,32,1024]{3,2,0,1:T(8,128)(2,1)S(1)} %fusion.18), channel_id=1, source_target_pairs={{0,8},{8,0},{16,24},{24,16},{1,9},{9,1},{17,25},{25,17},{2,10},{10... | collective-permute-start | bytes 786440 | tf_op jit(solution)/shard_map/ppermute | solution.py:282
  83.7 4.9 %copy-start.4 = (f32[128,128]{1,0:T(8,128)S(1)}, f32[128,128]{1,0:T(8,128)}, u32[]{:S(2)}) copy-start(f32[128,128]{1,0:T(8,128)} %one_ref) | copy-start | bytes 196612
  86.6 6.0 %collective-permute-start.19 = (bf16[2,1,32,1024]{3,2,1,0:T(8,128)(2,1)S(1)}, bf16[2,1,32,1024]{3,2,1,0:T(8,128)(2,1)S(1)}, u32[]{:S(2)}, u32[]{:S(2)}) collective-permute-start(bf16[2,1,32,1024]{3,2,1,0:T(8,128)(2,1)S(1)} %fusion.19), channel_id=1, source_target_pairs={{0,16},{8,24},{16,0},{24,8},{1,17},{9,25},{17,1},{25,9},{2,18},{10... | collective-permute-start | bytes 393224 | tf_op jit(solution)/shard_map/ppermute | solution.py:282
  (9 other events, 18.9 us)

commit v7 on v5

--- a/solution.py
+++ b/solution.py
@@ -90,10 +90,11 @@
     inv_one_ref[...] = inverse_one
     inv_two_ref[...] = inverse_two
     chosen = halves(jnp.where(side_ref[0] == 1, inverse_two, inverse_one))
+    whole_ref[:panel, :] = jnp.zeros((panel, panel), BF16)
     fetch.wait()
     for (start, stop), piece_ref in zip(cuts, piece_refs):
         product = split_dot(halves(rows_ref[start:stop, :]), chosen).astype(BF16)
-        whole_ref[start:stop, :] = product
+        whole_ref[panel + start : panel + stop, :] = product
         piece_ref[:panel, :] = jnp.zeros((panel, panel), BF16)
         piece_ref[panel:, :] = product
 
@@ -102,62 +103,33 @@
     height = adj_trail.shape[0]
     panel = diag_one.shape[0]
     vmem = pl.BlockSpec(memory_space=pltpu.VMEM)
-    hbm = pl.BlockSpec(memory_space=pl.ANY)
+    hbm = pl.BlockSpec(memory_space=pltpu.HBM)
     sizes = [panel + stop - start for start, stop in cuts]
     return pl.pallas_call(
         functools.partial(prepare_kernel, cuts),
         in_specs=[pl.BlockSpec(memory_space=pltpu.SMEM), vmem, vmem, hbm],
         out_specs=[vmem] * (3 + len(cuts)),
         out_shape=[jax.ShapeDtypeStruct((panel, panel), F32)] * 2
-        + [jax.ShapeDtypeStruct((size, panel), BF16) for size in [height] + sizes],
-        scratch_shapes=[pltpu.VMEM((height, panel), F32), pltpu.SemaphoreType.DMA],
-        compiler_params=pltpu.CompilerParams(vmem_limit_bytes=56 * 2**20),
+        + [jax.ShapeDtypeStruct((size, panel), BF16) for size in [panel + height] + sizes],
+        scratch_shapes=[
+            pltpu.VMEM((height, panel), F32),
+            pltpu.SemaphoreType.DMA,
+        ],
+        compiler_params=pltpu.CompilerParams(vmem_limit_bytes=60 * 2**20),
         cost_estimate=pl.CostEstimate(
-            flops=8 * height * panel * panel, bytes_accessed=6 * height * panel, transcendentals=0
+            flops=8 * height * panel * panel, bytes_accessed=8 * height * panel, transcendentals=0
         ),
         name="prepare",
     )(side, diag_one, diag_two, adj_trail)
 
 
-def update_kernel(flags_ref, both_ref, rows_ref, adj_ref, *rest):
-    out_ref = rest[-1]
-    panel = both_ref.shape[1] // 2
-    last = out_ref.shape[1] - panel
-    both = both_ref[...]
-    left = adj_ref[...] - wide_dot(both, rows_ref[...])
-    out_ref[:, :last] = left[:, :last].astype(BF16)
-    block = jnp.where(flags_ref[0] == 1, both[:, panel:], left[:, last:].astype(BF16))
-    out_ref[:, last:] = jnp.where(flags_ref[1] == 1, both[:, :panel], block)
-
-
-def update(flags, both, full_both, adj_trail, start, previous):
-    height, width = adj_trail.shape
-    rows, depth = both.shape
-    tile = depth
-    first = start // tile
-    operands = [flags, both, full_both, adj_trail]
-    in_specs = [
-        pl.BlockSpec(memory_space=pltpu.SMEM),
-        pl.BlockSpec((tile, depth), lambda i: (i, 0)),
-        pl.BlockSpec((depth, width), lambda i: (0, 0)),
-        pl.BlockSpec((tile, width), lambda i: (first + i, 0)),
-    ]
-    if previous is not None:
-        operands.append(previous)
-        in_specs.append(pl.BlockSpec(memory_space=pl.ANY))
+def blank(shape):
     return pl.pallas_call(
-        update_kernel,
-        grid=(rows // tile,),
-        in_specs=in_specs,
-        out_specs=pl.BlockSpec((tile, width), lambda i: (first + i, 0)),
-        out_shape=jax.ShapeDtypeStruct((height, width), BF16),
-        input_output_aliases={} if previous is None else {4: 0},
-        compiler_params=pltpu.CompilerParams(vmem_limit_bytes=16 * 2**20),
-        cost_estimate=pl.CostEstimate(
-            flops=2 * rows * depth * width, bytes_accessed=6 * rows * width, transcendentals=0
-        ),
-        name="update",
-    )(*operands)
+        lambda out_ref: None,
+        out_specs=pl.BlockSpec(memory_space=pltpu.HBM),
+        out_shape=jax.ShapeDtypeStruct(shape, BF16),
+        name="blank",
+    )()
 
 
 def after(value, *others):
@@ -291,10 +263,9 @@
         side, after(diag_one, near_two, near_one), diag_two, adj_trail, cuts
     )
     own_cross = full_two[:, last:]
+    whole = lax.dynamic_update_slice(whole, own_cross, (0, 0))
     packets[0] = lax.dynamic_update_slice(packets[0], own_cross, (0, 0))
     full_one = gather_rest(after(near_one, packets[0]))
-    full_both = jnp.concatenate([full_two, full_one], 0)
-    edge = after(trail[:, last:], packets[0])
 
     def factor_of(cross):
         return jnp.concatenate(halves(exact_dot(cross.astype(F32), inverse_one)), 0)
@@ -307,21 +278,21 @@
         )
         return jnp.concatenate([solved_two, tail.astype(BF16)], 1)
 
-    whole_other = pair_swap(whole, [top])
+    one_owner, two_owner = col_count - 2, col_count - 1
+    early_two = lax.ppermute(whole, "col", [(two_owner, one_owner)])
     first, arrived = spread(packets, full_one)
+    early_one = lax.ppermute(after(whole, first[0]), "col", [(one_owner, two_owner)])
     at_top = level == top
-    other = []
     own = [jnp.where(at_top, a, b) for a, b in zip(packets, arrived)]
-    for k, value in enumerate(arrived):
-        value = own[0] if k == 0 else value
-        other.append(pair_swap(value, range(levels if k == 0 else levels - 1)))
-
-    whole_other = after(whole_other, first[final])
-    top_both = panels_of(whole, whole_other, factor_of(own_cross), height)
-    terms = wide_dot(top_both.T, edge)
+    other = [pair_swap(value, range(levels - 1)) for value in arrived]
+    full_both = jnp.concatenate([full_two, after(full_one, arrived[0])], 0)
+
+    early_two = after(early_two, arrived[final], other[0])
+    top_both = panels_of(whole, early_two, factor_of(own_cross), height)
+    terms = wide_dot(top_both.T, trail[:, last:])
     placed = lax.dynamic_update_slice_in_dim(
         jnp.zeros((2 * panel, panel), F32),
-        jnp.where(is_two, 0, adj_row_two[:, last:]),
+        jnp.where(is_two, 0, after(adj_row_two, first[final])[:, last:]),
         row_start,
         0,
     )
@@ -334,35 +305,53 @@
             for i in range(row_count)
             for c in (col_count - 2, col_count - 1)
         ]
-        terms = terms + lax.ppermute(terms, ("row", "col"), pairs)
-        if step == 1:
-            terms = after(terms, other[0])
+        if step > 1:
+            terms = terms.astype(BF16)
+        moved = lax.ppermute(terms, ("row", "col"), pairs)
+        terms = terms.astype(F32) + moved.astype(F32)
         step *= 2
-    terms = row_terms = terms.astype(BF16)
+    terms = terms.astype(BF16)
+
+    whole_other = jnp.where(is_two, early_one, early_two)
+    for k, (start, stop) in enumerate(cuts):
+        piece = whole_other[(0 if k == 0 else panel + start) : panel + stop]
+        low = other[k][-piece.shape[0] :]
+        other[k] = jnp.where(at_top, piece, after(low, own_terms))
+    cross = jnp.where(is_two, other[0][:panel], own[0][:panel])
+    factor = factor_of(cross)
+    column = lax.broadcasted_iota(jnp.int32, (1, width), 1)
+    in_block = column >= last
+
+    def put(matrix, block_one, block_two):
+        block = jnp.where(here_one, block_one, block_two).astype(matrix.dtype)
+        block = jnp.pad(block, ((0, 0), (last, 0)))
+        return jnp.where(in_block & (here_one | here_two), block, matrix)
+
+    def updated(both, start, previous):
+        rows = adj_trail[start : start + both.shape[0]]
+        left = (rows - wide_dot(both, full_both)).astype(BF16)
+        left = put(left, both[:, panel:], both[:, :panel])
+        return lax.dynamic_update_slice(previous, left, (start, 0))
+
+    sums = 0
+    grad_trail = blank((height, width))
+    for (start, stop), mine, theirs in zip(cuts[:-1], own, other):
+        both = panels_of(mine, theirs, factor, stop - start)
+        sums = sums + wide_dot(both.T, trail[start:stop])
+        grad_trail = updated(both, start, grad_trail)
     terms = choose(
         [([top], terms)] + [([k], hop(terms, [(top, k)])) for k in range(levels - 1)]
     )
-    terms_other = pair_swap(terms, range(levels))
+    terms_other = pair_swap(after(terms, sums), range(levels))
     terms, terms_other = terms.astype(F32), terms_other.astype(F32)
     diag_term_two = jnp.where(is_two, terms[:panel], terms_other[:panel])
     crossing = jnp.where(is_two, terms_other[:panel], terms[:panel])
     diag_term_one = jnp.where(is_two, terms_other[panel:], terms[panel:])
 
-    flags = jnp.stack([here_one, here_two]).astype(jnp.int32)
-    cross = jnp.where(is_two, other[0][:panel], own[0][:panel])
-    factor = factor_of(cross)
-    sums = 0
-    grad_trail = None
-    for k, (start, stop) in enumerate(cuts):
-        theirs = after(other[k], own_terms)
-        if k == final:
-            theirs = after(theirs, row_terms, grad_trail)
-        if k > 0:
-            theirs = jnp.where(at_top, whole_other[start:stop], theirs[panel:])
-        both = panels_of(own[k], theirs, factor, stop - start)
-        sums = sums + wide_dot(both.T, trail[start:stop])
-        if k < final:
-            grad_trail = update(flags, both, full_both, adj_trail, start, grad_trail)
+    start, stop = cuts[-1]
+    theirs = after(other[-1], terms, sums)
+    both = panels_of(own[-1], theirs, factor, stop - start)
+    sums = (sums + wide_dot(both.T, trail[start:stop])).astype(BF16)
 
     parts = sums.reshape(2, row_count, band, width)
     step = 1
@@ -372,16 +361,14 @@
         keep = jnp.where(low, parts[:, :, 0], parts[:, :, 1])
         give = jnp.where(low, parts[:, :, 1], parts[:, :, 0])
         give = give.astype(BF16)
-        if 2 * step >= row_count:
-            start = cuts[final][0]
-            grad_trail = update(flags, both, full_both, adj_trail, start, grad_trail)
-            give = sent = after(give, grad_trail)
+        sent = give
         parts = keep + row_swap(give, step).astype(F32)
         step *= 2
     parts = parts.reshape(2, band, width)
+    grad_trail = updated(after(both, sent), start, grad_trail)
 
     grad_diag_two = block_adjoint(
-        diag_two, inverse_two, jnp.tril(adj_diag_two - after(diag_term_two, sent))
+        diag_two, inverse_two, jnp.tril(adj_diag_two - after(diag_term_two, sums))
     )
     mirror_two = grad_diag_two + grad_diag_two.T
     adj_two = -crossing - exact_dot(mirror_two, cross.astype(F32))
@@ -400,14 +387,6 @@
     two_left = adj_row_two - mixed[:band] - parts[0]
     one_left = adj_row_one - mixed[band:] - parts[1]
 
-    column = lax.broadcasted_iota(jnp.int32, (1, width), 1)
-    in_block = column >= last
-
-    def put(matrix, block_one, block_two):
-        block = jnp.where(here_one, block_one, block_two).astype(F32)
-        block = jnp.pad(block, ((0, 0), (last, 0)))
-        return jnp.where(in_block & (here_one | here_two), block, matrix)
-
     nothing = jnp.zeros((band, panel), F32)
     grad_row_one = put(one_left, nothing, nothing)
     grad_row_two = put(two_left, own_rows(head_wide), nothing)

time: 87.2 us -> 76.8 us (0.88)
  Pallas kernels: 10.8 us -> 4.59 us
  waiting for transfers between devices: 36.3 us -> 30.4 us
  local copies, waits for them, and re-layouts: 8.34 us -> 3.01 us
  matrix products: 5.74 us -> 9.42 us
  starting transfers between devices: 20.7 us -> 23.6 us
    pallas_call x2 -> x1, Pallas kernels: 6.16 us -> 0.01 us  [blank(): pl.pallas_call(lambda out_ref: None, out_specs=pl.BlockSpec(memory_space=...]
    ppermute x8, waiting for transfers between devices: 28.4 us -> 23 us  [hop(): return lax.ppermute(value, 'col', pairs)]
    unnamed x36 -> x38, local copies, waits for them, and re-layouts: 7.29 us -> 1.96 us
    dot_general x8 -> x10, matrix products: 3.45 us -> 7.12 us  [wide_dot(): return jnp.dot(a, b, preferred_element_type=F32)]
    ppermute x4 -> x3, starting transfers between devices: 5.4 us -> 7.93 us  [pair_swap(): return lax.ppermute(value, 'col', pairs)]
    ppermute x2 -> x4, starting transfers between devices: 1.33 us -> 3.12 us  [the longest x2 1.6 us: per_device(): moved = lax.ppermute(terms, ('row', 'col'), pairs)]
    ppermute x6, starting transfers between devices: 6.76 us -> 5.32 us  [row_swap(): return lax.ppermute(value, 'row', [(i, i ^ step) for i in range(row_count)])]
    ppermute x4 -> x3, waiting for transfers between devices: 2.46 us -> 2.07 us  [pair_swap(): return lax.ppermute(value, 'col', pairs)]
  transfers between devices with their start and end apart: 20 -> 21, of which waited for: 8 -> 8; matrix products, arithmetic and copies ran while one was open for 4% -> 15% of each run, Pallas kernels for 12% -> 6%
where the time goes in v7:
time: 76.8 us; the launch traced here: 76.3 us
  waiting for transfers between devices  30.4 us (40%)
  starting transfers between devices  23.6 us (31%)
  matrix products  9.42 us (12%)
  Pallas kernels  4.59 us (6%)
  other arithmetic  3.78 us (5%)
  local copies, waits for them, and re-layouts  3.01 us (4%)
  between operations  1.5 us (2%)
    ppermute x8, waiting for transfers between devices, hop(): return lax.ppermute(value, 'col', pairs)  23 us
    ppermute x3, starting transfers between devices, pair_swap(): return lax.ppermute(value, 'col', pairs)  7.93 us
    ppermute x8, starting transfers between devices, hop(): return lax.ppermute(value, 'col', pairs)  7.23 us
    dot_general x10, matrix products, wide_dot(): return jnp.dot(a, b, preferred_element_type=F32)  7.12 us
    ppermute x6, waiting for transfers between devices, row_swap(): return lax.ppermute(value, 'row', [(i, i ^ step) for i in range(row_count)])  5.4 us
    ppermute x6, starting transfers between devices, row_swap(): return lax.ppermute(value, 'row', [(i, i ^ step) for i in range(row_count)])  5.32 us
    pallas_call x1, Pallas kernels, prepare(): pl.pallas_call(functools.partial(prepare_kernel, cuts), in_specs=[pl.Bloc...  4.59 us
    dot_general x10, matrix products, exact_dot(): return jnp.dot(a, b, precision=EXACT, preferred_element_type=F32)  2.3 us
  transfers between devices with their start and end apart: 21, of which 8 were waited for; matrix products, arithmetic and copies ran while one was open for 15% of the time, Pallas kernels for 6%

profile of v7, /device:TPU:0, one launch (start us, length us, event | category | flops | bytes accessed | tf_op | source)
XLA Modules:
  0.0 76.3 jit_solution(18286171747678631026)
XLA Ops:
  1.2 1.0 %collective-permute-done = bf16[1,1,32,1024]{3,2,1,0:T(8,128)(2,1)S(1)} collective-permute-done((bf16[1,1,32,1024]{3,2,1,0:T(8,128)(2,1)}, bf16[1,1,32,1024]{3,2,1,0:T(8,128)(2,1)S(1)}, u32[]{:S(2)}, u32[]{:S(2)}) %collective-permute-start) | collective-permute-done | bytes 65568 | tf_op jit(solution)/shard_map/ppermute | solution.py:181
  2.6 0.9 %broadcast_select_fusion.12 = (bf16[1,1,32,1024]{3,2,1,0:T(8,128)(2,1)S(1)}, bf16[1,1,32,1024]{3,2,1,0:T(8,128)(2,1)S(1)}, bf16[1,1,32,1024]{3,2,1,0:T(8,128)(2,1)S(1)}, bf16[1,1,32,1024]{3,2,1,0:T(8,128)(2,1)S(1)}) fusion(bf16[1,1,32,1024]{3,2,1,0:T(8,128)(2,1)S(1)} %collective-permute-done.1, pred[]{:T(512)S(6)} %eq.66, bf16[32,1024]{1,0:T(8,128)(2,1)} %param.11, ...), kind=kLoop, calls=%fused_computation.120 | loop fusion | flops 131072 | bytes 524289 | tf_op jit(solution)/shard_map/jit(_where)/select_n | solution.py:191
  3.5 2.7 %collective-permute-start.2 = (bf16[1,2,32,1024]{3,2,1,0:T(8,128)(2,1)S(1)}, bf16[1,2,32,1024]{3,2,1,0:T(8,128)(2,1)S(1)}, u32[]{:S(2)}, u32[]{:S(2)}) collective-permute-start(bf16[1,2,32,1024]{3,2,1,0:T(8,128)(2,1)S(1)} %pad_maximum_fusion.17), channel_id=1, source_target_pairs={{0,16},{8,24},{16,0},{24,8},{1,17},{9,25},{17,1},{25,9},{2,18},{10... | collective-permute-start | bytes 393224 | tf_op jit(solution)/shard_map/ppermute | solution.py:181
  6.3 4.6 %prepare.1 = (f32[128,128]{1,0:T(8,128)}, f32[128,128]{1,0:T(8,128)}, bf16[2176,128]{1,0:T(8,128)(2,1)}, bf16[1152,128]{1,0:T(8,128)(2,1)}, bf16[1152,128]{1,0:T(8,128)(2,1)}) custom-call(s32[1]{0:T(128)} %bitcast.side_ref, f32[128,128]{1,0:T(8,128)} %one_ref, f32[128,128]{1,0:T(8,128)} %two_ref.1, f32[2048,1024]{1,0:T(8,128)} %adj_ref.1), custom_call_target="tpu_custom_call" | custom-call | flops 268435456 | bytes 2097152 | tf_op jit(solution)/shard_map/prepare/pallas_call | solution.py:108
  11.6 1.1 %collective-permute-start.4 = (bf16[1,2,32,1024]{3,2,1,0:T(8,128)(2,1)S(1)}, bf16[1,2,32,1024]{3,2,1,0:T(8,128)(2,1)S(1)}, u32[]{:S(2)}, u32[]{:S(2)}) collective-permute-start(bf16[1,2,32,1024]{3,2,1,0:T(8,128)(2,1)S(1)} %pad_maximum_fusion.18), channel_id=1, source_target_pairs={{0,16},{8,24},{16,0},{24,8},{1,17},{9,25},{17,1},{25,9},{2,18},{10... | collective-permute-start | bytes 393224 | tf_op jit(solution)/shard_map/ppermute | solution.py:181
  13.5 3.6 %collective-permute-done.4 = bf16[1,2,32,1024]{3,2,1,0:T(8,128)(2,1)S(1)} collective-permute-done((bf16[1,2,32,1024]{3,2,1,0:T(8,128)(2,1)S(1)}, bf16[1,2,32,1024]{3,2,1,0:T(8,128)(2,1)S(1)}, u32[]{:S(2)}, u32[]{:S(2)}) %collective-permute-start.4) | collective-permute-done | bytes 131104 | tf_op jit(solution)/shard_map/ppermute | solution.py:181
  17.9 1.3 %collective-permute-start.7 = (bf16[1152,128]{1,0:T(8,128)(2,1)S(1)}, bf16[1152,128]{1,0:T(8,128)(2,1)S(1)}, u32[]{:S(2)}, u32[]{:S(2)}) collective-permute-start(bf16[1152,128]{1,0:T(8,128)(2,1)S(1)} %broadcast_select_fusion.3), channel_id=1, source_target_pairs={{6,2},{7,3},{2,0},{3,1},{14,10},{15,11},{10,8},{11,9},{22,18},{23,... | collective-permute-start | bytes 884744 | tf_op jit(solution)/shard_map/ppermute | solution.py:218
  20.1 0.8 %collective-permute-start.5 = (bf16[2176,128]{1,0:T(8,128)(2,1)S(1)}, bf16[2176,128]{1,0:T(8,128)(2,1)S(1)}, u32[]{:S(2)}, u32[]{:S(2)}) collective-permute-start(bf16[2176,128]{1,0:T(8,128)(2,1)S(1)} %copy-done.7), channel_id=1, source_target_pairs={{6,7},{14,15},{22,23},{30,31}} | collective-permute-start | bytes 1671176 | tf_op jit(solution)/shard_map/ppermute | solution.py:284
  21.0 14.4 %collective-permute-done.7 = bf16[1152,128]{1,0:T(8,128)(2,1)S(1)} collective-permute-done((bf16[1152,128]{1,0:T(8,128)(2,1)S(1)}, bf16[1152,128]{1,0:T(8,128)(2,1)S(1)}, u32[]{:S(2)}, u32[]{:S(2)}) %collective-permute-start.7) | collective-permute-done | bytes 294944 | tf_op jit(solution)/shard_map/ppermute | solution.py:218
  35.3 1.3 %collective-permute-start.10 = (bf16[1152,128]{1,0:T(8,128)(2,1)S(1)}, bf16[1152,128]{1,0:T(8,128)(2,1)S(1)}, u32[]{:S(2)}, u32[]{:S(2)}) collective-permute-start(bf16[1152,128]{1,0:T(8,128)(2,1)S(1)} %collective-permute-done.7), channel_id=1, source_target_pairs={{2,0},{3,1},{10,8},{11,9},{18,16},{19,17},{26,24},{27,25}} | collective-permute-start | bytes 884744 | tf_op jit(solution)/shard_map/ppermute | solution.py:218
  37.4 3.4 %collective-permute-start.11 = (bf16[1152,128]{1,0:T(8,128)(2,1)S(1)}, bf16[1152,128]{1,0:T(8,128)(2,1)S(1)}, u32[]{:S(2)}, u32[]{:S(2)}) collective-permute-start(bf16[1152,128]{1,0:T(8,128)(2,1)S(1)} %get-tuple-element.56), channel_id=1, source_target_pairs={{0,1},{1,0},{2,3},{3,2},{4,5},{5,4},{8,9},{9,8},{10,11},{11,10},{1... | collective-permute-start | bytes 884744 | tf_op jit(solution)/shard_map/ppermute | solution.py:185
  40.9 3.6 %collective-permute-done.10 = bf16[1152,128]{1,0:T(8,128)(2,1)S(1)} collective-permute-done((bf16[1152,128]{1,0:T(8,128)(2,1)S(1)}, bf16[1152,128]{1,0:T(8,128)(2,1)S(1)}, u32[]{:S(2)}, u32[]{:S(2)}) %collective-permute-start.10) | collective-permute-done | bytes 294944 | tf_op jit(solution)/shard_map/ppermute | solution.py:218
  44.5 3.7 %collective-permute-start.12 = (bf16[1152,128]{1,0:T(8,128)(2,1)S(1)}, bf16[1152,128]{1,0:T(8,128)(2,1)S(1)}, u32[]{:S(2)}, u32[]{:S(2)}) collective-permute-start(bf16[1152,128]{1,0:T(8,128)(2,1)S(1)} %select_select_fusion), channel_id=1, source_target_pairs={{0,1},{1,0},{2,3},{3,2},{4,5},{5,4},{8,9},{9,8},{10,11},{11,10},{1... | collective-permute-start | bytes 884744 | tf_op jit(solution)/shard_map/ppermute | solution.py:185
  49.3 0.8 %collective-permute-start.13 = (f32[256,128]{1,0:T(8,128)S(1)}, f32[256,128]{1,0:T(8,128)S(1)}, u32[]{:S(2)}, u32[]{:S(2)}) collective-permute-start(f32[256,128]{1,0:T(8,128)S(1)} %convolution_subtract_fusion.3), channel_id=1, source_target_pairs={{6,14},{7,15},{14,6},{15,7},{22,30},{23,31},{30,22},{31,23}} | collective-permute-start | bytes 393224 | tf_op jit(solution)/shard_map/ppermute | solution.py:310
  50.8 0.8 %collective-permute-start.14 = (bf16[256,128]{1,0:T(8,128)(2,1)S(1)}, bf16[256,128]{1,0:T(8,128)(2,1)S(1)}, u32[]{:S(2)}, u32[]{:S(2)}) collective-permute-start(bf16[256,128]{1,0:T(8,128)(2,1)S(1)} %add_convert_fusion.1), channel_id=1, source_target_pairs={{6,22},{7,23},{14,30},{15,31},{22,6},{23,7},{30,14},{31,15}} | collective-permute-start | bytes 196616 | tf_op jit(solution)/shard_map/ppermute | solution.py:310
  53.0 1.3 %collective-permute-start.17 = (bf16[256,128]{1,0:T(8,128)(2,1)S(1)}, bf16[256,128]{1,0:T(8,128)(2,1)S(1)}, u32[]{:S(2)}, u32[]{:S(2)}) collective-permute-start(bf16[256,128]{1,0:T(8,128)(2,1)S(1)} %add_convert_fusion), channel_id=1, source_target_pairs={{6,0},{7,1},{14,8},{15,9},{22,16},{23,17},{30,24},{31,25}} | collective-permute-start | bytes 196616 | tf_op jit(solution)/shard_map/ppermute | solution.py:218
  56.4 5.0 %collective-permute-done.17 = bf16[256,128]{1,0:T(8,128)(2,1)S(1)} collective-permute-done((bf16[256,128]{1,0:T(8,128)(2,1)S(1)}, bf16[256,128]{1,0:T(8,128)(2,1)S(1)}, u32[]{:S(2)}, u32[]{:S(2)}) %collective-permute-start.17) | collective-permute-done | bytes 65568 | tf_op jit(solution)/shard_map/ppermute | solution.py:218
  61.4 0.8 %collective-permute-start.19 = (bf16[256,128]{1,0:T(8,128)(2,1)S(1)}, bf16[256,128]{1,0:T(8,128)(2,1)S(1)}, u32[]{:S(2)}, u32[]{:S(2)}) collective-permute-start(bf16[256,128]{1,0:T(8,128)(2,1)S(1)} %get-tuple-element.45), channel_id=1, source_target_pairs={{0,1},{1,0},{2,3},{3,2},{4,5},{5,4},{6,7},{7,6},{8,9},{9,8},{10,11... | collective-permute-start | bytes 196616 | tf_op jit(solution)/shard_map/ppermute | solution.py:185
  62.7 0.7 fusion.8
  63.7 2.1 %collective-permute-done.19 = bf16[256,128]{1,0:T(8,128)(2,1)S(1)} collective-permute-done((bf16[256,128]{1,0:T(8,128)(2,1)S(1)}, bf16[256,128]{1,0:T(8,128)(2,1)S(1)}, u32[]{:S(2)}, u32[]{:S(2)}) %collective-permute-start.19) | collective-permute-done | bytes 65568 | tf_op jit(solution)/shard_map/ppermute | solution.py:185
  69.6 0.8 %collective-permute-start.20 = (bf16[2,1,32,1024]{3,2,1,0:T(8,128)(2,1)S(1)}, bf16[2,1,32,1024]{3,2,1,0:T(8,128)(2,1)S(1)}, u32[]{:S(2)}, u32[]{:S(2)}) collective-permute-start(bf16[2,1,32,1024]{3,2,1,0:T(8,128)(2,1)S(1)} %fusion.27), channel_id=1, source_target_pairs={{0,16},{8,24},{16,0},{24,8},{1,17},{9,25},{17,1},{25,9},{2,18},{10... | collective-permute-start | bytes 393224 | tf_op jit(solution)/shard_map/ppermute | solution.py:181
  70.5 0.8 %copy-done.3 = bf16[2048,1024]{1,0:T(8,128)(2,1)S(1)} copy-done((bf16[2048,1024]{1,0:T(8,128)(2,1)S(1)}, bf16[2048,1024]{1,0:T(8,128)(2,1)}, u32[]{:S(2)}) %copy-start.3) | copy-done | bytes 4194328
  71.3 2.9 %select_dynamic-update-slice_fusion = bf16[2048,1024]{1,0:T(8,128)(2,1)S(1)} fusion(bf16[2048,1024]{1,0:T(8,128)(2,1)S(1)} %copy-done.3, bf16[1024,128]{1,0:T(8,128)(2,1)S(1)} %slice_select_fusion.3, pred[1024]{0:T(1024)(128)(4,1)S(1)} %fusion.70, bf16[1024,256]{1,0:T(8,128)(2,1)S(1)} %pad_maximum_fusion.7, f32[2048,1024]{1,0:T(8,128)} %adj_ref.1, ...), kind=kOutput, calls=%fused_computation.4 | convolution fusion | flops 541065216 | bytes 7603200 | tf_op jit(solution)/shard_map/dot_general | solution.py:21
  74.7 1.2 %fusion.29 = (f32[32,1024]{1,0:T(8,128)}, f32[32,1024]{1,0:T(8,128)}) fusion(f32[2,1,32,1024]{3,2,1,0:T(8,128)S(1)} %bitcast_add_fusion, f32[32,1024]{1,0:T(8,128)S(1)} %copy-done.12, f32[64,1024]{1,0:T(8,128)S(1)} %fusion.15, f32[32,128]{1,0:T(8,128)S(1)} %get-tuple-element.47, pred[1024]{0:T(1024)(128)(4,1)S(1)} %fusion.70, f32[32,1024]{1,0:T(8,128)S(1)} %copy-done.13, ...), kind=kLoop, calls=%fused_computation.64 | loop fusion | flops 196608 | bytes 1070080 | tf_op jit(solution)/shard_map/jit(_where)/select_n | solution.py:328
  (127 shorter events, 15.1 us)
Async XLA Ops:
  0.6 1.6 %collective-permute-start = (bf16[1,1,32,1024]{3,2,1,0:T(8,128)(2,1)}, bf16[1,1,32,1024]{3,2,1,0:T(8,128)(2,1)S(1)}, u32[]{:S(2)}, u32[]{:S(2)}) collective-permute-start(bf16[1,1,32,1024]{3,2,1,0:T(8,128)(2,1)} %bitcast.81), channel_id=1, source_target_pairs={{0,8},{8,0},{16,24},{24,16},{1,9},{9,1},{17,25},{25,17},{2,10},{10... | collective-permute-start | bytes 196616 | tf_op jit(solution)/shard_map/ppermute | solution.py:181
  1.1 1.5 %collective-permute-start.1 = (bf16[1,1,32,1024]{3,2,1,0:T(8,128)(2,1)}, bf16[1,1,32,1024]{3,2,1,0:T(8,128)(2,1)S(1)}, u32[]{:S(2)}, u32[]{:S(2)}) collective-permute-start(bf16[1,1,32,1024]{3,2,1,0:T(8,128)(2,1)} %bitcast.80), channel_id=1, source_target_pairs={{0,8},{8,0},{16,24},{24,16},{1,9},{9,1},{17,25},{25,17},{2,10},{10... | collective-permute-start | bytes 196616 | tf_op jit(solution)/shard_map/ppermute | solution.py:181
  3.5 7.3 %collective-permute-start.2 = (bf16[1,2,32,1024]{3,2,1,0:T(8,128)(2,1)S(1)}, bf16[1,2,32,1024]{3,2,1,0:T(8,128)(2,1)S(1)}, u32[]{:S(2)}, u32[]{:S(2)}) collective-permute-start(bf16[1,2,32,1024]{3,2,1,0:T(8,128)(2,1)S(1)} %pad_maximum_fusion.17), channel_id=1, source_target_pairs={{0,16},{8,24},{16,0},{24,8},{1,17},{9,25},{17,1},{25,9},{2,18},{10... | collective-permute-start | bytes 393224 | tf_op jit(solution)/shard_map/ppermute | solution.py:181
  11.0 29.9 %copy-start.12 = (f32[32,1024]{1,0:T(8,128)S(1)}, f32[32,1024]{1,0:T(8,128)}, u32[]{:S(2)}) copy-start(f32[32,1024]{1,0:T(8,128)} %param.17) | copy-start | bytes 393220
  11.6 5.5 %collective-permute-start.4 = (bf16[1,2,32,1024]{3,2,1,0:T(8,128)(2,1)S(1)}, bf16[1,2,32,1024]{3,2,1,0:T(8,128)(2,1)S(1)}, u32[]{:S(2)}, u32[]{:S(2)}) collective-permute-start(bf16[1,2,32,1024]{3,2,1,0:T(8,128)(2,1)S(1)} %pad_maximum_fusion.18), channel_id=1, source_target_pairs={{0,16},{8,24},{16,0},{24,8},{1,17},{9,25},{17,1},{25,9},{2,18},{10... | collective-permute-start | bytes 393224 | tf_op jit(solution)/shard_map/ppermute | solution.py:181
  12.8 4.4 %collective-permute-start.3 = (bf16[1152,128]{1,0:T(8,128)(2,1)S(1)}, bf16[1152,128]{1,0:T(8,128)(2,1)S(1)}, u32[]{:S(2)}, u32[]{:S(2)}) collective-permute-start(bf16[1152,128]{1,0:T(8,128)(2,1)S(1)} %copy-done.8), channel_id=1, source_target_pairs={{6,2},{7,3},{14,10},{15,11},{22,18},{23,19},{30,26},{31,27}} | collective-permute-start | bytes 884744 | tf_op jit(solution)/shard_map/ppermute | solution.py:218
  17.2 20.2 %collective-permute-start.9 = (bf16[1152,128]{1,0:T(8,128)(2,1)S(1)}, bf16[1152,128]{1,0:T(8,128)(2,1)S(1)}, u32[]{:S(2)}, u32[]{:S(2)}) collective-permute-start(bf16[1152,128]{1,0:T(8,128)(2,1)S(1)} %collective-permute-done.3), channel_id=1, source_target_pairs={{2,4},{3,5},{10,12},{11,13},{18,20},{19,21},{26,28},{27,29}} | collective-permute-start | bytes 884744 | tf_op jit(solution)/shard_map/ppermute | solution.py:218
  17.9 17.4 %collective-permute-start.7 = (bf16[1152,128]{1,0:T(8,128)(2,1)S(1)}, bf16[1152,128]{1,0:T(8,128)(2,1)S(1)}, u32[]{:S(2)}, u32[]{:S(2)}) collective-permute-start(bf16[1152,128]{1,0:T(8,128)(2,1)S(1)} %broadcast_select_fusion.3), channel_id=1, source_target_pairs={{6,2},{7,3},{2,0},{3,1},{14,10},{15,11},{10,8},{11,9},{22,18},{23,... | collective-permute-start | bytes 884744 | tf_op jit(solution)/shard_map/ppermute | solution.py:218
  19.2 29.0 %collective-permute-start.6 = (bf16[2176,128]{1,0:T(8,128)(2,1)S(1)}, bf16[2176,128]{1,0:T(8,128)(2,1)S(1)}, u32[]{:S(2)}, u32[]{:S(2)}) collective-permute-start(bf16[2176,128]{1,0:T(8,128)(2,1)S(1)} %copy-done.7), channel_id=1, source_target_pairs={{7,6},{15,14},{23,22},{31,30}} | collective-permute-start | bytes 1671176 | tf_op jit(solution)/shard_map/ppermute | solution.py:282
  20.1 28.6 %copy-start = (bf16[2048,1024]{1,0:T(8,128)(2,1)S(1)}, bf16[2048,1024]{1,0:T(8,128)(2,1)}, u32[]{:S(2)}) copy-start(bf16[2048,1024]{1,0:T(8,128)(2,1)} %param.10) | copy-start | bytes 12582916
  20.1 29.9 %collective-permute-start.5 = (bf16[2176,128]{1,0:T(8,128)(2,1)S(1)}, bf16[2176,128]{1,0:T(8,128)(2,1)S(1)}, u32[]{:S(2)}, u32[]{:S(2)}) collective-permute-start(bf16[2176,128]{1,0:T(8,128)(2,1)S(1)} %copy-done.7), channel_id=1, source_target_pairs={{6,7},{14,15},{22,23},{30,31}} | collective-permute-start | bytes 1671176 | tf_op jit(solution)/shard_map/ppermute | solution.py:284
  35.3 9.1 %collective-permute-start.10 = (bf16[1152,128]{1,0:T(8,128)(2,1)S(1)}, bf16[1152,128]{1,0:T(8,128)(2,1)S(1)}, u32[]{:S(2)}, u32[]{:S(2)}) collective-permute-start(bf16[1152,128]{1,0:T(8,128)(2,1)S(1)} %collective-permute-done.7), channel_id=1, source_target_pairs={{2,0},{3,1},{10,8},{11,9},{18,16},{19,17},{26,24},{27,25}} | collective-permute-start | bytes 884744 | tf_op jit(solution)/shard_map/ppermute | solution.py:218
  36.6 7.9 %collective-permute-start.8 = (bf16[1152,128]{1,0:T(8,128)(2,1)S(1)}, bf16[1152,128]{1,0:T(8,128)(2,1)S(1)}, u32[]{:S(2)}, u32[]{:S(2)}) collective-permute-start(bf16[1152,128]{1,0:T(8,128)(2,1)S(1)} %collective-permute-done.7), channel_id=1, source_target_pairs={{2,4},{3,5},{10,12},{11,13},{18,20},{19,21},{26,28},{27,29}} | collective-permute-start | bytes 884744 | tf_op jit(solution)/shard_map/ppermute | solution.py:218
  37.4 10.8 %collective-permute-start.11 = (bf16[1152,128]{1,0:T(8,128)(2,1)S(1)}, bf16[1152,128]{1,0:T(8,128)(2,1)S(1)}, u32[]{:S(2)}, u32[]{:S(2)}) collective-permute-start(bf16[1152,128]{1,0:T(8,128)(2,1)S(1)} %get-tuple-element.56), channel_id=1, source_target_pairs={{0,1},{1,0},{2,3},{3,2},{4,5},{5,4},{8,9},{9,8},{10,11},{11,10},{1... | collective-permute-start | bytes 884744 | tf_op jit(solution)/shard_map/ppermute | solution.py:185
  44.5 17.7 %collective-permute-start.12 = (bf16[1152,128]{1,0:T(8,128)(2,1)S(1)}, bf16[1152,128]{1,0:T(8,128)(2,1)S(1)}, u32[]{:S(2)}, u32[]{:S(2)}) collective-permute-start(bf16[1152,128]{1,0:T(8,128)(2,1)S(1)} %select_select_fusion), channel_id=1, source_target_pairs={{0,1},{1,0},{2,3},{3,2},{4,5},{5,4},{8,9},{9,8},{10,11},{11,10},{1... | collective-permute-start | bytes 884744 | tf_op jit(solution)/shard_map/ppermute | solution.py:185
  49.3 1.5 %collective-permute-start.13 = (f32[256,128]{1,0:T(8,128)S(1)}, f32[256,128]{1,0:T(8,128)S(1)}, u32[]{:S(2)}, u32[]{:S(2)}) collective-permute-start(f32[256,128]{1,0:T(8,128)S(1)} %convolution_subtract_fusion.3), channel_id=1, source_target_pairs={{6,14},{7,15},{14,6},{15,7},{22,30},{23,31},{30,22},{31,23}} | collective-permute-start | bytes 393224 | tf_op jit(solution)/shard_map/ppermute | solution.py:310
  50.8 2.2 %collective-permute-start.14 = (bf16[256,128]{1,0:T(8,128)(2,1)S(1)}, bf16[256,128]{1,0:T(8,128)(2,1)S(1)}, u32[]{:S(2)}, u32[]{:S(2)}) collective-permute-start(bf16[256,128]{1,0:T(8,128)(2,1)S(1)} %add_convert_fusion.1), channel_id=1, source_target_pairs={{6,22},{7,23},{14,30},{15,31},{22,6},{23,7},{30,14},{31,15}} | collective-permute-start | bytes 196616 | tf_op jit(solution)/shard_map/ppermute | solution.py:310
  53.0 10.5 %copy-start.2 = (bf16[2048,1024]{1,0:T(8,128)(2,1)}, bf16[2048,1024]{1,0:T(8,128)(2,1)S(1)}, u32[]{:S(2)}) copy-start(bf16[2048,1024]{1,0:T(8,128)(2,1)S(1)} %select_dynamic-update-slice_fusion.1) | copy-start | bytes 12582916
  53.0 8.4 %collective-permute-start.17 = (bf16[256,128]{1,0:T(8,128)(2,1)S(1)}, bf16[256,128]{1,0:T(8,128)(2,1)S(1)}, u32[]{:S(2)}, u32[]{:S(2)}) collective-permute-start(bf16[256,128]{1,0:T(8,128)(2,1)S(1)} %add_convert_fusion), channel_id=1, source_target_pairs={{6,0},{7,1},{14,8},{15,9},{22,16},{23,17},{30,24},{31,25}} | collective-permute-start | bytes 196616 | tf_op jit(solution)/shard_map/ppermute | solution.py:218
  54.3 7.1 %collective-permute-start.16 = (bf16[256,128]{1,0:T(8,128)(2,1)S(1)}, bf16[256,128]{1,0:T(8,128)(2,1)S(1)}, u32[]{:S(2)}, u32[]{:S(2)}) collective-permute-start(bf16[256,128]{1,0:T(8,128)(2,1)S(1)} %add_convert_fusion), channel_id=1, source_target_pairs={{6,2},{7,3},{14,10},{15,11},{22,18},{23,19},{30,26},{31,27}} | collective-permute-start | bytes 196616 | tf_op jit(solution)/shard_map/ppermute | solution.py:218
  55.0 6.4 %collective-permute-start.15 = (bf16[256,128]{1,0:T(8,128)(2,1)S(1)}, bf16[256,128]{1,0:T(8,128)(2,1)S(1)}, u32[]{:S(2)}, u32[]{:S(2)}) collective-permute-start(bf16[256,128]{1,0:T(8,128)(2,1)S(1)} %add_convert_fusion), channel_id=1, source_target_pairs={{6,4},{7,5},{14,12},{15,13},{22,20},{23,21},{30,28},{31,29}} | collective-permute-start | bytes 196616 | tf_op jit(solution)/shard_map/ppermute | solution.py:218
  61.4 4.3 %collective-permute-start.19 = (bf16[256,128]{1,0:T(8,128)(2,1)S(1)}, bf16[256,128]{1,0:T(8,128)(2,1)S(1)}, u32[]{:S(2)}, u32[]{:S(2)}) collective-permute-start(bf16[256,128]{1,0:T(8,128)(2,1)S(1)} %get-tuple-element.45), channel_id=1, source_target_pairs={{0,1},{1,0},{2,3},{3,2},{4,5},{5,4},{6,7},{7,6},{8,9},{9,8},{10,11... | collective-permute-start | bytes 196616 | tf_op jit(solution)/shard_map/ppermute | solution.py:185
  63.6 5.9 %collective-permute-start.18 = (bf16[2,2,32,1024]{3,2,0,1:T(8,128)(2,1)S(1)}, bf16[2,2,32,1024]{3,2,0,1:T(8,128)(2,1)S(1)}, u32[]{:S(2)}, u32[]{:S(2)}) collective-permute-start(bf16[2,2,32,1024]{3,2,0,1:T(8,128)(2,1)S(1)} %select_bitcast_fusion), channel_id=1, source_target_pairs={{0,8},{8,0},{16,24},{24,16},{1,9},{9,1},{17,25},{25,17},{2,10},{10... | collective-permute-start | bytes 786440 | tf_op jit(solution)/shard_map/ppermute | solution.py:181
  69.6 5.0 %collective-permute-start.20 = (bf16[2,1,32,1024]{3,2,1,0:T(8,128)(2,1)S(1)}, bf16[2,1,32,1024]{3,2,1,0:T(8,128)(2,1)S(1)}, u32[]{:S(2)}, u32[]{:S(2)}) collective-permute-start(bf16[2,1,32,1024]{3,2,1,0:T(8,128)(2,1)S(1)} %fusion.27), channel_id=1, source_target_pairs={{0,16},{8,24},{16,0},{24,8},{1,17},{9,25},{17,1},{25,9},{2,18},{10... | collective-permute-start | bytes 393224 | tf_op jit(solution)/shard_map/ppermute | solution.py:181
  (16 other events, 71.6 us)

commit v8 on v7

--- a/solution.py
+++ b/solution.py
@@ -90,11 +90,10 @@
     inv_one_ref[...] = inverse_one
     inv_two_ref[...] = inverse_two
     chosen = halves(jnp.where(side_ref[0] == 1, inverse_two, inverse_one))
-    whole_ref[:panel, :] = jnp.zeros((panel, panel), BF16)
     fetch.wait()
     for (start, stop), piece_ref in zip(cuts, piece_refs):
         product = split_dot(halves(rows_ref[start:stop, :]), chosen).astype(BF16)
-        whole_ref[panel + start : panel + stop, :] = product
+        whole_ref[start:stop, :] = product
         piece_ref[:panel, :] = jnp.zeros((panel, panel), BF16)
         piece_ref[panel:, :] = product
 
@@ -110,7 +109,7 @@
         in_specs=[pl.BlockSpec(memory_space=pltpu.SMEM), vmem, vmem, hbm],
         out_specs=[vmem] * (3 + len(cuts)),
         out_shape=[jax.ShapeDtypeStruct((panel, panel), F32)] * 2
-        + [jax.ShapeDtypeStruct((size, panel), BF16) for size in [panel + height] + sizes],
+        + [jax.ShapeDtypeStruct((size, panel), BF16) for size in [height] + sizes],
         scratch_shapes=[
             pltpu.VMEM((height, panel), F32),
             pltpu.SemaphoreType.DMA,
@@ -260,12 +259,14 @@
     full_two = gather_rest(near_two)
     side = is_two.astype(jnp.int32)[None]
     inverse_one, inverse_two, whole, *packets = prepare(
-        side, after(diag_one, near_two, near_one), diag_two, adj_trail, cuts
+        side, diag_one, diag_two, adj_trail, cuts
     )
     own_cross = full_two[:, last:]
-    whole = lax.dynamic_update_slice(whole, own_cross, (0, 0))
-    packets[0] = lax.dynamic_update_slice(packets[0], own_cross, (0, 0))
-    full_one = gather_rest(after(near_one, packets[0]))
+    one_owner, two_owner = col_count - 2, col_count - 1
+    lent_cross = lax.ppermute(own_cross, "col", [(one_owner, two_owner)])
+    packets[final] = lax.dynamic_update_slice(
+        packets[final], jnp.where(is_two, lent_cross, own_cross), (0, 0)
+    )
 
     def factor_of(cross):
         return jnp.concatenate(halves(exact_dot(cross.astype(F32), inverse_one)), 0)
@@ -278,15 +279,18 @@
         )
         return jnp.concatenate([solved_two, tail.astype(BF16)], 1)
 
-    one_owner, two_owner = col_count - 2, col_count - 1
-    early_two = lax.ppermute(whole, "col", [(two_owner, one_owner)])
-    first, arrived = spread(packets, full_one)
+    early_two = [
+        lax.ppermute(packet, "col", [(two_owner, one_owner)]) for packet in packets
+    ]
+    first, arrived = spread(packets, early_two[0])
+    full_one = gather_rest(after(near_one, first[0]))
     early_one = lax.ppermute(after(whole, first[0]), "col", [(one_owner, two_owner)])
     at_top = level == top
     own = [jnp.where(at_top, a, b) for a, b in zip(packets, arrived)]
     other = [pair_swap(value, range(levels - 1)) for value in arrived]
     full_both = jnp.concatenate([full_two, after(full_one, arrived[0])], 0)
 
+    early_two = jnp.concatenate([piece[panel:] for piece in early_two], 0)
     early_two = after(early_two, arrived[final], other[0])
     top_both = panels_of(whole, early_two, factor_of(own_cross), height)
     terms = wide_dot(top_both.T, trail[:, last:])
@@ -312,12 +316,11 @@
         step *= 2
     terms = terms.astype(BF16)
 
-    whole_other = jnp.where(is_two, early_one, early_two)
+    whole_other = jnp.where(is_two, after(early_one, own_terms), early_two)
     for k, (start, stop) in enumerate(cuts):
-        piece = whole_other[(0 if k == 0 else panel + start) : panel + stop]
-        low = other[k][-piece.shape[0] :]
-        other[k] = jnp.where(at_top, piece, after(low, own_terms))
-    cross = jnp.where(is_two, other[0][:panel], own[0][:panel])
+        low = after(other[k][panel:], own_terms, *other[:k])
+        other[k] = jnp.where(at_top, whole_other[start:stop], low)
+    cross = own[final][:panel]
     factor = factor_of(cross)
     column = lax.broadcasted_iota(jnp.int32, (1, width), 1)
     in_block = column >= last
@@ -368,7 +371,7 @@
     grad_trail = updated(after(both, sent), start, grad_trail)
 
     grad_diag_two = block_adjoint(
-        diag_two, inverse_two, jnp.tril(adj_diag_two - after(diag_term_two, sums))
+        diag_two, inverse_two, jnp.tril(adj_diag_two - diag_term_two)
     )
     mirror_two = grad_diag_two + grad_diag_two.T
     adj_two = -crossing - exact_dot(mirror_two, cross.astype(F32))

time: 76.8 us -> 77.4 us (level)
  the two profiles are of different devices: /device:TPU:0 before, /device:TPU:20 now
where the time goes in v8:
time: 77.4 us; the launch traced here: 77 us
  waiting for transfers between devices  35.2 us (45%)
  starting transfers between devices  20.5 us (26%)
  matrix products  9.41 us (12%)
  Pallas kernels  4.61 us (6%)
  other arithmetic  2.94 us (4%)
  local copies, waits for them, and re-layouts  2.66 us (3%)
  between operations  1.69 us (2%)
    ppermute x8, waiting for transfers between devices, hop(): return lax.ppermute(value, 'col', pairs)  26.6 us
    ppermute x8, starting transfers between devices, hop(): return lax.ppermute(value, 'col', pairs)  7.51 us
    dot_general x10, matrix products, wide_dot(): return jnp.dot(a, b, preferred_element_type=F32)  7.11 us
    ppermute x6, waiting for transfers between devices, row_swap(): return lax.ppermute(value, 'row', [(i, i ^ step) for i in range(row_count)])  5.73 us
    pallas_call x1, Pallas kernels, prepare(): pl.pallas_call(functools.partial(prepare_kernel, cuts), in_specs=[pl.Bloc...  4.61 us
    ppermute x6, starting transfers between devices, row_swap(): return lax.ppermute(value, 'row', [(i, i ^ step) for i in range(row_count)])  4.35 us
    ppermute x3, starting transfers between devices, pair_swap(): return lax.ppermute(value, 'col', pairs)  4.18 us
    ppermute x3, waiting for transfers between devices, pair_swap(): return lax.ppermute(value, 'col', pairs)  2.8 us
  transfers between devices with their start and end apart: 23, of which 8 were waited for; matrix products, arithmetic and copies ran while one was open for 15% of the time, Pallas kernels for 0%

profile of v8, /device:TPU:20, one launch (start us, length us, event | category | flops | bytes accessed | tf_op | source)
XLA Modules:
  0.0 77.0 jit_solution(4946756801736137677)
XLA Ops:
  0.7 4.6 %prepare.1 = (f32[128,128]{1,0:T(8,128)}, f32[128,128]{1,0:T(8,128)}, bf16[2048,128]{1,0:T(8,128)(2,1)}, bf16[1152,128]{1,0:T(8,128)(2,1)}, bf16[1152,128]{1,0:T(8,128)(2,1)}) custom-call(s32[1]{0:T(128)} %bitcast.side_ref, f32[128,128]{1,0:T(8,128)} %one_ref.1, f32[128,128]{1,0:T(8,128)} %two_ref.1, f32[2048,1024]{1,0:T(8,128)} %adj_ref.1), custom_call_target="tpu_custom_call" | custom-call | flops 268435456 | bytes 2097152 | tf_op jit(solution)/shard_map/prepare/pallas_call | solution.py:107
  5.3 0.8 %collective-permute-start.1 = (bf16[1152,128]{1,0:T(8,128)(2,1)}, bf16[1152,128]{1,0:T(8,128)(2,1)S(1)}, u32[]{:S(2)}, u32[]{:S(2)}) collective-permute-start(bf16[1152,128]{1,0:T(8,128)(2,1)} %get-tuple-element.26), channel_id=1, source_target_pairs={{7,6},{15,14},{23,22},{31,30}} | collective-permute-start | bytes 884744 | tf_op jit(solution)/shard_map/ppermute | solution.py:283
  8.2 1.6 %collective-permute-start.4 = (bf16[1,2,32,1024]{3,2,1,0:T(8,128)(2,1)S(1)}, bf16[1,2,32,1024]{3,2,1,0:T(8,128)(2,1)S(1)}, u32[]{:S(2)}, u32[]{:S(2)}) collective-permute-start(bf16[1,2,32,1024]{3,2,1,0:T(8,128)(2,1)S(1)} %pad_maximum_fusion.18), channel_id=1, source_target_pairs={{0,16},{8,24},{16,0},{24,8},{1,17},{9,25},{17,1},{25,9},{2,18},{10... | collective-permute-start | bytes 393224 | tf_op jit(solution)/shard_map/ppermute | solution.py:180
  9.8 4.0 %collective-permute-done.4 = bf16[1,2,32,1024]{3,2,1,0:T(8,128)(2,1)S(1)} collective-permute-done((bf16[1,2,32,1024]{3,2,1,0:T(8,128)(2,1)S(1)}, bf16[1,2,32,1024]{3,2,1,0:T(8,128)(2,1)S(1)}, u32[]{:S(2)}, u32[]{:S(2)}) %collective-permute-start.4) | collective-permute-done | bytes 131104 | tf_op jit(solution)/shard_map/ppermute | solution.py:180
  15.5 1.6 %collective-permute-start.13 = (bf16[1,2,32,1024]{3,2,1,0:T(8,128)(2,1)S(1)}, bf16[1,2,32,1024]{3,2,1,0:T(8,128)(2,1)S(1)}, u32[]{:S(2)}, u32[]{:S(2)}) collective-permute-start(bf16[1,2,32,1024]{3,2,1,0:T(8,128)(2,1)S(1)} %pad_maximum_fusion.19), channel_id=1, source_target_pairs={{0,16},{8,24},{16,0},{24,8},{1,17},{9,25},{17,1},{25,9},{2,18},{10... | collective-permute-start | bytes 393224 | tf_op jit(solution)/shard_map/ppermute | solution.py:180
  17.1 1.3 %collective-permute-start.9 = (bf16[1152,128]{1,0:T(8,128)(2,1)S(1)}, bf16[1152,128]{1,0:T(8,128)(2,1)S(1)}, u32[]{:S(2)}, u32[]{:S(2)}) collective-permute-start(bf16[1152,128]{1,0:T(8,128)(2,1)S(1)} %collective-permute-done), channel_id=1, source_target_pairs={{2,4},{3,5},{10,12},{11,13},{18,20},{19,21},{26,28},{27,29}} | collective-permute-start | bytes 884744 | tf_op jit(solution)/shard_map/ppermute | solution.py:217
  19.8 0.7 collective-permute-done.13
  20.7 0.8 %collective-permute-start.10 = (bf16[1152,128]{1,0:T(8,128)(2,1)S(1)}, bf16[1152,128]{1,0:T(8,128)(2,1)S(1)}, u32[]{:S(2)}, u32[]{:S(2)}) collective-permute-start(bf16[1152,128]{1,0:T(8,128)(2,1)S(1)} %collective-permute-done.7), channel_id=1, source_target_pairs={{2,0},{3,1},{10,8},{11,9},{18,16},{19,17},{26,24},{27,25}} | collective-permute-start | bytes 884744 | tf_op jit(solution)/shard_map/ppermute | solution.py:217
  21.5 1.4 %collective-permute-start.8 = (bf16[1152,128]{1,0:T(8,128)(2,1)S(1)}, bf16[1152,128]{1,0:T(8,128)(2,1)S(1)}, u32[]{:S(2)}, u32[]{:S(2)}) collective-permute-start(bf16[1152,128]{1,0:T(8,128)(2,1)S(1)} %collective-permute-done.7), channel_id=1, source_target_pairs={{2,4},{3,5},{10,12},{11,13},{18,20},{19,21},{26,28},{27,29}} | collective-permute-start | bytes 884744 | tf_op jit(solution)/shard_map/ppermute | solution.py:217
  23.0 4.8 %collective-permute-done.9 = bf16[1152,128]{1,0:T(8,128)(2,1)S(1)} collective-permute-done((bf16[1152,128]{1,0:T(8,128)(2,1)S(1)}, bf16[1152,128]{1,0:T(8,128)(2,1)S(1)}, u32[]{:S(2)}, u32[]{:S(2)}) %collective-permute-start.9) | collective-permute-done | bytes 294944 | tf_op jit(solution)/shard_map/ppermute | solution.py:217
  27.8 1.9 %collective-permute-start.11 = (bf16[1152,128]{1,0:T(8,128)(2,1)S(1)}, bf16[1152,128]{1,0:T(8,128)(2,1)S(1)}, u32[]{:S(2)}, u32[]{:S(2)}) collective-permute-start(bf16[1152,128]{1,0:T(8,128)(2,1)S(1)} %select_select_fusion.1), channel_id=1, source_target_pairs={{0,1},{1,0},{2,3},{3,2},{4,5},{5,4},{8,9},{9,8},{10,11},{11,10},{1... | collective-permute-start | bytes 884744 | tf_op jit(solution)/shard_map/ppermute | solution.py:184
  29.8 12.9 %collective-permute-done.8 = bf16[1152,128]{1,0:T(8,128)(2,1)S(1)} collective-permute-done((bf16[1152,128]{1,0:T(8,128)(2,1)S(1)}, bf16[1152,128]{1,0:T(8,128)(2,1)S(1)}, u32[]{:S(2)}, u32[]{:S(2)}) %collective-permute-start.8) | collective-permute-done | bytes 294944 | tf_op jit(solution)/shard_map/ppermute | solution.py:217
  42.8 2.2 %collective-permute-start.14 = (bf16[1152,128]{1,0:T(8,128)(2,1)S(1)}, bf16[1152,128]{1,0:T(8,128)(2,1)S(1)}, u32[]{:S(2)}, u32[]{:S(2)}) collective-permute-start(bf16[1152,128]{1,0:T(8,128)(2,1)S(1)} %get-tuple-element.52), channel_id=1, source_target_pairs={{0,1},{1,0},{2,3},{3,2},{4,5},{5,4},{8,9},{9,8},{10,11},{11,10},{1... | collective-permute-start | bytes 884744 | tf_op jit(solution)/shard_map/ppermute | solution.py:184
  46.0 0.8 %collective-permute-start.15 = (f32[256,128]{1,0:T(8,128)S(1)}, f32[256,128]{1,0:T(8,128)S(1)}, u32[]{:S(2)}, u32[]{:S(2)}) collective-permute-start(f32[256,128]{1,0:T(8,128)S(1)} %convolution_subtract_fusion.2), channel_id=1, source_target_pairs={{6,14},{7,15},{14,6},{15,7},{22,30},{23,31},{30,22},{31,23}} | collective-permute-start | bytes 393224 | tf_op jit(solution)/shard_map/ppermute | solution.py:314
  47.5 0.8 %collective-permute-start.16 = (bf16[256,128]{1,0:T(8,128)(2,1)S(1)}, bf16[256,128]{1,0:T(8,128)(2,1)S(1)}, u32[]{:S(2)}, u32[]{:S(2)}) collective-permute-start(bf16[256,128]{1,0:T(8,128)(2,1)S(1)} %add_convert_fusion.1), channel_id=1, source_target_pairs={{6,22},{7,23},{14,30},{15,31},{22,6},{23,7},{30,14},{31,15}} | collective-permute-start | bytes 196616 | tf_op jit(solution)/shard_map/ppermute | solution.py:314
  49.0 0.7 select_dynamic-update-slice_fusion.1
  51.1 1.3 %collective-permute-start.17 = (bf16[256,128]{1,0:T(8,128)(2,1)S(1)}, bf16[256,128]{1,0:T(8,128)(2,1)S(1)}, u32[]{:S(2)}, u32[]{:S(2)}) collective-permute-start(bf16[256,128]{1,0:T(8,128)(2,1)S(1)} %add_convert_fusion), channel_id=1, source_target_pairs={{6,4},{7,5},{14,12},{15,13},{22,20},{23,21},{30,28},{31,29}} | collective-permute-start | bytes 196616 | tf_op jit(solution)/shard_map/ppermute | solution.py:217
  52.4 0.7 fusion.2
  53.2 8.9 %collective-permute-done.17 = bf16[256,128]{1,0:T(8,128)(2,1)S(1)} collective-permute-done((bf16[256,128]{1,0:T(8,128)(2,1)S(1)}, bf16[256,128]{1,0:T(8,128)(2,1)S(1)}, u32[]{:S(2)}, u32[]{:S(2)}) %collective-permute-start.17) | collective-permute-done | bytes 65568 | tf_op jit(solution)/shard_map/ppermute | solution.py:217
  62.6 0.7 fusion.7
  63.6 2.8 %collective-permute-done.21 = bf16[256,128]{1,0:T(8,128)(2,1)S(1)} collective-permute-done((bf16[256,128]{1,0:T(8,128)(2,1)S(1)}, bf16[256,128]{1,0:T(8,128)(2,1)S(1)}, u32[]{:S(2)}, u32[]{:S(2)}) %collective-permute-start.21) | collective-permute-done | bytes 65568 | tf_op jit(solution)/shard_map/ppermute | solution.py:184
  70.9 1.0 %copy-done.3 = bf16[2048,1024]{1,0:T(8,128)(2,1)S(1)} copy-done((bf16[2048,1024]{1,0:T(8,128)(2,1)S(1)}, bf16[2048,1024]{1,0:T(8,128)(2,1)}, u32[]{:S(2)}) %copy-start.3) | copy-done | bytes 4194328
  71.9 2.9 %select_dynamic-update-slice_fusion = bf16[2048,1024]{1,0:T(8,128)(2,1)S(1)} fusion(bf16[2048,1024]{1,0:T(8,128)(2,1)S(1)} %copy-done.3, bf16[1024,128]{1,0:T(8,128)(2,1)S(1)} %slice_select_fusion.3, pred[1024]{0:T(1024)(128)(4,1)S(1)} %fusion.75, bf16[1024,256]{1,0:T(8,128)(2,1)S(1)} %pad_maximum_fusion.7, f32[2048,1024]{1,0:T(8,128)} %adj_ref.1, ...), kind=kOutput, calls=%fused_computation.2 | convolution fusion | flops 541065216 | bytes 7603200 | tf_op jit(solution)/shard_map/dot_general | solution.py:21
  75.3 1.2 %fusion.31 = (f32[32,1024]{1,0:T(8,128)}, f32[32,1024]{1,0:T(8,128)}) fusion(f32[2,1,32,1024]{3,2,1,0:T(8,128)S(1)} %bitcast_add_fusion, f32[32,1024]{1,0:T(8,128)S(1)} %copy-done.12, f32[64,1024]{1,0:T(8,128)S(1)} %fusion.17, f32[32,128]{1,0:T(8,128)S(1)} %get-tuple-element.45, pred[1024]{0:T(1024)(128)(4,1)S(1)} %fusion.75, f32[32,1024]{1,0:T(8,128)S(1)} %copy-done.13, ...), kind=kLoop, calls=%fused_computation.67 | loop fusion | flops 196608 | bytes 1070080 | tf_op jit(solution)/shard_map/jit(_where)/select_n | solution.py:331
  (138 shorter events, 14.7 us)
Async XLA Ops:
  5.3 10.2 %collective-permute-start.1 = (bf16[1152,128]{1,0:T(8,128)(2,1)}, bf16[1152,128]{1,0:T(8,128)(2,1)S(1)}, u32[]{:S(2)}, u32[]{:S(2)}) collective-permute-start(bf16[1152,128]{1,0:T(8,128)(2,1)} %get-tuple-element.26), channel_id=1, source_target_pairs={{7,6},{15,14},{23,22},{31,30}} | collective-permute-start | bytes 884744 | tf_op jit(solution)/shard_map/ppermute | solution.py:283
  6.1 9.4 %collective-permute-start = (bf16[1152,128]{1,0:T(8,128)(2,1)}, bf16[1152,128]{1,0:T(8,128)(2,1)S(1)}, u32[]{:S(2)}, u32[]{:S(2)}) collective-permute-start(bf16[1152,128]{1,0:T(8,128)(2,1)} %get-tuple-element.26), channel_id=1, source_target_pairs={{6,2},{7,3},{14,10},{15,11},{22,18},{23,19},{30,26},{31,27}} | collective-permute-start | bytes 884744 | tf_op jit(solution)/shard_map/ppermute | solution.py:217
  6.8 1.3 %collective-permute-start.3 = (bf16[1,1,32,1024]{3,2,1,0:T(8,128)(2,1)S(1)}, bf16[1,1,32,1024]{3,2,1,0:T(8,128)(2,1)S(1)}, u32[]{:S(2)}, u32[]{:S(2)}) collective-permute-start(bf16[1,1,32,1024]{3,2,1,0:T(8,128)(2,1)S(1)} %bitcast.79), channel_id=1, source_target_pairs={{0,8},{8,0},{16,24},{24,16},{1,9},{9,1},{17,25},{25,17},{2,10},{10... | collective-permute-start | bytes 196616 | tf_op jit(solution)/shard_map/ppermute | solution.py:180
  6.9 2.8 %collective-permute-start.12 = (bf16[1,1,32,1024]{3,2,1,0:T(8,128)(2,1)S(1)}, bf16[1,1,32,1024]{3,2,1,0:T(8,128)(2,1)S(1)}, u32[]{:S(2)}, u32[]{:S(2)}) collective-permute-start(bf16[1,1,32,1024]{3,2,1,0:T(8,128)(2,1)S(1)} %bitcast.80), channel_id=1, source_target_pairs={{0,8},{8,0},{16,24},{24,16},{1,9},{9,1},{17,25},{25,17},{2,10},{10... | collective-permute-start | bytes 196616 | tf_op jit(solution)/shard_map/ppermute | solution.py:180
  8.2 5.6 %collective-permute-start.4 = (bf16[1,2,32,1024]{3,2,1,0:T(8,128)(2,1)S(1)}, bf16[1,2,32,1024]{3,2,1,0:T(8,128)(2,1)S(1)}, u32[]{:S(2)}, u32[]{:S(2)}) collective-permute-start(bf16[1,2,32,1024]{3,2,1,0:T(8,128)(2,1)S(1)} %pad_maximum_fusion.18), channel_id=1, source_target_pairs={{0,16},{8,24},{16,0},{24,8},{1,17},{9,25},{17,1},{25,9},{2,18},{10... | collective-permute-start | bytes 393224 | tf_op jit(solution)/shard_map/ppermute | solution.py:180
  13.9 0.9 %collective-permute-start.5 = (bf16[128,128]{1,0:T(8,128)(2,1)S(1)}, bf16[128,128]{1,0:T(8,128)(2,1)S(1)}, u32[]{:S(2)}, u32[]{:S(2)}) collective-permute-start(bf16[128,128]{1,0:T(8,128)(2,1)S(1)} %slice.131), channel_id=1, source_target_pairs={{6,7},{14,15},{22,23},{30,31}} | collective-permute-start | bytes 98312 | tf_op jit(solution)/shard_map/ppermute | solution.py:266
  14.8 5.8 %collective-permute-start.6 = (bf16[1152,128]{1,0:T(8,128)(2,1)S(1)}, bf16[1152,128]{1,0:T(8,128)(2,1)S(1)}, u32[]{:S(2)}, u32[]{:S(2)}) collective-permute-start(bf16[1152,128]{1,0:T(8,128)(2,1)S(1)} %select_dynamic-update-slice_fusion.2), channel_id=1, source_target_pairs={{7,6},{15,14},{23,22},{31,30}} | collective-permute-start | bytes 884744 | tf_op jit(solution)/shard_map/ppermute | solution.py:283
  15.5 5.0 %collective-permute-start.13 = (bf16[1,2,32,1024]{3,2,1,0:T(8,128)(2,1)S(1)}, bf16[1,2,32,1024]{3,2,1,0:T(8,128)(2,1)S(1)}, u32[]{:S(2)}, u32[]{:S(2)}) collective-permute-start(bf16[1,2,32,1024]{3,2,1,0:T(8,128)(2,1)S(1)} %pad_maximum_fusion.19), channel_id=1, source_target_pairs={{0,16},{8,24},{16,0},{24,8},{1,17},{9,25},{17,1},{25,9},{2,18},{10... | collective-permute-start | bytes 393224 | tf_op jit(solution)/shard_map/ppermute | solution.py:180
  17.1 10.7 %collective-permute-start.9 = (bf16[1152,128]{1,0:T(8,128)(2,1)S(1)}, bf16[1152,128]{1,0:T(8,128)(2,1)S(1)}, u32[]{:S(2)}, u32[]{:S(2)}) collective-permute-start(bf16[1152,128]{1,0:T(8,128)(2,1)S(1)} %collective-permute-done), channel_id=1, source_target_pairs={{2,4},{3,5},{10,12},{11,13},{18,20},{19,21},{26,28},{27,29}} | collective-permute-start | bytes 884744 | tf_op jit(solution)/shard_map/ppermute | solution.py:217
  18.4 2.3 %collective-permute-start.7 = (bf16[1152,128]{1,0:T(8,128)(2,1)S(1)}, bf16[1152,128]{1,0:T(8,128)(2,1)S(1)}, u32[]{:S(2)}, u32[]{:S(2)}) collective-permute-start(bf16[1152,128]{1,0:T(8,128)(2,1)S(1)} %broadcast_select_fusion.3), channel_id=1, source_target_pairs={{6,2},{7,3},{2,0},{3,1},{14,10},{15,11},{10,8},{11,9},{22,18},{23,... | collective-permute-start | bytes 884744 | tf_op jit(solution)/shard_map/ppermute | solution.py:217
  19.1 27.9 %collective-permute-start.2 = (bf16[2048,128]{1,0:T(8,128)(2,1)S(1)}, bf16[2048,128]{1,0:T(8,128)(2,1)S(1)}, u32[]{:S(2)}, u32[]{:S(2)}) collective-permute-start(bf16[2048,128]{1,0:T(8,128)(2,1)S(1)} %copy-done.7), channel_id=1, source_target_pairs={{6,7},{14,15},{22,23},{30,31}} | collective-permute-start | bytes 1572872 | tf_op jit(solution)/shard_map/ppermute | solution.py:287
  20.7 24.8 %copy-start = (bf16[2048,1024]{1,0:T(8,128)(2,1)S(1)}, bf16[2048,1024]{1,0:T(8,128)(2,1)}, u32[]{:S(2)}) copy-start(bf16[2048,1024]{1,0:T(8,128)(2,1)} %param.10) | copy-start | bytes 12582916
  20.7 9.1 %collective-permute-start.10 = (bf16[1152,128]{1,0:T(8,128)(2,1)S(1)}, bf16[1152,128]{1,0:T(8,128)(2,1)S(1)}, u32[]{:S(2)}, u32[]{:S(2)}) collective-permute-start(bf16[1152,128]{1,0:T(8,128)(2,1)S(1)} %collective-permute-done.7), channel_id=1, source_target_pairs={{2,0},{3,1},{10,8},{11,9},{18,16},{19,17},{26,24},{27,25}} | collective-permute-start | bytes 884744 | tf_op jit(solution)/shard_map/ppermute | solution.py:217
  21.5 21.2 %collective-permute-start.8 = (bf16[1152,128]{1,0:T(8,128)(2,1)S(1)}, bf16[1152,128]{1,0:T(8,128)(2,1)S(1)}, u32[]{:S(2)}, u32[]{:S(2)}) collective-permute-start(bf16[1152,128]{1,0:T(8,128)(2,1)S(1)} %collective-permute-done.7), channel_id=1, source_target_pairs={{2,4},{3,5},{10,12},{11,13},{18,20},{19,21},{26,28},{27,29}} | collective-permute-start | bytes 884744 | tf_op jit(solution)/shard_map/ppermute | solution.py:217
  27.8 17.1 %collective-permute-start.11 = (bf16[1152,128]{1,0:T(8,128)(2,1)S(1)}, bf16[1152,128]{1,0:T(8,128)(2,1)S(1)}, u32[]{:S(2)}, u32[]{:S(2)}) collective-permute-start(bf16[1152,128]{1,0:T(8,128)(2,1)S(1)} %select_select_fusion.1), channel_id=1, source_target_pairs={{0,1},{1,0},{2,3},{3,2},{4,5},{5,4},{8,9},{9,8},{10,11},{11,10},{1... | collective-permute-start | bytes 884744 | tf_op jit(solution)/shard_map/ppermute | solution.py:184
  42.8 19.4 %collective-permute-start.14 = (bf16[1152,128]{1,0:T(8,128)(2,1)S(1)}, bf16[1152,128]{1,0:T(8,128)(2,1)S(1)}, u32[]{:S(2)}, u32[]{:S(2)}) collective-permute-start(bf16[1152,128]{1,0:T(8,128)(2,1)S(1)} %get-tuple-element.52), channel_id=1, source_target_pairs={{0,1},{1,0},{2,3},{3,2},{4,5},{5,4},{8,9},{9,8},{10,11},{11,10},{1... | collective-permute-start | bytes 884744 | tf_op jit(solution)/shard_map/ppermute | solution.py:184
  46.0 1.5 %collective-permute-start.15 = (f32[256,128]{1,0:T(8,128)S(1)}, f32[256,128]{1,0:T(8,128)S(1)}, u32[]{:S(2)}, u32[]{:S(2)}) collective-permute-start(f32[256,128]{1,0:T(8,128)S(1)} %convolution_subtract_fusion.2), channel_id=1, source_target_pairs={{6,14},{7,15},{14,6},{15,7},{22,30},{23,31},{30,22},{31,23}} | collective-permute-start | bytes 393224 | tf_op jit(solution)/shard_map/ppermute | solution.py:314
  47.5 2.2 %collective-permute-start.16 = (bf16[256,128]{1,0:T(8,128)(2,1)S(1)}, bf16[256,128]{1,0:T(8,128)(2,1)S(1)}, u32[]{:S(2)}, u32[]{:S(2)}) collective-permute-start(bf16[256,128]{1,0:T(8,128)(2,1)S(1)} %add_convert_fusion.1), channel_id=1, source_target_pairs={{6,22},{7,23},{14,30},{15,31},{22,6},{23,7},{30,14},{31,15}} | collective-permute-start | bytes 196616 | tf_op jit(solution)/shard_map/ppermute | solution.py:314
  49.8 3.4 %collective-permute-start.19 = (bf16[256,128]{1,0:T(8,128)(2,1)S(1)}, bf16[256,128]{1,0:T(8,128)(2,1)S(1)}, u32[]{:S(2)}, u32[]{:S(2)}) collective-permute-start(bf16[256,128]{1,0:T(8,128)(2,1)S(1)} %add_convert_fusion), channel_id=1, source_target_pairs={{6,0},{7,1},{14,8},{15,9},{22,16},{23,17},{30,24},{31,25}} | collective-permute-start | bytes 196616 | tf_op jit(solution)/shard_map/ppermute | solution.py:217
  50.5 2.7 %collective-permute-start.18 = (bf16[256,128]{1,0:T(8,128)(2,1)S(1)}, bf16[256,128]{1,0:T(8,128)(2,1)S(1)}, u32[]{:S(2)}, u32[]{:S(2)}) collective-permute-start(bf16[256,128]{1,0:T(8,128)(2,1)S(1)} %add_convert_fusion), channel_id=1, source_target_pairs={{6,2},{7,3},{14,10},{15,11},{22,18},{23,19},{30,26},{31,27}} | collective-permute-start | bytes 196616 | tf_op jit(solution)/shard_map/ppermute | solution.py:217
  51.1 10.9 %collective-permute-start.17 = (bf16[256,128]{1,0:T(8,128)(2,1)S(1)}, bf16[256,128]{1,0:T(8,128)(2,1)S(1)}, u32[]{:S(2)}, u32[]{:S(2)}) collective-permute-start(bf16[256,128]{1,0:T(8,128)(2,1)S(1)} %add_convert_fusion), channel_id=1, source_target_pairs={{6,4},{7,5},{14,12},{15,13},{22,20},{23,21},{30,28},{31,29}} | collective-permute-start | bytes 196616 | tf_op jit(solution)/shard_map/ppermute | solution.py:217
  62.1 4.3 %collective-permute-start.21 = (bf16[256,128]{1,0:T(8,128)(2,1)S(1)}, bf16[256,128]{1,0:T(8,128)(2,1)S(1)}, u32[]{:S(2)}, u32[]{:S(2)}) collective-permute-start(bf16[256,128]{1,0:T(8,128)(2,1)S(1)} %get-tuple-element.44), channel_id=1, source_target_pairs={{0,1},{1,0},{2,3},{3,2},{4,5},{5,4},{6,7},{7,6},{8,9},{9,8},{10,11... | collective-permute-start | bytes 196616 | tf_op jit(solution)/shard_map/ppermute | solution.py:184
  63.5 6.6 %collective-permute-start.20 = (bf16[2,2,32,1024]{3,2,0,1:T(8,128)(2,1)S(1)}, bf16[2,2,32,1024]{3,2,0,1:T(8,128)(2,1)S(1)}, u32[]{:S(2)}, u32[]{:S(2)}) collective-permute-start(bf16[2,2,32,1024]{3,2,0,1:T(8,128)(2,1)S(1)} %select_bitcast_fusion), channel_id=1, source_target_pairs={{0,8},{8,0},{16,24},{24,16},{1,9},{9,1},{17,25},{25,17},{2,10},{10... | collective-permute-start | bytes 786440 | tf_op jit(solution)/shard_map/ppermute | solution.py:180
  70.2 5.0 %collective-permute-start.22 = (bf16[2,1,32,1024]{3,2,1,0:T(8,128)(2,1)S(1)}, bf16[2,1,32,1024]{3,2,1,0:T(8,128)(2,1)S(1)}, u32[]{:S(2)}, u32[]{:S(2)}) collective-permute-start(bf16[2,1,32,1024]{3,2,1,0:T(8,128)(2,1)S(1)} %fusion.29), channel_id=1, source_target_pairs={{0,16},{8,24},{16,0},{24,8},{1,17},{9,25},{17,1},{25,9},{2,18},{10... | collective-permute-start | bytes 393224 | tf_op jit(solution)/shard_map/ppermute | solution.py:180
  (20 other events, 132.5 us)

commit v9 on v8

--- a/solution.py
+++ b/solution.py
@@ -216,9 +216,10 @@
         pairs = [(2 * a + s, 2 * b + s) for a, b in hops for s in range(2)]
         return lax.ppermute(value, "col", pairs)
 
-    def spread(pieces, gate):
+    def spread(pieces, gates, extra):
         middle, span = levels // 2 - 1, levels // 4
         first, down = [], []
+        extra_moved = hop(extra, [(top, middle)])
         for k in range(len(pieces) + 1):
             if k == 0:
                 operand, hops = pieces[0], [(top, middle)]
@@ -231,7 +232,10 @@
             if k > 0:
                 down.append(moved)
             if k < len(pieces):
-                first.append(after(moved, gate) if k == 0 else moved)
+                moved = after(moved, gates[k]) if k < len(gates) else moved
+                if k == len(pieces) - 1:
+                    moved = lax.dynamic_update_slice(moved, extra_moved, (0, 0))
+                first.append(moved)
         held = [
             {middle: here, middle - span: low, middle + span: hop(here, [(middle, middle + span)])}
             for here, low in zip(first, down)
@@ -264,9 +268,7 @@
     own_cross = full_two[:, last:]
     one_owner, two_owner = col_count - 2, col_count - 1
     lent_cross = lax.ppermute(own_cross, "col", [(one_owner, two_owner)])
-    packets[final] = lax.dynamic_update_slice(
-        packets[final], jnp.where(is_two, lent_cross, own_cross), (0, 0)
-    )
+    side_cross = jnp.where(is_two, lent_cross, own_cross)
 
     def factor_of(cross):
         return jnp.concatenate(halves(exact_dot(cross.astype(F32), inverse_one)), 0)
@@ -282,8 +284,8 @@
     early_two = [
         lax.ppermute(packet, "col", [(two_owner, one_owner)]) for packet in packets
     ]
-    first, arrived = spread(packets, early_two[0])
-    full_one = gather_rest(after(near_one, first[0]))
+    full_one = gather_rest(after(near_one, full_two))
+    first, arrived = spread(packets, [early_two[0], full_one], side_cross)
     early_one = lax.ppermute(after(whole, first[0]), "col", [(one_owner, two_owner)])
     at_top = level == top
     own = [jnp.where(at_top, a, b) for a, b in zip(packets, arrived)]
@@ -315,12 +317,13 @@
         terms = terms.astype(F32) + moved.astype(F32)
         step *= 2
     terms = terms.astype(BF16)
+    terms_other = pair_swap(terms, [top])
 
     whole_other = jnp.where(is_two, after(early_one, own_terms), early_two)
     for k, (start, stop) in enumerate(cuts):
         low = after(other[k][panel:], own_terms, *other[:k])
         other[k] = jnp.where(at_top, whole_other[start:stop], low)
-    cross = own[final][:panel]
+    cross = jnp.where(at_top, side_cross, own[final][:panel])
     factor = factor_of(cross)
     column = lax.broadcasted_iota(jnp.int32, (1, width), 1)
     in_block = column >= last
@@ -342,14 +345,15 @@
         both = panels_of(mine, theirs, factor, stop - start)
         sums = sums + wide_dot(both.T, trail[start:stop])
         grad_trail = updated(both, start, grad_trail)
+    diag_term_two = jnp.where(is_two, terms, terms_other)[:panel]
+    terms = jnp.concatenate([diag_term_two, jnp.where(is_two, terms_other, terms)], 0)
     terms = choose(
         [([top], terms)] + [([k], hop(terms, [(top, k)])) for k in range(levels - 1)]
     )
-    terms_other = pair_swap(after(terms, sums), range(levels))
-    terms, terms_other = terms.astype(F32), terms_other.astype(F32)
-    diag_term_two = jnp.where(is_two, terms[:panel], terms_other[:panel])
-    crossing = jnp.where(is_two, terms_other[:panel], terms[:panel])
-    diag_term_one = jnp.where(is_two, terms_other[panel:], terms[panel:])
+    whole_terms = terms.astype(F32)
+    diag_term_two = whole_terms[:panel]
+    crossing = whole_terms[panel : 2 * panel]
+    diag_term_one = whole_terms[2 * panel :]
 
     start, stop = cuts[-1]
     theirs = after(other[-1], terms, sums)
@@ -371,7 +375,7 @@
     grad_trail = updated(after(both, sent), start, grad_trail)
 
     grad_diag_two = block_adjoint(
-        diag_two, inverse_two, jnp.tril(adj_diag_two - diag_term_two)
+        diag_two, inverse_two, jnp.tril(adj_diag_two - after(diag_term_two, sums))
     )
     mirror_two = grad_diag_two + grad_diag_two.T
     adj_two = -crossing - exact_dot(mirror_two, cross.astype(F32))

time: 77.4 us -> 76.5 us (0.988)
  the two profiles are of different devices: /device:TPU:20 before, /device:TPU:21 now
where the time goes in v9:
time: 76.5 us; the launch traced here: 76.1 us
  starting transfers between devices  30.8 us (40%)
  waiting for transfers between devices  25 us (33%)
  matrix products  9.45 us (12%)
  Pallas kernels  4.61 us (6%)
  other arithmetic  3.08 us (4%)
  between operations  1.72 us (2%)
  local copies, waits for them, and re-layouts  1.52 us (2%)
    ppermute x9, waiting for transfers between devices, hop(): return lax.ppermute(value, 'col', pairs)  19.6 us
    ppermute x6, starting transfers between devices, row_swap(): return lax.ppermute(value, 'row', [(i, i ^ step) for i in range(row_count)])  11.9 us
    ppermute x9, starting transfers between devices, hop(): return lax.ppermute(value, 'col', pairs)  8.17 us
    dot_general x10, matrix products, wide_dot(): return jnp.dot(a, b, preferred_element_type=F32)  7.15 us
    ppermute x3, starting transfers between devices, pair_swap(): return lax.ppermute(value, 'col', pairs)  6.24 us
    ppermute x6, waiting for transfers between devices, row_swap(): return lax.ppermute(value, 'row', [(i, i ^ step) for i in range(row_count)])  5.31 us
    pallas_call x1, Pallas kernels, prepare(): pl.pallas_call(functools.partial(prepare_kernel, cuts), in_specs=[pl.Bloc...  4.61 us
    dot_general x10, matrix products, exact_dot(): return jnp.dot(a, b, precision=EXACT, preferred_element_type=F32)  2.3 us
  transfers between devices with their start and end apart: 24, of which 8 were waited for; matrix products, arithmetic and copies ran while one was open for 10% of the time, Pallas kernels for 0%

profile of v9, /device:TPU:21, one launch (start us, length us, event | category | flops | bytes accessed | tf_op | source)
XLA Modules:
  0.0 76.1 jit_solution(14308095671932037193)
XLA Ops:
  0.7 4.6 %prepare.1 = (f32[128,128]{1,0:T(8,128)}, f32[128,128]{1,0:T(8,128)}, bf16[2048,128]{1,0:T(8,128)(2,1)}, bf16[1152,128]{1,0:T(8,128)(2,1)}, bf16[1152,128]{1,0:T(8,128)(2,1)}) custom-call(s32[1]{0:T(128)} %bitcast.side_ref, f32[128,128]{1,0:T(8,128)} %one_ref.1, f32[128,128]{1,0:T(8,128)} %two_ref.1, f32[2048,1024]{1,0:T(8,128)} %adj_ref.1), custom_call_target="tpu_custom_call" | custom-call | flops 268435456 | bytes 2097152 | tf_op jit(solution)/shard_map/prepare/pallas_call | solution.py:107
  5.3 0.8 %collective-permute-start.1 = (bf16[1152,128]{1,0:T(8,128)(2,1)}, bf16[1152,128]{1,0:T(8,128)(2,1)S(1)}, u32[]{:S(2)}, u32[]{:S(2)}) collective-permute-start(bf16[1152,128]{1,0:T(8,128)(2,1)} %get-tuple-element.27), channel_id=1, source_target_pairs={{7,6},{15,14},{23,22},{31,30}} | collective-permute-start | bytes 884744 | tf_op jit(solution)/shard_map/ppermute | solution.py:285
  6.8 0.7 collective-permute-start.6
  8.9 1.3 %collective-permute-start.7 = (bf16[1,2,32,1024]{3,2,1,0:T(8,128)(2,1)S(1)}, bf16[1,2,32,1024]{3,2,1,0:T(8,128)(2,1)S(1)}, u32[]{:S(2)}, u32[]{:S(2)}) collective-permute-start(bf16[1,2,32,1024]{3,2,1,0:T(8,128)(2,1)S(1)} %pad_maximum_fusion.19), channel_id=1, source_target_pairs={{0,16},{8,24},{16,0},{24,8},{1,17},{9,25},{17,1},{25,9},{2,18},{10... | collective-permute-start | bytes 393224 | tf_op jit(solution)/shard_map/ppermute | solution.py:180
  10.2 3.7 %collective-permute-done.7 = bf16[1,2,32,1024]{3,2,1,0:T(8,128)(2,1)S(1)} collective-permute-done((bf16[1,2,32,1024]{3,2,1,0:T(8,128)(2,1)S(1)}, bf16[1,2,32,1024]{3,2,1,0:T(8,128)(2,1)S(1)}, u32[]{:S(2)}, u32[]{:S(2)}) %collective-permute-start.7) | collective-permute-done | bytes 131104 | tf_op jit(solution)/shard_map/ppermute | solution.py:180
  14.6 1.3 %collective-permute-start.8 = (bf16[1,2,32,1024]{3,2,1,0:T(8,128)(2,1)S(1)}, bf16[1,2,32,1024]{3,2,1,0:T(8,128)(2,1)S(1)}, u32[]{:S(2)}, u32[]{:S(2)}) collective-permute-start(bf16[1,2,32,1024]{3,2,1,0:T(8,128)(2,1)S(1)} %pad_maximum_fusion.18), channel_id=1, source_target_pairs={{0,16},{8,24},{16,0},{24,8},{1,17},{9,25},{17,1},{25,9},{2,18},{10... | collective-permute-start | bytes 393224 | tf_op jit(solution)/shard_map/ppermute | solution.py:180
  16.8 1.3 %collective-permute-start.12 = (bf16[1152,128]{1,0:T(8,128)(2,1)S(1)}, bf16[1152,128]{1,0:T(8,128)(2,1)S(1)}, u32[]{:S(2)}, u32[]{:S(2)}) collective-permute-start(bf16[1152,128]{1,0:T(8,128)(2,1)S(1)} %collective-permute-done), channel_id=1, source_target_pairs={{2,4},{3,5},{10,12},{11,13},{18,20},{19,21},{26,28},{27,29}} | collective-permute-start | bytes 884744 | tf_op jit(solution)/shard_map/ppermute | solution.py:217
  19.7 6.3 %collective-permute-done.12 = bf16[1152,128]{1,0:T(8,128)(2,1)S(1)} collective-permute-done((bf16[1152,128]{1,0:T(8,128)(2,1)S(1)}, bf16[1152,128]{1,0:T(8,128)(2,1)S(1)}, u32[]{:S(2)}, u32[]{:S(2)}) %collective-permute-start.12) | collective-permute-done | bytes 294944 | tf_op jit(solution)/shard_map/ppermute | solution.py:217
  26.1 0.8 %collective-permute-start.13 = (bf16[1152,128]{1,0:T(8,128)(2,1)S(1)}, bf16[1152,128]{1,0:T(8,128)(2,1)S(1)}, u32[]{:S(2)}, u32[]{:S(2)}) collective-permute-start(bf16[1152,128]{1,0:T(8,128)(2,1)S(1)} %constant_dynamic-update-slice_fusion), channel_id=1, source_target_pairs={{2,0},{3,1},{10,8},{11,9},{18,16},{19,17},{26,24},{27,25}} | collective-permute-start | bytes 884744 | tf_op jit(solution)/shard_map/ppermute | solution.py:217
  26.9 1.4 %collective-permute-start.11 = (bf16[1152,128]{1,0:T(8,128)(2,1)S(1)}, bf16[1152,128]{1,0:T(8,128)(2,1)S(1)}, u32[]{:S(2)}, u32[]{:S(2)}) collective-permute-start(bf16[1152,128]{1,0:T(8,128)(2,1)S(1)} %constant_dynamic-update-slice_fusion), channel_id=1, source_target_pairs={{2,4},{3,5},{10,12},{11,13},{18,20},{19,21},{26,28},{27,29}} | collective-permute-start | bytes 884744 | tf_op jit(solution)/shard_map/ppermute | solution.py:217
  28.4 2.1 %collective-permute-start.14 = (bf16[1152,128]{1,0:T(8,128)(2,1)S(1)}, bf16[1152,128]{1,0:T(8,128)(2,1)S(1)}, u32[]{:S(2)}, u32[]{:S(2)}) collective-permute-start(bf16[1152,128]{1,0:T(8,128)(2,1)S(1)} %select_select_fusion.1), channel_id=1, source_target_pairs={{0,1},{1,0},{2,3},{3,2},{4,5},{5,4},{8,9},{9,8},{10,11},{11,10},{1... | collective-permute-start | bytes 884744 | tf_op jit(solution)/shard_map/ppermute | solution.py:184
  30.6 8.5 %collective-permute-done.11 = bf16[1152,128]{1,0:T(8,128)(2,1)S(1)} collective-permute-done((bf16[1152,128]{1,0:T(8,128)(2,1)S(1)}, bf16[1152,128]{1,0:T(8,128)(2,1)S(1)}, u32[]{:S(2)}, u32[]{:S(2)}) %collective-permute-start.11) | collective-permute-done | bytes 294944 | tf_op jit(solution)/shard_map/ppermute | solution.py:217
  39.2 3.4 %collective-permute-start.15 = (bf16[1152,128]{1,0:T(8,128)(2,1)S(1)}, bf16[1152,128]{1,0:T(8,128)(2,1)S(1)}, u32[]{:S(2)}, u32[]{:S(2)}) collective-permute-start(bf16[1152,128]{1,0:T(8,128)(2,1)S(1)} %get-tuple-element.54), channel_id=1, source_target_pairs={{0,1},{1,0},{2,3},{3,2},{4,5},{5,4},{8,9},{9,8},{10,11},{11,10},{1... | collective-permute-start | bytes 884744 | tf_op jit(solution)/shard_map/ppermute | solution.py:184
  43.7 0.8 %collective-permute-start.16 = (f32[256,128]{1,0:T(8,128)S(1)}, f32[256,128]{1,0:T(8,128)S(1)}, u32[]{:S(2)}, u32[]{:S(2)}) collective-permute-start(f32[256,128]{1,0:T(8,128)S(1)} %convolution_subtract_fusion.2), channel_id=1, source_target_pairs={{6,14},{7,15},{14,6},{15,7},{22,30},{23,31},{30,22},{31,23}} | collective-permute-start | bytes 393224 | tf_op jit(solution)/shard_map/ppermute | solution.py:316
  45.2 0.8 %collective-permute-start.17 = (bf16[256,128]{1,0:T(8,128)(2,1)S(1)}, bf16[256,128]{1,0:T(8,128)(2,1)S(1)}, u32[]{:S(2)}, u32[]{:S(2)}) collective-permute-start(bf16[256,128]{1,0:T(8,128)(2,1)S(1)} %add_convert_fusion.1), channel_id=1, source_target_pairs={{6,22},{7,23},{14,30},{15,31},{22,6},{23,7},{30,14},{31,15}} | collective-permute-start | bytes 196616 | tf_op jit(solution)/shard_map/ppermute | solution.py:316
  48.1 0.7 fusion.2
  50.3 1.3 %collective-permute-start.19 = (bf16[384,128]{1,0:T(8,128)(2,1)S(1)}, bf16[384,128]{1,0:T(8,128)(2,1)S(1)}, u32[]{:S(2)}, u32[]{:S(2)}) collective-permute-start(bf16[384,128]{1,0:T(8,128)(2,1)S(1)} %pad_maximum_fusion.20), channel_id=1, source_target_pairs={{6,4},{7,5},{14,12},{15,13},{22,20},{23,21},{30,28},{31,29}} | collective-permute-start | bytes 294920 | tf_op jit(solution)/shard_map/ppermute | solution.py:217
  51.7 4.8 %collective-permute-done.19 = bf16[384,128]{1,0:T(8,128)(2,1)S(1)} collective-permute-done((bf16[384,128]{1,0:T(8,128)(2,1)S(1)}, bf16[384,128]{1,0:T(8,128)(2,1)S(1)}, u32[]{:S(2)}, u32[]{:S(2)}) %collective-permute-start.19) | collective-permute-done | bytes 98336 | tf_op jit(solution)/shard_map/ppermute | solution.py:217
  57.0 0.7 fusion.7
  61.1 7.3 %collective-permute-start.22 = (bf16[2,2,32,1024]{3,2,0,1:T(8,128)(2,1)S(1)}, bf16[2,2,32,1024]{3,2,0,1:T(8,128)(2,1)S(1)}, u32[]{:S(2)}, u32[]{:S(2)}) collective-permute-start(bf16[2,2,32,1024]{3,2,0,1:T(8,128)(2,1)S(1)} %select_bitcast_fusion), channel_id=1, source_target_pairs={{0,8},{8,0},{16,24},{24,16},{1,9},{9,1},{17,25},{25,17},{2,10},{10... | collective-permute-start | bytes 786440 | tf_op jit(solution)/shard_map/ppermute | solution.py:180
  68.8 0.8 collective-permute-done.22
  69.7 1.3 %collective-permute-start.23 = (bf16[2,1,32,1024]{3,2,1,0:T(8,128)(2,1)S(1)}, bf16[2,1,32,1024]{3,2,1,0:T(8,128)(2,1)S(1)}, u32[]{:S(2)}, u32[]{:S(2)}) collective-permute-start(bf16[2,1,32,1024]{3,2,1,0:T(8,128)(2,1)S(1)} %fusion.29), channel_id=1, source_target_pairs={{0,16},{8,24},{16,0},{24,8},{1,17},{9,25},{17,1},{25,9},{2,18},{10... | collective-permute-start | bytes 393224 | tf_op jit(solution)/shard_map/ppermute | solution.py:180
  71.0 3.0 %select_dynamic-update-slice_fusion = bf16[2048,1024]{1,0:T(8,128)(2,1)S(1)} fusion(bf16[2048,1024]{1,0:T(8,128)(2,1)S(1)} %copy-done.3, bf16[1024,128]{1,0:T(8,128)(2,1)S(1)} %slice_select_fusion.3, pred[1024]{0:T(1024)(128)(4,1)S(1)} %fusion.62, bf16[1024,256]{1,0:T(8,128)(2,1)S(1)} %pad_maximum_fusion.7, f32[2048,1024]{1,0:T(8,128)} %adj_ref.1, ...), kind=kOutput, calls=%fused_computation.2 | convolution fusion | flops 541065216 | bytes 7603200 | tf_op jit(solution)/shard_map/dot_general | solution.py:21
  74.5 1.3 %fusion.31 = (f32[32,1024]{1,0:T(8,128)}, f32[32,1024]{1,0:T(8,128)}) fusion(f32[2,1,32,1024]{3,2,1,0:T(8,128)S(1)} %bitcast_add_fusion, f32[32,1024]{1,0:T(8,128)S(1)} %copy-done.12, f32[64,1024]{1,0:T(8,128)S(1)} %fusion.17, f32[32,128]{1,0:T(8,128)S(1)} %get-tuple-element.47, pred[1024]{0:T(1024)(128)(4,1)S(1)} %fusion.62, f32[32,1024]{1,0:T(8,128)S(1)} %copy-done.13, ...), kind=kLoop, calls=%fused_computation.67 | loop fusion | flops 196608 | bytes 1070080 | tf_op jit(solution)/shard_map/jit(_where)/select_n | solution.py:334
  (144 shorter events, 15.4 us)
Async XLA Ops:
  5.3 11.5 %collective-permute-start.1 = (bf16[1152,128]{1,0:T(8,128)(2,1)}, bf16[1152,128]{1,0:T(8,128)(2,1)S(1)}, u32[]{:S(2)}, u32[]{:S(2)}) collective-permute-start(bf16[1152,128]{1,0:T(8,128)(2,1)} %get-tuple-element.27), channel_id=1, source_target_pairs={{7,6},{15,14},{23,22},{31,30}} | collective-permute-start | bytes 884744 | tf_op jit(solution)/shard_map/ppermute | solution.py:285
  6.1 10.7 %collective-permute-start = (bf16[1152,128]{1,0:T(8,128)(2,1)}, bf16[1152,128]{1,0:T(8,128)(2,1)S(1)}, u32[]{:S(2)}, u32[]{:S(2)}) collective-permute-start(bf16[1152,128]{1,0:T(8,128)(2,1)} %get-tuple-element.27), channel_id=1, source_target_pairs={{6,2},{7,3},{14,10},{15,11},{22,18},{23,19},{30,26},{31,27}} | collective-permute-start | bytes 884744 | tf_op jit(solution)/shard_map/ppermute | solution.py:217
  6.8 1.6 %collective-permute-start.6 = (bf16[1,1,32,1024]{3,2,1,0:T(8,128)(2,1)S(1)}, bf16[1,1,32,1024]{3,2,1,0:T(8,128)(2,1)S(1)}, u32[]{:S(2)}, u32[]{:S(2)}) collective-permute-start(bf16[1,1,32,1024]{3,2,1,0:T(8,128)(2,1)S(1)} %bitcast.82), channel_id=1, source_target_pairs={{0,8},{8,0},{16,24},{24,16},{1,9},{9,1},{17,25},{25,17},{2,10},{10... | collective-permute-start | bytes 196616 | tf_op jit(solution)/shard_map/ppermute | solution.py:180
  7.6 1.3 %collective-permute-start.5 = (bf16[1,1,32,1024]{3,2,1,0:T(8,128)(2,1)S(1)}, bf16[1,1,32,1024]{3,2,1,0:T(8,128)(2,1)S(1)}, u32[]{:S(2)}, u32[]{:S(2)}) collective-permute-start(bf16[1,1,32,1024]{3,2,1,0:T(8,128)(2,1)S(1)} %bitcast.83), channel_id=1, source_target_pairs={{0,8},{8,0},{16,24},{24,16},{1,9},{9,1},{17,25},{25,17},{2,10},{10... | collective-permute-start | bytes 196616 | tf_op jit(solution)/shard_map/ppermute | solution.py:180
  7.7 11.2 %collective-permute-start.3 = (bf16[1152,128]{1,0:T(8,128)(2,1)}, bf16[1152,128]{1,0:T(8,128)(2,1)S(1)}, u32[]{:S(2)}, u32[]{:S(2)}) collective-permute-start(bf16[1152,128]{1,0:T(8,128)(2,1)} %get-tuple-element.30), channel_id=1, source_target_pairs={{7,6},{15,14},{23,22},{31,30}} | collective-permute-start | bytes 884744 | tf_op jit(solution)/shard_map/ppermute | solution.py:285
  8.9 5.0 %collective-permute-start.7 = (bf16[1,2,32,1024]{3,2,1,0:T(8,128)(2,1)S(1)}, bf16[1,2,32,1024]{3,2,1,0:T(8,128)(2,1)S(1)}, u32[]{:S(2)}, u32[]{:S(2)}) collective-permute-start(bf16[1,2,32,1024]{3,2,1,0:T(8,128)(2,1)S(1)} %pad_maximum_fusion.19), channel_id=1, source_target_pairs={{0,16},{8,24},{16,0},{24,8},{1,17},{9,25},{17,1},{25,9},{2,18},{10... | collective-permute-start | bytes 393224 | tf_op jit(solution)/shard_map/ppermute | solution.py:180
  14.0 2.1 %collective-permute-start.9 = (bf16[128,128]{1,0:T(8,128)(2,1)S(1)}, bf16[128,128]{1,0:T(8,128)(2,1)S(1)}, u32[]{:S(2)}, u32[]{:S(2)}) collective-permute-start(bf16[128,128]{1,0:T(8,128)(2,1)S(1)} %slice.130), channel_id=1, source_target_pairs={{6,7},{14,15},{22,23},{30,31}} | collective-permute-start | bytes 98312 | tf_op jit(solution)/shard_map/ppermute | solution.py:270
  14.6 5.0 %collective-permute-start.8 = (bf16[1,2,32,1024]{3,2,1,0:T(8,128)(2,1)S(1)}, bf16[1,2,32,1024]{3,2,1,0:T(8,128)(2,1)S(1)}, u32[]{:S(2)}, u32[]{:S(2)}) collective-permute-start(bf16[1,2,32,1024]{3,2,1,0:T(8,128)(2,1)S(1)} %pad_maximum_fusion.18), channel_id=1, source_target_pairs={{0,16},{8,24},{16,0},{24,8},{1,17},{9,25},{17,1},{25,9},{2,18},{10... | collective-permute-start | bytes 393224 | tf_op jit(solution)/shard_map/ppermute | solution.py:180
  16.1 9.9 %collective-permute-start.10 = (bf16[128,128]{1,0:T(8,128)(2,1)S(1)}, bf16[128,128]{1,0:T(8,128)(2,1)S(1)}, u32[]{:S(2)}, u32[]{:S(2)}) collective-permute-start(bf16[128,128]{1,0:T(8,128)(2,1)S(1)} %broadcast_select_fusion.16), channel_id=1, source_target_pairs={{6,2},{7,3},{14,10},{15,11},{22,18},{23,19},{30,26},{31,27}} | collective-permute-start | bytes 98312 | tf_op jit(solution)/shard_map/ppermute | solution.py:217
  16.8 9.2 %collective-permute-start.12 = (bf16[1152,128]{1,0:T(8,128)(2,1)S(1)}, bf16[1152,128]{1,0:T(8,128)(2,1)S(1)}, u32[]{:S(2)}, u32[]{:S(2)}) collective-permute-start(bf16[1152,128]{1,0:T(8,128)(2,1)S(1)} %collective-permute-done), channel_id=1, source_target_pairs={{2,4},{3,5},{10,12},{11,13},{18,20},{19,21},{26,28},{27,29}} | collective-permute-start | bytes 884744 | tf_op jit(solution)/shard_map/ppermute | solution.py:217
  18.2 1.5 %collective-permute-start.4 = (bf16[1152,128]{1,0:T(8,128)(2,1)S(1)}, bf16[1152,128]{1,0:T(8,128)(2,1)S(1)}, u32[]{:S(2)}, u32[]{:S(2)}) collective-permute-start(bf16[1152,128]{1,0:T(8,128)(2,1)S(1)} %broadcast_select_fusion.3), channel_id=1, source_target_pairs={{6,2},{7,3},{2,0},{3,1},{14,10},{15,11},{10,8},{11,9},{22,18},{23,... | collective-permute-start | bytes 884744 | tf_op jit(solution)/shard_map/ppermute | solution.py:217
  18.9 25.8 %collective-permute-start.2 = (bf16[2048,128]{1,0:T(8,128)(2,1)S(1)}, bf16[2048,128]{1,0:T(8,128)(2,1)S(1)}, u32[]{:S(2)}, u32[]{:S(2)}) collective-permute-start(bf16[2048,128]{1,0:T(8,128)(2,1)S(1)} %copy-done.7), channel_id=1, source_target_pairs={{6,7},{14,15},{22,23},{30,31}} | collective-permute-start | bytes 1572872 | tf_op jit(solution)/shard_map/ppermute | solution.py:289
  26.1 4.5 %collective-permute-start.13 = (bf16[1152,128]{1,0:T(8,128)(2,1)S(1)}, bf16[1152,128]{1,0:T(8,128)(2,1)S(1)}, u32[]{:S(2)}, u32[]{:S(2)}) collective-permute-start(bf16[1152,128]{1,0:T(8,128)(2,1)S(1)} %constant_dynamic-update-slice_fusion), channel_id=1, source_target_pairs={{2,0},{3,1},{10,8},{11,9},{18,16},{19,17},{26,24},{27,25}} | collective-permute-start | bytes 884744 | tf_op jit(solution)/shard_map/ppermute | solution.py:217
  26.9 12.2 %collective-permute-start.11 = (bf16[1152,128]{1,0:T(8,128)(2,1)S(1)}, bf16[1152,128]{1,0:T(8,128)(2,1)S(1)}, u32[]{:S(2)}, u32[]{:S(2)}) collective-permute-start(bf16[1152,128]{1,0:T(8,128)(2,1)S(1)} %constant_dynamic-update-slice_fusion), channel_id=1, source_target_pairs={{2,4},{3,5},{10,12},{11,13},{18,20},{19,21},{26,28},{27,29}} | collective-permute-start | bytes 884744 | tf_op jit(solution)/shard_map/ppermute | solution.py:217
  28.4 14.3 %collective-permute-start.14 = (bf16[1152,128]{1,0:T(8,128)(2,1)S(1)}, bf16[1152,128]{1,0:T(8,128)(2,1)S(1)}, u32[]{:S(2)}, u32[]{:S(2)}) collective-permute-start(bf16[1152,128]{1,0:T(8,128)(2,1)S(1)} %select_select_fusion.1), channel_id=1, source_target_pairs={{0,1},{1,0},{2,3},{3,2},{4,5},{5,4},{8,9},{9,8},{10,11},{11,10},{1... | collective-permute-start | bytes 884744 | tf_op jit(solution)/shard_map/ppermute | solution.py:184
  39.2 12.4 %collective-permute-start.15 = (bf16[1152,128]{1,0:T(8,128)(2,1)S(1)}, bf16[1152,128]{1,0:T(8,128)(2,1)S(1)}, u32[]{:S(2)}, u32[]{:S(2)}) collective-permute-start(bf16[1152,128]{1,0:T(8,128)(2,1)S(1)} %get-tuple-element.54), channel_id=1, source_target_pairs={{0,1},{1,0},{2,3},{3,2},{4,5},{5,4},{8,9},{9,8},{10,11},{11,10},{1... | collective-permute-start | bytes 884744 | tf_op jit(solution)/shard_map/ppermute | solution.py:184
  43.7 1.5 %collective-permute-start.16 = (f32[256,128]{1,0:T(8,128)S(1)}, f32[256,128]{1,0:T(8,128)S(1)}, u32[]{:S(2)}, u32[]{:S(2)}) collective-permute-start(f32[256,128]{1,0:T(8,128)S(1)} %convolution_subtract_fusion.2), channel_id=1, source_target_pairs={{6,14},{7,15},{14,6},{15,7},{22,30},{23,31},{30,22},{31,23}} | collective-permute-start | bytes 393224 | tf_op jit(solution)/shard_map/ppermute | solution.py:316
  45.2 2.2 %collective-permute-start.17 = (bf16[256,128]{1,0:T(8,128)(2,1)S(1)}, bf16[256,128]{1,0:T(8,128)(2,1)S(1)}, u32[]{:S(2)}, u32[]{:S(2)}) collective-permute-start(bf16[256,128]{1,0:T(8,128)(2,1)S(1)} %add_convert_fusion.1), channel_id=1, source_target_pairs={{6,22},{7,23},{14,30},{15,31},{22,6},{23,7},{30,14},{31,15}} | collective-permute-start | bytes 196616 | tf_op jit(solution)/shard_map/ppermute | solution.py:316
  47.4 1.4 %collective-permute-start.18 = (bf16[256,128]{1,0:T(8,128)(2,1)S(1)}, bf16[256,128]{1,0:T(8,128)(2,1)S(1)}, u32[]{:S(2)}, u32[]{:S(2)}) collective-permute-start(bf16[256,128]{1,0:T(8,128)(2,1)S(1)} %add_convert_fusion), channel_id=1, source_target_pairs={{6,7},{7,6},{14,15},{15,14},{22,23},{23,22},{30,31},{31,30}} | collective-permute-start | bytes 196616 | tf_op jit(solution)/shard_map/ppermute | solution.py:184
  48.9 2.8 %collective-permute-start.21 = (bf16[384,128]{1,0:T(8,128)(2,1)S(1)}, bf16[384,128]{1,0:T(8,128)(2,1)S(1)}, u32[]{:S(2)}, u32[]{:S(2)}) collective-permute-start(bf16[384,128]{1,0:T(8,128)(2,1)S(1)} %pad_maximum_fusion.20), channel_id=1, source_target_pairs={{6,0},{7,1},{14,8},{15,9},{22,16},{23,17},{30,24},{31,25}} | collective-permute-start | bytes 294920 | tf_op jit(solution)/shard_map/ppermute | solution.py:217
  49.6 2.1 %collective-permute-start.20 = (bf16[384,128]{1,0:T(8,128)(2,1)S(1)}, bf16[384,128]{1,0:T(8,128)(2,1)S(1)}, u32[]{:S(2)}, u32[]{:S(2)}) collective-permute-start(bf16[384,128]{1,0:T(8,128)(2,1)S(1)} %pad_maximum_fusion.20), channel_id=1, source_target_pairs={{6,2},{7,3},{14,10},{15,11},{22,18},{23,19},{30,26},{31,27}} | collective-permute-start | bytes 294920 | tf_op jit(solution)/shard_map/ppermute | solution.py:217
  50.3 6.3 %collective-permute-start.19 = (bf16[384,128]{1,0:T(8,128)(2,1)S(1)}, bf16[384,128]{1,0:T(8,128)(2,1)S(1)}, u32[]{:S(2)}, u32[]{:S(2)}) collective-permute-start(bf16[384,128]{1,0:T(8,128)(2,1)S(1)} %pad_maximum_fusion.20), channel_id=1, source_target_pairs={{6,4},{7,5},{14,12},{15,13},{22,20},{23,21},{30,28},{31,29}} | collective-permute-start | bytes 294920 | tf_op jit(solution)/shard_map/ppermute | solution.py:217
  61.1 8.4 %collective-permute-start.22 = (bf16[2,2,32,1024]{3,2,0,1:T(8,128)(2,1)S(1)}, bf16[2,2,32,1024]{3,2,0,1:T(8,128)(2,1)S(1)}, u32[]{:S(2)}, u32[]{:S(2)}) collective-permute-start(bf16[2,2,32,1024]{3,2,0,1:T(8,128)(2,1)S(1)} %select_bitcast_fusion), channel_id=1, source_target_pairs={{0,8},{8,0},{16,24},{24,16},{1,9},{9,1},{17,25},{25,17},{2,10},{10... | collective-permute-start | bytes 786440 | tf_op jit(solution)/shard_map/ppermute | solution.py:180
  69.7 4.8 %collective-permute-start.23 = (bf16[2,1,32,1024]{3,2,1,0:T(8,128)(2,1)S(1)}, bf16[2,1,32,1024]{3,2,1,0:T(8,128)(2,1)S(1)}, u32[]{:S(2)}, u32[]{:S(2)}) collective-permute-start(bf16[2,1,32,1024]{3,2,1,0:T(8,128)(2,1)S(1)} %fusion.29), channel_id=1, source_target_pairs={{0,16},{8,24},{16,0},{24,8},{1,17},{9,25},{17,1},{25,9},{2,18},{10... | collective-permute-start | bytes 393224 | tf_op jit(solution)/shard_map/ppermute | solution.py:180
  (21 other events, 162.9 us)

commit v10 on v9

--- a/solution.py
+++ b/solution.py
@@ -216,10 +216,9 @@
         pairs = [(2 * a + s, 2 * b + s) for a, b in hops for s in range(2)]
         return lax.ppermute(value, "col", pairs)
 
-    def spread(pieces, gates, extra):
+    def spread(pieces, gates, lend):
         middle, span = levels // 2 - 1, levels // 4
-        first, down = [], []
-        extra_moved = hop(extra, [(top, middle)])
+        first, down, up = [], [], []
         for k in range(len(pieces) + 1):
             if k == 0:
                 operand, hops = pieces[0], [(top, middle)]
@@ -229,16 +228,21 @@
             else:
                 operand, hops = first[-1], [(middle, middle - span)]
             moved = hop(operand, hops)
+            if k == len(pieces) - 1:
+                block = lend(up[0])
+                block_moved = hop(block, [(top, middle)])
+                moved = after(moved, block_moved)
             if k > 0:
                 down.append(moved)
             if k < len(pieces):
-                moved = after(moved, gates[k]) if k < len(gates) else moved
+                moved = after(moved, *gates[k]) if k < len(gates) else moved
                 if k == len(pieces) - 1:
-                    moved = lax.dynamic_update_slice(moved, extra_moved, (0, 0))
+                    moved = lax.dynamic_update_slice(moved, block_moved, (0, 0))
                 first.append(moved)
+                up.append(hop(moved, [(middle, middle + span)]))
         held = [
-            {middle: here, middle - span: low, middle + span: hop(here, [(middle, middle + span)])}
-            for here, low in zip(first, down)
+            {middle: here, middle - span: low, middle + span: high}
+            for here, low, high in zip(first, down, up)
         ]
         span //= 2
         while span >= 1:
@@ -256,7 +260,7 @@
         for piece in held:
             options = [([k], after(piece[k], *arrived)) for k in sorted(piece)]
             arrived.append(choose(options))
-        return first, arrived
+        return block, first, arrived
 
     near_two = gather_step(row_two[None, None], 1)
     near_one = gather_step(row_one[None, None], 1)
@@ -267,8 +271,10 @@
     )
     own_cross = full_two[:, last:]
     one_owner, two_owner = col_count - 2, col_count - 1
-    lent_cross = lax.ppermute(own_cross, "col", [(one_owner, two_owner)])
-    side_cross = jnp.where(is_two, lent_cross, own_cross)
+
+    def lend(gate):
+        lent = lax.ppermute(after(own_cross, gate), "col", [(one_owner, two_owner)])
+        return jnp.where(is_two, lent, own_cross)
 
     def factor_of(cross):
         return jnp.concatenate(halves(exact_dot(cross.astype(F32), inverse_one)), 0)
@@ -285,15 +291,17 @@
         lax.ppermute(packet, "col", [(two_owner, one_owner)]) for packet in packets
     ]
     full_one = gather_rest(after(near_one, full_two))
-    first, arrived = spread(packets, [early_two[0], full_one], side_cross)
+    gates = [(early_two[0],), (full_one,)]
+    side_cross, first, arrived = spread(packets, gates, lend)
     early_one = lax.ppermute(after(whole, first[0]), "col", [(one_owner, two_owner)])
     at_top = level == top
     own = [jnp.where(at_top, a, b) for a, b in zip(packets, arrived)]
     other = [pair_swap(value, range(levels - 1)) for value in arrived]
     full_both = jnp.concatenate([full_two, after(full_one, arrived[0])], 0)
 
-    early_two = jnp.concatenate([piece[panel:] for piece in early_two], 0)
-    early_two = after(early_two, arrived[final], other[0])
+    early_two = jnp.concatenate(
+        [after(piece, arrived[final], other[0])[panel:] for piece in early_two], 0
+    )
     top_both = panels_of(whole, early_two, factor_of(own_cross), height)
     terms = wide_dot(top_both.T, trail[:, last:])
     placed = lax.dynamic_update_slice_in_dim(
@@ -319,6 +327,9 @@
     terms = terms.astype(BF16)
     terms_other = pair_swap(terms, [top])
 
+    diag_term_two = jnp.where(is_two, terms, terms_other)[:panel]
+    terms = jnp.concatenate([diag_term_two, jnp.where(is_two, terms_other, terms)], 0)
+
     whole_other = jnp.where(is_two, after(early_one, own_terms), early_two)
     for k, (start, stop) in enumerate(cuts):
         low = after(other[k][panel:], own_terms, *other[:k])
@@ -344,9 +355,7 @@
     for (start, stop), mine, theirs in zip(cuts[:-1], own, other):
         both = panels_of(mine, theirs, factor, stop - start)
         sums = sums + wide_dot(both.T, trail[start:stop])
-        grad_trail = updated(both, start, grad_trail)
-    diag_term_two = jnp.where(is_two, terms, terms_other)[:panel]
-    terms = jnp.concatenate([diag_term_two, jnp.where(is_two, terms_other, terms)], 0)
+        grad_trail = updated(after(both, terms), start, grad_trail)
     terms = choose(
         [([top], terms)] + [([k], hop(terms, [(top, k)])) for k in range(levels - 1)]
     )

time: 76.5 us -> 80.7 us (1.055)
  the two profiles are of different devices: /device:TPU:21 before, /device:TPU:0 now
where the time goes in v10:
time: 80.7 us; the launch traced here: 80.3 us
  waiting for transfers between devices  32.9 us (41%)
  starting transfers between devices  28 us (35%)
  matrix products  9.45 us (12%)
  Pallas kernels  4.6 us (6%)
  other arithmetic  2.94 us (4%)
  between operations  1.73 us (2%)
    ppermute x9, waiting for transfers between devices, hop(): return lax.ppermute(value, 'col', pairs)  25.6 us
    ppermute x3, starting transfers between devices, pair_swap(): return lax.ppermute(value, 'col', pairs)  9.08 us
    ppermute x9, starting transfers between devices, hop(): return lax.ppermute(value, 'col', pairs)  7.9 us
    ppermute x6, waiting for transfers between devices, row_swap(): return lax.ppermute(value, 'row', [(i, i ^ step) for i in range(row_count)])  7.28 us
    dot_general x10, matrix products, wide_dot(): return jnp.dot(a, b, preferred_element_type=F32)  7.16 us
    ppermute x6, starting transfers between devices, row_swap(): return lax.ppermute(value, 'row', [(i, i ^ step) for i in range(row_count)])  6.62 us
    pallas_call x1, Pallas kernels, prepare(): pl.pallas_call(functools.partial(prepare_kernel, cuts), in_specs=[pl.Bloc...  4.6 us
    dot_general x10, matrix products, exact_dot(): return jnp.dot(a, b, precision=EXACT, preferred_element_type=F32)  2.3 us
  transfers between devices with their start and end apart: 24, of which 9 were waited for; matrix products, arithmetic and copies ran while one was open for 9% of the time, Pallas kernels for 0%

profile of v10, /device:TPU:0, one launch (start us, length us, event | category | flops | bytes accessed | tf_op | source)
XLA Modules:
  0.0 80.3 jit_solution(15902849869558063996)
XLA Ops:
  0.7 4.6 %prepare.1 = (f32[128,128]{1,0:T(8,128)}, f32[128,128]{1,0:T(8,128)}, bf16[2048,128]{1,0:T(8,128)(2,1)}, bf16[1152,128]{1,0:T(8,128)(2,1)}, bf16[1152,128]{1,0:T(8,128)(2,1)}) custom-call(s32[1]{0:T(128)} %bitcast.side_ref, f32[128,128]{1,0:T(8,128)} %one_ref.1, f32[128,128]{1,0:T(8,128)} %two_ref.1, f32[2048,1024]{1,0:T(8,128)} %adj_ref.1), custom_call_target="tpu_custom_call" | custom-call | flops 268435456 | bytes 2097152 | tf_op jit(solution)/shard_map/prepare/pallas_call | solution.py:107
  5.3 0.8 %collective-permute-start.1 = (bf16[1152,128]{1,0:T(8,128)(2,1)}, bf16[1152,128]{1,0:T(8,128)(2,1)S(1)}, u32[]{:S(2)}, u32[]{:S(2)}) collective-permute-start(bf16[1152,128]{1,0:T(8,128)(2,1)} %get-tuple-element.30), channel_id=1, source_target_pairs={{7,6},{15,14},{23,22},{31,30}} | collective-permute-start | bytes 884744 | tf_op jit(solution)/shard_map/ppermute | solution.py:291
  8.6 2.7 %collective-permute-start.5 = (bf16[1,2,32,1024]{3,2,1,0:T(8,128)(2,1)S(1)}, bf16[1,2,32,1024]{3,2,1,0:T(8,128)(2,1)S(1)}, u32[]{:S(2)}, u32[]{:S(2)}) collective-permute-start(bf16[1,2,32,1024]{3,2,1,0:T(8,128)(2,1)S(1)} %pad_maximum_fusion.16), channel_id=1, source_target_pairs={{0,16},{8,24},{16,0},{24,8},{1,17},{9,25},{17,1},{25,9},{2,18},{10... | collective-permute-start | bytes 393224 | tf_op jit(solution)/shard_map/ppermute | solution.py:180
  11.4 3.9 %collective-permute-done.5 = bf16[1,2,32,1024]{3,2,1,0:T(8,128)(2,1)S(1)} collective-permute-done((bf16[1,2,32,1024]{3,2,1,0:T(8,128)(2,1)S(1)}, bf16[1,2,32,1024]{3,2,1,0:T(8,128)(2,1)S(1)}, u32[]{:S(2)}, u32[]{:S(2)}) %collective-permute-start.5) | collective-permute-done | bytes 131104 | tf_op jit(solution)/shard_map/ppermute | solution.py:180
  15.4 1.8 %collective-permute-start.10 = (bf16[1,2,32,1024]{3,2,1,0:T(8,128)(2,1)S(1)}, bf16[1,2,32,1024]{3,2,1,0:T(8,128)(2,1)S(1)}, u32[]{:S(2)}, u32[]{:S(2)}) collective-permute-start(bf16[1,2,32,1024]{3,2,1,0:T(8,128)(2,1)S(1)} %pad_maximum_fusion.17), channel_id=1, source_target_pairs={{0,16},{8,24},{16,0},{24,8},{1,17},{9,25},{17,1},{25,9},{2,18},{10... | collective-permute-start | bytes 393224 | tf_op jit(solution)/shard_map/ppermute | solution.py:180
  18.0 1.3 %collective-permute-start.3 = (bf16[1152,128]{1,0:T(8,128)(2,1)S(1)}, bf16[1152,128]{1,0:T(8,128)(2,1)S(1)}, u32[]{:S(2)}, u32[]{:S(2)}) collective-permute-start(bf16[1152,128]{1,0:T(8,128)(2,1)S(1)} %broadcast_select_fusion.3), channel_id=1, source_target_pairs={{6,2},{7,3},{2,0},{3,1},{14,10},{15,11},{10,8},{11,9},{22,18},{23,... | collective-permute-start | bytes 884744 | tf_op jit(solution)/shard_map/ppermute | solution.py:217
  21.4 9.0 %collective-permute-done.3 = bf16[1152,128]{1,0:T(8,128)(2,1)S(1)} collective-permute-done((bf16[1152,128]{1,0:T(8,128)(2,1)S(1)}, bf16[1152,128]{1,0:T(8,128)(2,1)S(1)}, u32[]{:S(2)}, u32[]{:S(2)}) %collective-permute-start.3) | collective-permute-done | bytes 294944 | tf_op jit(solution)/shard_map/ppermute | solution.py:217
  30.5 1.3 %collective-permute-start.12 = (bf16[1152,128]{1,0:T(8,128)(2,1)S(1)}, bf16[1152,128]{1,0:T(8,128)(2,1)S(1)}, u32[]{:S(2)}, u32[]{:S(2)}) collective-permute-start(bf16[1152,128]{1,0:T(8,128)(2,1)S(1)} %constant_dynamic-update-slice_fusion), channel_id=1, source_target_pairs={{2,0},{3,1},{10,8},{11,9},{18,16},{19,17},{26,24},{27,25}} | collective-permute-start | bytes 884744 | tf_op jit(solution)/shard_map/ppermute | solution.py:217
  33.4 4.1 %collective-permute-start.13 = (bf16[1152,128]{1,0:T(8,128)(2,1)S(1)}, bf16[1152,128]{1,0:T(8,128)(2,1)S(1)}, u32[]{:S(2)}, u32[]{:S(2)}) collective-permute-start(bf16[1152,128]{1,0:T(8,128)(2,1)S(1)} %select_select_fusion.1), channel_id=1, source_target_pairs={{0,1},{1,0},{2,3},{3,2},{4,5},{5,4},{8,9},{9,8},{10,11},{11,10},{1... | collective-permute-start | bytes 884744 | tf_op jit(solution)/shard_map/ppermute | solution.py:184
  37.5 4.6 %collective-permute-done.12 = bf16[1152,128]{1,0:T(8,128)(2,1)S(1)} collective-permute-done((bf16[1152,128]{1,0:T(8,128)(2,1)S(1)}, bf16[1152,128]{1,0:T(8,128)(2,1)S(1)}, u32[]{:S(2)}, u32[]{:S(2)}) %collective-permute-start.12) | collective-permute-done | bytes 294944 | tf_op jit(solution)/shard_map/ppermute | solution.py:217
  42.2 4.2 %collective-permute-start.18 = (bf16[1152,128]{1,0:T(8,128)(2,1)S(1)}, bf16[1152,128]{1,0:T(8,128)(2,1)S(1)}, u32[]{:S(2)}, u32[]{:S(2)}) collective-permute-start(bf16[1152,128]{1,0:T(8,128)(2,1)S(1)} %get-tuple-element.62), channel_id=1, source_target_pairs={{0,1},{1,0},{2,3},{3,2},{4,5},{5,4},{8,9},{9,8},{10,11},{11,10},{1... | collective-permute-start | bytes 884744 | tf_op jit(solution)/shard_map/ppermute | solution.py:184
  47.6 0.8 collective-permute-start.15
  49.3 0.8 collective-permute-start.16
  50.1 0.7 fusion.3
  50.9 0.8 collective-permute-start.17
  51.8 1.3 %collective-permute-start.21 = (bf16[384,128]{1,0:T(8,128)(2,1)S(1)}, bf16[384,128]{1,0:T(8,128)(2,1)S(1)}, u32[]{:S(2)}, u32[]{:S(2)}) collective-permute-start(bf16[384,128]{1,0:T(8,128)(2,1)S(1)} %pad_maximum_fusion.18), channel_id=1, source_target_pairs={{6,0},{7,1},{14,8},{15,9},{22,16},{23,17},{30,24},{31,25}} | collective-permute-start | bytes 294920 | tf_op jit(solution)/shard_map/ppermute | solution.py:217
  54.5 0.7 select_dynamic-update-slice_fusion.1
  55.4 12.0 %collective-permute-done.21 = bf16[384,128]{1,0:T(8,128)(2,1)S(1)} collective-permute-done((bf16[384,128]{1,0:T(8,128)(2,1)S(1)}, bf16[384,128]{1,0:T(8,128)(2,1)S(1)}, u32[]{:S(2)}, u32[]{:S(2)}) %collective-permute-start.21) | collective-permute-done | bytes 98336 | tf_op jit(solution)/shard_map/ppermute | solution.py:217
  67.8 0.7 fusion.8
  72.5 1.1 %collective-permute-done.22 = bf16[2,2,32,1024]{3,2,0,1:T(8,128)(2,1)S(1)} collective-permute-done((bf16[2,2,32,1024]{3,2,0,1:T(8,128)(2,1)S(1)}, bf16[2,2,32,1024]{3,2,0,1:T(8,128)(2,1)S(1)}, u32[]{:S(2)}, u32[]{:S(2)}) %collective-permute-start.22) | collective-permute-done | bytes 262176 | tf_op jit(solution)/shard_map/ppermute | solution.py:180
  73.7 1.4 %collective-permute-start.23 = (bf16[2,1,32,1024]{3,2,1,0:T(8,128)(2,1)S(1)}, bf16[2,1,32,1024]{3,2,1,0:T(8,128)(2,1)S(1)}, u32[]{:S(2)}, u32[]{:S(2)}) collective-permute-start(bf16[2,1,32,1024]{3,2,1,0:T(8,128)(2,1)S(1)} %fusion.29), channel_id=1, source_target_pairs={{0,16},{8,24},{16,0},{24,8},{1,17},{9,25},{17,1},{25,9},{2,18},{10... | collective-permute-start | bytes 393224 | tf_op jit(solution)/shard_map/ppermute | solution.py:180
  75.2 3.0 %select_dynamic-update-slice_fusion = bf16[2048,1024]{1,0:T(8,128)(2,1)S(1)} fusion(bf16[2048,1024]{1,0:T(8,128)(2,1)S(1)} %copy-done.3, bf16[1024,128]{1,0:T(8,128)(2,1)S(1)} %slice_select_fusion.3, pred[1024]{0:T(1024)(128)(4,1)S(1)} %fusion.60, bf16[1024,256]{1,0:T(8,128)(2,1)S(1)} %pad_maximum_fusion.7, f32[2048,1024]{1,0:T(8,128)} %adj_ref.1, ...), kind=kOutput, calls=%fused_computation.4 | convolution fusion | flops 541065216 | bytes 7603200 | tf_op jit(solution)/shard_map/dot_general | solution.py:21
  78.2 1.1 %collective-permute-done.23 = bf16[2,1,32,1024]{3,2,1,0:T(8,128)(2,1)S(1)} collective-permute-done((bf16[2,1,32,1024]{3,2,1,0:T(8,128)(2,1)S(1)}, bf16[2,1,32,1024]{3,2,1,0:T(8,128)(2,1)S(1)}, u32[]{:S(2)}, u32[]{:S(2)}) %collective-permute-start.23) | collective-permute-done | bytes 131104 | tf_op jit(solution)/shard_map/ppermute | solution.py:180
  79.4 0.9 %fusion.31 = (f32[32,1024]{1,0:T(8,128)}, f32[32,1024]{1,0:T(8,128)}) fusion(f32[2,1,32,1024]{3,2,1,0:T(8,128)S(1)} %bitcast_add_fusion, f32[32,1024]{1,0:T(8,128)S(1)} %copy-done.12, f32[64,1024]{1,0:T(8,128)S(1)} %fusion.17, f32[32,128]{1,0:T(8,128)S(1)} %get-tuple-element.55, pred[1024]{0:T(1024)(128)(4,1)S(1)} %fusion.60, f32[32,1024]{1,0:T(8,128)S(1)} %copy-done.13, ...), kind=kLoop, calls=%fused_computation.67 | loop fusion | flops 196608 | bytes 1070080 | tf_op jit(solution)/shard_map/jit(_where)/select_n | solution.py:345
  (145 shorter events, 14.9 us)
Async XLA Ops:
  5.3 12.0 %collective-permute-start.1 = (bf16[1152,128]{1,0:T(8,128)(2,1)}, bf16[1152,128]{1,0:T(8,128)(2,1)S(1)}, u32[]{:S(2)}, u32[]{:S(2)}) collective-permute-start(bf16[1152,128]{1,0:T(8,128)(2,1)} %get-tuple-element.30), channel_id=1, source_target_pairs={{7,6},{15,14},{23,22},{31,30}} | collective-permute-start | bytes 884744 | tf_op jit(solution)/shard_map/ppermute | solution.py:291
  6.1 11.1 %collective-permute-start = (bf16[1152,128]{1,0:T(8,128)(2,1)}, bf16[1152,128]{1,0:T(8,128)(2,1)S(1)}, u32[]{:S(2)}, u32[]{:S(2)}) collective-permute-start(bf16[1152,128]{1,0:T(8,128)(2,1)} %get-tuple-element.30), channel_id=1, source_target_pairs={{6,2},{7,3},{14,10},{15,11},{22,18},{23,19},{30,26},{31,27}} | collective-permute-start | bytes 884744 | tf_op jit(solution)/shard_map/ppermute | solution.py:217
  6.8 1.4 %collective-permute-start.4 = (bf16[1,1,32,1024]{3,2,1,0:T(8,128)(2,1)S(1)}, bf16[1,1,32,1024]{3,2,1,0:T(8,128)(2,1)S(1)}, u32[]{:S(2)}, u32[]{:S(2)}) collective-permute-start(bf16[1,1,32,1024]{3,2,1,0:T(8,128)(2,1)S(1)} %bitcast.84), channel_id=1, source_target_pairs={{0,8},{8,0},{16,24},{24,16},{1,9},{9,1},{17,25},{25,17},{2,10},{10... | collective-permute-start | bytes 196616 | tf_op jit(solution)/shard_map/ppermute | solution.py:180
  7.3 1.3 %collective-permute-start.9 = (bf16[1,1,32,1024]{3,2,1,0:T(8,128)(2,1)S(1)}, bf16[1,1,32,1024]{3,2,1,0:T(8,128)(2,1)S(1)}, u32[]{:S(2)}, u32[]{:S(2)}) collective-permute-start(bf16[1,1,32,1024]{3,2,1,0:T(8,128)(2,1)S(1)} %bitcast.83), channel_id=1, source_target_pairs={{0,8},{8,0},{16,24},{24,16},{1,9},{9,1},{17,25},{25,17},{2,10},{10... | collective-permute-start | bytes 196616 | tf_op jit(solution)/shard_map/ppermute | solution.py:180
  7.4 39.1 %collective-permute-start.14 = (bf16[1152,128]{1,0:T(8,128)(2,1)}, bf16[1152,128]{1,0:T(8,128)(2,1)S(1)}, u32[]{:S(2)}, u32[]{:S(2)}) collective-permute-start(bf16[1152,128]{1,0:T(8,128)(2,1)} %get-tuple-element.32), channel_id=1, source_target_pairs={{7,6},{15,14},{23,22},{31,30}} | collective-permute-start | bytes 884744 | tf_op jit(solution)/shard_map/ppermute | solution.py:291
  8.6 6.7 %collective-permute-start.5 = (bf16[1,2,32,1024]{3,2,1,0:T(8,128)(2,1)S(1)}, bf16[1,2,32,1024]{3,2,1,0:T(8,128)(2,1)S(1)}, u32[]{:S(2)}, u32[]{:S(2)}) collective-permute-start(bf16[1,2,32,1024]{3,2,1,0:T(8,128)(2,1)S(1)} %pad_maximum_fusion.16), channel_id=1, source_target_pairs={{0,16},{8,24},{16,0},{24,8},{1,17},{9,25},{17,1},{25,9},{2,18},{10... | collective-permute-start | bytes 393224 | tf_op jit(solution)/shard_map/ppermute | solution.py:180
  15.4 5.2 %collective-permute-start.10 = (bf16[1,2,32,1024]{3,2,1,0:T(8,128)(2,1)S(1)}, bf16[1,2,32,1024]{3,2,1,0:T(8,128)(2,1)S(1)}, u32[]{:S(2)}, u32[]{:S(2)}) collective-permute-start(bf16[1,2,32,1024]{3,2,1,0:T(8,128)(2,1)S(1)} %pad_maximum_fusion.17), channel_id=1, source_target_pairs={{0,16},{8,24},{16,0},{24,8},{1,17},{9,25},{17,1},{25,9},{2,18},{10... | collective-permute-start | bytes 393224 | tf_op jit(solution)/shard_map/ppermute | solution.py:180
  17.2 2.0 %collective-permute-start.2 = (bf16[1152,128]{1,0:T(8,128)(2,1)S(1)}, bf16[1152,128]{1,0:T(8,128)(2,1)S(1)}, u32[]{:S(2)}, u32[]{:S(2)}) collective-permute-start(bf16[1152,128]{1,0:T(8,128)(2,1)S(1)} %collective-permute-done), channel_id=1, source_target_pairs={{2,4},{3,5},{10,12},{11,13},{18,20},{19,21},{26,28},{27,29}} | collective-permute-start | bytes 884744 | tf_op jit(solution)/shard_map/ppermute | solution.py:217
  18.0 12.5 %collective-permute-start.3 = (bf16[1152,128]{1,0:T(8,128)(2,1)S(1)}, bf16[1152,128]{1,0:T(8,128)(2,1)S(1)}, u32[]{:S(2)}, u32[]{:S(2)}) collective-permute-start(bf16[1152,128]{1,0:T(8,128)(2,1)S(1)} %broadcast_select_fusion.3), channel_id=1, source_target_pairs={{6,2},{7,3},{2,0},{3,1},{14,10},{15,11},{10,8},{11,9},{22,18},{23,... | collective-permute-start | bytes 884744 | tf_op jit(solution)/shard_map/ppermute | solution.py:217
  19.3 1.4 %collective-permute-start.6 = (bf16[128,128]{1,0:T(8,128)(2,1)S(1)}, bf16[128,128]{1,0:T(8,128)(2,1)S(1)}, u32[]{:S(2)}, u32[]{:S(2)}) collective-permute-start(bf16[128,128]{1,0:T(8,128)(2,1)S(1)} %slice.136), channel_id=1, source_target_pairs={{6,7},{14,15},{22,23},{30,31}} | collective-permute-start | bytes 98312 | tf_op jit(solution)/shard_map/ppermute | solution.py:276
  20.7 9.7 %collective-permute-start.7 = (bf16[128,128]{1,0:T(8,128)(2,1)S(1)}, bf16[128,128]{1,0:T(8,128)(2,1)S(1)}, u32[]{:S(2)}, u32[]{:S(2)}) collective-permute-start(bf16[128,128]{1,0:T(8,128)(2,1)S(1)} %broadcast_select_fusion.15), channel_id=1, source_target_pairs={{6,2},{7,3},{14,10},{15,11},{22,18},{23,19},{30,26},{31,27}} | collective-permute-start | bytes 98312 | tf_op jit(solution)/shard_map/ppermute | solution.py:217
  30.5 11.6 %collective-permute-start.12 = (bf16[1152,128]{1,0:T(8,128)(2,1)S(1)}, bf16[1152,128]{1,0:T(8,128)(2,1)S(1)}, u32[]{:S(2)}, u32[]{:S(2)}) collective-permute-start(bf16[1152,128]{1,0:T(8,128)(2,1)S(1)} %constant_dynamic-update-slice_fusion), channel_id=1, source_target_pairs={{2,0},{3,1},{10,8},{11,9},{18,16},{19,17},{26,24},{27,25}} | collective-permute-start | bytes 884744 | tf_op jit(solution)/shard_map/ppermute | solution.py:217
  31.8 10.3 %collective-permute-start.11 = (bf16[1152,128]{1,0:T(8,128)(2,1)S(1)}, bf16[1152,128]{1,0:T(8,128)(2,1)S(1)}, u32[]{:S(2)}, u32[]{:S(2)}) collective-permute-start(bf16[1152,128]{1,0:T(8,128)(2,1)S(1)} %constant_dynamic-update-slice_fusion), channel_id=1, source_target_pairs={{2,4},{3,5},{10,12},{11,13},{18,20},{19,21},{26,28},{27,29}} | collective-permute-start | bytes 884744 | tf_op jit(solution)/shard_map/ppermute | solution.py:217
  32.7 16.0 %collective-permute-start.8 = (bf16[2048,128]{1,0:T(8,128)(2,1)S(1)}, bf16[2048,128]{1,0:T(8,128)(2,1)S(1)}, u32[]{:S(2)}, u32[]{:S(2)}) collective-permute-start(bf16[2048,128]{1,0:T(8,128)(2,1)S(1)} %copy-done.7), channel_id=1, source_target_pairs={{6,7},{14,15},{22,23},{30,31}} | collective-permute-start | bytes 1572872 | tf_op jit(solution)/shard_map/ppermute | solution.py:296
  33.4 13.1 %collective-permute-start.13 = (bf16[1152,128]{1,0:T(8,128)(2,1)S(1)}, bf16[1152,128]{1,0:T(8,128)(2,1)S(1)}, u32[]{:S(2)}, u32[]{:S(2)}) collective-permute-start(bf16[1152,128]{1,0:T(8,128)(2,1)S(1)} %select_select_fusion.1), channel_id=1, source_target_pairs={{0,1},{1,0},{2,3},{3,2},{4,5},{5,4},{8,9},{9,8},{10,11},{11,10},{1... | collective-permute-start | bytes 884744 | tf_op jit(solution)/shard_map/ppermute | solution.py:184
  42.2 13.0 %collective-permute-start.18 = (bf16[1152,128]{1,0:T(8,128)(2,1)S(1)}, bf16[1152,128]{1,0:T(8,128)(2,1)S(1)}, u32[]{:S(2)}, u32[]{:S(2)}) collective-permute-start(bf16[1152,128]{1,0:T(8,128)(2,1)S(1)} %get-tuple-element.62), channel_id=1, source_target_pairs={{0,1},{1,0},{2,3},{3,2},{4,5},{5,4},{8,9},{9,8},{10,11},{11,10},{1... | collective-permute-start | bytes 884744 | tf_op jit(solution)/shard_map/ppermute | solution.py:184
  47.6 1.6 %collective-permute-start.15 = (f32[256,128]{1,0:T(8,128)S(1)}, f32[256,128]{1,0:T(8,128)S(1)}, u32[]{:S(2)}, u32[]{:S(2)}) collective-permute-start(f32[256,128]{1,0:T(8,128)S(1)} %convolution_subtract_fusion.3), channel_id=1, source_target_pairs={{6,14},{7,15},{14,6},{15,7},{22,30},{23,31},{30,22},{31,23}} | collective-permute-start | bytes 393224 | tf_op jit(solution)/shard_map/ppermute | solution.py:324
  49.3 1.5 %collective-permute-start.16 = (bf16[256,128]{1,0:T(8,128)(2,1)S(1)}, bf16[256,128]{1,0:T(8,128)(2,1)S(1)}, u32[]{:S(2)}, u32[]{:S(2)}) collective-permute-start(bf16[256,128]{1,0:T(8,128)(2,1)S(1)} %add_convert_fusion.1), channel_id=1, source_target_pairs={{6,22},{7,23},{14,30},{15,31},{22,6},{23,7},{30,14},{31,15}} | collective-permute-start | bytes 196616 | tf_op jit(solution)/shard_map/ppermute | solution.py:324
  50.9 0.9 %collective-permute-start.17 = (bf16[256,128]{1,0:T(8,128)(2,1)S(1)}, bf16[256,128]{1,0:T(8,128)(2,1)S(1)}, u32[]{:S(2)}, u32[]{:S(2)}) collective-permute-start(bf16[256,128]{1,0:T(8,128)(2,1)S(1)} %add_convert_fusion), channel_id=1, source_target_pairs={{6,7},{7,6},{14,15},{15,14},{22,23},{23,22},{30,31},{31,30}} | collective-permute-start | bytes 196616 | tf_op jit(solution)/shard_map/ppermute | solution.py:184
  51.8 15.6 %collective-permute-start.21 = (bf16[384,128]{1,0:T(8,128)(2,1)S(1)}, bf16[384,128]{1,0:T(8,128)(2,1)S(1)}, u32[]{:S(2)}, u32[]{:S(2)}) collective-permute-start(bf16[384,128]{1,0:T(8,128)(2,1)S(1)} %pad_maximum_fusion.18), channel_id=1, source_target_pairs={{6,0},{7,1},{14,8},{15,9},{22,16},{23,17},{30,24},{31,25}} | collective-permute-start | bytes 294920 | tf_op jit(solution)/shard_map/ppermute | solution.py:217
  53.1 14.3 %collective-permute-start.20 = (bf16[384,128]{1,0:T(8,128)(2,1)S(1)}, bf16[384,128]{1,0:T(8,128)(2,1)S(1)}, u32[]{:S(2)}, u32[]{:S(2)}) collective-permute-start(bf16[384,128]{1,0:T(8,128)(2,1)S(1)} %pad_maximum_fusion.18), channel_id=1, source_target_pairs={{6,2},{7,3},{14,10},{15,11},{22,18},{23,19},{30,26},{31,27}} | collective-permute-start | bytes 294920 | tf_op jit(solution)/shard_map/ppermute | solution.py:217
  53.8 13.6 %collective-permute-start.19 = (bf16[384,128]{1,0:T(8,128)(2,1)S(1)}, bf16[384,128]{1,0:T(8,128)(2,1)S(1)}, u32[]{:S(2)}, u32[]{:S(2)}) collective-permute-start(bf16[384,128]{1,0:T(8,128)(2,1)S(1)} %pad_maximum_fusion.18), channel_id=1, source_target_pairs={{6,4},{7,5},{14,12},{15,13},{22,20},{23,21},{30,28},{31,29}} | collective-permute-start | bytes 294920 | tf_op jit(solution)/shard_map/ppermute | solution.py:217
  72.0 1.6 %collective-permute-start.22 = (bf16[2,2,32,1024]{3,2,0,1:T(8,128)(2,1)S(1)}, bf16[2,2,32,1024]{3,2,0,1:T(8,128)(2,1)S(1)}, u32[]{:S(2)}, u32[]{:S(2)}) collective-permute-start(bf16[2,2,32,1024]{3,2,0,1:T(8,128)(2,1)S(1)} %select_bitcast_fusion), channel_id=1, source_target_pairs={{0,8},{8,0},{16,24},{24,16},{1,9},{9,1},{17,25},{25,17},{2,10},{10... | collective-permute-start | bytes 786440 | tf_op jit(solution)/shard_map/ppermute | solution.py:180
  73.7 5.6 %collective-permute-start.23 = (bf16[2,1,32,1024]{3,2,1,0:T(8,128)(2,1)S(1)}, bf16[2,1,32,1024]{3,2,1,0:T(8,128)(2,1)S(1)}, u32[]{:S(2)}, u32[]{:S(2)}) collective-permute-start(bf16[2,1,32,1024]{3,2,1,0:T(8,128)(2,1)S(1)} %fusion.29), channel_id=1, source_target_pairs={{0,16},{8,24},{16,0},{24,8},{1,17},{9,25},{17,1},{25,9},{2,18},{10... | collective-permute-start | bytes 393224 | tf_op jit(solution)/shard_map/ppermute | solution.py:180
  (21 other events, 195.9 us)

commit v11 on v9

--- a/solution.py
+++ b/solution.py
@@ -195,7 +195,7 @@
         while step < row_count:
             value = gather_step(value, step)
             step *= 2
-        return value.reshape(panel, width)
+        return value.reshape(panel, value.shape[-1])
 
     def choose(options):
         merged = []
@@ -258,17 +258,19 @@
             arrived.append(choose(options))
         return first, arrived
 
-    near_two = gather_step(row_two[None, None], 1)
+    one_owner, two_owner = col_count - 2, col_count - 1
+    own_rows_cross = row_two[:, last:]
+    lent_rows = lax.ppermute(own_rows_cross, "col", [(one_owner, two_owner)])
+    rows_cross = jnp.where(is_two, lent_rows, own_rows_cross)
+    near_two = gather_step(jnp.concatenate([row_two, rows_cross], 1)[None, None], 1)
     near_one = gather_step(row_one[None, None], 1)
-    full_two = gather_rest(near_two)
+    extended = gather_rest(near_two)
+    full_two, side_cross = extended[:, :width], extended[:, width:]
     side = is_two.astype(jnp.int32)[None]
     inverse_one, inverse_two, whole, *packets = prepare(
-        side, diag_one, diag_two, adj_trail, cuts
-    )
-    own_cross = full_two[:, last:]
-    one_owner, two_owner = col_count - 2, col_count - 1
-    lent_cross = lax.ppermute(own_cross, "col", [(one_owner, two_owner)])
-    side_cross = jnp.where(is_two, lent_cross, own_cross)
+        side, after(diag_one, rows_cross), diag_two, adj_trail, cuts
+    )
+    own_cross = side_cross
 
     def factor_of(cross):
         return jnp.concatenate(halves(exact_dot(cross.astype(F32), inverse_one)), 0)
@@ -284,7 +286,7 @@
     early_two = [
         lax.ppermute(packet, "col", [(two_owner, one_owner)]) for packet in packets
     ]
-    full_one = gather_rest(after(near_one, full_two))
+    full_one = gather_rest(after(near_one, side_cross))
     first, arrived = spread(packets, [early_two[0], full_one], side_cross)
     early_one = lax.ppermute(after(whole, first[0]), "col", [(one_owner, two_owner)])
     at_top = level == top
@@ -344,7 +346,7 @@
     for (start, stop), mine, theirs in zip(cuts[:-1], own, other):
         both = panels_of(mine, theirs, factor, stop - start)
         sums = sums + wide_dot(both.T, trail[start:stop])
-        grad_trail = updated(both, start, grad_trail)
+        grad_trail = updated(after(both, terms), start, grad_trail)
     diag_term_two = jnp.where(is_two, terms, terms_other)[:panel]
     terms = jnp.concatenate([diag_term_two, jnp.where(is_two, terms_other, terms)], 0)
     terms = choose(

time: 76.5 us -> 82.4 us (1.077)
  the two profiles are of different devices: /device:TPU:21 before, /device:TPU:0 now
where the time goes in v11:
time: 82.4 us; the launch traced here: 81.8 us
  waiting for transfers between devices  29.9 us (36%)
  starting transfers between devices  28.6 us (35%)
  matrix products  10.3 us (12%)
  other arithmetic  4.79 us (6%)
  Pallas kernels  4.61 us (6%)
  local copies, waits for them, and re-layouts  1.81 us (2%)
  between operations  1.76 us (2%)
    ppermute x9, waiting for transfers between devices, hop(): return lax.ppermute(value, 'col', pairs)  24 us
    ppermute x3, starting transfers between devices, pair_swap(): return lax.ppermute(value, 'col', pairs)  8.6 us
    ppermute x9, starting transfers between devices, hop(): return lax.ppermute(value, 'col', pairs)  8.17 us
    ppermute x6, starting transfers between devices, row_swap(): return lax.ppermute(value, 'row', [(i, i ^ step) for i in range(row_count)])  7.3 us
    dot_general x10, matrix products, wide_dot(): return jnp.dot(a, b, preferred_element_type=F32)  7.13 us
    ppermute x6, waiting for transfers between devices, row_swap(): return lax.ppermute(value, 'row', [(i, i ^ step) for i in range(row_count)])  5.94 us
    pallas_call x1, Pallas kernels, prepare(): pl.pallas_call(functools.partial(prepare_kernel, cuts), in_specs=[pl.Bloc...  4.61 us
    dot_general x10, matrix products, exact_dot(): return jnp.dot(a, b, precision=EXACT, preferred_element_type=F32)  3.13 us
  transfers between devices with their start and end apart: 24, of which 6 were waited for; matrix products, arithmetic and copies ran while one was open for 12% of the time, Pallas kernels for 6%

profile of v11, /device:TPU:0, one launch (start us, length us, event | category | flops | bytes accessed | tf_op | source)
XLA Modules:
  0.0 81.8 jit_solution(7879573804278345489)
XLA Ops:
  3.3 0.8 %maximum_bitcast_fusion = bf16[1,1,32,1152]{3,2,1,0:T(8,128)(2,1)S(1)} fusion(bf16[32,128]{1,0:T(8,128)(2,1)S(1)} %broadcast_select_fusion.16, bf16[32,1024]{1,0:T(8,128)(2,1)} %param.12), kind=kLoop, calls=%fused_computation.81 | loop fusion | flops 147456 | bytes 147456 | tf_op jit(solution)/shard_map/broadcast_in_dim | solution.py:265
  4.3 4.6 %prepare.1 = (f32[128,128]{1,0:T(8,128)}, f32[128,128]{1,0:T(8,128)}, bf16[2048,128]{1,0:T(8,128)(2,1)}, bf16[1152,128]{1,0:T(8,128)(2,1)}, bf16[1152,128]{1,0:T(8,128)(2,1)}) custom-call(s32[1]{0:T(128)} %bitcast.side_ref, f32[128,128]{1,0:T(8,128)} %one_ref, f32[128,128]{1,0:T(8,128)} %two_ref.1, f32[2048,1024]{1,0:T(8,128)} %adj_ref.1), custom_call_target="tpu_custom_call" | custom-call | flops 268435456 | bytes 2097152 | tf_op jit(solution)/shard_map/prepare/pallas_call | solution.py:107
  8.9 0.8 collective-permute-start.2
  10.5 0.8 collective-permute-start.6
  11.4 2.9 %collective-permute-start.9 = (bf16[1,2,32,1152]{3,2,1,0:T(8,128)(2,1)S(1)}, bf16[1,2,32,1152]{3,2,1,0:T(8,128)(2,1)S(1)}, u32[]{:S(2)}, u32[]{:S(2)}) collective-permute-start(bf16[1,2,32,1152]{3,2,1,0:T(8,128)(2,1)S(1)} %pad_maximum_fusion.16), channel_id=1, source_target_pairs={{0,16},{8,24},{16,0},{24,8},{1,17},{9,25},{17,1},{25,9},{2,18},{10... | collective-permute-start | bytes 442376 | tf_op jit(solution)/shard_map/ppermute | solution.py:180
  14.4 4.1 %collective-permute-done.9 = bf16[1,2,32,1152]{3,2,1,0:T(8,128)(2,1)S(1)} collective-permute-done((bf16[1,2,32,1152]{3,2,1,0:T(8,128)(2,1)S(1)}, bf16[1,2,32,1152]{3,2,1,0:T(8,128)(2,1)S(1)}, u32[]{:S(2)}, u32[]{:S(2)}) %collective-permute-start.9) | collective-permute-done | bytes 147488 | tf_op jit(solution)/shard_map/ppermute | solution.py:180
  19.2 1.8 %collective-permute-start.10 = (bf16[1,2,32,1024]{3,2,1,0:T(8,128)(2,1)S(1)}, bf16[1,2,32,1024]{3,2,1,0:T(8,128)(2,1)S(1)}, u32[]{:S(2)}, u32[]{:S(2)}) collective-permute-start(bf16[1,2,32,1024]{3,2,1,0:T(8,128)(2,1)S(1)} %pad_maximum_fusion.17), channel_id=1, source_target_pairs={{0,16},{8,24},{16,0},{24,8},{1,17},{9,25},{17,1},{25,9},{2,18},{10... | collective-permute-start | bytes 393224 | tf_op jit(solution)/shard_map/ppermute | solution.py:180
  21.0 1.0 %subtract_convert_fusion.5 = (bf16[128,128]{1,0:T(8,128)(2,1)S(1)}, bf16[128,128]{1,0:T(8,128)(2,1)S(1)}) fusion(f32[128,128]{1,0:T(8,128)} %get-tuple-element.40, bf16[128,1152]{1,0:T(8,128)(2,1)S(1)} %bitcast.77), kind=kOutput, calls=%fused_computation.120 | convolution fusion | flops 25231360 | bytes 163840 | tf_op jit(solution)/shard_map/dot_general | solution.py:17
  22.8 1.3 %collective-permute-start.4 = (bf16[1152,128]{1,0:T(8,128)(2,1)S(1)}, bf16[1152,128]{1,0:T(8,128)(2,1)S(1)}, u32[]{:S(2)}, u32[]{:S(2)}) collective-permute-start(bf16[1152,128]{1,0:T(8,128)(2,1)S(1)} %broadcast_select_fusion.3), channel_id=1, source_target_pairs={{6,2},{7,3},{2,0},{3,1},{14,10},{15,11},{10,8},{11,9},{22,18},{23,... | collective-permute-start | bytes 884744 | tf_op jit(solution)/shard_map/ppermute | solution.py:217
  25.0 13.8 %collective-permute-done.4 = bf16[1152,128]{1,0:T(8,128)(2,1)S(1)} collective-permute-done((bf16[1152,128]{1,0:T(8,128)(2,1)S(1)}, bf16[1152,128]{1,0:T(8,128)(2,1)S(1)}, u32[]{:S(2)}, u32[]{:S(2)}) %collective-permute-start.4) | collective-permute-done | bytes 294944 | tf_op jit(solution)/shard_map/ppermute | solution.py:217
  38.9 1.6 %collective-permute-start.13 = (bf16[1152,128]{1,0:T(8,128)(2,1)S(1)}, bf16[1152,128]{1,0:T(8,128)(2,1)S(1)}, u32[]{:S(2)}, u32[]{:S(2)}) collective-permute-start(bf16[1152,128]{1,0:T(8,128)(2,1)S(1)} %constant_dynamic-update-slice_fusion), channel_id=1, source_target_pairs={{2,0},{3,1},{10,8},{11,9},{18,16},{19,17},{26,24},{27,25}} | collective-permute-start | bytes 884744 | tf_op jit(solution)/shard_map/ppermute | solution.py:217
  41.2 4.0 %collective-permute-start.14 = (bf16[1152,128]{1,0:T(8,128)(2,1)S(1)}, bf16[1152,128]{1,0:T(8,128)(2,1)S(1)}, u32[]{:S(2)}, u32[]{:S(2)}) collective-permute-start(bf16[1152,128]{1,0:T(8,128)(2,1)S(1)} %select_select_fusion.1), channel_id=1, source_target_pairs={{0,1},{1,0},{2,3},{3,2},{4,5},{5,4},{8,9},{9,8},{10,11},{11,10},{1... | collective-permute-start | bytes 884744 | tf_op jit(solution)/shard_map/ppermute | solution.py:184
  45.3 4.4 %collective-permute-done.13 = bf16[1152,128]{1,0:T(8,128)(2,1)S(1)} collective-permute-done((bf16[1152,128]{1,0:T(8,128)(2,1)S(1)}, bf16[1152,128]{1,0:T(8,128)(2,1)S(1)}, u32[]{:S(2)}, u32[]{:S(2)}) %collective-permute-start.13) | collective-permute-done | bytes 294944 | tf_op jit(solution)/shard_map/ppermute | solution.py:217
  49.8 3.8 %collective-permute-start.17 = (bf16[1152,128]{1,0:T(8,128)(2,1)S(1)}, bf16[1152,128]{1,0:T(8,128)(2,1)S(1)}, u32[]{:S(2)}, u32[]{:S(2)}) collective-permute-start(bf16[1152,128]{1,0:T(8,128)(2,1)S(1)} %get-tuple-element.58), channel_id=1, source_target_pairs={{0,1},{1,0},{2,3},{3,2},{4,5},{5,4},{8,9},{9,8},{10,11},{11,10},{1... | collective-permute-start | bytes 884744 | tf_op jit(solution)/shard_map/ppermute | solution.py:184
  54.6 0.8 collective-permute-start.15
  56.9 0.8 collective-permute-start.16
  57.8 0.8 collective-permute-start.18
  59.9 1.3 %collective-permute-start.21 = (bf16[384,128]{1,0:T(8,128)(2,1)S(1)}, bf16[384,128]{1,0:T(8,128)(2,1)S(1)}, u32[]{:S(2)}, u32[]{:S(2)}) collective-permute-start(bf16[384,128]{1,0:T(8,128)(2,1)S(1)} %pad_maximum_fusion.18), channel_id=1, source_target_pairs={{6,0},{7,1},{14,8},{15,9},{22,16},{23,17},{30,24},{31,25}} | collective-permute-start | bytes 294920 | tf_op jit(solution)/shard_map/ppermute | solution.py:217
  62.7 5.7 %collective-permute-done.21 = bf16[384,128]{1,0:T(8,128)(2,1)S(1)} collective-permute-done((bf16[384,128]{1,0:T(8,128)(2,1)S(1)}, bf16[384,128]{1,0:T(8,128)(2,1)S(1)}, u32[]{:S(2)}, u32[]{:S(2)}) %collective-permute-start.21) | collective-permute-done | bytes 98336 | tf_op jit(solution)/shard_map/ppermute | solution.py:217
  73.5 1.1 %collective-permute-done.22 = bf16[2,2,32,1024]{3,2,0,1:T(8,128)(2,1)S(1)} collective-permute-done((bf16[2,2,32,1024]{3,2,0,1:T(8,128)(2,1)S(1)}, bf16[2,2,32,1024]{3,2,0,1:T(8,128)(2,1)S(1)}, u32[]{:S(2)}, u32[]{:S(2)}) %collective-permute-start.22) | collective-permute-done | bytes 262176 | tf_op jit(solution)/shard_map/ppermute | solution.py:180
  74.8 1.9 %collective-permute-start.23 = (bf16[2,1,32,1024]{3,2,1,0:T(8,128)(2,1)S(1)}, bf16[2,1,32,1024]{3,2,1,0:T(8,128)(2,1)S(1)}, u32[]{:S(2)}, u32[]{:S(2)}) collective-permute-start(bf16[2,1,32,1024]{3,2,1,0:T(8,128)(2,1)S(1)} %fusion.27), channel_id=1, source_target_pairs={{0,16},{8,24},{16,0},{24,8},{1,17},{9,25},{17,1},{25,9},{2,18},{10... | collective-permute-start | bytes 393224 | tf_op jit(solution)/shard_map/ppermute | solution.py:180
  76.7 3.0 %select_dynamic-update-slice_fusion = bf16[2048,1024]{1,0:T(8,128)(2,1)S(1)} fusion(bf16[2048,1024]{1,0:T(8,128)(2,1)S(1)} %copy-done.3, bf16[1024,128]{1,0:T(8,128)(2,1)S(1)} %slice_select_fusion.3, pred[1024]{0:T(1024)(128)(4,1)S(1)} %fusion.63, bf16[1024,256]{1,0:T(8,128)(2,1)S(1)} %pad_maximum_fusion.7, f32[2048,1024]{1,0:T(8,128)} %adj_ref.1, ...), kind=kOutput, calls=%fused_computation.2 | convolution fusion | flops 541065216 | bytes 7603200 | tf_op jit(solution)/shard_map/dot_general | solution.py:21
  79.7 0.8 collective-permute-done.23
  80.5 1.2 %fusion.29 = (f32[32,1024]{1,0:T(8,128)}, f32[32,1024]{1,0:T(8,128)}) fusion(f32[2,1,32,1024]{3,2,1,0:T(8,128)S(1)} %bitcast_add_fusion, f32[32,1024]{1,0:T(8,128)S(1)} %copy-done.13, f32[64,1024]{1,0:T(8,128)S(1)} %fusion.15, f32[32,128]{1,0:T(8,128)S(1)} %get-tuple-element.51, pred[1024]{0:T(1024)(128)(4,1)S(1)} %fusion.63, f32[32,1024]{1,0:T(8,128)S(1)} %copy-done.14, ...), kind=kLoop, calls=%fused_computation.68 | loop fusion | flops 196608 | bytes 1070080 | tf_op jit(solution)/shard_map/jit(_where)/select_n | solution.py:336
  (150 shorter events, 16.9 us)
Async XLA Ops:
  1.3 1.2 %collective-permute-start = (bf16[32,128]{1,0:T(8,128)(2,1)S(1)}, bf16[32,128]{1,0:T(8,128)(2,1)S(1)}, u32[]{:S(2)}, u32[]{:S(2)}) collective-permute-start(bf16[32,128]{1,0:T(8,128)(2,1)S(1)} %slice.110), channel_id=1, source_target_pairs={{6,7},{14,15},{22,23},{30,31}} | collective-permute-start | bytes 24584 | tf_op jit(solution)/shard_map/ppermute | solution.py:263
  2.0 12.3 %collective-permute-start.7 = (bf16[1,1,32,1024]{3,2,1,0:T(8,128)(2,1)}, bf16[1,1,32,1024]{3,2,1,0:T(8,128)(2,1)S(1)}, u32[]{:S(2)}, u32[]{:S(2)}) collective-permute-start(bf16[1,1,32,1024]{3,2,1,0:T(8,128)(2,1)} %bitcast.83), channel_id=1, source_target_pairs={{0,8},{8,0},{16,24},{24,16},{1,9},{9,1},{17,25},{25,17},{2,10},{10... | collective-permute-start | bytes 196616 | tf_op jit(solution)/shard_map/ppermute | solution.py:180
  4.1 7.1 %collective-permute-start.8 = (bf16[1,1,32,1152]{3,2,1,0:T(8,128)(2,1)S(1)}, bf16[1,1,32,1152]{3,2,1,0:T(8,128)(2,1)S(1)}, u32[]{:S(2)}, u32[]{:S(2)}) collective-permute-start(bf16[1,1,32,1152]{3,2,1,0:T(8,128)(2,1)S(1)} %maximum_bitcast_fusion), channel_id=1, source_target_pairs={{0,8},{8,0},{16,24},{24,16},{1,9},{9,1},{17,25},{25,17},{2,10},{10... | collective-permute-start | bytes 221192 | tf_op jit(solution)/shard_map/ppermute | solution.py:180
  8.9 13.1 %collective-permute-start.2 = (bf16[1152,128]{1,0:T(8,128)(2,1)}, bf16[1152,128]{1,0:T(8,128)(2,1)S(1)}, u32[]{:S(2)}, u32[]{:S(2)}) collective-permute-start(bf16[1152,128]{1,0:T(8,128)(2,1)} %get-tuple-element.29), channel_id=1, source_target_pairs={{7,6},{15,14},{23,22},{31,30}} | collective-permute-start | bytes 884744 | tf_op jit(solution)/shard_map/ppermute | solution.py:287
  9.7 12.3 %collective-permute-start.1 = (bf16[1152,128]{1,0:T(8,128)(2,1)}, bf16[1152,128]{1,0:T(8,128)(2,1)S(1)}, u32[]{:S(2)}, u32[]{:S(2)}) collective-permute-start(bf16[1152,128]{1,0:T(8,128)(2,1)} %get-tuple-element.29), channel_id=1, source_target_pairs={{6,2},{7,3},{14,10},{15,11},{22,18},{23,19},{30,26},{31,27}} | collective-permute-start | bytes 884744 | tf_op jit(solution)/shard_map/ppermute | solution.py:217
  10.5 13.7 %collective-permute-start.6 = (bf16[1152,128]{1,0:T(8,128)(2,1)}, bf16[1152,128]{1,0:T(8,128)(2,1)S(1)}, u32[]{:S(2)}, u32[]{:S(2)}) collective-permute-start(bf16[1152,128]{1,0:T(8,128)(2,1)} %get-tuple-element.31), channel_id=1, source_target_pairs={{7,6},{15,14},{23,22},{31,30}} | collective-permute-start | bytes 884744 | tf_op jit(solution)/shard_map/ppermute | solution.py:287
  11.4 7.1 %collective-permute-start.9 = (bf16[1,2,32,1152]{3,2,1,0:T(8,128)(2,1)S(1)}, bf16[1,2,32,1152]{3,2,1,0:T(8,128)(2,1)S(1)}, u32[]{:S(2)}, u32[]{:S(2)}) collective-permute-start(bf16[1,2,32,1152]{3,2,1,0:T(8,128)(2,1)S(1)} %pad_maximum_fusion.16), channel_id=1, source_target_pairs={{0,16},{8,24},{16,0},{24,8},{1,17},{9,25},{17,1},{25,9},{2,18},{10... | collective-permute-start | bytes 442376 | tf_op jit(solution)/shard_map/ppermute | solution.py:180
  18.6 20.3 %collective-permute-start.11 = (bf16[128,128]{1,0:T(8,128)(2,1)S(1)}, bf16[128,128]{1,0:T(8,128)(2,1)S(1)}, u32[]{:S(2)}, u32[]{:S(2)}) collective-permute-start(bf16[128,128]{1,0:T(8,128)(2,1)S(1)} %slice.148), channel_id=1, source_target_pairs={{6,2},{7,3},{14,10},{15,11},{22,18},{23,19},{30,26},{31,27}} | collective-permute-start | bytes 98312 | tf_op jit(solution)/shard_map/ppermute | solution.py:217
  19.2 5.7 %collective-permute-start.10 = (bf16[1,2,32,1024]{3,2,1,0:T(8,128)(2,1)S(1)}, bf16[1,2,32,1024]{3,2,1,0:T(8,128)(2,1)S(1)}, u32[]{:S(2)}, u32[]{:S(2)}) collective-permute-start(bf16[1,2,32,1024]{3,2,1,0:T(8,128)(2,1)S(1)} %pad_maximum_fusion.17), channel_id=1, source_target_pairs={{0,16},{8,24},{16,0},{24,8},{1,17},{9,25},{17,1},{25,9},{2,18},{10... | collective-permute-start | bytes 393224 | tf_op jit(solution)/shard_map/ppermute | solution.py:180
  22.1 16.7 %collective-permute-start.3 = (bf16[1152,128]{1,0:T(8,128)(2,1)S(1)}, bf16[1152,128]{1,0:T(8,128)(2,1)S(1)}, u32[]{:S(2)}, u32[]{:S(2)}) collective-permute-start(bf16[1152,128]{1,0:T(8,128)(2,1)S(1)} %collective-permute-done.1), channel_id=1, source_target_pairs={{2,4},{3,5},{10,12},{11,13},{18,20},{19,21},{26,28},{27,29}} | collective-permute-start | bytes 884744 | tf_op jit(solution)/shard_map/ppermute | solution.py:217
  22.8 16.0 %collective-permute-start.4 = (bf16[1152,128]{1,0:T(8,128)(2,1)S(1)}, bf16[1152,128]{1,0:T(8,128)(2,1)S(1)}, u32[]{:S(2)}, u32[]{:S(2)}) collective-permute-start(bf16[1152,128]{1,0:T(8,128)(2,1)S(1)} %broadcast_select_fusion.3), channel_id=1, source_target_pairs={{6,2},{7,3},{2,0},{3,1},{14,10},{15,11},{10,8},{11,9},{22,18},{23,... | collective-permute-start | bytes 884744 | tf_op jit(solution)/shard_map/ppermute | solution.py:217
  24.2 31.5 %collective-permute-start.5 = (bf16[2048,128]{1,0:T(8,128)(2,1)S(1)}, bf16[2048,128]{1,0:T(8,128)(2,1)S(1)}, u32[]{:S(2)}, u32[]{:S(2)}) collective-permute-start(bf16[2048,128]{1,0:T(8,128)(2,1)S(1)} %copy-done.7), channel_id=1, source_target_pairs={{6,7},{14,15},{22,23},{30,31}} | collective-permute-start | bytes 1572872 | tf_op jit(solution)/shard_map/ppermute | solution.py:291
  38.9 10.8 %collective-permute-start.13 = (bf16[1152,128]{1,0:T(8,128)(2,1)S(1)}, bf16[1152,128]{1,0:T(8,128)(2,1)S(1)}, u32[]{:S(2)}, u32[]{:S(2)}) collective-permute-start(bf16[1152,128]{1,0:T(8,128)(2,1)S(1)} %constant_dynamic-update-slice_fusion), channel_id=1, source_target_pairs={{2,0},{3,1},{10,8},{11,9},{18,16},{19,17},{26,24},{27,25}} | collective-permute-start | bytes 884744 | tf_op jit(solution)/shard_map/ppermute | solution.py:217
  40.5 9.2 %collective-permute-start.12 = (bf16[1152,128]{1,0:T(8,128)(2,1)S(1)}, bf16[1152,128]{1,0:T(8,128)(2,1)S(1)}, u32[]{:S(2)}, u32[]{:S(2)}) collective-permute-start(bf16[1152,128]{1,0:T(8,128)(2,1)S(1)} %constant_dynamic-update-slice_fusion), channel_id=1, source_target_pairs={{2,4},{3,5},{10,12},{11,13},{18,20},{19,21},{26,28},{27,29}} | collective-permute-start | bytes 884744 | tf_op jit(solution)/shard_map/ppermute | solution.py:217
  41.2 12.4 %collective-permute-start.14 = (bf16[1152,128]{1,0:T(8,128)(2,1)S(1)}, bf16[1152,128]{1,0:T(8,128)(2,1)S(1)}, u32[]{:S(2)}, u32[]{:S(2)}) collective-permute-start(bf16[1152,128]{1,0:T(8,128)(2,1)S(1)} %select_select_fusion.1), channel_id=1, source_target_pairs={{0,1},{1,0},{2,3},{3,2},{4,5},{5,4},{8,9},{9,8},{10,11},{11,10},{1... | collective-permute-start | bytes 884744 | tf_op jit(solution)/shard_map/ppermute | solution.py:184
  49.8 12.8 %collective-permute-start.17 = (bf16[1152,128]{1,0:T(8,128)(2,1)S(1)}, bf16[1152,128]{1,0:T(8,128)(2,1)S(1)}, u32[]{:S(2)}, u32[]{:S(2)}) collective-permute-start(bf16[1152,128]{1,0:T(8,128)(2,1)S(1)} %get-tuple-element.58), channel_id=1, source_target_pairs={{0,1},{1,0},{2,3},{3,2},{4,5},{5,4},{8,9},{9,8},{10,11},{11,10},{1... | collective-permute-start | bytes 884744 | tf_op jit(solution)/shard_map/ppermute | solution.py:184
  54.6 2.3 %collective-permute-start.15 = (f32[256,128]{1,0:T(8,128)S(1)}, f32[256,128]{1,0:T(8,128)S(1)}, u32[]{:S(2)}, u32[]{:S(2)}) collective-permute-start(f32[256,128]{1,0:T(8,128)S(1)} %convolution_subtract_fusion.2), channel_id=1, source_target_pairs={{6,14},{7,15},{14,6},{15,7},{22,30},{23,31},{30,22},{31,23}} | collective-permute-start | bytes 393224 | tf_op jit(solution)/shard_map/ppermute | solution.py:318
  56.9 0.9 %collective-permute-start.16 = (bf16[256,128]{1,0:T(8,128)(2,1)S(1)}, bf16[256,128]{1,0:T(8,128)(2,1)S(1)}, u32[]{:S(2)}, u32[]{:S(2)}) collective-permute-start(bf16[256,128]{1,0:T(8,128)(2,1)S(1)} %add_convert_fusion.1), channel_id=1, source_target_pairs={{6,22},{7,23},{14,30},{15,31},{22,6},{23,7},{30,14},{31,15}} | collective-permute-start | bytes 196616 | tf_op jit(solution)/shard_map/ppermute | solution.py:318
  57.8 2.1 %collective-permute-start.18 = (bf16[256,128]{1,0:T(8,128)(2,1)S(1)}, bf16[256,128]{1,0:T(8,128)(2,1)S(1)}, u32[]{:S(2)}, u32[]{:S(2)}) collective-permute-start(bf16[256,128]{1,0:T(8,128)(2,1)S(1)} %add_convert_fusion), channel_id=1, source_target_pairs={{6,7},{7,6},{14,15},{15,14},{22,23},{23,22},{30,31},{31,30}} | collective-permute-start | bytes 196616 | tf_op jit(solution)/shard_map/ppermute | solution.py:184
  59.9 8.5 %collective-permute-start.21 = (bf16[384,128]{1,0:T(8,128)(2,1)S(1)}, bf16[384,128]{1,0:T(8,128)(2,1)S(1)}, u32[]{:S(2)}, u32[]{:S(2)}) collective-permute-start(bf16[384,128]{1,0:T(8,128)(2,1)S(1)} %pad_maximum_fusion.18), channel_id=1, source_target_pairs={{6,0},{7,1},{14,8},{15,9},{22,16},{23,17},{30,24},{31,25}} | collective-permute-start | bytes 294920 | tf_op jit(solution)/shard_map/ppermute | solution.py:217
  61.2 7.2 %collective-permute-start.20 = (bf16[384,128]{1,0:T(8,128)(2,1)S(1)}, bf16[384,128]{1,0:T(8,128)(2,1)S(1)}, u32[]{:S(2)}, u32[]{:S(2)}) collective-permute-start(bf16[384,128]{1,0:T(8,128)(2,1)S(1)} %pad_maximum_fusion.18), channel_id=1, source_target_pairs={{6,2},{7,3},{14,10},{15,11},{22,18},{23,19},{30,26},{31,27}} | collective-permute-start | bytes 294920 | tf_op jit(solution)/shard_map/ppermute | solution.py:217
  61.9 6.5 %collective-permute-start.19 = (bf16[384,128]{1,0:T(8,128)(2,1)S(1)}, bf16[384,128]{1,0:T(8,128)(2,1)S(1)}, u32[]{:S(2)}, u32[]{:S(2)}) collective-permute-start(bf16[384,128]{1,0:T(8,128)(2,1)S(1)} %pad_maximum_fusion.18), channel_id=1, source_target_pairs={{6,4},{7,5},{14,12},{15,13},{22,20},{23,21},{30,28},{31,29}} | collective-permute-start | bytes 294920 | tf_op jit(solution)/shard_map/ppermute | solution.py:217
  73.0 1.6 %collective-permute-start.22 = (bf16[2,2,32,1024]{3,2,0,1:T(8,128)(2,1)S(1)}, bf16[2,2,32,1024]{3,2,0,1:T(8,128)(2,1)S(1)}, u32[]{:S(2)}, u32[]{:S(2)}) collective-permute-start(bf16[2,2,32,1024]{3,2,0,1:T(8,128)(2,1)S(1)} %select_bitcast_fusion), channel_id=1, source_target_pairs={{0,8},{8,0},{16,24},{24,16},{1,9},{9,1},{17,25},{25,17},{2,10},{10... | collective-permute-start | bytes 786440 | tf_op jit(solution)/shard_map/ppermute | solution.py:180
  74.8 5.7 %collective-permute-start.23 = (bf16[2,1,32,1024]{3,2,1,0:T(8,128)(2,1)S(1)}, bf16[2,1,32,1024]{3,2,1,0:T(8,128)(2,1)S(1)}, u32[]{:S(2)}, u32[]{:S(2)}) collective-permute-start(bf16[2,1,32,1024]{3,2,1,0:T(8,128)(2,1)S(1)} %fusion.27), channel_id=1, source_target_pairs={{0,16},{8,24},{16,0},{24,8},{1,17},{9,25},{17,1},{25,9},{2,18},{10... | collective-permute-start | bytes 393224 | tf_op jit(solution)/shard_map/ppermute | solution.py:180
  (21 other events, 189.9 us)

commit v12 on v9

--- a/solution.py
+++ b/solution.py
@@ -282,7 +282,10 @@
         return jnp.concatenate([solved_two, tail.astype(BF16)], 1)
 
     early_two = [
-        lax.ppermute(packet, "col", [(two_owner, one_owner)]) for packet in packets
+        lax.ppermute(
+            packet if k == 0 else after(packet, side_cross), "col", [(two_owner, one_owner)]
+        )
+        for k, packet in enumerate(packets)
     ]
     full_one = gather_rest(after(near_one, full_two))
     first, arrived = spread(packets, [early_two[0], full_one], side_cross)

time: 76.5 us -> 77.8 us (1.017)
  the two profiles are of different devices: /device:TPU:21 before, /device:TPU:0 now
where the time goes in v12:
time: 77.8 us; the launch traced here: 77.1 us
  waiting for transfers between devices  30.7 us (39%)
  starting transfers between devices  26.9 us (35%)
  matrix products  9.47 us (12%)
  Pallas kernels  4.61 us (6%)
  other arithmetic  2.56 us (3%)
  between operations  1.69 us (2%)
  local copies, waits for them, and re-layouts  1.22 us (2%)
    ppermute x9, waiting for transfers between devices, hop(): return lax.ppermute(value, 'col', pairs)  22.7 us
    ppermute x3, starting transfers between devices, pair_swap(): return lax.ppermute(value, 'col', pairs)  8.36 us
    ppermute x9, starting transfers between devices, hop(): return lax.ppermute(value, 'col', pairs)  8.17 us
    ppermute x6, waiting for transfers between devices, row_swap(): return lax.ppermute(value, 'row', [(i, i ^ step) for i in range(row_count)])  7.96 us
    dot_general x10, matrix products, wide_dot(): return jnp.dot(a, b, preferred_element_type=F32)  7.17 us
    ppermute x6, starting transfers between devices, row_swap(): return lax.ppermute(value, 'row', [(i, i ^ step) for i in range(row_count)])  5.95 us
    pallas_call x1, Pallas kernels, prepare(): pl.pallas_call(functools.partial(prepare_kernel, cuts), in_specs=[pl.Bloc...  4.61 us
    dot_general x10, matrix products, exact_dot(): return jnp.dot(a, b, precision=EXACT, preferred_element_type=F32)  2.3 us
  transfers between devices with their start and end apart: 24, of which 8 were waited for; matrix products, arithmetic and copies ran while one was open for 9% of the time, Pallas kernels for 0%

profile of v12, /device:TPU:0, one launch (start us, length us, event | category | flops | bytes accessed | tf_op | source)
XLA Modules:
  0.0 77.1 jit_solution(8838236169261060063)
XLA Ops:
  0.7 4.6 %prepare.1 = (f32[128,128]{1,0:T(8,128)}, f32[128,128]{1,0:T(8,128)}, bf16[2048,128]{1,0:T(8,128)(2,1)}, bf16[1152,128]{1,0:T(8,128)(2,1)}, bf16[1152,128]{1,0:T(8,128)(2,1)}) custom-call(s32[1]{0:T(128)} %bitcast.side_ref, f32[128,128]{1,0:T(8,128)} %one_ref.1, f32[128,128]{1,0:T(8,128)} %two_ref.1, f32[2048,1024]{1,0:T(8,128)} %adj_ref.1), custom_call_target="tpu_custom_call" | custom-call | flops 268435456 | bytes 2097152 | tf_op jit(solution)/shard_map/prepare/pallas_call | solution.py:107
  5.3 0.8 %collective-permute-start.1 = (bf16[1152,128]{1,0:T(8,128)(2,1)}, bf16[1152,128]{1,0:T(8,128)(2,1)S(1)}, u32[]{:S(2)}, u32[]{:S(2)}) collective-permute-start(bf16[1152,128]{1,0:T(8,128)(2,1)} %get-tuple-element.28), channel_id=1, source_target_pairs={{7,6},{15,14},{23,22},{31,30}} | collective-permute-start | bytes 884744 | tf_op jit(solution)/shard_map/ppermute | solution.py:285
  7.5 0.8 %collective-permute-done.3 = bf16[1,1,32,1024]{3,2,1,0:T(8,128)(2,1)S(1)} collective-permute-done((bf16[1,1,32,1024]{3,2,1,0:T(8,128)(2,1)S(1)}, bf16[1,1,32,1024]{3,2,1,0:T(8,128)(2,1)S(1)}, u32[]{:S(2)}, u32[]{:S(2)}) %collective-permute-start.3) | collective-permute-done | bytes 65568 | tf_op jit(solution)/shard_map/ppermute | solution.py:180
  8.7 2.7 %collective-permute-start.4 = (bf16[1,2,32,1024]{3,2,1,0:T(8,128)(2,1)S(1)}, bf16[1,2,32,1024]{3,2,1,0:T(8,128)(2,1)S(1)}, u32[]{:S(2)}, u32[]{:S(2)}) collective-permute-start(bf16[1,2,32,1024]{3,2,1,0:T(8,128)(2,1)S(1)} %pad_maximum_fusion.18), channel_id=1, source_target_pairs={{0,16},{8,24},{16,0},{24,8},{1,17},{9,25},{17,1},{25,9},{2,18},{10... | collective-permute-start | bytes 393224 | tf_op jit(solution)/shard_map/ppermute | solution.py:180
  11.4 3.9 %collective-permute-done.4 = bf16[1,2,32,1024]{3,2,1,0:T(8,128)(2,1)S(1)} collective-permute-done((bf16[1,2,32,1024]{3,2,1,0:T(8,128)(2,1)S(1)}, bf16[1,2,32,1024]{3,2,1,0:T(8,128)(2,1)S(1)}, u32[]{:S(2)}, u32[]{:S(2)}) %collective-permute-start.4) | collective-permute-done | bytes 131104 | tf_op jit(solution)/shard_map/ppermute | solution.py:180
  16.1 1.8 %collective-permute-start.9 = (bf16[1,2,32,1024]{3,2,1,0:T(8,128)(2,1)S(1)}, bf16[1,2,32,1024]{3,2,1,0:T(8,128)(2,1)S(1)}, u32[]{:S(2)}, u32[]{:S(2)}) collective-permute-start(bf16[1,2,32,1024]{3,2,1,0:T(8,128)(2,1)S(1)} %pad_maximum_fusion.19), channel_id=1, source_target_pairs={{0,16},{8,24},{16,0},{24,8},{1,17},{9,25},{17,1},{25,9},{2,18},{10... | collective-permute-start | bytes 393224 | tf_op jit(solution)/shard_map/ppermute | solution.py:180
  20.3 1.3 %collective-permute-start.7 = (bf16[1152,128]{1,0:T(8,128)(2,1)S(1)}, bf16[1152,128]{1,0:T(8,128)(2,1)S(1)}, u32[]{:S(2)}, u32[]{:S(2)}) collective-permute-start(bf16[1152,128]{1,0:T(8,128)(2,1)S(1)} %broadcast_select_fusion.3), channel_id=1, source_target_pairs={{6,2},{7,3},{2,0},{3,1},{14,10},{15,11},{10,8},{11,9},{22,18},{23,... | collective-permute-start | bytes 884744 | tf_op jit(solution)/shard_map/ppermute | solution.py:217
  22.4 10.3 %collective-permute-done.7 = bf16[1152,128]{1,0:T(8,128)(2,1)S(1)} collective-permute-done((bf16[1152,128]{1,0:T(8,128)(2,1)S(1)}, bf16[1152,128]{1,0:T(8,128)(2,1)S(1)}, u32[]{:S(2)}, u32[]{:S(2)}) %collective-permute-start.7) | collective-permute-done | bytes 294944 | tf_op jit(solution)/shard_map/ppermute | solution.py:217
  32.8 1.6 %collective-permute-start.13 = (bf16[1152,128]{1,0:T(8,128)(2,1)S(1)}, bf16[1152,128]{1,0:T(8,128)(2,1)S(1)}, u32[]{:S(2)}, u32[]{:S(2)}) collective-permute-start(bf16[1152,128]{1,0:T(8,128)(2,1)S(1)} %constant_dynamic-update-slice_fusion), channel_id=1, source_target_pairs={{2,0},{3,1},{10,8},{11,9},{18,16},{19,17},{26,24},{27,25}} | collective-permute-start | bytes 884744 | tf_op jit(solution)/shard_map/ppermute | solution.py:217
  35.1 3.4 %collective-permute-start.14 = (bf16[1152,128]{1,0:T(8,128)(2,1)S(1)}, bf16[1152,128]{1,0:T(8,128)(2,1)S(1)}, u32[]{:S(2)}, u32[]{:S(2)}) collective-permute-start(bf16[1152,128]{1,0:T(8,128)(2,1)S(1)} %select_select_fusion.1), channel_id=1, source_target_pairs={{0,1},{1,0},{2,3},{3,2},{4,5},{5,4},{8,9},{9,8},{10,11},{11,10},{1... | collective-permute-start | bytes 884744 | tf_op jit(solution)/shard_map/ppermute | solution.py:184
  38.6 6.8 %collective-permute-done.13 = bf16[1152,128]{1,0:T(8,128)(2,1)S(1)} collective-permute-done((bf16[1152,128]{1,0:T(8,128)(2,1)S(1)}, bf16[1152,128]{1,0:T(8,128)(2,1)S(1)}, u32[]{:S(2)}, u32[]{:S(2)}) %collective-permute-start.13) | collective-permute-done | bytes 294944 | tf_op jit(solution)/shard_map/ppermute | solution.py:217
  45.5 4.3 %collective-permute-start.15 = (bf16[1152,128]{1,0:T(8,128)(2,1)S(1)}, bf16[1152,128]{1,0:T(8,128)(2,1)S(1)}, u32[]{:S(2)}, u32[]{:S(2)}) collective-permute-start(bf16[1152,128]{1,0:T(8,128)(2,1)S(1)} %get-tuple-element.56), channel_id=1, source_target_pairs={{0,1},{1,0},{2,3},{3,2},{4,5},{5,4},{8,9},{9,8},{10,11},{11,10},{1... | collective-permute-start | bytes 884744 | tf_op jit(solution)/shard_map/ppermute | solution.py:184
  50.8 0.8 %collective-permute-start.16 = (f32[256,128]{1,0:T(8,128)S(1)}, f32[256,128]{1,0:T(8,128)S(1)}, u32[]{:S(2)}, u32[]{:S(2)}) collective-permute-start(f32[256,128]{1,0:T(8,128)S(1)} %convolution_subtract_fusion.2), channel_id=1, source_target_pairs={{6,14},{7,15},{14,6},{15,7},{22,30},{23,31},{30,22},{31,23}} | collective-permute-start | bytes 393224 | tf_op jit(solution)/shard_map/ppermute | solution.py:319
  52.4 0.8 %collective-permute-start.17 = (bf16[256,128]{1,0:T(8,128)(2,1)S(1)}, bf16[256,128]{1,0:T(8,128)(2,1)S(1)}, u32[]{:S(2)}, u32[]{:S(2)}) collective-permute-start(bf16[256,128]{1,0:T(8,128)(2,1)S(1)} %add_convert_fusion.1), channel_id=1, source_target_pairs={{6,22},{7,23},{14,30},{15,31},{22,6},{23,7},{30,14},{31,15}} | collective-permute-start | bytes 196616 | tf_op jit(solution)/shard_map/ppermute | solution.py:319
  53.8 0.7 select_dynamic-update-slice_fusion.1
  55.2 0.7 fusion.2
  56.0 1.3 %collective-permute-start.21 = (bf16[384,128]{1,0:T(8,128)(2,1)S(1)}, bf16[384,128]{1,0:T(8,128)(2,1)S(1)}, u32[]{:S(2)}, u32[]{:S(2)}) collective-permute-start(bf16[384,128]{1,0:T(8,128)(2,1)S(1)} %pad_maximum_fusion.20), channel_id=1, source_target_pairs={{6,0},{7,1},{14,8},{15,9},{22,16},{23,17},{30,24},{31,25}} | collective-permute-start | bytes 294920 | tf_op jit(solution)/shard_map/ppermute | solution.py:217
  58.8 5.5 %collective-permute-done.21 = bf16[384,128]{1,0:T(8,128)(2,1)S(1)} collective-permute-done((bf16[384,128]{1,0:T(8,128)(2,1)S(1)}, bf16[384,128]{1,0:T(8,128)(2,1)S(1)}, u32[]{:S(2)}, u32[]{:S(2)}) %collective-permute-start.21) | collective-permute-done | bytes 98336 | tf_op jit(solution)/shard_map/ppermute | solution.py:217
  64.8 0.7 fusion.7
  69.5 1.1 %collective-permute-done.22 = bf16[2,2,32,1024]{3,2,0,1:T(8,128)(2,1)S(1)} collective-permute-done((bf16[2,2,32,1024]{3,2,0,1:T(8,128)(2,1)S(1)}, bf16[2,2,32,1024]{3,2,0,1:T(8,128)(2,1)S(1)}, u32[]{:S(2)}, u32[]{:S(2)}) %collective-permute-start.22) | collective-permute-done | bytes 262176 | tf_op jit(solution)/shard_map/ppermute | solution.py:180
  70.7 0.8 collective-permute-start.23
  71.6 3.0 %select_dynamic-update-slice_fusion = bf16[2048,1024]{1,0:T(8,128)(2,1)S(1)} fusion(bf16[2048,1024]{1,0:T(8,128)(2,1)S(1)} %copy-done.3, bf16[1024,128]{1,0:T(8,128)(2,1)S(1)} %slice_select_fusion.3, pred[1024]{0:T(1024)(128)(4,1)S(1)} %fusion.62, bf16[1024,256]{1,0:T(8,128)(2,1)S(1)} %pad_maximum_fusion.7, f32[2048,1024]{1,0:T(8,128)} %adj_ref.1, ...), kind=kOutput, calls=%fused_computation.2 | convolution fusion | flops 541065216 | bytes 7603200 | tf_op jit(solution)/shard_map/dot_general | solution.py:21
  74.5 1.8 %collective-permute-done.23 = bf16[2,1,32,1024]{3,2,1,0:T(8,128)(2,1)S(1)} collective-permute-done((bf16[2,1,32,1024]{3,2,1,0:T(8,128)(2,1)S(1)}, bf16[2,1,32,1024]{3,2,1,0:T(8,128)(2,1)S(1)}, u32[]{:S(2)}, u32[]{:S(2)}) %collective-permute-start.23) | collective-permute-done | bytes 131104 | tf_op jit(solution)/shard_map/ppermute | solution.py:180
  76.4 0.8 fusion.31
  (144 shorter events, 15.1 us)
Async XLA Ops:
  5.3 14.2 %collective-permute-start.1 = (bf16[1152,128]{1,0:T(8,128)(2,1)}, bf16[1152,128]{1,0:T(8,128)(2,1)S(1)}, u32[]{:S(2)}, u32[]{:S(2)}) collective-permute-start(bf16[1152,128]{1,0:T(8,128)(2,1)} %get-tuple-element.28), channel_id=1, source_target_pairs={{7,6},{15,14},{23,22},{31,30}} | collective-permute-start | bytes 884744 | tf_op jit(solution)/shard_map/ppermute | solution.py:285
  6.1 13.4 %collective-permute-start = (bf16[1152,128]{1,0:T(8,128)(2,1)}, bf16[1152,128]{1,0:T(8,128)(2,1)S(1)}, u32[]{:S(2)}, u32[]{:S(2)}) collective-permute-start(bf16[1152,128]{1,0:T(8,128)(2,1)} %get-tuple-element.28), channel_id=1, source_target_pairs={{6,2},{7,3},{14,10},{15,11},{22,18},{23,19},{30,26},{31,27}} | collective-permute-start | bytes 884744 | tf_op jit(solution)/shard_map/ppermute | solution.py:217
  6.8 1.4 %collective-permute-start.3 = (bf16[1,1,32,1024]{3,2,1,0:T(8,128)(2,1)S(1)}, bf16[1,1,32,1024]{3,2,1,0:T(8,128)(2,1)S(1)}, u32[]{:S(2)}, u32[]{:S(2)}) collective-permute-start(bf16[1,1,32,1024]{3,2,1,0:T(8,128)(2,1)S(1)} %bitcast.83), channel_id=1, source_target_pairs={{0,8},{8,0},{16,24},{24,16},{1,9},{9,1},{17,25},{25,17},{2,10},{10... | collective-permute-start | bytes 196616 | tf_op jit(solution)/shard_map/ppermute | solution.py:180
  7.3 1.3 %collective-permute-start.8 = (bf16[1,1,32,1024]{3,2,1,0:T(8,128)(2,1)S(1)}, bf16[1,1,32,1024]{3,2,1,0:T(8,128)(2,1)S(1)}, u32[]{:S(2)}, u32[]{:S(2)}) collective-permute-start(bf16[1,1,32,1024]{3,2,1,0:T(8,128)(2,1)S(1)} %bitcast.82), channel_id=1, source_target_pairs={{0,8},{8,0},{16,24},{24,16},{1,9},{9,1},{17,25},{25,17},{2,10},{10... | collective-permute-start | bytes 196616 | tf_op jit(solution)/shard_map/ppermute | solution.py:180
  8.7 6.7 %collective-permute-start.4 = (bf16[1,2,32,1024]{3,2,1,0:T(8,128)(2,1)S(1)}, bf16[1,2,32,1024]{3,2,1,0:T(8,128)(2,1)S(1)}, u32[]{:S(2)}, u32[]{:S(2)}) collective-permute-start(bf16[1,2,32,1024]{3,2,1,0:T(8,128)(2,1)S(1)} %pad_maximum_fusion.18), channel_id=1, source_target_pairs={{0,16},{8,24},{16,0},{24,8},{1,17},{9,25},{17,1},{25,9},{2,18},{10... | collective-permute-start | bytes 393224 | tf_op jit(solution)/shard_map/ppermute | solution.py:180
  15.5 2.7 %collective-permute-start.5 = (bf16[128,128]{1,0:T(8,128)(2,1)S(1)}, bf16[128,128]{1,0:T(8,128)(2,1)S(1)}, u32[]{:S(2)}, u32[]{:S(2)}) collective-permute-start(bf16[128,128]{1,0:T(8,128)(2,1)S(1)} %slice.129), channel_id=1, source_target_pairs={{6,7},{14,15},{22,23},{30,31}} | collective-permute-start | bytes 98312 | tf_op jit(solution)/shard_map/ppermute | solution.py:270
  16.1 5.5 %collective-permute-start.9 = (bf16[1,2,32,1024]{3,2,1,0:T(8,128)(2,1)S(1)}, bf16[1,2,32,1024]{3,2,1,0:T(8,128)(2,1)S(1)}, u32[]{:S(2)}, u32[]{:S(2)}) collective-permute-start(bf16[1,2,32,1024]{3,2,1,0:T(8,128)(2,1)S(1)} %pad_maximum_fusion.19), channel_id=1, source_target_pairs={{0,16},{8,24},{16,0},{24,8},{1,17},{9,25},{17,1},{25,9},{2,18},{10... | collective-permute-start | bytes 393224 | tf_op jit(solution)/shard_map/ppermute | solution.py:180
  18.2 14.7 %collective-permute-start.10 = (bf16[128,128]{1,0:T(8,128)(2,1)S(1)}, bf16[128,128]{1,0:T(8,128)(2,1)S(1)}, u32[]{:S(2)}, u32[]{:S(2)}) collective-permute-start(bf16[128,128]{1,0:T(8,128)(2,1)S(1)} %broadcast_select_fusion.16), channel_id=1, source_target_pairs={{6,2},{7,3},{14,10},{15,11},{22,18},{23,19},{30,26},{31,27}} | collective-permute-start | bytes 98312 | tf_op jit(solution)/shard_map/ppermute | solution.py:217
  18.8 3.6 %collective-permute-start.6 = (bf16[1152,128]{1,0:T(8,128)(2,1)S(1)}, bf16[1152,128]{1,0:T(8,128)(2,1)S(1)}, u32[]{:S(2)}, u32[]{:S(2)}) collective-permute-start(bf16[1152,128]{1,0:T(8,128)(2,1)S(1)} %copy-done.6), channel_id=1, source_target_pairs={{7,6},{15,14},{23,22},{31,30}} | collective-permute-start | bytes 884744 | tf_op jit(solution)/shard_map/ppermute | solution.py:285
  19.5 13.2 %collective-permute-start.12 = (bf16[1152,128]{1,0:T(8,128)(2,1)S(1)}, bf16[1152,128]{1,0:T(8,128)(2,1)S(1)}, u32[]{:S(2)}, u32[]{:S(2)}) collective-permute-start(bf16[1152,128]{1,0:T(8,128)(2,1)S(1)} %collective-permute-done), channel_id=1, source_target_pairs={{2,4},{3,5},{10,12},{11,13},{18,20},{19,21},{26,28},{27,29}} | collective-permute-start | bytes 884744 | tf_op jit(solution)/shard_map/ppermute | solution.py:217
  20.3 12.5 %collective-permute-start.7 = (bf16[1152,128]{1,0:T(8,128)(2,1)S(1)}, bf16[1152,128]{1,0:T(8,128)(2,1)S(1)}, u32[]{:S(2)}, u32[]{:S(2)}) collective-permute-start(bf16[1152,128]{1,0:T(8,128)(2,1)S(1)} %broadcast_select_fusion.3), channel_id=1, source_target_pairs={{6,2},{7,3},{2,0},{3,1},{14,10},{15,11},{10,8},{11,9},{22,18},{23,... | collective-permute-start | bytes 884744 | tf_op jit(solution)/shard_map/ppermute | solution.py:217
  21.6 30.2 %collective-permute-start.2 = (bf16[2048,128]{1,0:T(8,128)(2,1)S(1)}, bf16[2048,128]{1,0:T(8,128)(2,1)S(1)}, u32[]{:S(2)}, u32[]{:S(2)}) collective-permute-start(bf16[2048,128]{1,0:T(8,128)(2,1)S(1)} %copy-done.7), channel_id=1, source_target_pairs={{6,7},{14,15},{22,23},{30,31}} | collective-permute-start | bytes 1572872 | tf_op jit(solution)/shard_map/ppermute | solution.py:292
  32.8 12.6 %collective-permute-start.13 = (bf16[1152,128]{1,0:T(8,128)(2,1)S(1)}, bf16[1152,128]{1,0:T(8,128)(2,1)S(1)}, u32[]{:S(2)}, u32[]{:S(2)}) collective-permute-start(bf16[1152,128]{1,0:T(8,128)(2,1)S(1)} %constant_dynamic-update-slice_fusion), channel_id=1, source_target_pairs={{2,0},{3,1},{10,8},{11,9},{18,16},{19,17},{26,24},{27,25}} | collective-permute-start | bytes 884744 | tf_op jit(solution)/shard_map/ppermute | solution.py:217
  34.4 11.0 %collective-permute-start.11 = (bf16[1152,128]{1,0:T(8,128)(2,1)S(1)}, bf16[1152,128]{1,0:T(8,128)(2,1)S(1)}, u32[]{:S(2)}, u32[]{:S(2)}) collective-permute-start(bf16[1152,128]{1,0:T(8,128)(2,1)S(1)} %constant_dynamic-update-slice_fusion), channel_id=1, source_target_pairs={{2,4},{3,5},{10,12},{11,13},{18,20},{19,21},{26,28},{27,29}} | collective-permute-start | bytes 884744 | tf_op jit(solution)/shard_map/ppermute | solution.py:217
  35.1 14.6 %collective-permute-start.14 = (bf16[1152,128]{1,0:T(8,128)(2,1)S(1)}, bf16[1152,128]{1,0:T(8,128)(2,1)S(1)}, u32[]{:S(2)}, u32[]{:S(2)}) collective-permute-start(bf16[1152,128]{1,0:T(8,128)(2,1)S(1)} %select_select_fusion.1), channel_id=1, source_target_pairs={{0,1},{1,0},{2,3},{3,2},{4,5},{5,4},{8,9},{9,8},{10,11},{11,10},{1... | collective-permute-start | bytes 884744 | tf_op jit(solution)/shard_map/ppermute | solution.py:184
  45.5 13.2 %collective-permute-start.15 = (bf16[1152,128]{1,0:T(8,128)(2,1)S(1)}, bf16[1152,128]{1,0:T(8,128)(2,1)S(1)}, u32[]{:S(2)}, u32[]{:S(2)}) collective-permute-start(bf16[1152,128]{1,0:T(8,128)(2,1)S(1)} %get-tuple-element.56), channel_id=1, source_target_pairs={{0,1},{1,0},{2,3},{3,2},{4,5},{5,4},{8,9},{9,8},{10,11},{11,10},{1... | collective-permute-start | bytes 884744 | tf_op jit(solution)/shard_map/ppermute | solution.py:184
  50.8 1.5 %collective-permute-start.16 = (f32[256,128]{1,0:T(8,128)S(1)}, f32[256,128]{1,0:T(8,128)S(1)}, u32[]{:S(2)}, u32[]{:S(2)}) collective-permute-start(f32[256,128]{1,0:T(8,128)S(1)} %convolution_subtract_fusion.2), channel_id=1, source_target_pairs={{6,14},{7,15},{14,6},{15,7},{22,30},{23,31},{30,22},{31,23}} | collective-permute-start | bytes 393224 | tf_op jit(solution)/shard_map/ppermute | solution.py:319
  52.4 2.2 %collective-permute-start.17 = (bf16[256,128]{1,0:T(8,128)(2,1)S(1)}, bf16[256,128]{1,0:T(8,128)(2,1)S(1)}, u32[]{:S(2)}, u32[]{:S(2)}) collective-permute-start(bf16[256,128]{1,0:T(8,128)(2,1)S(1)} %add_convert_fusion.1), channel_id=1, source_target_pairs={{6,22},{7,23},{14,30},{15,31},{22,6},{23,7},{30,14},{31,15}} | collective-permute-start | bytes 196616 | tf_op jit(solution)/shard_map/ppermute | solution.py:319
  54.6 1.4 %collective-permute-start.18 = (bf16[256,128]{1,0:T(8,128)(2,1)S(1)}, bf16[256,128]{1,0:T(8,128)(2,1)S(1)}, u32[]{:S(2)}, u32[]{:S(2)}) collective-permute-start(bf16[256,128]{1,0:T(8,128)(2,1)S(1)} %add_convert_fusion), channel_id=1, source_target_pairs={{6,7},{7,6},{14,15},{15,14},{22,23},{23,22},{30,31},{31,30}} | collective-permute-start | bytes 196616 | tf_op jit(solution)/shard_map/ppermute | solution.py:184
  56.0 8.3 %collective-permute-start.21 = (bf16[384,128]{1,0:T(8,128)(2,1)S(1)}, bf16[384,128]{1,0:T(8,128)(2,1)S(1)}, u32[]{:S(2)}, u32[]{:S(2)}) collective-permute-start(bf16[384,128]{1,0:T(8,128)(2,1)S(1)} %pad_maximum_fusion.20), channel_id=1, source_target_pairs={{6,0},{7,1},{14,8},{15,9},{22,16},{23,17},{30,24},{31,25}} | collective-permute-start | bytes 294920 | tf_op jit(solution)/shard_map/ppermute | solution.py:217
  57.3 7.0 %collective-permute-start.20 = (bf16[384,128]{1,0:T(8,128)(2,1)S(1)}, bf16[384,128]{1,0:T(8,128)(2,1)S(1)}, u32[]{:S(2)}, u32[]{:S(2)}) collective-permute-start(bf16[384,128]{1,0:T(8,128)(2,1)S(1)} %pad_maximum_fusion.20), channel_id=1, source_target_pairs={{6,2},{7,3},{14,10},{15,11},{22,18},{23,19},{30,26},{31,27}} | collective-permute-start | bytes 294920 | tf_op jit(solution)/shard_map/ppermute | solution.py:217
  58.0 6.3 %collective-permute-start.19 = (bf16[384,128]{1,0:T(8,128)(2,1)S(1)}, bf16[384,128]{1,0:T(8,128)(2,1)S(1)}, u32[]{:S(2)}, u32[]{:S(2)}) collective-permute-start(bf16[384,128]{1,0:T(8,128)(2,1)S(1)} %pad_maximum_fusion.20), channel_id=1, source_target_pairs={{6,4},{7,5},{14,12},{15,13},{22,20},{23,21},{30,28},{31,29}} | collective-permute-start | bytes 294920 | tf_op jit(solution)/shard_map/ppermute | solution.py:217
  69.0 1.6 %collective-permute-start.22 = (bf16[2,2,32,1024]{3,2,0,1:T(8,128)(2,1)S(1)}, bf16[2,2,32,1024]{3,2,0,1:T(8,128)(2,1)S(1)}, u32[]{:S(2)}, u32[]{:S(2)}) collective-permute-start(bf16[2,2,32,1024]{3,2,0,1:T(8,128)(2,1)S(1)} %select_bitcast_fusion), channel_id=1, source_target_pairs={{0,8},{8,0},{16,24},{24,16},{1,9},{9,1},{17,25},{25,17},{2,10},{10... | collective-permute-start | bytes 786440 | tf_op jit(solution)/shard_map/ppermute | solution.py:180
  70.7 5.6 %collective-permute-start.23 = (bf16[2,1,32,1024]{3,2,1,0:T(8,128)(2,1)S(1)}, bf16[2,1,32,1024]{3,2,1,0:T(8,128)(2,1)S(1)}, u32[]{:S(2)}, u32[]{:S(2)}) collective-permute-start(bf16[2,1,32,1024]{3,2,1,0:T(8,128)(2,1)S(1)} %fusion.29), channel_id=1, source_target_pairs={{0,16},{8,24},{16,0},{24,8},{1,17},{9,25},{17,1},{25,9},{2,18},{10... | collective-permute-start | bytes 393224 | tf_op jit(solution)/shard_map/ppermute | solution.py:180
  (21 other events, 166.7 us)

commit v13 on v9

--- a/solution.py
+++ b/solution.py
@@ -356,7 +356,7 @@
     diag_term_one = whole_terms[2 * panel :]
 
     start, stop = cuts[-1]
-    theirs = after(other[-1], terms, sums)
+    theirs = after(other[-1], sums)
     both = panels_of(own[-1], theirs, factor, stop - start)
     sums = (sums + wide_dot(both.T, trail[start:stop])).astype(BF16)
 

time: 76.5 us -> 74.1 us (0.969)
  the two profiles are of different devices: /device:TPU:21 before, /device:TPU:20 now
where the time goes in v13:
time: 74.1 us; the launch traced here: 73.6 us
  waiting for transfers between devices  29 us (39%)
  starting transfers between devices  24.2 us (33%)
  matrix products  9.4 us (13%)
  Pallas kernels  4.6 us (6%)
  other arithmetic  2.99 us (4%)
  local copies, waits for them, and re-layouts  1.75 us (2%)
  between operations  1.75 us (2%)
    ppermute x9, waiting for transfers between devices, hop(): return lax.ppermute(value, 'col', pairs)  24.2 us
    ppermute x9, starting transfers between devices, hop(): return lax.ppermute(value, 'col', pairs)  8.17 us
    dot_general x10, matrix products, wide_dot(): return jnp.dot(a, b, preferred_element_type=F32)  7.11 us
    ppermute x3, starting transfers between devices, pair_swap(): return lax.ppermute(value, 'col', pairs)  6.28 us
    ppermute x6, starting transfers between devices, row_swap(): return lax.ppermute(value, 'row', [(i, i ^ step) for i in range(row_count)])  5.29 us
    ppermute x6, waiting for transfers between devices, row_swap(): return lax.ppermute(value, 'row', [(i, i ^ step) for i in range(row_count)])  4.74 us
    pallas_call x1, Pallas kernels, prepare(): pl.pallas_call(functools.partial(prepare_kernel, cuts), in_specs=[pl.Bloc...  4.6 us
    dot_general x10, matrix products, exact_dot(): return jnp.dot(a, b, precision=EXACT, preferred_element_type=F32)  2.29 us
  transfers between devices with their start and end apart: 24, of which 6 were waited for; matrix products, arithmetic and copies ran while one was open for 16% of the time, Pallas kernels for 0%

profile of v13, /device:TPU:20, one launch (start us, length us, event | category | flops | bytes accessed | tf_op | source)
XLA Modules:
  0.0 73.6 jit_solution(9820750670440317501)
XLA Ops:
  0.7 4.6 %prepare.1 = (f32[128,128]{1,0:T(8,128)}, f32[128,128]{1,0:T(8,128)}, bf16[2048,128]{1,0:T(8,128)(2,1)}, bf16[1152,128]{1,0:T(8,128)(2,1)}, bf16[1152,128]{1,0:T(8,128)(2,1)}) custom-call(s32[1]{0:T(128)} %bitcast.side_ref, f32[128,128]{1,0:T(8,128)} %one_ref.1, f32[128,128]{1,0:T(8,128)} %two_ref.1, f32[2048,1024]{1,0:T(8,128)} %adj_ref.1), custom_call_target="tpu_custom_call" | custom-call | flops 268435456 | bytes 2097152 | tf_op jit(solution)/shard_map/prepare/pallas_call | solution.py:107
  5.3 0.8 %collective-permute-start.1 = (bf16[1152,128]{1,0:T(8,128)(2,1)}, bf16[1152,128]{1,0:T(8,128)(2,1)S(1)}, u32[]{:S(2)}, u32[]{:S(2)}) collective-permute-start(bf16[1152,128]{1,0:T(8,128)(2,1)} %get-tuple-element.27), channel_id=1, source_target_pairs={{7,6},{15,14},{23,22},{31,30}} | collective-permute-start | bytes 884744 | tf_op jit(solution)/shard_map/ppermute | solution.py:285
  6.1 0.7 collective-permute-start
  8.4 1.6 %collective-permute-start.7 = (bf16[1,2,32,1024]{3,2,1,0:T(8,128)(2,1)S(1)}, bf16[1,2,32,1024]{3,2,1,0:T(8,128)(2,1)S(1)}, u32[]{:S(2)}, u32[]{:S(2)}) collective-permute-start(bf16[1,2,32,1024]{3,2,1,0:T(8,128)(2,1)S(1)} %pad_maximum_fusion.19), channel_id=1, source_target_pairs={{0,16},{8,24},{16,0},{24,8},{1,17},{9,25},{17,1},{25,9},{2,18},{10... | collective-permute-start | bytes 393224 | tf_op jit(solution)/shard_map/ppermute | solution.py:180
  10.0 4.2 %collective-permute-done.7 = bf16[1,2,32,1024]{3,2,1,0:T(8,128)(2,1)S(1)} collective-permute-done((bf16[1,2,32,1024]{3,2,1,0:T(8,128)(2,1)S(1)}, bf16[1,2,32,1024]{3,2,1,0:T(8,128)(2,1)S(1)}, u32[]{:S(2)}, u32[]{:S(2)}) %collective-permute-start.7) | collective-permute-done | bytes 131104 | tf_op jit(solution)/shard_map/ppermute | solution.py:180
  14.9 1.6 %collective-permute-start.8 = (bf16[1,2,32,1024]{3,2,1,0:T(8,128)(2,1)S(1)}, bf16[1,2,32,1024]{3,2,1,0:T(8,128)(2,1)S(1)}, u32[]{:S(2)}, u32[]{:S(2)}) collective-permute-start(bf16[1,2,32,1024]{3,2,1,0:T(8,128)(2,1)S(1)} %pad_maximum_fusion.18), channel_id=1, source_target_pairs={{0,16},{8,24},{16,0},{24,8},{1,17},{9,25},{17,1},{25,9},{2,18},{10... | collective-permute-start | bytes 393224 | tf_op jit(solution)/shard_map/ppermute | solution.py:180
  17.4 1.3 %collective-permute-start.12 = (bf16[1152,128]{1,0:T(8,128)(2,1)S(1)}, bf16[1152,128]{1,0:T(8,128)(2,1)S(1)}, u32[]{:S(2)}, u32[]{:S(2)}) collective-permute-start(bf16[1152,128]{1,0:T(8,128)(2,1)S(1)} %collective-permute-done), channel_id=1, source_target_pairs={{2,4},{3,5},{10,12},{11,13},{18,20},{19,21},{26,28},{27,29}} | collective-permute-start | bytes 884744 | tf_op jit(solution)/shard_map/ppermute | solution.py:217
  19.5 0.7 collective-permute-start.2
  20.3 7.2 %collective-permute-done.12 = bf16[1152,128]{1,0:T(8,128)(2,1)S(1)} collective-permute-done((bf16[1152,128]{1,0:T(8,128)(2,1)S(1)}, bf16[1152,128]{1,0:T(8,128)(2,1)S(1)}, u32[]{:S(2)}, u32[]{:S(2)}) %collective-permute-start.12) | collective-permute-done | bytes 294944 | tf_op jit(solution)/shard_map/ppermute | solution.py:217
  27.6 0.8 %collective-permute-start.13 = (bf16[1152,128]{1,0:T(8,128)(2,1)S(1)}, bf16[1152,128]{1,0:T(8,128)(2,1)S(1)}, u32[]{:S(2)}, u32[]{:S(2)}) collective-permute-start(bf16[1152,128]{1,0:T(8,128)(2,1)S(1)} %constant_dynamic-update-slice_fusion), channel_id=1, source_target_pairs={{2,0},{3,1},{10,8},{11,9},{18,16},{19,17},{26,24},{27,25}} | collective-permute-start | bytes 884744 | tf_op jit(solution)/shard_map/ppermute | solution.py:217
  28.4 1.4 %collective-permute-start.11 = (bf16[1152,128]{1,0:T(8,128)(2,1)S(1)}, bf16[1152,128]{1,0:T(8,128)(2,1)S(1)}, u32[]{:S(2)}, u32[]{:S(2)}) collective-permute-start(bf16[1152,128]{1,0:T(8,128)(2,1)S(1)} %constant_dynamic-update-slice_fusion), channel_id=1, source_target_pairs={{2,4},{3,5},{10,12},{11,13},{18,20},{19,21},{26,28},{27,29}} | collective-permute-start | bytes 884744 | tf_op jit(solution)/shard_map/ppermute | solution.py:217
  29.9 2.4 %collective-permute-start.14 = (bf16[1152,128]{1,0:T(8,128)(2,1)S(1)}, bf16[1152,128]{1,0:T(8,128)(2,1)S(1)}, u32[]{:S(2)}, u32[]{:S(2)}) collective-permute-start(bf16[1152,128]{1,0:T(8,128)(2,1)S(1)} %select_select_fusion.1), channel_id=1, source_target_pairs={{0,1},{1,0},{2,3},{3,2},{4,5},{5,4},{8,9},{9,8},{10,11},{11,10},{1... | collective-permute-start | bytes 884744 | tf_op jit(solution)/shard_map/ppermute | solution.py:184
  32.4 9.7 %collective-permute-done.11 = bf16[1152,128]{1,0:T(8,128)(2,1)S(1)} collective-permute-done((bf16[1152,128]{1,0:T(8,128)(2,1)S(1)}, bf16[1152,128]{1,0:T(8,128)(2,1)S(1)}, u32[]{:S(2)}, u32[]{:S(2)}) %collective-permute-start.11) | collective-permute-done | bytes 294944 | tf_op jit(solution)/shard_map/ppermute | solution.py:217
  42.1 3.2 %collective-permute-start.15 = (bf16[1152,128]{1,0:T(8,128)(2,1)S(1)}, bf16[1152,128]{1,0:T(8,128)(2,1)S(1)}, u32[]{:S(2)}, u32[]{:S(2)}) collective-permute-start(bf16[1152,128]{1,0:T(8,128)(2,1)S(1)} %get-tuple-element.52), channel_id=1, source_target_pairs={{0,1},{1,0},{2,3},{3,2},{4,5},{5,4},{8,9},{9,8},{10,11},{11,10},{1... | collective-permute-start | bytes 884744 | tf_op jit(solution)/shard_map/ppermute | solution.py:184
  46.4 0.8 %collective-permute-start.17 = (f32[256,128]{1,0:T(8,128)S(1)}, f32[256,128]{1,0:T(8,128)S(1)}, u32[]{:S(2)}, u32[]{:S(2)}) collective-permute-start(f32[256,128]{1,0:T(8,128)S(1)} %convolution_subtract_fusion.2), channel_id=1, source_target_pairs={{6,14},{7,15},{14,6},{15,7},{22,30},{23,31},{30,22},{31,23}} | collective-permute-start | bytes 393224 | tf_op jit(solution)/shard_map/ppermute | solution.py:316
  47.9 0.8 %collective-permute-start.18 = (bf16[256,128]{1,0:T(8,128)(2,1)S(1)}, bf16[256,128]{1,0:T(8,128)(2,1)S(1)}, u32[]{:S(2)}, u32[]{:S(2)}) collective-permute-start(bf16[256,128]{1,0:T(8,128)(2,1)S(1)} %add_convert_fusion.1), channel_id=1, source_target_pairs={{6,22},{7,23},{14,30},{15,31},{22,6},{23,7},{30,14},{31,15}} | collective-permute-start | bytes 196616 | tf_op jit(solution)/shard_map/ppermute | solution.py:316
  49.3 0.7 select_dynamic-update-slice_fusion.1
  50.8 0.7 fusion.2
  52.9 1.3 %collective-permute-start.20 = (bf16[384,128]{1,0:T(8,128)(2,1)S(1)}, bf16[384,128]{1,0:T(8,128)(2,1)S(1)}, u32[]{:S(2)}, u32[]{:S(2)}) collective-permute-start(bf16[384,128]{1,0:T(8,128)(2,1)S(1)} %pad_maximum_fusion.20), channel_id=1, source_target_pairs={{6,4},{7,5},{14,12},{15,13},{22,20},{23,21},{30,28},{31,29}} | collective-permute-start | bytes 294920 | tf_op jit(solution)/shard_map/ppermute | solution.py:217
  54.7 0.7 %fusion.7 = bf16[256,1024]{1,0:T(8,128)(2,1)S(1)} fusion(f32[256,1024]{1,0:T(8,128)S(1)} %fusion.2, bf16[2048,1024]{1,0:T(8,128)(2,1)S(1)} %copy-done, bf16[1024,128]{1,0:T(8,128)(2,1)S(1)} %broadcast_select_fusion.4, bf16[1024,128]{1,0:T(8,128)(2,1)S(1)} %fusion.11), kind=kOutput, calls=%fused_computation.9 | convolution fusion | flops 538443776 | bytes 4194304 | tf_op jit(solution)/shard_map/dot_general | solution.py:21
  55.7 7.3 %collective-permute-done.20 = bf16[384,128]{1,0:T(8,128)(2,1)S(1)} collective-permute-done((bf16[384,128]{1,0:T(8,128)(2,1)S(1)}, bf16[384,128]{1,0:T(8,128)(2,1)S(1)}, u32[]{:S(2)}, u32[]{:S(2)}) %collective-permute-start.20) | collective-permute-done | bytes 98336 | tf_op jit(solution)/shard_map/ppermute | solution.py:217
  66.9 1.6 %collective-permute-start.23 = (bf16[2,1,32,1024]{3,2,1,0:T(8,128)(2,1)S(1)}, bf16[2,1,32,1024]{3,2,1,0:T(8,128)(2,1)S(1)}, u32[]{:S(2)}, u32[]{:S(2)}) collective-permute-start(bf16[2,1,32,1024]{3,2,1,0:T(8,128)(2,1)S(1)} %fusion.29), channel_id=1, source_target_pairs={{0,16},{8,24},{16,0},{24,8},{1,17},{9,25},{17,1},{25,9},{2,18},{10... | collective-permute-start | bytes 393224 | tf_op jit(solution)/shard_map/ppermute | solution.py:180
  68.6 2.9 %select_dynamic-update-slice_fusion = bf16[2048,1024]{1,0:T(8,128)(2,1)S(1)} fusion(bf16[2048,1024]{1,0:T(8,128)(2,1)S(1)} %copy-done.3, bf16[1024,128]{1,0:T(8,128)(2,1)S(1)} %slice_select_fusion.3, pred[1024]{0:T(1024)(128)(4,1)S(1)} %fusion.62, bf16[1024,256]{1,0:T(8,128)(2,1)S(1)} %pad_maximum_fusion.7, f32[2048,1024]{1,0:T(8,128)} %adj_ref.1, ...), kind=kOutput, calls=%fused_computation.2 | convolution fusion | flops 541065216 | bytes 7603200 | tf_op jit(solution)/shard_map/dot_general | solution.py:21
  72.0 1.2 %fusion.31 = (f32[32,1024]{1,0:T(8,128)}, f32[32,1024]{1,0:T(8,128)}) fusion(f32[2,1,32,1024]{3,2,1,0:T(8,128)S(1)} %bitcast_add_fusion, f32[32,1024]{1,0:T(8,128)S(1)} %copy-done.12, f32[64,1024]{1,0:T(8,128)S(1)} %fusion.17, f32[32,128]{1,0:T(8,128)S(1)} %get-tuple-element.47, pred[1024]{0:T(1024)(128)(4,1)S(1)} %fusion.62, f32[32,1024]{1,0:T(8,128)S(1)} %copy-done.13, ...), kind=kLoop, calls=%fused_computation.67 | loop fusion | flops 196608 | bytes 1070080 | tf_op jit(solution)/shard_map/jit(_where)/select_n | solution.py:334
  (144 shorter events, 13.7 us)
Async XLA Ops:
  5.3 12.1 %collective-permute-start.1 = (bf16[1152,128]{1,0:T(8,128)(2,1)}, bf16[1152,128]{1,0:T(8,128)(2,1)S(1)}, u32[]{:S(2)}, u32[]{:S(2)}) collective-permute-start(bf16[1152,128]{1,0:T(8,128)(2,1)} %get-tuple-element.27), channel_id=1, source_target_pairs={{7,6},{15,14},{23,22},{31,30}} | collective-permute-start | bytes 884744 | tf_op jit(solution)/shard_map/ppermute | solution.py:285
  6.1 11.3 %collective-permute-start = (bf16[1152,128]{1,0:T(8,128)(2,1)}, bf16[1152,128]{1,0:T(8,128)(2,1)S(1)}, u32[]{:S(2)}, u32[]{:S(2)}) collective-permute-start(bf16[1152,128]{1,0:T(8,128)(2,1)} %get-tuple-element.27), channel_id=1, source_target_pairs={{6,2},{7,3},{14,10},{15,11},{22,18},{23,19},{30,26},{31,27}} | collective-permute-start | bytes 884744 | tf_op jit(solution)/shard_map/ppermute | solution.py:217
  6.8 1.3 %collective-permute-start.6 = (bf16[1,1,32,1024]{3,2,1,0:T(8,128)(2,1)S(1)}, bf16[1,1,32,1024]{3,2,1,0:T(8,128)(2,1)S(1)}, u32[]{:S(2)}, u32[]{:S(2)}) collective-permute-start(bf16[1,1,32,1024]{3,2,1,0:T(8,128)(2,1)S(1)} %bitcast.82), channel_id=1, source_target_pairs={{0,8},{8,0},{16,24},{24,16},{1,9},{9,1},{17,25},{25,17},{2,10},{10... | collective-permute-start | bytes 196616 | tf_op jit(solution)/shard_map/ppermute | solution.py:180
  6.9 1.4 %collective-permute-start.5 = (bf16[1,1,32,1024]{3,2,1,0:T(8,128)(2,1)S(1)}, bf16[1,1,32,1024]{3,2,1,0:T(8,128)(2,1)S(1)}, u32[]{:S(2)}, u32[]{:S(2)}) collective-permute-start(bf16[1,1,32,1024]{3,2,1,0:T(8,128)(2,1)S(1)} %bitcast.83), channel_id=1, source_target_pairs={{0,8},{8,0},{16,24},{24,16},{1,9},{9,1},{17,25},{25,17},{2,10},{10... | collective-permute-start | bytes 196616 | tf_op jit(solution)/shard_map/ppermute | solution.py:180
  7.4 12.1 %collective-permute-start.3 = (bf16[1152,128]{1,0:T(8,128)(2,1)}, bf16[1152,128]{1,0:T(8,128)(2,1)S(1)}, u32[]{:S(2)}, u32[]{:S(2)}) collective-permute-start(bf16[1152,128]{1,0:T(8,128)(2,1)} %get-tuple-element.30), channel_id=1, source_target_pairs={{7,6},{15,14},{23,22},{31,30}} | collective-permute-start | bytes 884744 | tf_op jit(solution)/shard_map/ppermute | solution.py:285
  8.4 5.8 %collective-permute-start.7 = (bf16[1,2,32,1024]{3,2,1,0:T(8,128)(2,1)S(1)}, bf16[1,2,32,1024]{3,2,1,0:T(8,128)(2,1)S(1)}, u32[]{:S(2)}, u32[]{:S(2)}) collective-permute-start(bf16[1,2,32,1024]{3,2,1,0:T(8,128)(2,1)S(1)} %pad_maximum_fusion.19), channel_id=1, source_target_pairs={{0,16},{8,24},{16,0},{24,8},{1,17},{9,25},{17,1},{25,9},{2,18},{10... | collective-permute-start | bytes 393224 | tf_op jit(solution)/shard_map/ppermute | solution.py:180
  14.3 2.4 %collective-permute-start.9 = (bf16[128,128]{1,0:T(8,128)(2,1)S(1)}, bf16[128,128]{1,0:T(8,128)(2,1)S(1)}, u32[]{:S(2)}, u32[]{:S(2)}) collective-permute-start(bf16[128,128]{1,0:T(8,128)(2,1)S(1)} %slice.130), channel_id=1, source_target_pairs={{6,7},{14,15},{22,23},{30,31}} | collective-permute-start | bytes 98312 | tf_op jit(solution)/shard_map/ppermute | solution.py:270
  14.9 5.3 %collective-permute-start.8 = (bf16[1,2,32,1024]{3,2,1,0:T(8,128)(2,1)S(1)}, bf16[1,2,32,1024]{3,2,1,0:T(8,128)(2,1)S(1)}, u32[]{:S(2)}, u32[]{:S(2)}) collective-permute-start(bf16[1,2,32,1024]{3,2,1,0:T(8,128)(2,1)S(1)} %pad_maximum_fusion.18), channel_id=1, source_target_pairs={{0,16},{8,24},{16,0},{24,8},{1,17},{9,25},{17,1},{25,9},{2,18},{10... | collective-permute-start | bytes 393224 | tf_op jit(solution)/shard_map/ppermute | solution.py:180
  16.7 10.9 %collective-permute-start.10 = (bf16[128,128]{1,0:T(8,128)(2,1)S(1)}, bf16[128,128]{1,0:T(8,128)(2,1)S(1)}, u32[]{:S(2)}, u32[]{:S(2)}) collective-permute-start(bf16[128,128]{1,0:T(8,128)(2,1)S(1)} %broadcast_select_fusion.16), channel_id=1, source_target_pairs={{6,2},{7,3},{14,10},{15,11},{22,18},{23,19},{30,26},{31,27}} | collective-permute-start | bytes 98312 | tf_op jit(solution)/shard_map/ppermute | solution.py:217
  17.4 10.1 %collective-permute-start.12 = (bf16[1152,128]{1,0:T(8,128)(2,1)S(1)}, bf16[1152,128]{1,0:T(8,128)(2,1)S(1)}, u32[]{:S(2)}, u32[]{:S(2)}) collective-permute-start(bf16[1152,128]{1,0:T(8,128)(2,1)S(1)} %collective-permute-done), channel_id=1, source_target_pairs={{2,4},{3,5},{10,12},{11,13},{18,20},{19,21},{26,28},{27,29}} | collective-permute-start | bytes 884744 | tf_op jit(solution)/shard_map/ppermute | solution.py:217
  18.7 1.5 %collective-permute-start.4 = (bf16[1152,128]{1,0:T(8,128)(2,1)S(1)}, bf16[1152,128]{1,0:T(8,128)(2,1)S(1)}, u32[]{:S(2)}, u32[]{:S(2)}) collective-permute-start(bf16[1152,128]{1,0:T(8,128)(2,1)S(1)} %broadcast_select_fusion.3), channel_id=1, source_target_pairs={{6,2},{7,3},{2,0},{3,1},{14,10},{15,11},{10,8},{11,9},{22,18},{23,... | collective-permute-start | bytes 884744 | tf_op jit(solution)/shard_map/ppermute | solution.py:217
  19.5 27.9 %collective-permute-start.2 = (bf16[2048,128]{1,0:T(8,128)(2,1)S(1)}, bf16[2048,128]{1,0:T(8,128)(2,1)S(1)}, u32[]{:S(2)}, u32[]{:S(2)}) collective-permute-start(bf16[2048,128]{1,0:T(8,128)(2,1)S(1)} %copy-done.7), channel_id=1, source_target_pairs={{6,7},{14,15},{22,23},{30,31}} | collective-permute-start | bytes 1572872 | tf_op jit(solution)/shard_map/ppermute | solution.py:289
  27.6 4.8 %collective-permute-start.13 = (bf16[1152,128]{1,0:T(8,128)(2,1)S(1)}, bf16[1152,128]{1,0:T(8,128)(2,1)S(1)}, u32[]{:S(2)}, u32[]{:S(2)}) collective-permute-start(bf16[1152,128]{1,0:T(8,128)(2,1)S(1)} %constant_dynamic-update-slice_fusion), channel_id=1, source_target_pairs={{2,0},{3,1},{10,8},{11,9},{18,16},{19,17},{26,24},{27,25}} | collective-permute-start | bytes 884744 | tf_op jit(solution)/shard_map/ppermute | solution.py:217
  28.4 13.7 %collective-permute-start.11 = (bf16[1152,128]{1,0:T(8,128)(2,1)S(1)}, bf16[1152,128]{1,0:T(8,128)(2,1)S(1)}, u32[]{:S(2)}, u32[]{:S(2)}) collective-permute-start(bf16[1152,128]{1,0:T(8,128)(2,1)S(1)} %constant_dynamic-update-slice_fusion), channel_id=1, source_target_pairs={{2,4},{3,5},{10,12},{11,13},{18,20},{19,21},{26,28},{27,29}} | collective-permute-start | bytes 884744 | tf_op jit(solution)/shard_map/ppermute | solution.py:217
  29.9 15.5 %collective-permute-start.14 = (bf16[1152,128]{1,0:T(8,128)(2,1)S(1)}, bf16[1152,128]{1,0:T(8,128)(2,1)S(1)}, u32[]{:S(2)}, u32[]{:S(2)}) collective-permute-start(bf16[1152,128]{1,0:T(8,128)(2,1)S(1)} %select_select_fusion.1), channel_id=1, source_target_pairs={{0,1},{1,0},{2,3},{3,2},{4,5},{5,4},{8,9},{9,8},{10,11},{11,10},{1... | collective-permute-start | bytes 884744 | tf_op jit(solution)/shard_map/ppermute | solution.py:184
  42.1 12.1 %collective-permute-start.15 = (bf16[1152,128]{1,0:T(8,128)(2,1)S(1)}, bf16[1152,128]{1,0:T(8,128)(2,1)S(1)}, u32[]{:S(2)}, u32[]{:S(2)}) collective-permute-start(bf16[1152,128]{1,0:T(8,128)(2,1)S(1)} %get-tuple-element.52), channel_id=1, source_target_pairs={{0,1},{1,0},{2,3},{3,2},{4,5},{5,4},{8,9},{9,8},{10,11},{11,10},{1... | collective-permute-start | bytes 884744 | tf_op jit(solution)/shard_map/ppermute | solution.py:184
  46.4 1.5 %collective-permute-start.17 = (f32[256,128]{1,0:T(8,128)S(1)}, f32[256,128]{1,0:T(8,128)S(1)}, u32[]{:S(2)}, u32[]{:S(2)}) collective-permute-start(f32[256,128]{1,0:T(8,128)S(1)} %convolution_subtract_fusion.2), channel_id=1, source_target_pairs={{6,14},{7,15},{14,6},{15,7},{22,30},{23,31},{30,22},{31,23}} | collective-permute-start | bytes 393224 | tf_op jit(solution)/shard_map/ppermute | solution.py:316
  47.9 2.2 %collective-permute-start.18 = (bf16[256,128]{1,0:T(8,128)(2,1)S(1)}, bf16[256,128]{1,0:T(8,128)(2,1)S(1)}, u32[]{:S(2)}, u32[]{:S(2)}) collective-permute-start(bf16[256,128]{1,0:T(8,128)(2,1)S(1)} %add_convert_fusion.1), channel_id=1, source_target_pairs={{6,22},{7,23},{14,30},{15,31},{22,6},{23,7},{30,14},{31,15}} | collective-permute-start | bytes 196616 | tf_op jit(solution)/shard_map/ppermute | solution.py:316
  50.1 1.4 %collective-permute-start.19 = (bf16[256,128]{1,0:T(8,128)(2,1)S(1)}, bf16[256,128]{1,0:T(8,128)(2,1)S(1)}, u32[]{:S(2)}, u32[]{:S(2)}) collective-permute-start(bf16[256,128]{1,0:T(8,128)(2,1)S(1)} %add_convert_fusion), channel_id=1, source_target_pairs={{6,7},{7,6},{14,15},{15,14},{22,23},{23,22},{30,31},{31,30}} | collective-permute-start | bytes 196616 | tf_op jit(solution)/shard_map/ppermute | solution.py:184
  51.6 4.1 %collective-permute-start.22 = (bf16[384,128]{1,0:T(8,128)(2,1)S(1)}, bf16[384,128]{1,0:T(8,128)(2,1)S(1)}, u32[]{:S(2)}, u32[]{:S(2)}) collective-permute-start(bf16[384,128]{1,0:T(8,128)(2,1)S(1)} %pad_maximum_fusion.20), channel_id=1, source_target_pairs={{6,0},{7,1},{14,8},{15,9},{22,16},{23,17},{30,24},{31,25}} | collective-permute-start | bytes 294920 | tf_op jit(solution)/shard_map/ppermute | solution.py:217
  52.3 3.5 %collective-permute-start.21 = (bf16[384,128]{1,0:T(8,128)(2,1)S(1)}, bf16[384,128]{1,0:T(8,128)(2,1)S(1)}, u32[]{:S(2)}, u32[]{:S(2)}) collective-permute-start(bf16[384,128]{1,0:T(8,128)(2,1)S(1)} %pad_maximum_fusion.20), channel_id=1, source_target_pairs={{6,2},{7,3},{14,10},{15,11},{22,18},{23,19},{30,26},{31,27}} | collective-permute-start | bytes 294920 | tf_op jit(solution)/shard_map/ppermute | solution.py:217
  52.9 10.1 %collective-permute-start.20 = (bf16[384,128]{1,0:T(8,128)(2,1)S(1)}, bf16[384,128]{1,0:T(8,128)(2,1)S(1)}, u32[]{:S(2)}, u32[]{:S(2)}) collective-permute-start(bf16[384,128]{1,0:T(8,128)(2,1)S(1)} %pad_maximum_fusion.20), channel_id=1, source_target_pairs={{6,4},{7,5},{14,12},{15,13},{22,20},{23,21},{30,28},{31,29}} | collective-permute-start | bytes 294920 | tf_op jit(solution)/shard_map/ppermute | solution.py:217
  55.5 11.2 %collective-permute-start.16 = (bf16[2,2,32,1024]{3,2,0,1:T(8,128)(2,1)S(1)}, bf16[2,2,32,1024]{3,2,0,1:T(8,128)(2,1)S(1)}, u32[]{:S(2)}, u32[]{:S(2)}) collective-permute-start(bf16[2,2,32,1024]{3,2,0,1:T(8,128)(2,1)S(1)} %select_bitcast_fusion), channel_id=1, source_target_pairs={{0,8},{8,0},{16,24},{24,16},{1,9},{9,1},{17,25},{25,17},{2,10},{10... | collective-permute-start | bytes 786440 | tf_op jit(solution)/shard_map/ppermute | solution.py:180
  66.9 5.0 %collective-permute-start.23 = (bf16[2,1,32,1024]{3,2,1,0:T(8,128)(2,1)S(1)}, bf16[2,1,32,1024]{3,2,1,0:T(8,128)(2,1)S(1)}, u32[]{:S(2)}, u32[]{:S(2)}) collective-permute-start(bf16[2,1,32,1024]{3,2,1,0:T(8,128)(2,1)S(1)} %fusion.29), channel_id=1, source_target_pairs={{0,16},{8,24},{16,0},{24,8},{1,17},{9,25},{17,1},{25,9},{2,18},{10... | collective-permute-start | bytes 393224 | tf_op jit(solution)/shard_map/ppermute | solution.py:180
  (21 other events, 172.3 us)

commit v14 on v13

--- a/solution.py
+++ b/solution.py
@@ -368,11 +368,12 @@
         keep = jnp.where(low, parts[:, :, 0], parts[:, :, 1])
         give = jnp.where(low, parts[:, :, 1], parts[:, :, 0])
         give = give.astype(BF16)
-        sent = give
+        if 2 * step >= row_count:
+            grad_trail = updated(both, start, grad_trail)
+            give = after(give, grad_trail[:16, :panel])
         parts = keep + row_swap(give, step).astype(F32)
         step *= 2
     parts = parts.reshape(2, band, width)
-    grad_trail = updated(after(both, sent), start, grad_trail)
 
     grad_diag_two = block_adjoint(
         diag_two, inverse_two, jnp.tril(adj_diag_two - after(diag_term_two, sums))

time: 74.1 us -> 73.7 us (level)
  the two profiles are of different devices: /device:TPU:20 before, /device:TPU:28 now
where the time goes in v14:
time: 73.7 us; the launch traced here: 73.3 us
  starting transfers between devices  33.7 us (46%)
  waiting for transfers between devices  21 us (28%)
  matrix products  7.2 us (10%)
  Pallas kernels  4.61 us (6%)
  local copies, waits for them, and re-layouts  2.6 us (4%)
  other arithmetic  2.45 us (3%)
  between operations  1.71 us (2%)
    ppermute x9, starting transfers between devices, hop(): return lax.ppermute(value, 'col', pairs)  12.6 us
    ppermute x6, waiting for transfers between devices, row_swap(): return lax.ppermute(value, 'row', [(i, i ^ step) for i in range(row_count)])  7.71 us
    ppermute x2, starting transfers between devices, per_device(): moved = lax.ppermute(terms, ('row', 'col'), pairs)  5.71 us
    ppermute x6, starting transfers between devices, row_swap(): return lax.ppermute(value, 'row', [(i, i ^ step) for i in range(row_count)])  5.29 us
    dot_general x10, matrix products, wide_dot(): return jnp.dot(a, b, preferred_element_type=F32)  4.91 us
    pallas_call x1, Pallas kernels, prepare(): pl.pallas_call(functools.partial(prepare_kernel, cuts), in_specs=[pl.Bloc...  4.61 us
    ppermute x2, starting transfers between devices, per_device(): lax.ppermute(packet, 'col', [(two_owner, one_owner)])  4.18 us
    ppermute x3, waiting for transfers between devices, pair_swap(): return lax.ppermute(value, 'col', pairs)  3.51 us
  transfers between devices with their start and end apart: 24, of which 7 were waited for; matrix products, arithmetic and copies ran while one was open for 13% of the time, Pallas kernels for 0%

profile of v14, /device:TPU:28, one launch (start us, length us, event | category | flops | bytes accessed | tf_op | source)
XLA Modules:
  0.0 73.3 jit_solution(6315155810786858209)
XLA Ops:
  0.7 4.6 %prepare.1 = (f32[128,128]{1,0:T(8,128)}, f32[128,128]{1,0:T(8,128)}, bf16[2048,128]{1,0:T(8,128)(2,1)}, bf16[1152,128]{1,0:T(8,128)(2,1)}, bf16[1152,128]{1,0:T(8,128)(2,1)}) custom-call(s32[1]{0:T(128)} %bitcast.side_ref, f32[128,128]{1,0:T(8,128)} %one_ref.1, f32[128,128]{1,0:T(8,128)} %two_ref.1, f32[2048,1024]{1,0:T(8,128)} %adj_ref.1), custom_call_target="tpu_custom_call" | custom-call | flops 268435456 | bytes 2097152 | tf_op jit(solution)/shard_map/prepare/pallas_call | solution.py:107
  5.3 2.6 %collective-permute-start.1 = (bf16[1152,128]{1,0:T(8,128)(2,1)}, bf16[1152,128]{1,0:T(8,128)(2,1)S(1)}, u32[]{:S(2)}, u32[]{:S(2)}) collective-permute-start(bf16[1152,128]{1,0:T(8,128)(2,1)} %get-tuple-element.26), channel_id=1, source_target_pairs={{7,6},{15,14},{23,22},{31,30}} | collective-permute-start | bytes 884744 | tf_op jit(solution)/shard_map/ppermute | solution.py:285
  7.9 1.3 %collective-permute-start = (bf16[1152,128]{1,0:T(8,128)(2,1)}, bf16[1152,128]{1,0:T(8,128)(2,1)S(1)}, u32[]{:S(2)}, u32[]{:S(2)}) collective-permute-start(bf16[1152,128]{1,0:T(8,128)(2,1)} %get-tuple-element.26), channel_id=1, source_target_pairs={{6,2},{7,3},{14,10},{15,11},{22,18},{23,19},{30,26},{31,27}} | collective-permute-start | bytes 884744 | tf_op jit(solution)/shard_map/ppermute | solution.py:217
  9.8 1.6 %collective-permute-start.3 = (bf16[1152,128]{1,0:T(8,128)(2,1)}, bf16[1152,128]{1,0:T(8,128)(2,1)S(1)}, u32[]{:S(2)}, u32[]{:S(2)}) collective-permute-start(bf16[1152,128]{1,0:T(8,128)(2,1)} %get-tuple-element.29), channel_id=1, source_target_pairs={{7,6},{15,14},{23,22},{31,30}} | collective-permute-start | bytes 884744 | tf_op jit(solution)/shard_map/ppermute | solution.py:285
  11.5 1.6 %collective-permute-start.7 = (bf16[1,2,32,1024]{3,2,1,0:T(8,128)(2,1)S(1)}, bf16[1,2,32,1024]{3,2,1,0:T(8,128)(2,1)S(1)}, u32[]{:S(2)}, u32[]{:S(2)}) collective-permute-start(bf16[1,2,32,1024]{3,2,1,0:T(8,128)(2,1)S(1)} %pad_maximum_fusion.21), channel_id=1, source_target_pairs={{0,16},{8,24},{16,0},{24,8},{1,17},{9,25},{17,1},{25,9},{2,18},{10... | collective-permute-start | bytes 393224 | tf_op jit(solution)/shard_map/ppermute | solution.py:180
  13.2 3.6 %collective-permute-done.7 = bf16[1,2,32,1024]{3,2,1,0:T(8,128)(2,1)S(1)} collective-permute-done((bf16[1,2,32,1024]{3,2,1,0:T(8,128)(2,1)S(1)}, bf16[1,2,32,1024]{3,2,1,0:T(8,128)(2,1)S(1)}, u32[]{:S(2)}, u32[]{:S(2)}) %collective-permute-start.7) | collective-permute-done | bytes 131104 | tf_op jit(solution)/shard_map/ppermute | solution.py:180
  16.9 1.3 %collective-permute-start.9 = (bf16[128,128]{1,0:T(8,128)(2,1)S(1)}, bf16[128,128]{1,0:T(8,128)(2,1)S(1)}, u32[]{:S(2)}, u32[]{:S(2)}) collective-permute-start(bf16[128,128]{1,0:T(8,128)(2,1)S(1)} %slice.123), channel_id=1, source_target_pairs={{6,7},{14,15},{22,23},{30,31}} | collective-permute-start | bytes 98312 | tf_op jit(solution)/shard_map/ppermute | solution.py:270
  18.2 1.6 %collective-permute-start.8 = (bf16[1,2,32,1024]{3,2,1,0:T(8,128)(2,1)S(1)}, bf16[1,2,32,1024]{3,2,1,0:T(8,128)(2,1)S(1)}, u32[]{:S(2)}, u32[]{:S(2)}) collective-permute-start(bf16[1,2,32,1024]{3,2,1,0:T(8,128)(2,1)S(1)} %pad_maximum_fusion.20), channel_id=1, source_target_pairs={{0,16},{8,24},{16,0},{24,8},{1,17},{9,25},{17,1},{25,9},{2,18},{10... | collective-permute-start | bytes 393224 | tf_op jit(solution)/shard_map/ppermute | solution.py:180
  19.9 2.8 %collective-permute-done.9 = bf16[128,128]{1,0:T(8,128)(2,1)S(1)} collective-permute-done((bf16[128,128]{1,0:T(8,128)(2,1)S(1)}, bf16[128,128]{1,0:T(8,128)(2,1)S(1)}, u32[]{:S(2)}, u32[]{:S(2)}) %collective-permute-start.9) | collective-permute-done | bytes 32800 | tf_op jit(solution)/shard_map/ppermute | solution.py:270
  24.8 1.3 %collective-permute-start.4 = (bf16[1152,128]{1,0:T(8,128)(2,1)S(1)}, bf16[1152,128]{1,0:T(8,128)(2,1)S(1)}, u32[]{:S(2)}, u32[]{:S(2)}) collective-permute-start(bf16[1152,128]{1,0:T(8,128)(2,1)S(1)} %broadcast_select_fusion.3), channel_id=1, source_target_pairs={{6,2},{7,3},{2,0},{3,1},{14,10},{15,11},{10,8},{11,9},{22,18},{23,... | collective-permute-start | bytes 884744 | tf_op jit(solution)/shard_map/ppermute | solution.py:217
  26.1 1.3 %collective-permute-start.2 = (bf16[2048,128]{1,0:T(8,128)(2,1)S(1)}, bf16[2048,128]{1,0:T(8,128)(2,1)S(1)}, u32[]{:S(2)}, u32[]{:S(2)}) collective-permute-start(bf16[2048,128]{1,0:T(8,128)(2,1)S(1)} %copy-done.5), channel_id=1, source_target_pairs={{6,7},{14,15},{22,23},{30,31}} | collective-permute-start | bytes 1572872 | tf_op jit(solution)/shard_map/ppermute | solution.py:289
  27.5 3.4 %collective-permute-done.4 = bf16[1152,128]{1,0:T(8,128)(2,1)S(1)} collective-permute-done((bf16[1152,128]{1,0:T(8,128)(2,1)S(1)}, bf16[1152,128]{1,0:T(8,128)(2,1)S(1)}, u32[]{:S(2)}, u32[]{:S(2)}) %collective-permute-start.4) | collective-permute-done | bytes 294944 | tf_op jit(solution)/shard_map/ppermute | solution.py:217
  35.4 2.3 %collective-permute-start.16 = (f32[256,128]{1,0:T(8,128)S(1)}, f32[256,128]{1,0:T(8,128)S(1)}, u32[]{:S(2)}, u32[]{:S(2)}) collective-permute-start(f32[256,128]{1,0:T(8,128)S(1)} %convolution_subtract_fusion.2), channel_id=1, source_target_pairs={{6,14},{7,15},{14,6},{15,7},{22,30},{23,31},{30,22},{31,23}} | collective-permute-start | bytes 393224 | tf_op jit(solution)/shard_map/ppermute | solution.py:316
  37.9 1.7 %collective-permute-done.2 = bf16[2048,128]{1,0:T(8,128)(2,1)S(1)} collective-permute-done((bf16[2048,128]{1,0:T(8,128)(2,1)S(1)}, bf16[2048,128]{1,0:T(8,128)(2,1)S(1)}, u32[]{:S(2)}, u32[]{:S(2)}) %collective-permute-start.2) | collective-permute-done | bytes 524320 | tf_op jit(solution)/shard_map/ppermute | solution.py:289
  40.1 3.4 %collective-permute-start.17 = (bf16[256,128]{1,0:T(8,128)(2,1)S(1)}, bf16[256,128]{1,0:T(8,128)(2,1)S(1)}, u32[]{:S(2)}, u32[]{:S(2)}) collective-permute-start(bf16[256,128]{1,0:T(8,128)(2,1)S(1)} %add_convert_fusion.1), channel_id=1, source_target_pairs={{6,22},{7,23},{14,30},{15,31},{22,6},{23,7},{30,14},{31,15}} | collective-permute-start | bytes 196616 | tf_op jit(solution)/shard_map/ppermute | solution.py:316
  44.3 2.0 %collective-permute-done.17 = bf16[256,128]{1,0:T(8,128)(2,1)S(1)} collective-permute-done((bf16[256,128]{1,0:T(8,128)(2,1)S(1)}, bf16[256,128]{1,0:T(8,128)(2,1)S(1)}, u32[]{:S(2)}, u32[]{:S(2)}) %collective-permute-start.17) | collective-permute-done | bytes 65568 | tf_op jit(solution)/shard_map/ppermute | solution.py:316
  46.3 1.9 %collective-permute-start.18 = (bf16[256,128]{1,0:T(8,128)(2,1)S(1)}, bf16[256,128]{1,0:T(8,128)(2,1)S(1)}, u32[]{:S(2)}, u32[]{:S(2)}) collective-permute-start(bf16[256,128]{1,0:T(8,128)(2,1)S(1)} %add_convert_fusion), channel_id=1, source_target_pairs={{6,7},{7,6},{14,15},{15,14},{22,23},{23,22},{30,31},{31,30}} | collective-permute-start | bytes 196616 | tf_op jit(solution)/shard_map/ppermute | solution.py:184
  49.0 3.5 %collective-permute-done.18 = bf16[256,128]{1,0:T(8,128)(2,1)S(1)} collective-permute-done((bf16[256,128]{1,0:T(8,128)(2,1)S(1)}, bf16[256,128]{1,0:T(8,128)(2,1)S(1)}, u32[]{:S(2)}, u32[]{:S(2)}) %collective-permute-start.18) | collective-permute-done | bytes 65568 | tf_op jit(solution)/shard_map/ppermute | solution.py:184
  52.5 1.3 %collective-permute-start.21 = (bf16[384,128]{1,0:T(8,128)(2,1)S(1)}, bf16[384,128]{1,0:T(8,128)(2,1)S(1)}, u32[]{:S(2)}, u32[]{:S(2)}) collective-permute-start(bf16[384,128]{1,0:T(8,128)(2,1)S(1)} %pad_maximum_fusion.22), channel_id=1, source_target_pairs={{6,0},{7,1},{14,8},{15,9},{22,16},{23,17},{30,24},{31,25}} | collective-permute-start | bytes 294920 | tf_op jit(solution)/shard_map/ppermute | solution.py:217
  53.8 3.8 %collective-permute-start.20 = (bf16[384,128]{1,0:T(8,128)(2,1)S(1)}, bf16[384,128]{1,0:T(8,128)(2,1)S(1)}, u32[]{:S(2)}, u32[]{:S(2)}) collective-permute-start(bf16[384,128]{1,0:T(8,128)(2,1)S(1)} %pad_maximum_fusion.22), channel_id=1, source_target_pairs={{6,2},{7,3},{14,10},{15,11},{22,18},{23,19},{30,26},{31,27}} | collective-permute-start | bytes 294920 | tf_op jit(solution)/shard_map/ppermute | solution.py:217
  57.6 1.3 %collective-permute-start.19 = (bf16[384,128]{1,0:T(8,128)(2,1)S(1)}, bf16[384,128]{1,0:T(8,128)(2,1)S(1)}, u32[]{:S(2)}, u32[]{:S(2)}) collective-permute-start(bf16[384,128]{1,0:T(8,128)(2,1)S(1)} %pad_maximum_fusion.22), channel_id=1, source_target_pairs={{6,4},{7,5},{14,12},{15,13},{22,20},{23,21},{30,28},{31,29}} | collective-permute-start | bytes 294920 | tf_op jit(solution)/shard_map/ppermute | solution.py:217
  61.0 2.0 %copy-done.2 = bf16[2048,1024]{1,0:T(8,128)(2,1)} copy-done((bf16[2048,1024]{1,0:T(8,128)(2,1)}, bf16[2048,1024]{1,0:T(8,128)(2,1)S(1)}, u32[]{:S(2)}) %copy-start.2) | copy-done | bytes 4194328
  66.6 1.6 %collective-permute-start.23 = (bf16[2,1,32,1024]{3,2,1,0:T(8,128)(2,1)S(1)}, bf16[2,1,32,1024]{3,2,1,0:T(8,128)(2,1)S(1)}, u32[]{:S(2)}, u32[]{:S(2)}) collective-permute-start(bf16[2,1,32,1024]{3,2,1,0:T(8,128)(2,1)S(1)} %fusion.29), channel_id=1, source_target_pairs={{0,16},{8,24},{16,0},{24,8},{1,17},{9,25},{17,1},{25,9},{2,18},{10... | collective-permute-start | bytes 393224 | tf_op jit(solution)/shard_map/ppermute | solution.py:180
  68.4 4.1 %collective-permute-done.23 = bf16[2,1,32,1024]{3,2,1,0:T(8,128)(2,1)S(1)} collective-permute-done((bf16[2,1,32,1024]{3,2,1,0:T(8,128)(2,1)S(1)}, bf16[2,1,32,1024]{3,2,1,0:T(8,128)(2,1)S(1)}, u32[]{:S(2)}, u32[]{:S(2)}) %collective-permute-start.23) | collective-permute-done | bytes 131104 | tf_op jit(solution)/shard_map/ppermute | solution.py:180
  (138 shorter events, 16.0 us)
Async XLA Ops:
  5.3 18.7 %collective-permute-start.1 = (bf16[1152,128]{1,0:T(8,128)(2,1)}, bf16[1152,128]{1,0:T(8,128)(2,1)S(1)}, u32[]{:S(2)}, u32[]{:S(2)}) collective-permute-start(bf16[1152,128]{1,0:T(8,128)(2,1)} %get-tuple-element.26), channel_id=1, source_target_pairs={{7,6},{15,14},{23,22},{31,30}} | collective-permute-start | bytes 884744 | tf_op jit(solution)/shard_map/ppermute | solution.py:285
  7.9 16.2 %collective-permute-start = (bf16[1152,128]{1,0:T(8,128)(2,1)}, bf16[1152,128]{1,0:T(8,128)(2,1)S(1)}, u32[]{:S(2)}, u32[]{:S(2)}) collective-permute-start(bf16[1152,128]{1,0:T(8,128)(2,1)} %get-tuple-element.26), channel_id=1, source_target_pairs={{6,2},{7,3},{14,10},{15,11},{22,18},{23,19},{30,26},{31,27}} | collective-permute-start | bytes 884744 | tf_op jit(solution)/shard_map/ppermute | solution.py:217
  9.2 2.3 %collective-permute-start.6 = (bf16[1,1,32,1024]{3,2,1,0:T(8,128)(2,1)S(1)}, bf16[1,1,32,1024]{3,2,1,0:T(8,128)(2,1)S(1)}, u32[]{:S(2)}, u32[]{:S(2)}) collective-permute-start(bf16[1,1,32,1024]{3,2,1,0:T(8,128)(2,1)S(1)} %bitcast.81), channel_id=1, source_target_pairs={{0,8},{8,0},{16,24},{24,16},{1,9},{9,1},{17,25},{25,17},{2,10},{10... | collective-permute-start | bytes 196616 | tf_op jit(solution)/shard_map/ppermute | solution.py:180
  9.3 2.2 %collective-permute-start.5 = (bf16[1,1,32,1024]{3,2,1,0:T(8,128)(2,1)S(1)}, bf16[1,1,32,1024]{3,2,1,0:T(8,128)(2,1)S(1)}, u32[]{:S(2)}, u32[]{:S(2)}) collective-permute-start(bf16[1,1,32,1024]{3,2,1,0:T(8,128)(2,1)S(1)} %bitcast.82), channel_id=1, source_target_pairs={{0,8},{8,0},{16,24},{24,16},{1,9},{9,1},{17,25},{25,17},{2,10},{10... | collective-permute-start | bytes 196616 | tf_op jit(solution)/shard_map/ppermute | solution.py:180
  9.8 16.3 %collective-permute-start.3 = (bf16[1152,128]{1,0:T(8,128)(2,1)}, bf16[1152,128]{1,0:T(8,128)(2,1)S(1)}, u32[]{:S(2)}, u32[]{:S(2)}) collective-permute-start(bf16[1152,128]{1,0:T(8,128)(2,1)} %get-tuple-element.29), channel_id=1, source_target_pairs={{7,6},{15,14},{23,22},{31,30}} | collective-permute-start | bytes 884744 | tf_op jit(solution)/shard_map/ppermute | solution.py:285
  11.5 5.3 %collective-permute-start.7 = (bf16[1,2,32,1024]{3,2,1,0:T(8,128)(2,1)S(1)}, bf16[1,2,32,1024]{3,2,1,0:T(8,128)(2,1)S(1)}, u32[]{:S(2)}, u32[]{:S(2)}) collective-permute-start(bf16[1,2,32,1024]{3,2,1,0:T(8,128)(2,1)S(1)} %pad_maximum_fusion.21), channel_id=1, source_target_pairs={{0,16},{8,24},{16,0},{24,8},{1,17},{9,25},{17,1},{25,9},{2,18},{10... | collective-permute-start | bytes 393224 | tf_op jit(solution)/shard_map/ppermute | solution.py:180
  16.9 5.8 %collective-permute-start.9 = (bf16[128,128]{1,0:T(8,128)(2,1)S(1)}, bf16[128,128]{1,0:T(8,128)(2,1)S(1)}, u32[]{:S(2)}, u32[]{:S(2)}) collective-permute-start(bf16[128,128]{1,0:T(8,128)(2,1)S(1)} %slice.123), channel_id=1, source_target_pairs={{6,7},{14,15},{22,23},{30,31}} | collective-permute-start | bytes 98312 | tf_op jit(solution)/shard_map/ppermute | solution.py:270
  18.2 9.3 %collective-permute-start.8 = (bf16[1,2,32,1024]{3,2,1,0:T(8,128)(2,1)S(1)}, bf16[1,2,32,1024]{3,2,1,0:T(8,128)(2,1)S(1)}, u32[]{:S(2)}, u32[]{:S(2)}) collective-permute-start(bf16[1,2,32,1024]{3,2,1,0:T(8,128)(2,1)S(1)} %pad_maximum_fusion.20), channel_id=1, source_target_pairs={{0,16},{8,24},{16,0},{24,8},{1,17},{9,25},{17,1},{25,9},{2,18},{10... | collective-permute-start | bytes 393224 | tf_op jit(solution)/shard_map/ppermute | solution.py:180
  22.7 8.3 %collective-permute-start.10 = (bf16[128,128]{1,0:T(8,128)(2,1)S(1)}, bf16[128,128]{1,0:T(8,128)(2,1)S(1)}, u32[]{:S(2)}, u32[]{:S(2)}) collective-permute-start(bf16[128,128]{1,0:T(8,128)(2,1)S(1)} %broadcast_select_fusion.17), channel_id=1, source_target_pairs={{6,2},{7,3},{14,10},{15,11},{22,18},{23,19},{30,26},{31,27}} | collective-permute-start | bytes 98312 | tf_op jit(solution)/shard_map/ppermute | solution.py:217
  24.0 6.9 %collective-permute-start.12 = (bf16[1152,128]{1,0:T(8,128)(2,1)S(1)}, bf16[1152,128]{1,0:T(8,128)(2,1)S(1)}, u32[]{:S(2)}, u32[]{:S(2)}) collective-permute-start(bf16[1152,128]{1,0:T(8,128)(2,1)S(1)} %collective-permute-done), channel_id=1, source_target_pairs={{2,4},{3,5},{10,12},{11,13},{18,20},{19,21},{26,28},{27,29}} | collective-permute-start | bytes 884744 | tf_op jit(solution)/shard_map/ppermute | solution.py:217
  24.8 6.1 %collective-permute-start.4 = (bf16[1152,128]{1,0:T(8,128)(2,1)S(1)}, bf16[1152,128]{1,0:T(8,128)(2,1)S(1)}, u32[]{:S(2)}, u32[]{:S(2)}) collective-permute-start(bf16[1152,128]{1,0:T(8,128)(2,1)S(1)} %broadcast_select_fusion.3), channel_id=1, source_target_pairs={{6,2},{7,3},{2,0},{3,1},{14,10},{15,11},{10,8},{11,9},{22,18},{23,... | collective-permute-start | bytes 884744 | tf_op jit(solution)/shard_map/ppermute | solution.py:217
  26.1 13.5 %collective-permute-start.2 = (bf16[2048,128]{1,0:T(8,128)(2,1)S(1)}, bf16[2048,128]{1,0:T(8,128)(2,1)S(1)}, u32[]{:S(2)}, u32[]{:S(2)}) collective-permute-start(bf16[2048,128]{1,0:T(8,128)(2,1)S(1)} %copy-done.5), channel_id=1, source_target_pairs={{6,7},{14,15},{22,23},{30,31}} | collective-permute-start | bytes 1572872 | tf_op jit(solution)/shard_map/ppermute | solution.py:289
  31.0 2.4 %collective-permute-start.13 = (bf16[1152,128]{1,0:T(8,128)(2,1)S(1)}, bf16[1152,128]{1,0:T(8,128)(2,1)S(1)}, u32[]{:S(2)}, u32[]{:S(2)}) collective-permute-start(bf16[1152,128]{1,0:T(8,128)(2,1)S(1)} %constant_dynamic-update-slice_fusion), channel_id=1, source_target_pairs={{2,0},{3,1},{10,8},{11,9},{18,16},{19,17},{26,24},{27,25}} | collective-permute-start | bytes 884744 | tf_op jit(solution)/shard_map/ppermute | solution.py:217
  31.8 1.6 %collective-permute-start.11 = (bf16[1152,128]{1,0:T(8,128)(2,1)S(1)}, bf16[1152,128]{1,0:T(8,128)(2,1)S(1)}, u32[]{:S(2)}, u32[]{:S(2)}) collective-permute-start(bf16[1152,128]{1,0:T(8,128)(2,1)S(1)} %constant_dynamic-update-slice_fusion), channel_id=1, source_target_pairs={{2,4},{3,5},{10,12},{11,13},{18,20},{19,21},{26,28},{27,29}} | collective-permute-start | bytes 884744 | tf_op jit(solution)/shard_map/ppermute | solution.py:217
  32.7 1.7 %collective-permute-start.14 = (bf16[1152,128]{1,0:T(8,128)(2,1)S(1)}, bf16[1152,128]{1,0:T(8,128)(2,1)S(1)}, u32[]{:S(2)}, u32[]{:S(2)}) collective-permute-start(bf16[1152,128]{1,0:T(8,128)(2,1)S(1)} %select_select_fusion.1), channel_id=1, source_target_pairs={{0,1},{1,0},{2,3},{3,2},{4,5},{5,4},{8,9},{9,8},{10,11},{11,10},{1... | collective-permute-start | bytes 884744 | tf_op jit(solution)/shard_map/ppermute | solution.py:184
  33.5 25.4 %collective-permute-start.15 = (bf16[1152,128]{1,0:T(8,128)(2,1)S(1)}, bf16[1152,128]{1,0:T(8,128)(2,1)S(1)}, u32[]{:S(2)}, u32[]{:S(2)}) collective-permute-start(bf16[1152,128]{1,0:T(8,128)(2,1)S(1)} %get-tuple-element.50), channel_id=1, source_target_pairs={{0,1},{1,0},{2,3},{3,2},{4,5},{5,4},{8,9},{9,8},{10,11},{11,10},{1... | collective-permute-start | bytes 884744 | tf_op jit(solution)/shard_map/ppermute | solution.py:184
  35.4 4.7 %collective-permute-start.16 = (f32[256,128]{1,0:T(8,128)S(1)}, f32[256,128]{1,0:T(8,128)S(1)}, u32[]{:S(2)}, u32[]{:S(2)}) collective-permute-start(f32[256,128]{1,0:T(8,128)S(1)} %convolution_subtract_fusion.2), channel_id=1, source_target_pairs={{6,14},{7,15},{14,6},{15,7},{22,30},{23,31},{30,22},{31,23}} | collective-permute-start | bytes 393224 | tf_op jit(solution)/shard_map/ppermute | solution.py:316
  40.1 6.2 %collective-permute-start.17 = (bf16[256,128]{1,0:T(8,128)(2,1)S(1)}, bf16[256,128]{1,0:T(8,128)(2,1)S(1)}, u32[]{:S(2)}, u32[]{:S(2)}) collective-permute-start(bf16[256,128]{1,0:T(8,128)(2,1)S(1)} %add_convert_fusion.1), channel_id=1, source_target_pairs={{6,22},{7,23},{14,30},{15,31},{22,6},{23,7},{30,14},{31,15}} | collective-permute-start | bytes 196616 | tf_op jit(solution)/shard_map/ppermute | solution.py:316
  46.3 6.2 %collective-permute-start.18 = (bf16[256,128]{1,0:T(8,128)(2,1)S(1)}, bf16[256,128]{1,0:T(8,128)(2,1)S(1)}, u32[]{:S(2)}, u32[]{:S(2)}) collective-permute-start(bf16[256,128]{1,0:T(8,128)(2,1)S(1)} %add_convert_fusion), channel_id=1, source_target_pairs={{6,7},{7,6},{14,15},{15,14},{22,23},{23,22},{30,31},{31,30}} | collective-permute-start | bytes 196616 | tf_op jit(solution)/shard_map/ppermute | solution.py:184
  52.5 10.5 %collective-permute-start.21 = (bf16[384,128]{1,0:T(8,128)(2,1)S(1)}, bf16[384,128]{1,0:T(8,128)(2,1)S(1)}, u32[]{:S(2)}, u32[]{:S(2)}) collective-permute-start(bf16[384,128]{1,0:T(8,128)(2,1)S(1)} %pad_maximum_fusion.22), channel_id=1, source_target_pairs={{6,0},{7,1},{14,8},{15,9},{22,16},{23,17},{30,24},{31,25}} | collective-permute-start | bytes 294920 | tf_op jit(solution)/shard_map/ppermute | solution.py:217
  53.8 9.2 %collective-permute-start.20 = (bf16[384,128]{1,0:T(8,128)(2,1)S(1)}, bf16[384,128]{1,0:T(8,128)(2,1)S(1)}, u32[]{:S(2)}, u32[]{:S(2)}) collective-permute-start(bf16[384,128]{1,0:T(8,128)(2,1)S(1)} %pad_maximum_fusion.22), channel_id=1, source_target_pairs={{6,2},{7,3},{14,10},{15,11},{22,18},{23,19},{30,26},{31,27}} | collective-permute-start | bytes 294920 | tf_op jit(solution)/shard_map/ppermute | solution.py:217
  57.6 5.4 %collective-permute-start.19 = (bf16[384,128]{1,0:T(8,128)(2,1)S(1)}, bf16[384,128]{1,0:T(8,128)(2,1)S(1)}, u32[]{:S(2)}, u32[]{:S(2)}) collective-permute-start(bf16[384,128]{1,0:T(8,128)(2,1)S(1)} %pad_maximum_fusion.22), channel_id=1, source_target_pairs={{6,4},{7,5},{14,12},{15,13},{22,20},{23,21},{30,28},{31,29}} | collective-permute-start | bytes 294920 | tf_op jit(solution)/shard_map/ppermute | solution.py:217
  60.1 6.3 %collective-permute-start.22 = (bf16[2,2,32,1024]{3,2,0,1:T(8,128)(2,1)S(1)}, bf16[2,2,32,1024]{3,2,0,1:T(8,128)(2,1)S(1)}, u32[]{:S(2)}, u32[]{:S(2)}) collective-permute-start(bf16[2,2,32,1024]{3,2,0,1:T(8,128)(2,1)S(1)} %select_bitcast_fusion), channel_id=1, source_target_pairs={{0,8},{8,0},{16,24},{24,16},{1,9},{9,1},{17,25},{25,17},{2,10},{10... | collective-permute-start | bytes 786440 | tf_op jit(solution)/shard_map/ppermute | solution.py:180
  66.6 5.9 %collective-permute-start.23 = (bf16[2,1,32,1024]{3,2,1,0:T(8,128)(2,1)S(1)}, bf16[2,1,32,1024]{3,2,1,0:T(8,128)(2,1)S(1)}, u32[]{:S(2)}, u32[]{:S(2)}) collective-permute-start(bf16[2,1,32,1024]{3,2,1,0:T(8,128)(2,1)S(1)} %fusion.29), channel_id=1, source_target_pairs={{0,16},{8,24},{16,0},{24,8},{1,17},{9,25},{17,1},{25,9},{2,18},{10... | collective-permute-start | bytes 393224 | tf_op jit(solution)/shard_map/ppermute | solution.py:180
  (19 other events, 164.8 us)
